TPU v7x, 32 devices: a whole 2x2x4 slice. The times are simulated.
32 devices in a mesh: aa: 4 (over y, core), ba: 8 (over z, x).
Axes of the slice: x: 2, y: 2, z: 4, core: 2. Of those that a mesh axis runs over, the one named last changes fastest.
Arguments:
- grid_nodes: bfloat16 [32768, 512], P(('aa', 'ba')), may hold values from -6 to 6
- mesh_nodes: bfloat16 [6144, 512], P(('aa', 'ba')), may hold values from -6 to 6
- owned_nodes: int32 [32], P(('aa', 'ba')), may hold values from 96 to 192, as said below
- grid_rim: int32 [32, 8, 128], P(('aa', 'ba')), may hold values from 0 to 1023
- mesh_rim: int32 [32, 8, 16], P(('aa', 'ba')), may hold values from 0 to 95
- long_send: int32 [32, 32, 8], P(('aa', 'ba')), may hold values from 0 to 15
- g2m_edges: int32 [32, 2, 3072], P(('aa', 'ba')), may hold values from 0 to 2047, as said below
- short_edges: int32 [32, 2, 1536], P(('aa', 'ba')), may hold values from 0 to 319, as said below
- long_edges: int32 [32, 2, 1536], P(('aa', 'ba')), may hold values from 0 to 447, as said below
- m2g_edges: int32 [32, 3, 1024], P(('aa', 'ba')), may hold values from 0 to 319, as said below
- edge_first: bfloat16 [4, 2, 512, 512], replicated, may hold values from -0.1875 to 0.1875
- edge_second: bfloat16 [4, 512, 512], replicated, may hold values from -0.25 to 0.25
- edge_bias: float32 [4, 512], replicated, may hold values from -3 to 3
- edge_gain: float32 [4, 512], replicated, may hold values from 0.5 to 2
- node_first: bfloat16 [4, 2, 512, 512], replicated, may hold values from -0.1875 to 0.1875
- node_second: bfloat16 [4, 512, 512], replicated, may hold values from -0.25 to 0.25
- node_bias: float32 [4, 512], replicated, may hold values from -3 to 3
- node_gain: float32 [4, 512], replicated, may hold values from 0.5 to 2
Outputs:
- grid_out: bfloat16 [32768, 512], P(('aa', 'ba'))
- mesh_out: bfloat16 [6144, 512], P(('aa', 'ba'))
Inputs may be any that keep to these rules, and one draw needn't show every extreme that they name: `owned_nodes`: some device owns 192 nodes in every draw. `g2m_edges`: row 0 holds senders, row 1 receivers. On device d the first 16 * owned_nodes[d] slots are used, with receivers below owned_nodes[d]; the others have receiver 192. Senders at or above 1024 never name a direction with a_k = -1 on band i = 0 or a_k = 1 on band i = 3. `short_edges`: row 0 holds senders, row 1 receivers. On device d the first 8 * owned_nodes[d] slots are used, with receivers below owned_nodes[d]; the others have receiver 192. Senders below 192 are below owned_nodes[d]; senders at or above 192 never name a direction with a_k = -1 on band 0 or a_k = 1 on band 4 - 1. `long_edges`: row 0 holds senders, row 1 receivers. On device d the first 8 * owned_nodes[d] slots are used, with receivers below owned_nodes[d]; the others have receiver 192. Senders below 192 are below owned_nodes[d]. `m2g_edges`: senders below 192 are below owned_nodes[d]; senders at or above 192 never name a direction with a_k = -1 on band 0 or a_k = 1 on band 4 - 1.
All inputs are finite; a program needn't handle non-finite values.
Results may differ from a plain program's by a relative error of at most 0.013.
Values may be sent and summed in bfloat16 or wider, within the bound.
No kernel may reach another device: no remote copies, remote signals or barrier semaphores. Data moves between devices by JAX's collectives and lax.ppermute only.
A program may use at most 128 MiB of HBM per device.

v0:
```python
import math

import jax
import jax.numpy as jnp
from jax import lax
from jax.sharding import PartitionSpec as P

EPSILON = 1e-05
RIM_PICKS = (0, 2, 4, 10, 14, 20, 22, 24)


def extended_2(value, sides, width):
    for axis, dim in sides:
        count, length = (lax.axis_size(axis), value.shape[dim])
        up = [(i, (i + 1) % count) for i in range(count)]
        down = [(j, i) for i, j in up]
        last = lax.slice_in_dim(value, length - width, length, axis=dim)
        initial = lax.slice_in_dim(value, 0, width, axis=dim)
        before = lax.ppermute(last, axis, up)
        after = lax.ppermute(initial, axis, down)
        value = jnp.concatenate([before, value, after], axis=dim)
    return value


def layer_norm(values, norm_gain):
    average = jnp.mean(values, axis=-1, keepdims=True)
    centred = values - average
    spread = jnp.mean(centred * centred, axis=-1, keepdims=True)
    return centred * lax.rsqrt(spread + EPSILON) * norm_gain


def pick_rows(table, row_ids):
    total = row_ids.shape[0]
    block = math.gcd(total, 512)
    blocked_ids = row_ids.reshape(total // block, block)
    table_rows = table.shape[0]

    def one_block(block_ids):
        member = block_ids[:, None] == lax.broadcasted_iota(jnp.int32, (block, table_rows), 1)
        if table.dtype == jnp.float32:
            return jnp.dot(
                member.astype(jnp.float32),
                table,
                precision=lax.Precision.HIGHEST,
                preferred_element_type=jnp.float32,
            )
        return jnp.dot(
            member.astype(table.dtype), table, preferred_element_type=jnp.float32
        ).astype(table.dtype)

    picked = lax.map(one_block, blocked_ids)
    return picked.reshape(total, table.shape[1])


def rim_blocks(projected, rim_rows):
    feature_count = projected.shape[1]
    block_depth = rim_rows.shape[1]
    picked = pick_rows(projected, rim_rows.reshape(-1)).reshape(8, block_depth, feature_count)
    centre = jnp.zeros((1, block_depth, feature_count), projected.dtype)
    stacked = jnp.concatenate([picked[:4], centre, picked[4:]], 0)
    return stacked.reshape(3, 3, block_depth, feature_count)


def rim_sources(extended):
    flattened = extended.reshape((25,) + extended.shape[2:])
    chosen = [flattened[position] for position in RIM_PICKS]
    return jnp.concatenate(chosen, 0)


def messages(gathered, target_proj, biases, second, norm_gain):
    hidden = jax.nn.silu(gathered.astype(jnp.float32) + target_proj + biases).astype(jnp.bfloat16)
    result = jnp.dot(hidden, second, preferred_element_type=jnp.float32)
    return layer_norm(result, norm_gain).astype(jnp.bfloat16)


def node_update(node_rows, totals, first_layer, biases, second, norm_gain):
    summed_input = jnp.dot(node_rows, first_layer[0], preferred_element_type=jnp.float32)
    summed_input = (
        summed_input
        + jnp.dot(totals.astype(jnp.bfloat16), first_layer[1], preferred_element_type=jnp.float32)
        + biases
    )
    hidden = jax.nn.silu(summed_input).astype(jnp.bfloat16)
    result = jnp.dot(hidden, second, preferred_element_type=jnp.float32)
    return (node_rows.astype(jnp.float32) + layer_norm(result, norm_gain)).astype(jnp.bfloat16)


def mesh_round(source_table, node_rows, edge_list, weights, section_index):
    edge_first, edge_second, edge_bias, edge_gain, node_first, node_second, node_bias, node_gain = (
        weights
    )
    senders = edge_list[0, 0]
    targets = edge_list[0, 1]
    slot_count = node_rows.shape[0]
    target_proj = jnp.dot(
        node_rows, edge_first[section_index, 1], preferred_element_type=jnp.float32
    )
    picked = pick_rows(target_proj, jnp.minimum(targets, slot_count - 1))
    gathered = pick_rows(source_table, senders)
    message_rows = messages(
        gathered,
        picked,
        edge_bias[section_index],
        edge_second[section_index],
        edge_gain[section_index],
    )
    member = lax.broadcasted_iota(jnp.int32, (slot_count, targets.shape[0]), 0) == targets[None, :]
    totals = jnp.dot(member.astype(jnp.bfloat16), message_rows, preferred_element_type=jnp.float32)
    return node_update(
        node_rows,
        totals,
        node_first[section_index],
        node_bias[section_index],
        node_second[section_index],
        node_gain[section_index],
    )


def per_device(
    grid_nodes,
    mesh_nodes,
    owned_nodes,
    grid_rim,
    mesh_rim,
    long_send,
    g2m_edges,
    short_edges,
    long_edges,
    m2g_edges,
    edge_first,
    edge_second,
    edge_bias,
    edge_gain,
    node_first,
    node_second,
    node_bias,
    node_gain,
):
    weights = (
        edge_first,
        edge_second,
        edge_bias,
        edge_gain,
        node_first,
        node_second,
        node_bias,
        node_gain,
    )
    grid_proj = jnp.dot(grid_nodes, edge_first[0, 0], preferred_element_type=jnp.float32).astype(
        jnp.bfloat16
    )
    grid_extended = extended_2(rim_blocks(grid_proj, grid_rim[0]), (("aa", 0), ("ba", 1)), 1)
    source_table = jnp.concatenate([grid_proj, rim_sources(grid_extended)], 0)
    mesh_one = mesh_round(source_table, mesh_nodes, g2m_edges, weights, 0)
    short_proj = jnp.dot(mesh_one, edge_first[1, 0], preferred_element_type=jnp.float32).astype(
        jnp.bfloat16
    )
    short_extended = extended_2(rim_blocks(short_proj, mesh_rim[0]), (("aa", 0), ("ba", 1)), 1)
    source_table = jnp.concatenate([short_proj, rim_sources(short_extended)], 0)
    mesh_two = mesh_round(source_table, mesh_one, short_edges, weights, 1)
    long_proj = jnp.dot(mesh_two, edge_first[2, 0], preferred_element_type=jnp.float32).astype(
        jnp.bfloat16
    )
    send_lists = long_send[0]
    peer_count = send_lists.shape[0]
    list_depth = send_lists.shape[1]
    feature_count = long_proj.shape[1]
    outgoing = pick_rows(long_proj, send_lists.reshape(-1)).reshape(
        peer_count, list_depth, feature_count
    )
    incoming = lax.all_to_all(outgoing, ("aa", "ba"), split_axis=0, concat_axis=0, tiled=True)
    incoming = incoming.reshape(peer_count * list_depth, feature_count)
    source_table = jnp.concatenate([long_proj, incoming], 0)
    mesh_three = mesh_round(source_table, mesh_two, long_edges, weights, 2)
    decode_proj = jnp.dot(mesh_three, edge_first[3, 0], preferred_element_type=jnp.float32).astype(
        jnp.bfloat16
    )
    decode_extended = extended_2(rim_blocks(decode_proj, mesh_rim[0]), (("aa", 0), ("ba", 1)), 1)
    source_table = jnp.concatenate([decode_proj, rim_sources(decode_extended)], 0)
    grid_target = jnp.dot(grid_nodes, edge_first[3, 1], preferred_element_type=jnp.float32)
    grid_count = grid_nodes.shape[0]
    gathered = pick_rows(source_table, m2g_edges[0].reshape(-1))
    repeated = jnp.concatenate([grid_target, grid_target, grid_target], 0)
    message_rows = messages(gathered, repeated, edge_bias[3], edge_second[3], edge_gain[3])
    message_rows = message_rows.reshape(3, grid_count, feature_count)
    totals = jnp.sum(message_rows.astype(jnp.float32), axis=0)
    grid_out = node_update(
        grid_nodes, totals, node_first[3], node_bias[3], node_second[3], node_gain[3]
    )
    alive_rows = lax.broadcasted_iota(jnp.int32, (mesh_three.shape[0], 1), 0) < owned_nodes[0]
    mesh_out = jnp.where(alive_rows, mesh_three, jnp.zeros_like(mesh_three))
    return (grid_out, mesh_out)


def solution(mesh):
    in_specs = (
        P(("aa", "ba"), None),
        P(("aa", "ba"), None),
        P(("aa", "ba")),
        P(("aa", "ba"), None, None),
        P(("aa", "ba"), None, None),
        P(("aa", "ba"), None, None),
        P(("aa", "ba"), None, None),
        P(("aa", "ba"), None, None),
        P(("aa", "ba"), None, None),
        P(("aa", "ba"), None, None),
        P(),
        P(),
        P(),
        P(),
        P(),
        P(),
        P(),
        P(),
    )
    out_specs = (P(("aa", "ba"), None), P(("aa", "ba"), None))
    return jax.shard_map(
        per_device, mesh=mesh, in_specs=in_specs, out_specs=out_specs, check_vma=False
    )
```

profile of v0, /device:TPU:0, one launch (start us, length us, event | category | flops | bytes accessed | tf_op | source)
XLA Modules:
  0.0 229.8 jit_solution(2598636741590396922)
XLA Ops:
  1.3 3.1 %constant_dynamic-update-slice_fusion = (bf16[2048,512]{1,0:T(8,128)(2,1)}, bf16[1024,512]{1,0:T(8,128)(2,1)S(1)}) fusion(bf16[1024,512]{1,0:T(8,128)(2,1)} %param.34, bf16[4,2,512,512]{3,2,1,0:T(8,128)(2,1)} %param.44), kind=kOutput, calls=%fused_computation.208 | convolution fusion | flops 537395200 | bytes 3670016 | tf_op jit(solution)/shard_map/dot_general | solution.py:149
  11.5 9.8 %while.94 = (s32[]{:T(128)}, f32[6,512,512]{2,1,0:T(8,128)}, s32[6,512]{1,0:T(8,128)S(1)}, f32[192,512]{1,0:T(8,128)S(1)}, s32[]{:T(128)}) while((s32[]{:T(128)}, f32[6,512,512]{2,1,0:T(8,128)}, s32[6,512]{1,0:T(8,128)S(1)}, f32[192,512]{1,0:T(8,128)S(1)}, s32[]{:T(128)}) %tuple.160), condition=%wide.region_5.6_spmd, body=%wide.region_4.5_spmd.sunk | while | flops 604078080 | bytes 1448513 | solution.py:51
  33.5 3.0 %collective-permute-start.3 = (bf16[5,1,128,512]{3,2,1,0:T(8,128)(2,1)}, bf16[5,1,128,512]{3,2,1,0:T(8,128)(2,1)}, u32[]{:S(2)}, u32[]{:S(2)}) collective-permute-start(bf16[5,1,128,512]{3,2,1,0:T(8,128)(2,1)} %get-tuple-element.301), channel_id=1, source_target_pairs={{1,0},{2,1},{3,2},{4,3},{5,4},{6,5},{7,6},{0,7},{9,8},{10,9},{11,1... | collective-permute-start | bytes 1966088 | tf_op jit(solution)/shard_map/ppermute | solution.py:20
  40.9 3.5 %pad_maximum_fusion = f32[3072,512]{1,0:T(8,128)} fusion(f32[1024,512]{1,0:T(8,128)S(1)} %fusion.54), kind=kLoop, calls=%fused_computation.47 | loop fusion | flops 3145728 | bytes 8388608 | tf_op jit(solution)/shard_map/concatenate | solution.py:183
  44.4 17.5 %collective-permute-done.2 = bf16[5,1,128,512]{3,2,1,0:T(8,128)(2,1)} collective-permute-done((bf16[5,1,128,512]{3,2,1,0:T(8,128)(2,1)}, bf16[5,1,128,512]{3,2,1,0:T(8,128)(2,1)}, u32[]{:S(2)}, u32[]{:S(2)}) %collective-permute-start.2) | collective-permute-done | bytes 655392 | tf_op jit(solution)/shard_map/ppermute | solution.py:19
  71.5 17.5 %while.93 = (s32[]{:T(128)}, bf16[6,512,512]{2,1,0:T(8,128)(2,1)S(1)}, s32[6,512]{1,0:T(8,128)S(1)}, bf16[2048,512]{1,0:T(8,128)(2,1)}, s32[]{:T(128)}) while((s32[]{:T(128)}, bf16[6,512,512]{2,1,0:T(8,128)(2,1)S(1)}, s32[6,512]{1,0:T(8,128)S(1)}, bf16[2048,512]{1,0:T(8,128)(2,1)}, s32[]{:T(128)}) %tuple.166), condition=%wide.region_3.4_spmd, body=%wide.region_2.3_spmd.sunk | while | flops 1075052544 | bytes 2627653 | solution.py:51
  71.5 2.9 %fusion.202 = bf16[6,512,512]{2,1,0:T(8,128)(2,1)S(1)} fusion(bf16[6,512,512]{2,1,0:T(8,128)(2,1)S(1)} %get-tuple-element.593, s32[]{:T(128)} %get-tuple-element.592, bf16[2048,512]{1,0:T(8,128)(2,1)} %get-tuple-element.600, s32[512]{0:T(512)S(1)} %bitcast.412), kind=kOutput, calls=%fused_computation.12.clone.1 | convolution fusion | flops 1075052544 | bytes 2623492 | tf_op jit(solution)/shard_map/while/body/eval_jaxpr/dot_general | solution.py:47
  74.4 2.9 %fusion.202 = bf16[6,512,512]{2,1,0:T(8,128)(2,1)S(1)} fusion(bf16[6,512,512]{2,1,0:T(8,128)(2,1)S(1)} %get-tuple-element.593, s32[]{:T(128)} %get-tuple-element.592, bf16[2048,512]{1,0:T(8,128)(2,1)} %get-tuple-element.600, s32[512]{0:T(512)S(1)} %bitcast.412), kind=kOutput, calls=%fused_computation.12.clone.1 | convolution fusion | flops 1075052544 | bytes 2623492 | tf_op jit(solution)/shard_map/while/body/eval_jaxpr/dot_general | solution.py:47
  83.2 2.9 %fusion.202 = bf16[6,512,512]{2,1,0:T(8,128)(2,1)S(1)} fusion(bf16[6,512,512]{2,1,0:T(8,128)(2,1)S(1)} %get-tuple-element.593, s32[]{:T(128)} %get-tuple-element.592, bf16[2048,512]{1,0:T(8,128)(2,1)} %get-tuple-element.600, s32[512]{0:T(512)S(1)} %bitcast.412), kind=kOutput, calls=%fused_computation.12.clone.1 | convolution fusion | flops 1075052544 | bytes 2623492 | tf_op jit(solution)/shard_map/while/body/eval_jaxpr/dot_general | solution.py:47
  89.1 3.8 %multiply_convert_fusion.3 = bf16[6,512,512]{2,1,0:T(8,128)(2,1)S(1)} fusion(f32[6,512,512]{2,1,0:T(8,128)} %get-tuple-element.216, bf16[6,512,512]{2,1,0:T(8,128)(2,1)S(1)} %get-tuple-element.215, f32[512]{0:T(512)S(1)} %bitcast.427), kind=kLoop, calls=%fused_computation.53 | loop fusion | flops 12582912 | bytes 12584960 | tf_op jit(solution)/shard_map/convert_element_type | solution.py:71
  92.9 3.0 %fusion.142 = (f32[3072]{0:T(1024)S(1)}, f32[3072,512]{0,1:T(8,128)S(1)}) fusion(bf16[3072,512]{1,0:T(8,128)(2,1)S(1)} %bitcast.367, bf16[4,512,512]{2,1,0:T(8,128)(2,1)} %param.45), kind=kOutput, calls=%fused_computation.279 | convolution fusion | flops 1612182528 | bytes 9973760 | tf_op jit(solution)/shard_map/dot_general | solution.py:72
  98.5 4.5 %multiply_convert_fusion.30 = bf16[192,512]{1,0:T(8,128)(2,1)S(1)} fusion(f32[192,512]{1,0:T(8,128)S(1)} %copy-done.10, bf16[4,2,512,512]{3,2,1,0:T(8,128)(2,1)} %param.48, f32[3072,512]{0,1:T(8,128)} %copy-done, f32[512]{0:T(512)S(1)} %bitcast.433, f32[3072]{0:T(1024)S(1)} %add_rsqrt_fusion.1, f32[3072]{0:T(1024)S(1)} %broadcast_multiply_fusion.1, ...), kind=kOutput, calls=%fused_computation.177 | convolution fusion | flops 712310784 | bytes 7446528 | tf_op jit(solution)/shard_map/dot_general | solution.py:80
  111.9 4.1 %while.96 = (s32[]{:T(128)}, f32[3,512,512]{2,1,0:T(8,128)S(1)}, s32[3,512]{1,0:T(4,128)}, f32[192,512]{1,0:T(8,128)S(1)}, s32[]{:T(128)}) while((s32[]{:T(128)}, f32[3,512,512]{2,1,0:T(8,128)S(1)}, s32[3,512]{1,0:T(4,128)}, f32[192,512]{1,0:T(8,128)S(1)}, s32[]{:T(128)}) %tuple.169), condition=%wide.region_13.14_spmd, body=%wide.region_12.13_spmd.sunk | while | flops 604078080 | bytes 1448005 | solution.py:51
  118.1 4.4 %collective-permute-start.7 = (bf16[5,1,16,512]{3,2,1,0:T(8,128)(2,1)S(1)}, bf16[5,1,16,512]{3,2,1,0:T(8,128)(2,1)S(1)}, u32[]{:S(2)}, u32[]{:S(2)}) collective-permute-start(bf16[5,1,16,512]{3,2,1,0:T(8,128)(2,1)S(1)} %get-tuple-element.309), channel_id=1, source_target_pairs={{1,0},{2,1},{3,2},{4,3},{5,4},{6,5},{7,6},{0,7},{9,8},{10,9},{11,1... | collective-permute-start | bytes 245768 | tf_op jit(solution)/shard_map/ppermute | solution.py:20
  131.9 8.9 %while.95 = (s32[]{:T(128)}, bf16[3,512,512]{2,1,0:T(8,128)(2,1)}, s32[3,512]{1,0:T(4,128)}, bf16[320,512]{1,0:T(8,128)(2,1)}, s32[]{:T(128)}) while((s32[]{:T(128)}, bf16[3,512,512]{2,1,0:T(8,128)(2,1)}, s32[3,512]{1,0:T(4,128)}, bf16[320,512]{1,0:T(8,128)(2,1)}, s32[]{:T(128)}) %tuple.172), condition=%wide.region_11.12_spmd, body=%wide.region_10.11_spmd.sunk | while | flops 168198144 | bytes 858689 | solution.py:51
  154.8 5.2 %all-to-all-start = ((bf16[32,8,512]{2,1,0:T(8,128)(2,1)}), bf16[32,8,512]{2,1,0:T(8,128)(2,1)}, u32[]{:S(2)}, u32[]{:S(2)}) async-start(bf16[32,8,512]{2,1,0:T(8,128)(2,1)} %fusion.42), calls=%async_computation | async-start | bytes 524288 | tf_op jit(solution)/shard_map/all_to_all | solution.py:171
  164.6 6.0 %all-to-all-done = bf16[32,8,512]{2,1,0:T(8,128)(2,1)} async-done(((bf16[32,8,512]{2,1,0:T(8,128)(2,1)}), bf16[32,8,512]{2,1,0:T(8,128)(2,1)}, u32[]{:S(2)}, u32[]{:S(2)}) %all-to-all-start) | async-done | bytes 262176 | tf_op jit(solution)/shard_map/all_to_all | solution.py:171
  173.7 6.9 %while.97 = (s32[]{:T(128)}, bf16[3,512,512]{2,1,0:T(8,128)(2,1)}, s32[3,512]{1,0:T(4,128)S(1)}, bf16[448,512]{1,0:T(8,128)(2,1)}, s32[]{:T(128)}) while((s32[]{:T(128)}, bf16[3,512,512]{2,1,0:T(8,128)(2,1)}, s32[3,512]{1,0:T(4,128)S(1)}, bf16[448,512]{1,0:T(8,128)(2,1)}, s32[]{:T(128)}) %tuple.178), condition=%wide.region_19.20_spmd, body=%wide.region_18.19_spmd.sunk | while | flops 235372544 | bytes 989761 | solution.py:51
  197.8 3.7 %collective-permute-start.11 = (bf16[5,1,16,512]{3,2,1,0:T(8,128)(2,1)S(1)}, bf16[5,1,16,512]{3,2,1,0:T(8,128)(2,1)S(1)}, u32[]{:S(2)}, u32[]{:S(2)}) collective-permute-start(bf16[5,1,16,512]{3,2,1,0:T(8,128)(2,1)S(1)} %get-tuple-element.307), channel_id=1, source_target_pairs={{1,0},{2,1},{3,2},{4,3},{5,4},{6,5},{7,6},{0,7},{9,8},{10,9},{11,1... | collective-permute-start | bytes 245768 | tf_op jit(solution)/shard_map/ppermute | solution.py:20
  201.5 3.1 %fusion.87 = f32[1024,512]{1,0:T(8,128)} fusion(bf16[1024,512]{1,0:T(8,128)(2,1)S(1)} %copy-done.2, bf16[4,2,512,512]{3,2,1,0:T(8,128)(2,1)} %param.48), kind=kOutput, calls=%fused_computation.140 | convolution fusion | flops 536870912 | bytes 3670016 | tf_op jit(solution)/shard_map/dot_general | solution.py:77
  206.4 3.1 %while.99 = (s32[]{:T(128)}, bf16[6,512,512]{2,1,0:T(8,128)(2,1)S(1)}, s32[6,512]{1,0:T(8,128)S(1)}, bf16[320,512]{1,0:T(8,128)(2,1)S(1)}, s32[]{:T(128)}) while((s32[]{:T(128)}, bf16[6,512,512]{2,1,0:T(8,128)(2,1)S(1)}, s32[6,512]{1,0:T(8,128)S(1)}, bf16[320,512]{1,0:T(8,128)(2,1)S(1)}, s32[]{:T(128)}) %tuple.181), condition=%wide.region_27.28_spmd, body=%wide.region_26.27_spmd.sunk | while | flops 168198144 | bytes 858181 | solution.py:51
  209.6 3.8 %multiply_convert_fusion.1 = bf16[6,512,512]{2,1,0:T(8,128)(2,1)S(1)} fusion(f32[6,512,512]{2,1,0:T(8,128)} %bitcast.366, bf16[6,512,512]{2,1,0:T(8,128)(2,1)S(1)} %get-tuple-element.221, f32[512]{0:T(512)S(1)} %bitcast.426), kind=kLoop, calls=%fused_computation.50 | loop fusion | flops 12582912 | bytes 12584960 | tf_op jit(solution)/shard_map/convert_element_type | solution.py:71
  213.4 2.9 %fusion.148 = (f32[3072]{0:T(1024)S(1)}, f32[3072,512]{1,0:T(8,128)S(1)}) fusion(bf16[3072,512]{1,0:T(8,128)(2,1)S(1)} %bitcast.368, bf16[4,512,512]{2,1,0:T(8,128)(2,1)} %param.45), kind=kOutput, calls=%fused_computation.285 | convolution fusion | flops 1612182528 | bytes 9973760 | tf_op jit(solution)/shard_map/dot_general | solution.py:72
  222.0 3.8 %fusion.149 = (f32[1024]{0:T(1024)S(1)}, f32[1024,512]{0,1:T(8,128)S(1)}) fusion(bf16[4,512,512]{2,1,0:T(8,128)(2,1)} %param.49, f32[1024,512]{1,0:T(8,128)} %fusion.87, bf16[1024,512]{1,0:T(8,128)(2,1)} %reduce_sum.170, f32[512]{0:T(512)S(1)} %bitcast.428, bf16[4,2,512,512]{3,2,1,0:T(8,128)(2,1)} %param.48), kind=kOutput, calls=%fused_computation.286 | convolution fusion | flops 1077935104 | bytes 6297600 | tf_op jit(solution)/shard_map/dot_general | solution.py:84
  (286 shorter events, 150.5 us)
Async XLA Ops:
  7.0 21.9 %collective-permute-start = (bf16[1,3,128,512]{3,2,1,0:T(8,128)(2,1)}, bf16[1,3,128,512]{3,2,1,0:T(8,128)(2,1)}, u32[]{:S(2)}, u32[]{:S(2)}) collective-permute-start(bf16[1,3,128,512]{3,2,1,0:T(8,128)(2,1)} %bitcast.20), channel_id=1, source_target_pairs={{0,8},{8,16},{16,24},{24,0},{1,9},{9,17},{17,25},{25,1},{2,10},{10... | collective-permute-start | bytes 1179656 | tf_op jit(solution)/shard_map/ppermute | solution.py:19
  7.4 21.4 %collective-permute-start.1 = (bf16[1,3,128,512]{3,2,1,0:T(8,128)(2,1)}, bf16[1,3,128,512]{3,2,1,0:T(8,128)(2,1)}, u32[]{:S(2)}, u32[]{:S(2)}) collective-permute-start(bf16[1,3,128,512]{3,2,1,0:T(8,128)(2,1)} %bitcast.24), channel_id=1, source_target_pairs={{8,0},{16,8},{24,16},{0,24},{9,1},{17,9},{25,17},{1,25},{10,2},{18... | collective-permute-start | bytes 1179656 | tf_op jit(solution)/shard_map/ppermute | solution.py:20
  11.4 9.9 %copy-start.23 = (f32[4,512]{1,0:T(4,128)S(1)}, f32[4,512]{1,0:T(4,128)}, u32[]{:S(2)}) copy-start(f32[4,512]{1,0:T(4,128)} %param.46) | copy-start | bytes 24580
  11.4 10.5 %copy-start.24 = (f32[4,512]{1,0:T(4,128)S(1)}, f32[4,512]{1,0:T(4,128)}, u32[]{:S(2)}) copy-start(f32[4,512]{1,0:T(4,128)} %param.47) | copy-start | bytes 24580
  11.4 11.1 %copy-start.25 = (f32[4,512]{1,0:T(4,128)S(1)}, f32[4,512]{1,0:T(4,128)}, u32[]{:S(2)}) copy-start(f32[4,512]{1,0:T(4,128)} %param.50) | copy-start | bytes 24580
  11.5 13.7 %copy-start.26 = (f32[4,512]{1,0:T(4,128)S(1)}, f32[4,512]{1,0:T(4,128)}, u32[]{:S(2)}) copy-start(f32[4,512]{1,0:T(4,128)} %param.51) | copy-start | bytes 24580
  27.1 9.4 %copy-start.15 = (s32[1,2,1536]{2,1,0:T(2,128)S(1)}, s32[1,2,1536]{2,1,0:T(2,128)}, u32[]{:S(2)}) copy-start(s32[1,2,1536]{2,1,0:T(2,128)} %param.42) | copy-start | bytes 36868
  27.1 10.1 %copy-start.35 = (s32[1,8,16]{2,1,0:T(8,128)S(1)}, s32[1,8,16]{2,1,0:T(8,128)}, u32[]{:S(2)}) copy-start(s32[1,8,16]{2,1,0:T(8,128)} %param.38) | copy-start | bytes 1540
  27.1 11.9 %copy-start.34 = (s32[1,32,8]{1,2,0:T(8,128)S(1)}, s32[1,32,8]{1,2,0:T(8,128)}, u32[]{:S(2)}) copy-start(s32[1,32,8]{1,2,0:T(8,128)} %param.39) | copy-start | bytes 3076
  31.2 30.7 %collective-permute-start.2 = (bf16[5,1,128,512]{3,2,1,0:T(8,128)(2,1)}, bf16[5,1,128,512]{3,2,1,0:T(8,128)(2,1)}, u32[]{:S(2)}, u32[]{:S(2)}) collective-permute-start(bf16[5,1,128,512]{3,2,1,0:T(8,128)(2,1)} %get-tuple-element.300), channel_id=1, source_target_pairs={{0,1},{1,2},{2,3},{3,4},{4,5},{5,6},{6,7},{7,0},{8,9},{9,10},{10,1... | collective-permute-start | bytes 1966088 | tf_op jit(solution)/shard_map/ppermute | solution.py:19
  33.5 30.6 %collective-permute-start.3 = (bf16[5,1,128,512]{3,2,1,0:T(8,128)(2,1)}, bf16[5,1,128,512]{3,2,1,0:T(8,128)(2,1)}, u32[]{:S(2)}, u32[]{:S(2)}) collective-permute-start(bf16[5,1,128,512]{3,2,1,0:T(8,128)(2,1)} %get-tuple-element.301), channel_id=1, source_target_pairs={{1,0},{2,1},{3,2},{4,3},{5,4},{6,5},{7,6},{0,7},{9,8},{10,9},{11,1... | collective-permute-start | bytes 1966088 | tf_op jit(solution)/shard_map/ppermute | solution.py:20
  71.5 17.6 %copy-start.28 = (f32[1,512]{1,0:T(1,128)S(1)}, f32[1,512]{1,0:T(1,128)}, u32[]{:S(2)}) copy-start(f32[1,512]{1,0:T(1,128)} %get-tuple-element.333) | copy-start | bytes 6148
  109.7 7.2 %collective-permute-start.4 = (bf16[1,3,16,512]{3,2,1,0:T(8,128)(2,1)}, bf16[1,3,16,512]{3,2,1,0:T(8,128)(2,1)}, u32[]{:S(2)}, u32[]{:S(2)}) collective-permute-start(bf16[1,3,16,512]{3,2,1,0:T(8,128)(2,1)} %bitcast.45), channel_id=1, source_target_pairs={{0,8},{8,16},{16,24},{24,0},{1,9},{9,17},{17,25},{25,1},{2,10},{10... | collective-permute-start | bytes 147464 | tf_op jit(solution)/shard_map/ppermute | solution.py:19
  109.8 7.2 %collective-permute-start.5 = (bf16[1,3,16,512]{3,2,1,0:T(8,128)(2,1)}, bf16[1,3,16,512]{3,2,1,0:T(8,128)(2,1)}, u32[]{:S(2)}, u32[]{:S(2)}) collective-permute-start(bf16[1,3,16,512]{3,2,1,0:T(8,128)(2,1)} %bitcast.49), channel_id=1, source_target_pairs={{8,0},{16,8},{24,16},{0,24},{9,1},{17,9},{25,17},{1,25},{10,2},{18... | collective-permute-start | bytes 147464 | tf_op jit(solution)/shard_map/ppermute | solution.py:20
  117.8 7.2 %collective-permute-start.6 = (bf16[5,1,16,512]{3,2,1,0:T(8,128)(2,1)S(1)}, bf16[5,1,16,512]{3,2,1,0:T(8,128)(2,1)S(1)}, u32[]{:S(2)}, u32[]{:S(2)}) collective-permute-start(bf16[5,1,16,512]{3,2,1,0:T(8,128)(2,1)S(1)} %get-tuple-element.308), channel_id=1, source_target_pairs={{0,1},{1,2},{2,3},{3,4},{4,5},{5,6},{6,7},{7,0},{8,9},{9,10},{10,1... | collective-permute-start | bytes 245768 | tf_op jit(solution)/shard_map/ppermute | solution.py:19
  118.1 6.8 %collective-permute-start.7 = (bf16[5,1,16,512]{3,2,1,0:T(8,128)(2,1)S(1)}, bf16[5,1,16,512]{3,2,1,0:T(8,128)(2,1)S(1)}, u32[]{:S(2)}, u32[]{:S(2)}) collective-permute-start(bf16[5,1,16,512]{3,2,1,0:T(8,128)(2,1)S(1)} %get-tuple-element.309), channel_id=1, source_target_pairs={{1,0},{2,1},{3,2},{4,3},{5,4},{6,5},{7,6},{0,7},{9,8},{10,9},{11,1... | collective-permute-start | bytes 245768 | tf_op jit(solution)/shard_map/ppermute | solution.py:20
  131.9 8.9 %copy-start.21 = (f32[1,512]{1,0:T(1,128)S(1)}, f32[1,512]{1,0:T(1,128)}, u32[]{:S(2)}) copy-start(f32[1,512]{1,0:T(1,128)} %get-tuple-element.332) | copy-start | bytes 6148
  154.8 15.8 %all-to-all-start = ((bf16[32,8,512]{2,1,0:T(8,128)(2,1)}), bf16[32,8,512]{2,1,0:T(8,128)(2,1)}, u32[]{:S(2)}, u32[]{:S(2)}) async-start(bf16[32,8,512]{2,1,0:T(8,128)(2,1)} %fusion.42), calls=%async_computation | async-start | bytes 524288 | tf_op jit(solution)/shard_map/all_to_all | solution.py:171
  188.4 13.1 %copy-start.2 = (bf16[1024,512]{1,0:T(8,128)(2,1)S(1)}, bf16[1024,512]{1,0:T(8,128)(2,1)}, u32[]{:S(2)}) copy-start(bf16[1024,512]{1,0:T(8,128)(2,1)} %param.34) | copy-start | bytes 3145732
  193.1 3.6 %collective-permute-start.8 = (bf16[1,3,16,512]{3,2,1,0:T(8,128)(2,1)S(1)}, bf16[1,3,16,512]{3,2,1,0:T(8,128)(2,1)S(1)}, u32[]{:S(2)}, u32[]{:S(2)}) collective-permute-start(bf16[1,3,16,512]{3,2,1,0:T(8,128)(2,1)S(1)} %bitcast.417), channel_id=1, source_target_pairs={{0,8},{8,16},{16,24},{24,0},{1,9},{9,17},{17,25},{25,1},{2,10},{10... | collective-permute-start | bytes 147464 | tf_op jit(solution)/shard_map/ppermute | solution.py:19
  193.2 3.5 %collective-permute-start.9 = (bf16[1,3,16,512]{3,2,1,0:T(8,128)(2,1)S(1)}, bf16[1,3,16,512]{3,2,1,0:T(8,128)(2,1)S(1)}, u32[]{:S(2)}, u32[]{:S(2)}) collective-permute-start(bf16[1,3,16,512]{3,2,1,0:T(8,128)(2,1)S(1)} %bitcast.416), channel_id=1, source_target_pairs={{8,0},{16,8},{24,16},{0,24},{9,1},{17,9},{25,17},{1,25},{10,2},{18... | collective-permute-start | bytes 147464 | tf_op jit(solution)/shard_map/ppermute | solution.py:20
  195.0 10.9 %copy-start.13 = (s32[1,3,1024]{2,0,1:T(1,128)S(1)}, s32[1,3,1024]{2,0,1:T(1,128)}, u32[]{:S(2)}) copy-start(s32[1,3,1024]{2,0,1:T(1,128)} %param.43) | copy-start | bytes 36868
  196.7 9.2 %collective-permute-start.10 = (bf16[5,1,16,512]{3,2,1,0:T(8,128)(2,1)S(1)}, bf16[5,1,16,512]{3,2,1,0:T(8,128)(2,1)S(1)}, u32[]{:S(2)}, u32[]{:S(2)}) collective-permute-start(bf16[5,1,16,512]{3,2,1,0:T(8,128)(2,1)S(1)} %get-tuple-element.306), channel_id=1, source_target_pairs={{0,1},{1,2},{2,3},{3,4},{4,5},{5,6},{6,7},{7,0},{8,9},{9,10},{10,1... | collective-permute-start | bytes 245768 | tf_op jit(solution)/shard_map/ppermute | solution.py:19
  197.8 8.2 %collective-permute-start.11 = (bf16[5,1,16,512]{3,2,1,0:T(8,128)(2,1)S(1)}, bf16[5,1,16,512]{3,2,1,0:T(8,128)(2,1)S(1)}, u32[]{:S(2)}, u32[]{:S(2)}) collective-permute-start(bf16[5,1,16,512]{3,2,1,0:T(8,128)(2,1)S(1)} %get-tuple-element.307), channel_id=1, source_target_pairs={{1,0},{2,1},{3,2},{4,3},{5,4},{6,5},{7,6},{0,7},{9,8},{10,9},{11,1... | collective-permute-start | bytes 245768 | tf_op jit(solution)/shard_map/ppermute | solution.py:20
  (29 other events, 102.4 us)
where the time goes:
time: 232 us; the launch traced here: 230 us
  matrix products  101 us (44%)
  other arithmetic  40.2 us (17%)
  local copies, waits for them, and re-layouts  32.5 us (14%)
  waiting for transfers between devices  27.6 us (12%)
  starting transfers between devices  26.1 us (11%)
    dot_general x23, matrix products, one_block(): jnp.dot(member.astype(table.dtype), table, preferred_element_type=jnp.flo...  36.8 us
    ppermute x6, waiting for transfers between devices, extended_2(): before = lax.ppermute(last, axis, up)  19.4 us
    ppermute x6, starting transfers between devices, extended_2(): after = lax.ppermute(initial, axis, down)  16.6 us
    unnamed x104, local copies, waits for them, and re-layouts  14.9 us
    dot_general x12, matrix products, one_block(): jnp.dot(member.astype(jnp.float32), table, precision=lax.Precision.HIGHES...  13.5 us
    convert_element_type x4, other arithmetic, messages(): jax.nn.silu(gathered.astype(jnp.float32) + target_proj + biases)  12.2 us
    dot_general x4, matrix products, messages(): result = jnp.dot(hidden, second, preferred_element_type=jnp.float32)  10.1 us
    dot_general x4, matrix products, node_update(): jnp.dot(node_rows, first_layer[0], preferred_element_type=jnp.float32)  9.52 us
  transfers between devices with their start and end apart: 13, of which 5 were waited for; matrix products, arithmetic and copies ran while one was open for 19% of the time, Pallas kernels for 0%

commit v1 on v0

v1 whole, which is shorter than its diff:
```python
import functools

import jax
import jax.numpy as jnp
from jax import lax
from jax.experimental import pallas as pl
from jax.experimental.pallas import tpu as pltpu
from jax.sharding import PartitionSpec as P

EPSILON = 1e-05
AXES = ("aa", "ba")
LANES = 128
BF16 = jnp.bfloat16
F32 = jnp.float32
LIMIT = pltpu.CompilerParams(vmem_limit_bytes=48 * 1024 * 1024)

UP_LISTS = (7, 5, 6)
DOWN_LISTS = (2, 0, 1)
RIGHT_LIST = 4
LEFT_LIST = 3
SEND_ORDER = UP_LISTS + DOWN_LISTS + (RIGHT_LIST, LEFT_LIST)


def dot(left, right):
    return jnp.dot(left, right, preferred_element_type=F32)


def round_up(value, unit):
    return -(-value // unit) * unit


def column(row):
    tall = jnp.broadcast_to(row, (LANES, row.shape[1]))
    return jnp.transpose(tall).astype(jnp.int16)


def one_hot(ids, width, base=0):
    lane = lax.broadcasted_iota(jnp.int16, ids.shape, 1)
    parts = [
        jnp.where(ids == lane + jnp.int16(base + start), BF16(1), BF16(0))
        for start in range(0, width, LANES)
    ]
    return parts[0] if len(parts) == 1 else jnp.concatenate(parts, 1)


def silu(value):
    half = 0.5 * value
    return half + half * jnp.tanh(half)


def normed(value, gain):
    average = jnp.mean(value, axis=-1, keepdims=True)
    centred = value - average
    spread = jnp.mean(centred * centred, axis=-1, keepdims=True)
    return centred * lax.rsqrt(spread + EPSILON) * gain


def whole(shape):
    return pl.BlockSpec(shape, lambda *_: (0,) * len(shape))


def layer(section, part, width):
    if part is None:
        return pl.BlockSpec((1, width, width), lambda *_: (section, 0, 0))
    return pl.BlockSpec((1, 1, width, width), lambda *_: (section, part, 0, 0))


def cost(macs, moved):
    return pl.CostEstimate(flops=2 * macs, bytes_accessed=moved, transcendentals=0)


def pick_kernel(rows_ref, rim_ref, up_ref, down_ref, right_ref, left_ref):
    count = rows_ref.shape[0]
    lists = rim_ref[0]
    for place, chosen in enumerate(SEND_ORDER):
        picked = one_hot(column(lists[chosen : chosen + 1]), count)
        block = dot(picked, rows_ref[...]).astype(BF16)
        if place < 3:
            up_ref[place] = block
        elif place < 6:
            down_ref[place - 3] = block
        elif place == 6:
            right_ref[0] = block
        else:
            left_ref[0] = block


def send_shapes(depth, width):
    return [jax.ShapeDtypeStruct((n, depth, width), BF16) for n in (3, 3, 1, 1)]


def pick_grid(rows, rim):
    count, width = rows.shape
    depth = rim.shape[2]
    return pl.pallas_call(
        pick_kernel,
        out_shape=send_shapes(depth, width),
        compiler_params=LIMIT,
        cost_estimate=cost(8 * depth * count * width, 2 * (count + 8 * depth) * width),
        name="pick_grid",
    )(rows, rim)


def fill(ref, value):
    rows = value.shape[0]
    ref[:rows] = value
    if ref.shape[0] > rows:
        ref[rows:] = jnp.zeros((ref.shape[0] - rows, ref.shape[1]), ref.dtype)


def local_kernel(
    section, project, source_ref, mesh_ref, edges_ref, first_s, first_r, bias_ref, out_ref, table, target
):
    @pl.when(pl.program_id(0) == 0)
    def _():
        source = source_ref[...]
        if project:
            source = dot(source, first_s[0, 0]).astype(BF16)
        fill(table, source)
        receiver = dot(mesh_ref[...], first_r[0, 0]) + bias_ref[section : section + 1]
        fill(target, receiver.astype(BF16))

    block = out_ref.shape[0]
    sub = math_block(block, 256)
    for start in range(0, block, sub):
        senders = column(edges_ref[0, 0:1, start : start + sub])
        targets = column(edges_ref[0, 1:2, start : start + sub])
        out_ref[start : start + sub] = dot(one_hot(senders, table.shape[0]), table[...]) + dot(
            one_hot(targets, target.shape[0]), target[...]
        )


def math_block(total, most):
    block = most
    while total % block:
        block -= LANES
    return block


def local_part(source, mesh_rows, edges, weights, section, project):
    total = edges.shape[2]
    width = source.shape[1]
    block = math_block(total, 512)
    count, slots = source.shape[0], mesh_rows.shape[0]
    first = weights["edge_first"]
    return pl.pallas_call(
        functools.partial(local_kernel, section, project),
        grid=(total // block,),
        in_specs=[
            whole(source.shape),
            whole(mesh_rows.shape),
            pl.BlockSpec((1, 2, block), lambda i: (0, 0, i)),
            layer(section, 0, width),
            layer(section, 1, width),
            whole(weights["edge_bias"].shape),
        ],
        out_specs=pl.BlockSpec((block, width), lambda i: (i, 0)),
        out_shape=jax.ShapeDtypeStruct((total, width), F32),
        scratch_shapes=[
            pltpu.VMEM((round_up(count, LANES), width), BF16),
            pltpu.VMEM((round_up(slots, LANES), width), BF16),
        ],
        compiler_params=LIMIT,
        cost_estimate=cost(total * (count + 256) * width, total * width * 4),
        name="local_part",
    )(source, mesh_rows, edges, first, first, weights["edge_bias"])


def place_remote(table, remote, places, weight):
    for ref, slots in zip(remote, places):
        depth = ref.shape[1]
        for index, slot in enumerate(slots):
            rows = ref[index]
            if weight is not None:
                rows = dot(rows, weight).astype(BF16)
            table[slot * depth : (slot + 1) * depth] = rows


def round_kernel(section, project, places, last, split, *refs):
    refs = list(refs)
    pre_ref, edges_ref, mesh_ref = refs[:3]
    remote = refs[3 : 3 + len(places)]
    (
        first_ref, second_ref, gain_ref, node0_ref, node1_ref, node2_ref, node_bias_ref, node_gain_ref,
        next_ref, lists_ref, owned_ref,
    ) = refs[3 + len(places) : 14 + len(places)]
    rest = refs[14 + len(places) :]
    mesh_out, proj_out = rest[:2]
    table, total = rest[-2:]
    sends = rest[2:-2]
    if last:
        masked_out, sends = sends[0], sends[1:]
    step = pl.program_id(0)
    slots = mesh_ref.shape[0]
    base = split

    @pl.when(step == 0)
    def _():
        place_remote(table, remote, places, first_ref[0, 0] if project else None)
        total[...] = jnp.zeros_like(total)

    block = pre_ref.shape[0]
    sub = math_block(block, 256)
    for start in range(0, block, sub):
        senders = column(edges_ref[0, 0:1, start : start + sub])
        pre = pre_ref[start : start + sub] + dot(one_hot(senders, table.shape[0], base), table[...])
        hidden = silu(pre).astype(BF16)
        message = normed(dot(hidden, second_ref[0]), gain_ref[section : section + 1]).astype(BF16)
        targets = edges_ref[0, 1:2, start : start + sub]
        member = lax.broadcasted_iota(jnp.int32, (slots, sub), 0) == targets
        total[...] += dot(member.astype(BF16), message)

    @pl.when(step == pl.num_programs(0) - 1)
    def _():
        rows = mesh_ref[...]
        inner = dot(rows, node0_ref[0, 0]) + dot(total[...].astype(BF16), node1_ref[0, 0])
        hidden = silu(inner + node_bias_ref[section : section + 1]).astype(BF16)
        update = normed(dot(hidden, node2_ref[0]), node_gain_ref[section : section + 1])
        fresh = (rows.astype(F32) + update).astype(BF16)
        mesh_out[...] = fresh
        if last:
            alive = lax.broadcasted_iota(jnp.int32, fresh.shape, 0) < owned_ref[0]
            masked_out[...] = jnp.where(alive, fresh, jnp.zeros_like(fresh))
        fill(proj_out, dot(fresh, next_ref[0, 0]).astype(BF16))
        listed = lists_ref.shape[1]
        size = math_block(listed, 256)
        made = []
        for start in range(0, listed, size):
            picked = one_hot(column(lists_ref[0:1, start : start + size]), proj_out.shape[0])
            made.append(dot(picked, proj_out[...]).astype(BF16))
        made = made[0] if len(made) == 1 else jnp.concatenate(made, 0)
        place = 0
        for ref in sends:
            if len(ref.shape) == 2:
                ref[...] = made
                continue
            depth = ref.shape[1]
            for index in range(ref.shape[0]):
                ref[index] = made[place : place + depth]
                place += depth


def round_part(pre, edges, mesh_rows, remote, places, weights, section, project, lists, owned, sends, split):
    total, width = pre.shape
    slots = mesh_rows.shape[0]
    last = section == 2
    block = math_block(total, 512)
    table_rows = sum(r.shape[0] * r.shape[1] for r in remote)
    padded = round_up(slots, LANES)
    out_shape = [
        jax.ShapeDtypeStruct((slots, width), BF16),
        jax.ShapeDtypeStruct((padded, width), BF16),
    ]
    if last:
        out_shape.append(jax.ShapeDtypeStruct((slots, width), BF16))
    out_shape += sends
    vectors = weights["edge_bias"].shape
    return pl.pallas_call(
        functools.partial(round_kernel, section, project, places, last, split),
        grid=(total // block,),
        in_specs=[
            pl.BlockSpec((block, width), lambda i: (i, 0)),
            pl.BlockSpec((1, 2, block), lambda i: (0, 0, i)),
            whole(mesh_rows.shape),
            *[whole(r.shape) for r in remote],
            layer(section, 0, width),
            layer(section, None, width),
            whole(vectors),
            layer(section, 0, width),
            layer(section, 1, width),
            layer(section, None, width),
            whole(vectors),
            whole(vectors),
            layer(section + 1, 0, width),
            whole(lists.shape),
            pl.BlockSpec(memory_space=pltpu.SMEM),
        ],
        out_specs=[whole(s.shape) for s in out_shape],
        out_shape=out_shape,
        scratch_shapes=[
            pltpu.VMEM((table_rows, width), BF16),
            pltpu.VMEM((slots, width), F32),
        ],
        compiler_params=LIMIT,
        cost_estimate=cost(total * (table_rows + 1024) * width, total * width * 4),
        name="round_part",
    )(
        pre, edges, mesh_rows, *remote,
        weights["edge_first"], weights["edge_second"], weights["edge_gain"],
        weights["node_first"], weights["node_first"], weights["node_second"],
        weights["node_bias"], weights["node_gain"], weights["edge_first"], lists, owned,
    )


def decode_local_kernel(section, grid_ref, table_ref, edges_ref, first_ref, bias_ref, node0_ref, node_bias_ref, pre_ref, inner_ref):
    rows = grid_ref[...]
    target = dot(rows, first_ref[0, 0]) + bias_ref[section : section + 1]
    inner_ref[...] = dot(rows, node0_ref[0, 0]) + node_bias_ref[section : section + 1]
    for sender in range(edges_ref.shape[1]):
        ids = column(edges_ref[0, sender : sender + 1, :])
        pre_ref[sender] = dot(one_hot(ids, table_ref.shape[0]), table_ref[...]) + target


def decode_local(grid_rows, table, edges, weights, section):
    count, width = grid_rows.shape
    senders = edges.shape[1]
    block = math_block(count, 256)
    vectors = weights["edge_bias"].shape
    return pl.pallas_call(
        functools.partial(decode_local_kernel, section),
        grid=(count // block,),
        in_specs=[
            pl.BlockSpec((block, width), lambda i: (i, 0)),
            whole(table.shape),
            pl.BlockSpec((1, senders, block), lambda i: (0, 0, i)),
            layer(section, 1, width),
            whole(vectors),
            layer(section, 0, width),
            whole(vectors),
        ],
        out_specs=[
            pl.BlockSpec((senders, block, width), lambda i: (0, i, 0)),
            pl.BlockSpec((block, width), lambda i: (i, 0)),
        ],
        out_shape=[
            jax.ShapeDtypeStruct((senders, count, width), F32),
            jax.ShapeDtypeStruct((count, width), F32),
        ],
        compiler_params=LIMIT,
        cost_estimate=cost(count * width * (2 * width + senders * table.shape[0]), count * width * 16),
        name="decode_local",
    )(grid_rows, table, edges, weights["edge_first"], weights["edge_bias"], weights["node_first"], weights["node_bias"])


def decode_kernel(section, places, split, *refs):
    pre_ref, inner_ref, grid_ref, edges_ref = refs[:4]
    remote = refs[4 : 4 + len(places)]
    second_ref, gain_ref, node1_ref, node2_ref, node_gain_ref, out_ref, table = refs[4 + len(places) :]

    @pl.when(pl.program_id(0) == 0)
    def _():
        place_remote(table, remote, places, None)

    total = None
    for sender in range(edges_ref.shape[1]):
        ids = column(edges_ref[0, sender : sender + 1, :])
        pre = pre_ref[sender] + dot(one_hot(ids, table.shape[0], split), table[...])
        hidden = silu(pre).astype(BF16)
        message = normed(dot(hidden, second_ref[0]), gain_ref[section : section + 1])
        message = message.astype(BF16).astype(F32)
        total = message if total is None else total + message
    inner = inner_ref[...] + dot(total.astype(BF16), node1_ref[0, 0])
    hidden = silu(inner).astype(BF16)
    update = normed(dot(hidden, node2_ref[0]), node_gain_ref[section : section + 1])
    out_ref[...] = (grid_ref[...].astype(F32) + update).astype(BF16)


def decode_part(pre, inner, grid_rows, edges, remote, places, weights, section, split):
    senders, count, width = pre.shape
    block = math_block(count, 256)
    table_rows = sum(r.shape[0] * r.shape[1] for r in remote)
    vectors = weights["edge_bias"].shape
    return pl.pallas_call(
        functools.partial(decode_kernel, section, places, split),
        grid=(count // block,),
        in_specs=[
            pl.BlockSpec((senders, block, width), lambda i: (0, i, 0)),
            pl.BlockSpec((block, width), lambda i: (i, 0)),
            pl.BlockSpec((block, width), lambda i: (i, 0)),
            pl.BlockSpec((1, senders, block), lambda i: (0, 0, i)),
            *[whole(r.shape) for r in remote],
            layer(section, None, width),
            whole(vectors),
            layer(section, 1, width),
            layer(section, None, width),
            whole(vectors),
        ],
        out_specs=pl.BlockSpec((block, width), lambda i: (i, 0)),
        out_shape=jax.ShapeDtypeStruct((count, width), BF16),
        scratch_shapes=[pltpu.VMEM((table_rows, width), BF16)],
        compiler_params=LIMIT,
        cost_estimate=cost(count * width * (5 * width + senders * table_rows), count * width * 16),
        name="decode_part",
    )(
        pre, inner, grid_rows, edges, *remote,
        weights["edge_second"], weights["edge_gain"], weights["node_first"],
        weights["node_second"], weights["node_gain"],
    )


def shift(value, along, step):
    bands, sectors = lax.axis_size("aa"), lax.axis_size("ba")
    pairs = []
    for i in range(bands):
        for j in range(sectors):
            if along == "aa":
                to = ((i + step) % bands) * sectors + j
            else:
                to = i * sectors + (j + step) % sectors
            pairs.append((i * sectors + j, to))
    return lax.ppermute(value, AXES, pairs)


def halo(up, down, right, left, together):
    from_up = shift(up, "aa", 1)
    from_down = shift(down, "aa", -1)
    if together:
        right = jnp.concatenate([right, from_up[0:1], from_down[0:1]], 0)
        left = jnp.concatenate([left, from_up[1:2], from_down[1:2]], 0)
        from_left = shift(right, "ba", 1)
        from_right = shift(left, "ba", -1)
        blocks = [from_up[2:3], from_down[2:3], from_left, from_right]
        places = ((1,), (6,), (3, 0, 5), (4, 2, 7))
        return blocks, places
    from_left = shift(right, "ba", 1)
    from_right = shift(left, "ba", -1)
    right = jnp.concatenate([from_up[0:1], from_down[0:1]], 0)
    left = jnp.concatenate([from_up[1:2], from_down[1:2]], 0)
    corner_left = shift(right, "ba", 1)
    corner_right = shift(left, "ba", -1)
    blocks = [from_up[2:3], from_down[2:3], from_left, from_right, corner_left, corner_right]
    places = ((1,), (6,), (3,), (4,), (0, 5), (2, 7))
    return blocks, places


def per_device(
    grid_nodes, mesh_nodes, owned_nodes, grid_rim, mesh_rim, long_send, g2m_edges, short_edges,
    long_edges, m2g_edges, edge_first, edge_second, edge_bias, edge_gain, node_first, node_second,
    node_bias, node_gain,
):
    weights = dict(
        edge_first=edge_first, edge_second=edge_second, edge_bias=edge_bias, edge_gain=edge_gain,
        node_first=node_first, node_second=node_second, node_bias=node_bias, node_gain=node_gain,
    )
    width = grid_nodes.shape[1]
    slots = mesh_nodes.shape[0]
    depth = mesh_rim.shape[2]
    peers, listed = long_send.shape[1:]
    rim_lists = jnp.concatenate([mesh_rim[0, m : m + 1] for m in SEND_ORDER], 0).reshape(1, 8 * depth)
    long_lists = long_send.reshape(1, peers * listed)
    rim_sends = send_shapes(depth, width)

    blocks, places = halo(*pick_grid(grid_nodes, grid_rim), together=False)
    pre = local_part(grid_nodes, mesh_nodes, g2m_edges, weights, 0, True)
    mesh_one, proj, *sends = round_part(
        pre, g2m_edges, mesh_nodes, blocks, places, weights, 0, True, rim_lists, owned_nodes,
        rim_sends, grid_nodes.shape[0],
    )

    blocks, places = halo(*sends, together=True)
    pre = local_part(proj, mesh_one, short_edges, weights, 1, False)
    mesh_two, proj, sent = round_part(
        pre, short_edges, mesh_one, blocks, places, weights, 1, False, long_lists, owned_nodes,
        [jax.ShapeDtypeStruct((peers * listed, width), BF16)], slots,
    )

    sent = sent.reshape(peers, listed, width)
    arrived = lax.all_to_all(sent, AXES, split_axis=0, concat_axis=0, tiled=True)
    pre = local_part(proj, mesh_two, long_edges, weights, 2, False)
    mesh_three, proj, mesh_out, *sends = round_part(
        pre, long_edges, mesh_two, [arrived.reshape(1, peers * listed, width)], ((0,),), weights, 2,
        False, rim_lists, owned_nodes, rim_sends, slots,
    )

    blocks, places = halo(*sends, together=True)
    pre, inner = decode_local(grid_nodes, proj, m2g_edges, weights, 3)
    grid_out = decode_part(pre, inner, grid_nodes, m2g_edges, blocks, places, weights, 3, slots)
    return grid_out, mesh_out


def solution(mesh):
    rows = P(AXES, None)
    lists = P(AXES, None, None)
    in_specs = (rows, rows, P(AXES)) + (lists,) * 7 + (P(),) * 8
    return jax.shard_map(
        per_device, mesh=mesh, in_specs=in_specs, out_specs=(rows, rows), check_vma=False
    )
```

time: 232 us -> 133 us (0.57)
  matrix products: 101 us -> 0 us
  Pallas kernels: 0 us -> 65.2 us
  other arithmetic: 40.2 us -> 2.93 us
  local copies, waits for them, and re-layouts: 32.5 us -> 18.7 us
  waiting for transfers between devices: 27.6 us -> 15.2 us
    dot_general x58 -> x0, matrix products: 101 us -> none  [the longest x23 36.8 us: one_block(): jnp.dot(member.astype(table.dtype), table, preferred_element_type=jnp.flo...]
    pallas_call x0 -> x9, Pallas kernels: none -> 65.2 us  [the longest x3 33.4 us: round_part(): pl.pallas_call(functools.partial(round_kernel, section, project, places,...]
    convert_element_type x8 -> x0, other arithmetic: 16.3 us -> none  [the longest x4 12.2 us: messages(): jax.nn.silu(gathered.astype(jnp.float32) + target_proj + biases)]
    ppermute x12 -> x14, waiting for transfers between devices: 21.6 us -> 9.24 us  [shift(): return lax.ppermute(value, AXES, pairs)]
    reduce_sum x9 -> x0, other arithmetic: 6.37 us -> none  [the longest x8 4.59 us: layer_norm(): spread = jnp.mean(centred * centred, axis=-1, keepdims=True)]
    concatenate x8 -> x6, other arithmetic: 9.28 us -> 2.93 us  [the longest x2 0.73 us: halo(): left = jnp.concatenate([left, from_up[1:2], from_down[1:2]], 0)]
    another operation x11 -> x0, local copies, waits for them, and re-layouts: 5.17 us -> none
    slice x6 -> x0, other arithmetic: 5.01 us -> none  [the longest x3 3.13 us: extended_2(): last = lax.slice_in_dim(value, length - width, length, axis=dim)]
  transfers between devices with their start and end apart: 13 -> 15, of which waited for: 5 -> 7; matrix products, arithmetic and copies ran while one was open for 19% -> 3% of each run, Pallas kernels for 0% -> 14%
where the time goes in v1:
time: 133 us; the launch traced here: 132 us
  Pallas kernels  65.2 us (49%)
  starting transfers between devices  28.2 us (21%)
  local copies, waits for them, and re-layouts  18.7 us (14%)
  waiting for transfers between devices  15.2 us (11%)
  other arithmetic  2.93 us (2%)
  between operations  1.5 us (1%)
    pallas_call x3, Pallas kernels, round_part(): pl.pallas_call(functools.partial(round_kernel, section, project, places,...  33.4 us
    ppermute x14, starting transfers between devices, shift(): return lax.ppermute(value, AXES, pairs)  25.6 us
    unnamed x68, local copies, waits for them, and re-layouts  17.9 us
    pallas_call x3, Pallas kernels, local_part(): pl.pallas_call(functools.partial(local_kernel, section, project), grid=(t...  13.5 us
    pallas_call x1, Pallas kernels, decode_part(): pl.pallas_call(functools.partial(decode_kernel, section, places, split),...  11.1 us
    ppermute x14, waiting for transfers between devices, shift(): return lax.ppermute(value, AXES, pairs)  9.24 us
    all_to_all x1, waiting for transfers between devices, per_device(): lax.all_to_all(sent, AXES, split_axis=0, concat_axis=0, tiled=True)  5.99 us
    pallas_call x1, Pallas kernels, decode_local(): pl.pallas_call(functools.partial(decode_local_kernel, section), grid=(cou...  5.46 us
  transfers between devices with their start and end apart: 15, of which 7 were waited for; matrix products, arithmetic and copies ran while one was open for 3% of the time, Pallas kernels for 14%

profile of v1, /device:TPU:0, one launch (start us, length us, event | category | flops | bytes accessed | tf_op | source)
XLA Modules:
  0.0 131.8 jit_solution(9151489330158910769)
XLA Ops:
  2.9 1.8 %pick_grid.1 = (bf16[3,128,512]{2,1,0:T(8,128)(2,1)S(1)}, bf16[3,128,512]{2,1,0:T(8,128)(2,1)S(1)}, bf16[1,128,512]{2,1,0:T(8,128)(2,1)}, bf16[1,128,512]{2,1,0:T(8,128)(2,1)S(1)}) custom-call(bf16[1024,512]{1,0:T(8,128)(2,1)S(1)} %copy-done.7, s32[1,8,128]{2,1,0:T(8,128)S(1)} %copy-done.30), custom_call_target="tpu_custom_call" | custom-call | flops 1073741824 | bytes 2097152 | tf_op jit(solution)/shard_map/pick_grid/pallas_call | solution.py:95
  5.2 2.0 %collective-permute-start.1 = (bf16[3,128,512]{2,1,0:T(8,128)(2,1)S(1)}, bf16[3,128,512]{2,1,0:T(8,128)(2,1)S(1)}, u32[]{:S(2)}, u32[]{:S(2)}) collective-permute-start(bf16[3,128,512]{2,1,0:T(8,128)(2,1)S(1)} %get-tuple-element.24), channel_id=1, source_target_pairs={{0,24},{1,25},{2,26},{3,27},{4,28},{5,29},{6,30},{7,31},{8,0},{9,1... | collective-permute-start | bytes 1179656 | tf_op jit(solution)/shard_map/ppermute | solution.py:401
  7.1 2.3 %collective-permute-start.2 = (bf16[1,128,512]{2,1,0:T(8,128)(2,1)}, bf16[1,128,512]{2,1,0:T(8,128)(2,1)S(1)}, u32[]{:S(2)}, u32[]{:S(2)}) collective-permute-start(bf16[1,128,512]{2,1,0:T(8,128)(2,1)} %get-tuple-element.25), channel_id=1, source_target_pairs={{0,1},{1,2},{2,3},{3,4},{4,5},{5,6},{6,7},{7,0},{8,9},{9,10},{10,1... | collective-permute-start | bytes 393224 | tf_op jit(solution)/shard_map/ppermute | solution.py:401
  9.4 3.0 %collective-permute-start.3 = (bf16[1,128,512]{2,1,0:T(8,128)(2,1)S(1)}, bf16[1,128,512]{2,1,0:T(8,128)(2,1)S(1)}, u32[]{:S(2)}, u32[]{:S(2)}) collective-permute-start(bf16[1,128,512]{2,1,0:T(8,128)(2,1)S(1)} %get-tuple-element.26), channel_id=1, source_target_pairs={{0,7},{1,0},{2,1},{3,2},{4,3},{5,4},{6,5},{7,6},{8,15},{9,8},{10,9... | collective-permute-start | bytes 393224 | tf_op jit(solution)/shard_map/ppermute | solution.py:401
  12.4 1.7 %collective-permute-done = bf16[3,128,512]{2,1,0:T(8,128)(2,1)S(1)} collective-permute-done((bf16[3,128,512]{2,1,0:T(8,128)(2,1)S(1)}, bf16[3,128,512]{2,1,0:T(8,128)(2,1)S(1)}, u32[]{:S(2)}, u32[]{:S(2)}) %collective-permute-start) | collective-permute-done | bytes 393248 | tf_op jit(solution)/shard_map/ppermute | solution.py:401
  14.2 2.5 %collective-permute-done.1 = bf16[3,128,512]{2,1,0:T(8,128)(2,1)S(1)} collective-permute-done((bf16[3,128,512]{2,1,0:T(8,128)(2,1)S(1)}, bf16[3,128,512]{2,1,0:T(8,128)(2,1)S(1)}, u32[]{:S(2)}, u32[]{:S(2)}) %collective-permute-start.1) | collective-permute-done | bytes 393248 | tf_op jit(solution)/shard_map/ppermute | solution.py:401
  19.6 3.3 %collective-permute-start.5 = (bf16[2,128,512]{2,1,0:T(8,128)(2,1)}, bf16[2,128,512]{2,1,0:T(8,128)(2,1)S(1)}, u32[]{:S(2)}, u32[]{:S(2)}) collective-permute-start(bf16[2,128,512]{2,1,0:T(8,128)(2,1)} %pad_maximum_fusion.1), channel_id=1, source_target_pairs={{0,7},{1,0},{2,1},{3,2},{4,3},{5,4},{6,5},{7,6},{8,15},{9,8},{10,9... | collective-permute-start | bytes 786440 | tf_op jit(solution)/shard_map/ppermute | solution.py:401
  22.9 7.4 %local_part.3.refs_0_ = f32[3072,512]{1,0:T(8,128)} custom-call(bf16[1024,512]{1,0:T(8,128)(2,1)S(1)} %copy-done.7, bf16[192,512]{1,0:T(8,128)(2,1)S(1)} %copy-done.9, s32[1,2,3072]{2,1,0:T(2,128)S(1)} %copy-done.21, bf16[4,2,512,512]{3,2,1,0:T(8,128)(2,1)S(1)} %copy-done, bf16[4,2,512,512]{3,2,1,0:T(8,128)(2,1)S(1)} %copy-done, f32[4,512]{1,0:T(4,128)S(1)} %copy-done.18), custom_call_target="tpu_custom_call" | custom-call | flops 4026531840 | bytes 6291456 | tf_op jit(solution)/shard_map/local_part/pallas_call | solution.py:146
  39.7 16.3 %round_part.3 = (bf16[192,512]{1,0:T(8,128)(2,1)S(1)}, bf16[256,512]{1,0:T(8,128)(2,1)S(1)}, bf16[3,16,512]{2,1,0:T(8,128)(2,1)}, bf16[3,16,512]{2,1,0:T(8,128)(...) custom-call(f32[3072,512]{1,0:T(8,128)} %local_part.3.refs_0_, s32[1,2,3072]{2,1,0:T(2,128)S(1)} %copy-done.22, ...), custom_call_target="tpu_custom_call" | custom-call | flops 6442450944 | bytes 6291456 | tf_op jit(solution)/shard_map/round_part/pallas_call | solution.py:258
  58.7 1.8 %collective-permute-start.7 = (bf16[3,16,512]{2,1,0:T(8,128)(2,1)}, bf16[3,16,512]{2,1,0:T(8,128)(2,1)S(1)}, u32[]{:S(2)}, u32[]{:S(2)}) collective-permute-start(bf16[3,16,512]{2,1,0:T(8,128)(2,1)} %copy-done.29), channel_id=1, source_target_pairs={{0,24},{1,25},{2,26},{3,27},{4,28},{5,29},{6,30},{7,31},{8,0},{9,1... | collective-permute-start | bytes 147464 | tf_op jit(solution)/shard_map/ppermute | solution.py:401
  64.0 4.7 %collective-permute-start.9 = (bf16[3,16,512]{2,1,0:T(8,128)(2,1)S(1)}, bf16[3,16,512]{2,1,0:T(8,128)(2,1)S(1)}, u32[]{:S(2)}, u32[]{:S(2)}) collective-permute-start(bf16[3,16,512]{2,1,0:T(8,128)(2,1)S(1)} %pad_maximum_fusion.3), channel_id=1, source_target_pairs={{0,7},{1,0},{2,1},{3,2},{4,3},{5,4},{6,5},{7,6},{8,15},{9,8},{10,9... | collective-permute-start | bytes 147464 | tf_op jit(solution)/shard_map/ppermute | solution.py:401
  70.1 3.1 %local_part.4.refs_0_ = f32[1536,512]{1,0:T(8,128)S(1)} custom-call(bf16[256,512]{1,0:T(8,128)(2,1)S(1)} %get-tuple-element.27.source_ref, bf16[192,512]{1,0:T(8,128)(2,1)S(1)} %get-tuple-element.28.mesh_ref.refs_2_, s32[1,2,1536]{2,1,0:T(2,128)S(1)} %copy-done.23, bf16[4,2,512,512]{3,2,1,0:T(8,128)(2,1)} %first_ref.1, bf16[4,2,512,512]{3,2,1,0:T(8,128)(2,1)} %first_ref.1, ...), custom_call_target="tpu_custom_call" | custom-call | flops 805306368 | bytes 3145728 | tf_op jit(solution)/shard_map/local_part/pallas_call | solution.py:146
  73.3 1.6 %copy-done.5 = f32[1536,512]{1,0:T(8,128)} copy-done((f32[1536,512]{1,0:T(8,128)}, f32[1536,512]{1,0:T(8,128)S(1)}, u32[]{:S(2)}) %copy-start.5) | copy-done | bytes 3145752
  74.9 8.5 %round_part.4 = (bf16[192,512]{1,0:T(8,128)(2,1)S(1)}, bf16[256,512]{1,0:T(8,128)(2,1)S(1)}, bf16[256,512]{1,0:T(8,128)(2,1)}) custom-call(f32[1536,512]{1,0:T(8,128)} %copy-done.5, s32[1,2,1536]{2,1,0:T(2,128)S(1)} %copy-done.23, bf16[192,512]{1,0:T(8,128)(2,1)S(1)} %get-tuple-element.28.mesh_ref.refs_2_, ...), custom_call_target="tpu_custom_call" | custom-call | flops 1811939328 | bytes 3145728 | tf_op jit(solution)/shard_map/round_part/pallas_call | solution.py:258
  83.4 2.6 %all-to-all-start = ((bf16[32,8,512]{2,1,0:T(8,128)(2,1)}), bf16[32,8,512]{2,1,0:T(8,128)(2,1)S(1)}, u32[]{:S(2)}, u32[]{:S(2)}) async-start(bf16[32,8,512]{2,1,0:T(8,128)(2,1)} %bitcast.8), calls=%async_computation | async-start | bytes 524288 | tf_op jit(solution)/shard_map/all_to_all | solution.py:458
  86.0 3.0 %local_part.5.refs_0_ = f32[1536,512]{1,0:T(8,128)S(1)} custom-call(bf16[256,512]{1,0:T(8,128)(2,1)S(1)} %get-tuple-element.33.source_ref, bf16[192,512]{1,0:T(8,128)(2,1)S(1)} %get-tuple-element.34.mesh_ref.refs_2_, s32[1,2,1536]{2,1,0:T(2,128)S(1)} %copy-done.24, bf16[4,2,512,512]{3,2,1,0:T(8,128)(2,1)} %first_ref.1, bf16[4,2,512,512]{3,2,1,0:T(8,128)(2,1)} %first_ref.1, ...), custom_call_target="tpu_custom_call" | custom-call | flops 805306368 | bytes 3145728 | tf_op jit(solution)/shard_map/local_part/pallas_call | solution.py:146
  89.1 1.6 %copy-done.6 = f32[1536,512]{1,0:T(8,128)} copy-done((f32[1536,512]{1,0:T(8,128)}, f32[1536,512]{1,0:T(8,128)S(1)}, u32[]{:S(2)}) %copy-start.6) | copy-done | bytes 3145752
  90.7 6.0 %all-to-all-done = bf16[32,8,512]{2,1,0:T(8,128)(2,1)S(1)} async-done(((bf16[32,8,512]{2,1,0:T(8,128)(2,1)}), bf16[32,8,512]{2,1,0:T(8,128)(2,1)S(1)}, u32[]{:S(2)}, u32[]{:S(2)}) %all-to-all-start) | async-done | bytes 262176 | tf_op jit(solution)/shard_map/all_to_all | solution.py:458
  98.3 8.6 %round_part.5 = (bf16[192,512]{1,0:T(8,128)(2,1)}, bf16[256,512]{1,0:T(8,128)(2,1)S(1)}, bf16[192,512]{1,0:T(8,128)(2,1)}, bf16[3,16,512]{2,1,0:T(8,128)(2,1)S(1...) custom-call(f32[1536,512]{1,0:T(8,128)} %copy-done.6, ...), custom_call_target="tpu_custom_call" | custom-call | flops 2013265920 | bytes 3145728 | tf_op jit(solution)/shard_map/round_part/pallas_call | solution.py:258
  106.9 1.8 %collective-permute-start.11 = (bf16[3,16,512]{2,1,0:T(8,128)(2,1)S(1)}, bf16[3,16,512]{2,1,0:T(8,128)(2,1)S(1)}, u32[]{:S(2)}, u32[]{:S(2)}) collective-permute-start(bf16[3,16,512]{2,1,0:T(8,128)(2,1)S(1)} %get-tuple-element.40), channel_id=1, source_target_pairs={{0,24},{1,25},{2,26},{3,27},{4,28},{5,29},{6,30},{7,31},{8,0},{9,1... | collective-permute-start | bytes 147464 | tf_op jit(solution)/shard_map/ppermute | solution.py:401
  108.7 1.7 %collective-permute-done.10 = bf16[3,16,512]{2,1,0:T(8,128)(2,1)S(1)} collective-permute-done((bf16[3,16,512]{2,1,0:T(8,128)(2,1)S(1)}, bf16[3,16,512]{2,1,0:T(8,128)(2,1)S(1)}, u32[]{:S(2)}, u32[]{:S(2)}) %collective-permute-start.10) | collective-permute-done | bytes 49184 | tf_op jit(solution)/shard_map/ppermute | solution.py:401
  111.5 3.8 %collective-permute-start.13 = (bf16[3,16,512]{2,1,0:T(8,128)(2,1)S(1)}, bf16[3,16,512]{2,1,0:T(8,128)(2,1)S(1)}, u32[]{:S(2)}, u32[]{:S(2)}) collective-permute-start(bf16[3,16,512]{2,1,0:T(8,128)(2,1)S(1)} %pad_maximum_fusion.5), channel_id=1, source_target_pairs={{0,7},{1,0},{2,1},{3,2},{4,3},{5,4},{6,5},{7,6},{8,15},{9,8},{10,9... | collective-permute-start | bytes 147464 | tf_op jit(solution)/shard_map/ppermute | solution.py:401
  115.3 5.5 %decode_local.1 = (f32[3,1024,512]{2,1,0:T(8,128)}, f32[1024,512]{1,0:T(8,128)S(1)}) custom-call(bf16[1024,512]{1,0:T(8,128)(2,1)S(1)} %copy-done.8, bf16[256,512]{1,0:T(8,128)(2,1)S(1)} %get-tuple-element.36.table_ref, s32[1,3,1024]{2,1,0:T(4,128)S(1)} %copy.24.edges_ref.refs_3_, bf16[4,2,512,512]{3,2,1,0:T(8,128)(2,1)} %first_ref.1, ...), custom_call_target="tpu_custom_call" | custom-call | flops 1879048192 | bytes 8388608 | tf_op jit(solution)/shard_map/decode_local/pallas_call | solution.py:309
  120.8 11.1 %decode_part.1 = bf16[1024,512]{1,0:T(8,128)(2,1)} custom-call(f32[3,1024,512]{2,1,0:T(8,128)} %get-tuple-element.37.refs_0_, f32[1024,512]{1,0:T(8,128)S(1)} %get-tuple-element.38.refs_1_, bf16[1024,512]{1,0:T(8,128)(2,1)S(1)} %copy-done.8, s32[1,3,1024]{2,1,0:T(4,128)S(1)} %copy.24.edges_ref.refs_3_, bf16[1,16,512]{2,1,0:T(8,128)(2,1)S(1)} %get-tuple-element.52.refs_4_, ...), custom_call_target="tpu_custom_call" | custom-call | flops 3087007744 | bytes 8388608 | tf_op jit(solution)/shard_map/decode_part/pallas_call | solution.py:363
  (99 shorter events, 24.8 us)
Async XLA Ops:
  0.6 22.3 %copy-start = (bf16[4,2,512,512]{3,2,1,0:T(8,128)(2,1)S(1)}, bf16[4,2,512,512]{3,2,1,0:T(8,128)(2,1)}, u32[]{:S(2)}) copy-start(bf16[4,2,512,512]{3,2,1,0:T(8,128)(2,1)} %first_ref.1) | copy-start | bytes 12582916
  2.9 20.0 %copy-start.9 = (bf16[192,512]{1,0:T(8,128)(2,1)S(1)}, bf16[192,512]{1,0:T(8,128)(2,1)}, u32[]{:S(2)}) copy-start(bf16[192,512]{1,0:T(8,128)(2,1)} %refs_2_.2) | copy-start | bytes 589828
  2.9 20.0 %copy-start.18 = (f32[4,512]{1,0:T(4,128)S(1)}, f32[4,512]{1,0:T(4,128)}, u32[]{:S(2)}) copy-start(f32[4,512]{1,0:T(4,128)} %bias_ref.7) | copy-start | bytes 24580
  2.9 20.0 %copy-start.21 = (s32[1,2,3072]{2,1,0:T(2,128)S(1)}, s32[1,2,3072]{2,1,0:T(2,128)}, u32[]{:S(2)}) copy-start(s32[1,2,3072]{2,1,0:T(2,128)} %refs_1_.3) | copy-start | bytes 73732
  4.7 9.4 %collective-permute-start = (bf16[3,128,512]{2,1,0:T(8,128)(2,1)S(1)}, bf16[3,128,512]{2,1,0:T(8,128)(2,1)S(1)}, u32[]{:S(2)}, u32[]{:S(2)}) collective-permute-start(bf16[3,128,512]{2,1,0:T(8,128)(2,1)S(1)} %get-tuple-element.23), channel_id=1, source_target_pairs={{0,8},{1,9},{2,10},{3,11},{4,12},{5,13},{6,14},{7,15},{8,16},{9,17... | collective-permute-start | bytes 1179656 | tf_op jit(solution)/shard_map/ppermute | solution.py:401
  5.2 11.5 %collective-permute-start.1 = (bf16[3,128,512]{2,1,0:T(8,128)(2,1)S(1)}, bf16[3,128,512]{2,1,0:T(8,128)(2,1)S(1)}, u32[]{:S(2)}, u32[]{:S(2)}) collective-permute-start(bf16[3,128,512]{2,1,0:T(8,128)(2,1)S(1)} %get-tuple-element.24), channel_id=1, source_target_pairs={{0,24},{1,25},{2,26},{3,27},{4,28},{5,29},{6,30},{7,31},{8,0},{9,1... | collective-permute-start | bytes 1179656 | tf_op jit(solution)/shard_map/ppermute | solution.py:401
  7.1 24.5 %collective-permute-start.2 = (bf16[1,128,512]{2,1,0:T(8,128)(2,1)}, bf16[1,128,512]{2,1,0:T(8,128)(2,1)S(1)}, u32[]{:S(2)}, u32[]{:S(2)}) collective-permute-start(bf16[1,128,512]{2,1,0:T(8,128)(2,1)} %get-tuple-element.25), channel_id=1, source_target_pairs={{0,1},{1,2},{2,3},{3,4},{4,5},{5,6},{6,7},{7,0},{8,9},{9,10},{10,1... | collective-permute-start | bytes 393224 | tf_op jit(solution)/shard_map/ppermute | solution.py:401
  9.4 22.9 %collective-permute-start.3 = (bf16[1,128,512]{2,1,0:T(8,128)(2,1)S(1)}, bf16[1,128,512]{2,1,0:T(8,128)(2,1)S(1)}, u32[]{:S(2)}, u32[]{:S(2)}) collective-permute-start(bf16[1,128,512]{2,1,0:T(8,128)(2,1)S(1)} %get-tuple-element.26), channel_id=1, source_target_pairs={{0,7},{1,0},{2,1},{3,2},{4,3},{5,4},{6,5},{7,6},{8,15},{9,8},{10,9... | collective-permute-start | bytes 393224 | tf_op jit(solution)/shard_map/ppermute | solution.py:401
  17.4 15.6 %collective-permute-start.4 = (bf16[2,128,512]{2,1,0:T(8,128)(2,1)}, bf16[2,128,512]{2,1,0:T(8,128)(2,1)S(1)}, u32[]{:S(2)}, u32[]{:S(2)}) collective-permute-start(bf16[2,128,512]{2,1,0:T(8,128)(2,1)} %pad_maximum_fusion), channel_id=1, source_target_pairs={{0,1},{1,2},{2,3},{3,4},{4,5},{5,6},{6,7},{7,0},{8,9},{9,10},{10,1... | collective-permute-start | bytes 786440 | tf_op jit(solution)/shard_map/ppermute | solution.py:401
  19.6 11.4 %copy-start.32 = (s32[1,8,16]{2,1,0:T(8,128)S(1)}, s32[1,8,16]{2,1,0:T(8,128)}, u32[]{:S(2)}) copy-start(s32[1,8,16]{2,1,0:T(8,128)} %param.22) | copy-start | bytes 1540
  19.6 14.6 %copy-start.1 = (bf16[4,512,512]{2,1,0:T(8,128)(2,1)S(1)}, bf16[4,512,512]{2,1,0:T(8,128)(2,1)}, u32[]{:S(2)}) copy-start(bf16[4,512,512]{2,1,0:T(8,128)(2,1)} %refs_8_.5) | copy-start | bytes 6291460
  19.6 14.6 %copy-start.14 = (f32[4,512]{1,0:T(4,128)S(1)}, f32[4,512]{1,0:T(4,128)}, u32[]{:S(2)}) copy-start(f32[4,512]{1,0:T(4,128)} %node_bias_ref.1) | copy-start | bytes 24580
  19.6 14.6 %copy-start.15 = (f32[4,512]{1,0:T(4,128)S(1)}, f32[4,512]{1,0:T(4,128)}, u32[]{:S(2)}) copy-start(f32[4,512]{1,0:T(4,128)} %refs_9_.7) | copy-start | bytes 24580
  19.6 14.6 %collective-permute-start.5 = (bf16[2,128,512]{2,1,0:T(8,128)(2,1)}, bf16[2,128,512]{2,1,0:T(8,128)(2,1)S(1)}, u32[]{:S(2)}, u32[]{:S(2)}) collective-permute-start(bf16[2,128,512]{2,1,0:T(8,128)(2,1)} %pad_maximum_fusion.1), channel_id=1, source_target_pairs={{0,7},{1,0},{2,1},{3,2},{4,3},{5,4},{6,5},{7,6},{8,15},{9,8},{10,9... | collective-permute-start | bytes 786440 | tf_op jit(solution)/shard_map/ppermute | solution.py:401
  57.8 3.7 %collective-permute-start.6 = (bf16[3,16,512]{2,1,0:T(8,128)(2,1)}, bf16[3,16,512]{2,1,0:T(8,128)(2,1)S(1)}, u32[]{:S(2)}, u32[]{:S(2)}) collective-permute-start(bf16[3,16,512]{2,1,0:T(8,128)(2,1)} %get-tuple-element.29), channel_id=1, source_target_pairs={{0,8},{1,9},{2,10},{3,11},{4,12},{5,13},{6,14},{7,15},{8,16},{9,17... | collective-permute-start | bytes 147464 | tf_op jit(solution)/shard_map/ppermute | solution.py:401
  58.7 3.9 %collective-permute-start.7 = (bf16[3,16,512]{2,1,0:T(8,128)(2,1)}, bf16[3,16,512]{2,1,0:T(8,128)(2,1)S(1)}, u32[]{:S(2)}, u32[]{:S(2)}) collective-permute-start(bf16[3,16,512]{2,1,0:T(8,128)(2,1)} %copy-done.29), channel_id=1, source_target_pairs={{0,24},{1,25},{2,26},{3,27},{4,28},{5,29},{6,30},{7,31},{8,0},{9,1... | collective-permute-start | bytes 147464 | tf_op jit(solution)/shard_map/ppermute | solution.py:401
  63.3 11.6 %collective-permute-start.8 = (bf16[3,16,512]{2,1,0:T(8,128)(2,1)S(1)}, bf16[3,16,512]{2,1,0:T(8,128)(2,1)S(1)}, u32[]{:S(2)}, u32[]{:S(2)}) collective-permute-start(bf16[3,16,512]{2,1,0:T(8,128)(2,1)S(1)} %pad_maximum_fusion.2), channel_id=1, source_target_pairs={{0,1},{1,2},{2,3},{3,4},{4,5},{5,6},{6,7},{7,0},{8,9},{9,10},{10,1... | collective-permute-start | bytes 147464 | tf_op jit(solution)/shard_map/ppermute | solution.py:401
  64.0 10.9 %collective-permute-start.9 = (bf16[3,16,512]{2,1,0:T(8,128)(2,1)S(1)}, bf16[3,16,512]{2,1,0:T(8,128)(2,1)S(1)}, u32[]{:S(2)}, u32[]{:S(2)}) collective-permute-start(bf16[3,16,512]{2,1,0:T(8,128)(2,1)S(1)} %pad_maximum_fusion.3), channel_id=1, source_target_pairs={{0,7},{1,0},{2,1},{3,2},{4,3},{5,4},{6,5},{7,6},{8,15},{9,8},{10,9... | collective-permute-start | bytes 147464 | tf_op jit(solution)/shard_map/ppermute | solution.py:401
  83.4 13.2 %all-to-all-start = ((bf16[32,8,512]{2,1,0:T(8,128)(2,1)}), bf16[32,8,512]{2,1,0:T(8,128)(2,1)S(1)}, u32[]{:S(2)}, u32[]{:S(2)}) async-start(bf16[32,8,512]{2,1,0:T(8,128)(2,1)} %bitcast.8), calls=%async_computation | async-start | bytes 524288 | tf_op jit(solution)/shard_map/all_to_all | solution.py:458
  98.3 17.0 %copy-start.8 = (bf16[1024,512]{1,0:T(8,128)(2,1)S(1)}, bf16[1024,512]{1,0:T(8,128)(2,1)}, u32[]{:S(2)}) copy-start(bf16[1024,512]{1,0:T(8,128)(2,1)} %refs_2_.3) | copy-start | bytes 3145732
  106.9 3.5 %collective-permute-start.10 = (bf16[3,16,512]{2,1,0:T(8,128)(2,1)S(1)}, bf16[3,16,512]{2,1,0:T(8,128)(2,1)S(1)}, u32[]{:S(2)}, u32[]{:S(2)}) collective-permute-start(bf16[3,16,512]{2,1,0:T(8,128)(2,1)S(1)} %get-tuple-element.39), channel_id=1, source_target_pairs={{0,8},{1,9},{2,10},{3,11},{4,12},{5,13},{6,14},{7,15},{8,16},{9,17... | collective-permute-start | bytes 147464 | tf_op jit(solution)/shard_map/ppermute | solution.py:401
  106.9 3.5 %collective-permute-start.11 = (bf16[3,16,512]{2,1,0:T(8,128)(2,1)S(1)}, bf16[3,16,512]{2,1,0:T(8,128)(2,1)S(1)}, u32[]{:S(2)}, u32[]{:S(2)}) collective-permute-start(bf16[3,16,512]{2,1,0:T(8,128)(2,1)S(1)} %get-tuple-element.40), channel_id=1, source_target_pairs={{0,24},{1,25},{2,26},{3,27},{4,28},{5,29},{6,30},{7,31},{8,0},{9,1... | collective-permute-start | bytes 147464 | tf_op jit(solution)/shard_map/ppermute | solution.py:401
  110.4 10.3 %collective-permute-start.12 = (bf16[3,16,512]{2,1,0:T(8,128)(2,1)S(1)}, bf16[3,16,512]{2,1,0:T(8,128)(2,1)S(1)}, u32[]{:S(2)}, u32[]{:S(2)}) collective-permute-start(bf16[3,16,512]{2,1,0:T(8,128)(2,1)S(1)} %pad_maximum_fusion.4), channel_id=1, source_target_pairs={{0,1},{1,2},{2,3},{3,4},{4,5},{5,6},{6,7},{7,0},{8,9},{9,10},{10,1... | collective-permute-start | bytes 147464 | tf_op jit(solution)/shard_map/ppermute | solution.py:401
  111.5 9.2 %collective-permute-start.13 = (bf16[3,16,512]{2,1,0:T(8,128)(2,1)S(1)}, bf16[3,16,512]{2,1,0:T(8,128)(2,1)S(1)}, u32[]{:S(2)}, u32[]{:S(2)}) collective-permute-start(bf16[3,16,512]{2,1,0:T(8,128)(2,1)S(1)} %pad_maximum_fusion.5), channel_id=1, source_target_pairs={{0,7},{1,0},{2,1},{3,2},{4,3},{5,4},{6,5},{7,6},{8,15},{9,8},{10,9... | collective-permute-start | bytes 147464 | tf_op jit(solution)/shard_map/ppermute | solution.py:401
  (24 other events, 68.1 us)

commit v2 on v1

v2 whole, which is shorter than its diff:
```python
import functools

import jax
import jax.numpy as jnp
from jax import lax
from jax.experimental import pallas as pl
from jax.experimental.pallas import tpu as pltpu
from jax.sharding import PartitionSpec as P

EPSILON = 1e-05
AXES = ("aa", "ba")
LANES = 128
BF16 = jnp.bfloat16
F32 = jnp.float32
LIMIT = pltpu.CompilerParams(vmem_limit_bytes=28 * 1024 * 1024)

ALONG_AA = (-1, -1, -1, 0, 0, 1, 1, 1)
ALONG_BA = (-1, 0, 1, -1, 1, -1, 0, 1)
UP_LISTS = (7, 5, 6)
DOWN_LISTS = (2, 0, 1)
RIGHT_LIST = 4
LEFT_LIST = 3
SEND_ORDER = UP_LISTS + DOWN_LISTS + (RIGHT_LIST, LEFT_LIST)


def dot(left, right):
    return jnp.dot(left, right, preferred_element_type=F32)


def math_block(total, most):
    block = most
    while total % block:
        block -= LANES
    return block


def round_up(value, unit):
    return -(-value // unit) * unit


def column(row):
    tall = jnp.broadcast_to(row, (LANES, row.shape[1]))
    return jnp.transpose(tall).astype(jnp.int16)


def one_hot(ids, width, base=0):
    lane = lax.broadcasted_iota(jnp.int16, ids.shape, 1)
    parts = [
        jnp.where(ids == lane + jnp.int16(base + start), BF16(1), BF16(0))
        for start in range(0, width, LANES)
    ]
    return parts[0] if len(parts) == 1 else jnp.concatenate(parts, 1)


def silu(value):
    half = 0.5 * value
    return half + half * jnp.tanh(half)


def normed(value):
    average = jnp.mean(value, axis=-1, keepdims=True)
    centred = value - average
    spread = jnp.mean(centred * centred, axis=-1, keepdims=True)
    return centred * lax.rsqrt(spread + EPSILON)


def whole(shape):
    return pl.BlockSpec(shape, lambda *_: (0,) * len(shape))


def cost(macs, moved):
    return pl.CostEstimate(flops=2 * macs, bytes_accessed=moved, transcendentals=0)


HBM = pl.BlockSpec(memory_space=pltpu.HBM)
SMEM = pl.BlockSpec(memory_space=pltpu.SMEM)


def fetch(sources, buffers, arrived):
    copies = [
        pltpu.make_async_copy(source, buffers.at[i], arrived.at[i]) for i, source in enumerate(sources)
    ]
    for copy in copies:
        copy.start()

    def take(index):
        copies[index].wait()
        return buffers[index]

    return take


def fetch_scratch(count, width):
    return [pltpu.VMEM((count, width, width), BF16), pltpu.SemaphoreType.DMA((count,))]


def fill(ref, value):
    rows = value.shape[0]
    ref[:rows] = value
    if ref.shape[0] > rows:
        ref[rows:] = jnp.zeros((ref.shape[0] - rows, ref.shape[1]), ref.dtype)


def clear_tail(ref, rows):
    ref[rows:] = jnp.zeros((ref.shape[0] - rows, ref.shape[1]), ref.dtype)


def row_of(ref, index):
    return ref[index : index + 1]


def added(pre, targets, second, slots):
    hidden = silu(pre).astype(BF16)
    message = normed(dot(hidden, second)).astype(BF16)
    member = lax.broadcasted_iota(jnp.int32, (slots, targets.shape[1]), 0) == targets
    return dot(member.astype(BF16), message)


def updated(rows, total, inner, take, places, gain):
    first, second = places
    inner = inner + dot(total.astype(BF16), take(first))
    update = normed(dot(silu(inner).astype(BF16), take(second))) * gain
    return (rows.astype(F32) + update).astype(BF16)


def pick_kernel(rows_ref, rim_ref, *outs):
    lists = rim_ref[0]
    for chosen, out in enumerate(outs):
        picked = one_hot(column(lists[chosen : chosen + 1]), rows_ref.shape[0])
        out[...] = dot(picked, rows_ref[...]).astype(BF16)


def pick_grid(rows, rim):
    count, width = rows.shape
    depth = rim.shape[2]
    return pl.pallas_call(
        pick_kernel,
        out_shape=[jax.ShapeDtypeStruct((depth, width), BF16)] * 8,
        compiler_params=LIMIT,
        cost_estimate=cost(8 * depth * count * width, 2 * (count + 8 * depth) * width),
        name="pick_grid",
    )(rows, rim)


def send_shapes(depth, width):
    return [jax.ShapeDtypeStruct((n, depth, width), BF16) for n in (3, 3, 1, 1)]


def list_rows(proj_out, lists_ref, sends):
    listed = lists_ref.shape[1]
    size = math_block(listed, 256)
    made = []
    for start in range(0, listed, size):
        picked = one_hot(column(lists_ref[0:1, start : start + size]), proj_out.shape[0])
        made.append(dot(picked, proj_out[...]).astype(BF16))
    made = made[0] if len(made) == 1 else jnp.concatenate(made, 0)
    place = 0
    for ref in sends:
        if len(ref.shape) == 2:
            ref[...] = made
            continue
        depth = ref.shape[1]
        for index in range(ref.shape[0]):
            ref[index] = made[place : place + depth]
            place += depth


WINDOW = 512
BLOCK = 512


def sorted_keys(edges, slots):
    shift = slots.bit_length()
    senders, targets = edges[0, 0:1], edges[0, 1:2]
    senders = jnp.where(targets < slots, senders, 1 << 14)
    return lax.sort((senders << shift) + targets, dimension=1), shift


def below(keys, limit):
    total = keys.shape[1]
    step = 1 << (total.bit_length() - 1)
    found = jnp.int32(0)
    while step:
        place = found + step
        inside = keys[0, jnp.minimum(place, total) - 1] < limit
        found = jnp.where((place <= total) & inside, place, found)
        step //= 2
    return found


def edge_block(start, used, shift, scalars, keys_ref, table, target, pre, second, slots):
    block = pre.shape[0]
    start = pl.multiple_of(start, LANES)
    keys = keys_ref[0:1, pl.ds(start, block)]
    senders = keys >> shift
    targets = keys & ((1 << shift) - 1)
    lowest = pl.multiple_of((scalars[0, start] >> shift) // 16 * 16, 16)
    highest = scalars[0, jnp.minimum(start + block, used) - 1] >> shift

    def window(base):
        ids = column(jnp.clip(senders - base, -1, 1 << 14))
        return dot(one_hot(ids, WINDOW), table[pl.ds(base, WINDOW)])

    pre[...] = window(lowest) + dot(one_hot(column(targets), target.shape[0]), target[...])

    def more(index, carry):
        pre[...] += window(pl.multiple_of(lowest + (index + 1) * WINDOW, 16))
        return carry

    lax.fori_loop(0, (highest - lowest) // WINDOW, more, 0)
    return added(pre[...], targets, second, slots)


def encode_local_kernel(
    section, shift, scalars, keys_ref, grid_ref, mesh_ref, bias_ref, node_bias_ref,
    edge_first, edge_second, node_first, table_out, target_out, total_out, inner_out,
    table, pre, buffers, arrived,
):
    take = fetch(
        [edge_first.at[section, 0], edge_first.at[section, 1], edge_second.at[section], node_first.at[section, 0]],
        buffers, arrived,
    )
    count, slots = grid_ref.shape[0], mesh_ref.shape[0]
    proj = dot(grid_ref[...], take(0)).astype(BF16)
    table_out[...] = proj
    fill(table, proj)
    rows = mesh_ref[...]
    fill(target_out, (dot(rows, take(1)) + row_of(bias_ref, section)).astype(BF16))
    second = take(2)
    inner_out[...] = dot(rows, take(3)) + row_of(node_bias_ref, section)
    total_out[...] = jnp.zeros_like(total_out)
    block = pre.shape[0]
    done = below(scalars, count << shift) // block

    def step(index, carry):
        total_out[...] += edge_block(
            index * block, done * block, shift, scalars, keys_ref, table, target_out, pre, buffers[2], slots
        )
        return carry

    lax.fori_loop(0, done, step, 0)


def encode_local(keys, shift, grid_rows, mesh_rows, weights, section):
    total = keys.shape[1]
    count, width = grid_rows.shape
    slots = mesh_rows.shape[0]
    vmem = pl.BlockSpec(memory_space=pltpu.VMEM)
    return pl.pallas_call(
        functools.partial(encode_local_kernel, section, shift),
        in_specs=[SMEM] + [vmem] * 5 + [HBM] * 3,
        out_shape=[
            jax.ShapeDtypeStruct((count, width), BF16),
            jax.ShapeDtypeStruct((round_up(slots, LANES), width), BF16),
            jax.ShapeDtypeStruct((slots, width), F32),
            jax.ShapeDtypeStruct((slots, width), F32),
        ],
        scratch_shapes=[
            pltpu.VMEM((count + WINDOW, width), BF16),
            pltpu.VMEM((math_block(total, BLOCK), width), F32),
            *fetch_scratch(4, width),
        ],
        compiler_params=LIMIT,
        cost_estimate=cost(total * 1500 * width, 6 * count * width),
        name="encode_local",
    )(
        keys, keys, grid_rows, mesh_rows, weights["edge_bias"], weights["node_bias"],
        weights["edge_first"], weights["edge_second"], weights["node_first"],
    )


def encode_kernel(section, shift, *refs):
    scalars, keys_ref, local_ref, target, total_ref, inner_ref, mesh_ref = refs[:7]
    remote = refs[7:15]
    (
        gain_ref, node_gain_ref, lists_ref, edge_first, edge_second, node_first, node_second,
        mesh_out, proj_out, up, down, right, left, table, pre, total, buffers, arrived,
    ) = refs[15:]
    take = fetch(
        [
            edge_first.at[section, 0], edge_second.at[section], node_first.at[section, 1],
            node_second.at[section], edge_first.at[section + 1, 0],
        ],
        buffers, arrived,
    )
    count, slots = local_ref.shape[0], mesh_ref.shape[0]
    depth = remote[0].shape[0]
    table[:count] = local_ref[...]
    clear_tail(table, count + 8 * depth)
    take(0)
    for chosen, ref in enumerate(remote):
        place = count + (7 - chosen) * depth
        table[place : place + depth] = dot(ref[...], buffers[0]).astype(BF16)
    take(1)
    total[...] = total_ref[...]
    block = pre.shape[0]
    start = below(scalars, count << shift) // block * block
    used = below(scalars, (count + 8 * depth) << shift)

    def step(index, carry):
        total[...] += edge_block(
            start + index * block, used, shift, scalars, keys_ref, table, target, pre, buffers[1], slots
        )
        return carry

    lax.fori_loop(0, (used - start + block - 1) // block, step, 0)
    summed = total[...] * row_of(gain_ref, section)
    fresh = updated(mesh_ref[...], summed, inner_ref[...], take, (2, 3), row_of(node_gain_ref, section))
    mesh_out[...] = fresh
    fill(proj_out, dot(fresh, take(4)).astype(BF16))
    list_rows(proj_out, lists_ref, (up, down, right, left))


def encode(keys, shift, local, target, total, inner, mesh_rows, remote, lists, depth, weights, section):
    edges = keys.shape[1]
    count, width = local.shape
    slots = mesh_rows.shape[0]
    vmem = pl.BlockSpec(memory_space=pltpu.VMEM)
    rows = count + 8 * remote[0].shape[0]
    return pl.pallas_call(
        functools.partial(encode_kernel, section, shift),
        in_specs=[SMEM] + [vmem] * 17 + [HBM] * 4,
        out_shape=[
            jax.ShapeDtypeStruct((slots, width), BF16),
            jax.ShapeDtypeStruct((round_up(slots, LANES), width), BF16),
        ]
        + send_shapes(depth, width),
        scratch_shapes=[
            pltpu.VMEM((rows + WINDOW, width), BF16),
            pltpu.VMEM((math_block(edges, BLOCK), width), F32),
            pltpu.VMEM((slots, width), F32),
            *fetch_scratch(5, width),
        ],
        compiler_params=LIMIT,
        cost_estimate=cost(edges * 1500 * width, 8 * rows * width),
        name="encode",
    )(
        keys, keys, local, target, total, inner, mesh_rows, *remote,
        weights["edge_gain"], weights["node_gain"], lists,
        weights["edge_first"], weights["edge_second"], weights["node_first"], weights["node_second"],
    )


def prepare_kernel(section, mesh_ref, bias_ref, node_bias_ref, edge_first, node_first, target_out, inner_out, buffers, arrived):
    take = fetch([edge_first.at[section, 1], node_first.at[section, 0]], buffers, arrived)
    rows = mesh_ref[...]
    fill(target_out, (dot(rows, take(0)) + row_of(bias_ref, section)).astype(BF16))
    inner_out[...] = dot(rows, take(1)) + row_of(node_bias_ref, section)


def prepare(mesh_rows, weights, section):
    slots, width = mesh_rows.shape
    vmem = pl.BlockSpec(memory_space=pltpu.VMEM)
    return pl.pallas_call(
        functools.partial(prepare_kernel, section),
        in_specs=[vmem] * 3 + [HBM] * 2,
        out_shape=[
            jax.ShapeDtypeStruct((round_up(slots, LANES), width), BF16),
            jax.ShapeDtypeStruct((slots, width), F32),
        ],
        scratch_shapes=fetch_scratch(2, width),
        compiler_params=LIMIT,
        cost_estimate=cost(2 * slots * width * width, 6 * width * width),
        name="prepare",
    )(mesh_rows, weights["edge_bias"], weights["node_bias"], weights["edge_first"], weights["node_first"])


def place_remote(table, remote, places, base):
    for ref, slots in zip(remote, places):
        depth = ref.shape[1]
        for index, slot in enumerate(slots):
            place = base + slot * depth
            table[place : place + depth] = ref[index]


def round_kernel(section, places, last, *refs):
    edges_ref, local_ref, target, inner_ref, mesh_ref = refs[:5]
    remote = refs[5 : 5 + len(places)]
    (
        gain_ref, node_gain_ref, lists_ref, owned_ref, edge_first, edge_second, node_first, node_second,
    ) = refs[5 + len(places) : 13 + len(places)]
    rest = refs[13 + len(places) :]
    mesh_out, proj_out = rest[:2]
    sends = rest[2:-3]
    table, buffers, arrived = rest[-3:]
    if last:
        masked_out, sends = sends[0], sends[1:]
    take = fetch(
        [
            edge_second.at[section], node_first.at[section, 1], node_second.at[section],
            edge_first.at[section + 1, 0],
        ],
        buffers, arrived,
    )
    slots, padded = mesh_ref.shape[0], local_ref.shape[0]
    table[:padded] = local_ref[...]
    place_remote(table, remote, places, padded)
    edges = edges_ref.shape[2]
    block = math_block(edges, 1536)
    summed = None
    for start in range(0, edges, block):
        senders = edges_ref[0, 0:1, start : start + block]
        senders = jnp.where(senders < slots, senders, senders + (padded - slots))
        targets = edges_ref[0, 1:2, start : start + block]
        pre = dot(one_hot(column(senders), table.shape[0]), table[...]) + dot(
            one_hot(column(targets), padded), target[...]
        )
        if start == 0:
            take(0)
        part = added(pre, targets, buffers[0], slots)
        summed = part if summed is None else summed + part
    summed = summed * row_of(gain_ref, section)
    fresh = updated(mesh_ref[...], summed, inner_ref[...], take, (1, 2), row_of(node_gain_ref, section))
    mesh_out[...] = fresh
    if last:
        alive = lax.broadcasted_iota(jnp.int32, fresh.shape, 0) < owned_ref[0]
        masked_out[...] = jnp.where(alive, fresh, jnp.zeros_like(fresh))
    fill(proj_out, dot(fresh, take(3)).astype(BF16))
    list_rows(proj_out, lists_ref, sends)


def round_part(edges, local, target, inner, mesh_rows, remote, places, lists, owned, sends, weights, section):
    slots, width = mesh_rows.shape
    last = section == 2
    padded = local.shape[0]
    table_rows = padded + sum(r.shape[0] * r.shape[1] for r in remote)
    out_shape = [
        jax.ShapeDtypeStruct((slots, width), BF16),
        jax.ShapeDtypeStruct((padded, width), BF16),
    ]
    if last:
        out_shape.append(jax.ShapeDtypeStruct((slots, width), BF16))
    vmem = pl.BlockSpec(memory_space=pltpu.VMEM)
    return pl.pallas_call(
        functools.partial(round_kernel, section, places, last),
        in_specs=[vmem] * (8 + len(remote)) + [SMEM] + [HBM] * 4,
        out_shape=out_shape + sends,
        scratch_shapes=[pltpu.VMEM((table_rows, width), BF16), *fetch_scratch(4, width)],
        compiler_params=LIMIT,
        cost_estimate=cost(edges.shape[2] * (table_rows + 1024) * width, 8 * width * width),
        name="round_part",
    )(
        edges, local, target, inner, mesh_rows, *remote, weights["edge_gain"], weights["node_gain"], lists, owned,
        weights["edge_first"], weights["edge_second"], weights["node_first"], weights["node_second"],
    )


def decode_local_kernel(section, grid_ref, table_ref, edges_ref, bias_ref, edge_first, pre_ref, buffers, arrived):
    @pl.when(pl.program_id(0) == 0)
    def _():
        fetch([edge_first.at[section, 1]], buffers, arrived)(0)

    target = dot(grid_ref[...], buffers[0]) + row_of(bias_ref, section)
    for sender in range(edges_ref.shape[1]):
        ids = column(edges_ref[0, sender : sender + 1, :])
        pre_ref[sender] = (dot(one_hot(ids, table_ref.shape[0]), table_ref[...]) + target).astype(BF16)


def decode_local(grid_rows, table, edges, weights, section):
    count, width = grid_rows.shape
    senders = edges.shape[1]
    block = math_block(count, 256)
    return pl.pallas_call(
        functools.partial(decode_local_kernel, section),
        grid=(count // block,),
        in_specs=[
            pl.BlockSpec((block, width), lambda i: (i, 0)),
            whole(table.shape),
            pl.BlockSpec((1, senders, block), lambda i: (0, 0, i)),
            whole(weights["edge_bias"].shape),
            HBM,
        ],
        out_specs=pl.BlockSpec((senders, block, width), lambda i: (0, i, 0)),
        out_shape=jax.ShapeDtypeStruct((senders, count, width), BF16),
        scratch_shapes=fetch_scratch(1, width),
        compiler_params=LIMIT,
        cost_estimate=cost(count * width * (width + senders * table.shape[0]), count * width * 8),
        name="decode_local",
    )(grid_rows, table, edges, weights["edge_bias"], weights["edge_first"])


def decode_kernel(section, places, split, *refs):
    pre_ref, grid_ref, edges_ref = refs[:3]
    remote = refs[3 : 3 + len(places)]
    (
        gain_ref, node_bias_ref, node_gain_ref, edge_second, node_first, node_second, out_ref,
        table, buffers, arrived,
    ) = refs[3 + len(places) :]

    @pl.when(pl.program_id(0) == 0)
    def _():
        take = fetch(
            [
                edge_second.at[section], node_first.at[section, 0], node_first.at[section, 1],
                node_second.at[section],
            ],
            buffers, arrived,
        )
        place_remote(table, remote, places, 0)
        for index in range(4):
            take(index)

    summed = None
    for sender in range(edges_ref.shape[1]):
        ids = column(edges_ref[0, sender : sender + 1, :])
        pre = pre_ref[sender].astype(F32) + dot(one_hot(ids, table.shape[0], split), table[...])
        message = normed(dot(silu(pre).astype(BF16), buffers[0])).astype(BF16).astype(F32)
        summed = message if summed is None else summed + message
    rows = grid_ref[...]
    summed = (summed * row_of(gain_ref, section)).astype(BF16)
    inner = dot(rows, buffers[1]) + dot(summed, buffers[2]) + row_of(node_bias_ref, section)
    update = normed(dot(silu(inner).astype(BF16), buffers[3])) * row_of(node_gain_ref, section)
    out_ref[...] = (rows.astype(F32) + update).astype(BF16)


def decode_part(pre, grid_rows, edges, remote, places, weights, section, split):
    senders, count, width = pre.shape
    block = math_block(count, 256)
    table_rows = sum(r.shape[0] * r.shape[1] for r in remote)
    vectors = whole(weights["edge_bias"].shape)
    return pl.pallas_call(
        functools.partial(decode_kernel, section, places, split),
        grid=(count // block,),
        in_specs=[
            pl.BlockSpec((senders, block, width), lambda i: (0, i, 0)),
            pl.BlockSpec((block, width), lambda i: (i, 0)),
            pl.BlockSpec((1, senders, block), lambda i: (0, 0, i)),
            *[whole(r.shape) for r in remote],
            vectors, vectors, vectors, HBM, HBM, HBM,
        ],
        out_specs=pl.BlockSpec((block, width), lambda i: (i, 0)),
        out_shape=jax.ShapeDtypeStruct((count, width), BF16),
        scratch_shapes=[pltpu.VMEM((table_rows, width), BF16), *fetch_scratch(4, width)],
        compiler_params=LIMIT,
        cost_estimate=cost(count * width * (6 * width + senders * table_rows), count * width * 12),
        name="decode_part",
    )(
        pre, grid_rows, edges, *remote, weights["edge_gain"], weights["node_bias"], weights["node_gain"],
        weights["edge_second"], weights["node_first"], weights["node_second"],
    )


def shift_rows(value, step_aa, step_ba):
    bands, sectors = lax.axis_size("aa"), lax.axis_size("ba")
    pairs = []
    for i in range(bands):
        for j in range(sectors):
            to = ((i + step_aa) % bands) * sectors + (j + step_ba) % sectors
            pairs.append((i * sectors + j, to))
    return lax.ppermute(value, AXES, pairs)


def direct_halo(lists):
    return [shift_rows(rows, ALONG_AA[m], ALONG_BA[m]) for m, rows in enumerate(lists)]


def join_kernel(up_ref, down_ref, right_ref, left_ref, right_out, left_out):
    for index, (own, out) in enumerate(((right_ref, right_out), (left_ref, left_out))):
        out[0] = own[0]
        out[1] = up_ref[index]
        out[2] = down_ref[index]


def halo(up, down, right, left):
    from_up = shift_rows(up, 1, 0)
    from_down = shift_rows(down, -1, 0)
    joined = jax.ShapeDtypeStruct((3,) + right.shape[1:], BF16)
    right, left = pl.pallas_call(
        join_kernel, out_shape=[joined, joined], compiler_params=LIMIT, name="join"
    )(from_up, from_down, right, left)
    from_left = shift_rows(right, 0, 1)
    from_right = shift_rows(left, 0, -1)
    return [from_up[2:3], from_down[2:3], from_left, from_right], ((1,), (6,), (3, 0, 5), (4, 2, 7))


def per_device(
    grid_nodes, mesh_nodes, owned_nodes, grid_rim, mesh_rim, long_send, g2m_edges, short_edges,
    long_edges, m2g_edges, edge_first, edge_second, edge_bias, edge_gain, node_first, node_second,
    node_bias, node_gain,
):
    weights = dict(
        edge_first=edge_first, edge_second=edge_second, edge_bias=edge_bias, edge_gain=edge_gain,
        node_first=node_first, node_second=node_second, node_bias=node_bias, node_gain=node_gain,
    )
    width = grid_nodes.shape[1]
    slots = mesh_nodes.shape[0]
    depth = mesh_rim.shape[2]
    peers, listed = long_send.shape[1:]

    remote = direct_halo(pick_grid(grid_nodes, grid_rim))
    keys, bits = sorted_keys(g2m_edges, slots)
    rim_lists = jnp.concatenate([mesh_rim[0, m : m + 1] for m in SEND_ORDER], 0).reshape(1, 8 * depth)
    long_lists = long_send.reshape(1, peers * listed)
    rim_sends = send_shapes(depth, width)
    proj, target, total, inner = encode_local(keys, bits, grid_nodes, mesh_nodes, weights, 0)
    mesh_one, proj, *sends = encode(
        keys, bits, proj, target, total, inner, mesh_nodes, remote, rim_lists, depth, weights, 0
    )

    remote, places = halo(*sends)
    target, inner = prepare(mesh_one, weights, 1)
    mesh_two, proj, sent = round_part(
        short_edges, proj, target, inner, mesh_one, remote, places, long_lists, owned_nodes,
        [jax.ShapeDtypeStruct((peers * listed, width), BF16)], weights, 1,
    )

    sent = sent.reshape(peers, listed, width)
    arrived = lax.all_to_all(sent, AXES, split_axis=0, concat_axis=0, tiled=True)
    target, inner = prepare(mesh_two, weights, 2)
    mesh_three, proj, mesh_out, *sends = round_part(
        long_edges, proj, target, inner, mesh_two, [arrived.reshape(1, peers * listed, width)], ((0,),),
        rim_lists, owned_nodes, rim_sends, weights, 2,
    )

    remote, places = halo(*sends)
    pre = decode_local(grid_nodes, proj, m2g_edges, weights, 3)
    grid_out = decode_part(pre, grid_nodes, m2g_edges, remote, places, weights, 3, slots)
    return grid_out, mesh_out


def solution(mesh):
    rows = P(AXES, None)
    lists = P(AXES, None, None)
    in_specs = (rows, rows, P(AXES)) + (lists,) * 7 + (P(),) * 8
    return jax.shard_map(
        per_device, mesh=mesh, in_specs=in_specs, out_specs=(rows, rows), check_vma=False
    )
```

time: 133 us -> 137 us (1.030)
  Pallas kernels: 65.2 us -> 42.8 us
  local copies, waits for them, and re-layouts: 18.7 us -> 37.2 us
  between operations: 1.5 us -> 15.1 us
  waiting for transfers between devices: 15.2 us -> 6.89 us
  starting transfers between devices: 28.2 us -> 32.9 us
  other arithmetic: 2.93 us -> 1.52 us
    unnamed x68 -> x99, local copies, waits for them, and re-layouts: 17.9 us -> 37 us
    pallas_call x7 -> x9, Pallas kernels: 48.7 us -> 30.1 us  [the longest x2 10.8 us: round_part(): pl.pallas_call(functools.partial(round_kernel, section, places, last), in...]
    ppermute x14 -> x16, waiting for transfers between devices: 9.24 us -> 3.65 us  [shift_rows(): return lax.ppermute(value, AXES, pairs)]
    ppermute x14 -> x16, starting transfers between devices: 25.6 us -> 30.3 us  [shift_rows(): return lax.ppermute(value, AXES, pairs)]
    pallas_call x1, Pallas kernels: 5.46 us -> 2.33 us  [decode_local(): pl.pallas_call(functools.partial(decode_local_kernel, section), grid=(cou...]
    concatenate x6 -> x0, other arithmetic: 2.93 us -> none  [the longest x2 0.73 us: halo(): left = jnp.concatenate([left, from_up[1:2], from_down[1:2]], 0)]
    all_to_all x1, waiting for transfers between devices: 5.99 us -> 3.24 us  [per_device(): lax.all_to_all(sent, AXES, split_axis=0, concat_axis=0, tiled=True)]
    add x0 -> x1, other arithmetic: none -> 1.52 us  [sorted_keys(): return (lax.sort((senders << shift) + targets, dimension=1), shift)]
  transfers between devices with their start and end apart: 15 -> 17, of which waited for: 7 -> 3; matrix products, arithmetic and copies ran while one was open for 3% -> 0% of each run, Pallas kernels for 14% -> 6%
where the time goes in v2:
time: 137 us
  Pallas kernels  42.8 us (31%)
  local copies, waits for them, and re-layouts  37.2 us (27%)
  starting transfers between devices  32.9 us (24%)
  between operations  15.1 us (11%)
  waiting for transfers between devices  6.89 us (5%)
  other arithmetic  1.52 us (1%)
    unnamed x99, local copies, waits for them, and re-layouts  37 us
    ppermute x16, starting transfers between devices, shift_rows(): return lax.ppermute(value, AXES, pairs)  30.3 us
    pallas_call x2, Pallas kernels, round_part(): pl.pallas_call(functools.partial(round_kernel, section, places, last), in...  10.8 us
    pallas_call x1, Pallas kernels, decode_part(): pl.pallas_call(functools.partial(decode_kernel, section, places, split),...  10.4 us
    pallas_call x1, Pallas kernels, encode(): pl.pallas_call(functools.partial(encode_kernel, section, shift), in_specs...  10.1 us
    pallas_call x1, Pallas kernels, encode_local(): pl.pallas_call(functools.partial(encode_local_kernel, section, shift), in...  5.24 us
    ppermute x16, waiting for transfers between devices, shift_rows(): return lax.ppermute(value, AXES, pairs)  3.65 us
    all_to_all x1, waiting for transfers between devices, per_device(): lax.all_to_all(sent, AXES, split_axis=0, concat_axis=0, tiled=True)  3.24 us
  transfers between devices with their start and end apart: 17, of which 3 were waited for; matrix products, arithmetic and copies ran while one was open for 0% of the time, Pallas kernels for 6%

profile of v2, /device:TPU:0, one launch (start us, length us, event | category | flops | bytes accessed | tf_op | source)
XLA Modules:
  0.0 136.5 jit_solution(4486438354380669935)
XLA Ops:
  10.7 2.0 %pick_grid.1 = (bf16[128,512]{1,0:T(8,128)(2,1)}, bf16[128,512]{1,0:T(8,128)(2,1)}, bf16[128,512]{1,0:T(8,128)(2,1)}, bf16[128,512]{1,0:T(8,128)(2,1)}, bf16[128...) custom-call(bf16[1024,512]{1,0:T(8,128)(2,1)S(1)} %copy-done.19, ...), custom_call_target="tpu_custom_call" | custom-call | flops 1073741824 | bytes 2097152 | tf_op jit(solution)/shard_map/pick_grid/pallas_call | solution.py:136
  14.0 6.4 %collective-permute-start = (bf16[128,512]{1,0:T(8,128)(2,1)}, bf16[128,512]{1,0:T(8,128)(2,1)}, u32[]{:S(2)}, u32[]{:S(2)}) collective-permute-start(bf16[128,512]{1,0:T(8,128)(2,1)} %get-tuple-element.41), channel_id=1, source_target_pairs={{0,31},{1,24},{2,25},{3,26},{4,27},{5,28},{6,29},{7,30},{8,7},{9,0... | collective-permute-start | bytes 393224 | tf_op jit(solution)/shard_map/ppermute | solution.py:550
  21.2 4.2 %collective-permute-start.3 = (bf16[128,512]{1,0:T(8,128)(2,1)}, bf16[128,512]{1,0:T(8,128)(2,1)}, u32[]{:S(2)}, u32[]{:S(2)}) collective-permute-start(bf16[128,512]{1,0:T(8,128)(2,1)} %get-tuple-element.44), channel_id=1, source_target_pairs={{0,7},{1,0},{2,1},{3,2},{4,3},{5,4},{6,5},{7,6},{8,15},{9,8},{10,9... | collective-permute-start | bytes 393224 | tf_op jit(solution)/shard_map/ppermute | solution.py:550
  25.5 4.5 %collective-permute-start.5 = (bf16[128,512]{1,0:T(8,128)(2,1)}, bf16[128,512]{1,0:T(8,128)(2,1)}, u32[]{:S(2)}, u32[]{:S(2)}) collective-permute-start(bf16[128,512]{1,0:T(8,128)(2,1)} %copy-done.42), channel_id=1, source_target_pairs={{0,15},{1,8},{2,9},{3,10},{4,11},{5,12},{6,13},{7,14},{8,23},{9,16... | collective-permute-start | bytes 393224 | tf_op jit(solution)/shard_map/ppermute | solution.py:550
  31.4 2.2 %copy-done = bf16[4,2,512,512]{3,2,1,0:T(8,128)(2,1)S(1)} copy-done((bf16[4,2,512,512]{3,2,1,0:T(8,128)(2,1)S(1)}, bf16[4,2,512,512]{3,2,1,0:T(8,128)(2,1)}, u32[]{:S(2)}) %copy-start) | copy-done | bytes 4194328
  33.6 2.2 %copy-done.7 = bf16[4,2,512,512]{3,2,1,0:T(8,128)(2,1)S(1)} copy-done((bf16[4,2,512,512]{3,2,1,0:T(8,128)(2,1)S(1)}, bf16[4,2,512,512]{3,2,1,0:T(8,128)(2,1)}, u32[]{:S(2)}) %copy-start.7) | copy-done | bytes 4194328
  36.5 5.2 %encode_local.1 = (bf16[1024,512]{1,0:T(8,128)(2,1)S(1)}, bf16[256,512]{1,0:T(8,128)(2,1)S(1)}, f32[192,512]{1,0:T(8,128)S(1)}, f32[192,512]{1,0:T(8,128)S(1)}) custom-call(s32[1,3072]{1,0:T(1,128)S(1)} %copy-done.43, s32[1,3072]{1,0:T(1,128)S(1)} %copy-done.43, bf16[1024,512]{1,0:T(8,128)(2,1)S(1)} %copy-done.20, bf16[192,512]{1,0:T(8,128)(2,1)S(1)} %copy-done.39, ...), custom_call_target="tpu_custom_call" | custom-call | flops 4718592000 | bytes 3145728 | tf_op jit(solution)/shard_map/encode_local/pallas_call | solution.py:249
  41.9 10.1 %encode.1 = (bf16[192,512]{1,0:T(8,128)(2,1)S(1)}, bf16[256,512]{1,0:T(8,128)(2,1)S(1)}, bf16[3,16,512]{2,1,0:T(8,128)(2,1)S(1)}, bf16[3,16,512]{2,1,0:T(8,128)(...) custom-call(s32[1,3072]{1,0:T(1,128)S(1)} %copy-done.43, s32[1,3072]{1,0:T(1,128)S(1)} %copy-done.43, ...), custom_call_target="tpu_custom_call" | custom-call | flops 4718592000 | bytes 8388608 | tf_op jit(solution)/shard_map/encode/pallas_call | solution.py:320
  54.5 1.9 %collective-permute-done.8.up_ref = bf16[3,16,512]{2,1,0:T(8,128)(2,1)S(1)} collective-permute-done((bf16[3,16,512]{2,1,0:T(8,128)(2,1)S(1)}, bf16[3,16,512]{2,1,0:T(8,128)(2,1)S(1)}, u32[]{:S(2)}, u32[]{:S(2)}) %collective-permute-start.8) | collective-permute-done | bytes 49184 | tf_op jit(solution)/shard_map/ppermute | solution.py:550
  57.0 4.7 %collective-permute-start.11 = (bf16[3,16,512]{2,1,0:T(8,128)(2,1)}, bf16[3,16,512]{2,1,0:T(8,128)(2,1)}, u32[]{:S(2)}, u32[]{:S(2)}) collective-permute-start(bf16[3,16,512]{2,1,0:T(8,128)(2,1)} %get-tuple-element.58), channel_id=1, source_target_pairs={{0,7},{1,0},{2,1},{3,2},{4,3},{5,4},{6,5},{7,6},{8,15},{9,8},{10,9... | collective-permute-start | bytes 147464 | tf_op jit(solution)/shard_map/ppermute | solution.py:550
  62.6 2.2 %copy-done.2 = bf16[4,2,512,512]{3,2,1,0:T(8,128)(2,1)S(1)} copy-done((bf16[4,2,512,512]{3,2,1,0:T(8,128)(2,1)S(1)}, bf16[4,2,512,512]{3,2,1,0:T(8,128)(2,1)}, u32[]{:S(2)}) %copy-start.2) | copy-done | bytes 4194328
  64.7 2.2 %copy-done.9 = bf16[4,2,512,512]{3,2,1,0:T(8,128)(2,1)S(1)} copy-done((bf16[4,2,512,512]{3,2,1,0:T(8,128)(2,1)S(1)}, bf16[4,2,512,512]{3,2,1,0:T(8,128)(2,1)}, u32[]{:S(2)}) %copy-start.9) | copy-done | bytes 4194328
  72.0 5.6 %round_part.2 = (bf16[192,512]{1,0:T(8,128)(2,1)S(1)}, bf16[256,512]{1,0:T(8,128)(2,1)S(1)}, bf16[256,512]{1,0:T(8,128)(2,1)S(1)}) custom-call(s32[1,2,1536]{2,1,0:T(2,128)S(1)} %copy-done.37, bf16[256,512]{1,0:T(8,128)(2,1)S(1)} %copy-done.27, bf16[256,512]{1,0:T(8,128)(2,1)S(1)} %get-tuple-element.51.refs_2_, f32[192,512]{1,0:T(8,128)S(1)} %get-tuple-element.52.refs_3_, ...), custom_call_target="tpu_custom_call" | custom-call | flops 2214592512 | bytes 2097152 | tf_op jit(solution)/shard_map/round_part/pallas_call | solution.py:434
  79.7 2.6 %all-to-all-start = ((bf16[32,8,512]{2,1,0:T(8,128)(2,1)}), bf16[32,8,512]{2,1,0:T(8,128)(2,1)S(1)}, u32[]{:S(2)}, u32[]{:S(2)}) async-start(bf16[32,8,512]{2,1,0:T(8,128)(2,1)} %bitcast.23), calls=%async_computation | async-start | bytes 524288 | tf_op jit(solution)/shard_map/all_to_all | solution.py:608
  82.3 2.2 %copy-done.4 = bf16[4,2,512,512]{3,2,1,0:T(8,128)(2,1)S(1)} copy-done((bf16[4,2,512,512]{3,2,1,0:T(8,128)(2,1)S(1)}, bf16[4,2,512,512]{3,2,1,0:T(8,128)(2,1)}, u32[]{:S(2)}) %copy-start.4) | copy-done | bytes 4194328
  84.5 2.2 %copy-done.11 = bf16[4,2,512,512]{3,2,1,0:T(8,128)(2,1)S(1)} copy-done((bf16[4,2,512,512]{3,2,1,0:T(8,128)(2,1)S(1)}, bf16[4,2,512,512]{3,2,1,0:T(8,128)(2,1)}, u32[]{:S(2)}) %copy-start.11) | copy-done | bytes 4194328
  89.7 3.2 %all-to-all-done = bf16[32,8,512]{2,1,0:T(8,128)(2,1)S(1)} async-done(((bf16[32,8,512]{2,1,0:T(8,128)(2,1)}), bf16[32,8,512]{2,1,0:T(8,128)(2,1)S(1)}, u32[]{:S(2)}, u32[]{:S(2)}) %all-to-all-start) | async-done | bytes 262176 | tf_op jit(solution)/shard_map/all_to_all | solution.py:608
  92.9 2.2 %copy-done.5 = bf16[4,2,512,512]{3,2,1,0:T(8,128)(2,1)S(1)} copy-done((bf16[4,2,512,512]{3,2,1,0:T(8,128)(2,1)S(1)}, bf16[4,2,512,512]{3,2,1,0:T(8,128)(2,1)}, u32[]{:S(2)}) %copy-start.5) | copy-done | bytes 4194328
  95.1 2.2 %copy-done.12 = bf16[4,2,512,512]{3,2,1,0:T(8,128)(2,1)S(1)} copy-done((bf16[4,2,512,512]{3,2,1,0:T(8,128)(2,1)S(1)}, bf16[4,2,512,512]{3,2,1,0:T(8,128)(2,1)}, u32[]{:S(2)}) %copy-start.12) | copy-done | bytes 4194328
  102.7 5.3 %round_part.3 = (bf16[192,512]{1,0:T(8,128)(2,1)}, bf16[256,512]{1,0:T(8,128)(2,1)S(1)}, bf16[192,512]{1,0:T(8,128)(2,1)}, bf16[3,16,512]{2,1,0:T(8,128)(2,1)S(1...) custom-call(s32[1,2,1536]{2,1,0:T(2,128)S(1)} %copy-done.38, ...), custom_call_target="tpu_custom_call" | custom-call | flops 2415919104 | bytes 2097152 | tf_op jit(solution)/shard_map/round_part/pallas_call | solution.py:434
  109.8 1.8 %collective-permute-done.12.up_ref = bf16[3,16,512]{2,1,0:T(8,128)(2,1)S(1)} collective-permute-done((bf16[3,16,512]{2,1,0:T(8,128)(2,1)S(1)}, bf16[3,16,512]{2,1,0:T(8,128)(2,1)S(1)}, u32[]{:S(2)}, u32[]{:S(2)}) %collective-permute-start.12) | collective-permute-done | bytes 49184 | tf_op jit(solution)/shard_map/ppermute | solution.py:550
  112.7 3.7 %collective-permute-start.15 = (bf16[3,16,512]{2,1,0:T(8,128)(2,1)S(1)}, bf16[3,16,512]{2,1,0:T(8,128)(2,1)S(1)}, u32[]{:S(2)}, u32[]{:S(2)}) collective-permute-start(bf16[3,16,512]{2,1,0:T(8,128)(2,1)S(1)} %get-tuple-element.70), channel_id=1, source_target_pairs={{0,7},{1,0},{2,1},{3,2},{4,3},{5,4},{6,5},{7,6},{8,15},{9,8},{10,9... | collective-permute-start | bytes 147464 | tf_op jit(solution)/shard_map/ppermute | solution.py:550
  116.4 2.3 %decode_local.1.refs_0_ = bf16[3,1024,512]{2,1,0:T(8,128)(2,1)S(1)} custom-call(bf16[1024,512]{1,0:T(8,128)(2,1)S(1)} %copy-done.20, bf16[256,512]{1,0:T(8,128)(2,1)S(1)} %get-tuple-element.64.table_ref, s32[1,3,1024]{2,1,0:T(4,128)S(1)} %copy.24.edges_ref.refs_2_, f32[4,512]{1,0:T(4,128)S(1)} %copy-done.35, bf16[4,2,512,512]{3,2,1,0:T(8,128)(2,1)S(1)} %copy-done.6), custom_call_target="tpu_custom_call" | custom-call | flops 1342177280 | bytes 4194304 | tf_op jit(solution)/shard_map/decode_local/pallas_call | solution.py:463
  119.2 10.4 %decode_part.1 = bf16[1024,512]{1,0:T(8,128)(2,1)} custom-call(bf16[3,1024,512]{2,1,0:T(8,128)(2,1)S(1)} %decode_local.1.refs_0_, bf16[1024,512]{1,0:T(8,128)(2,1)S(1)} %copy-done.20, s32[1,3,1024]{2,1,0:T(4,128)S(1)} %copy.24.edges_ref.refs_2_, bf16[1,16,512]{2,1,0:T(8,128)(2,1)S(1)} %slice.58.refs_3_, bf16[1,16,512]{2,1,0:T(8,128)(2,1)S(1)} %slice.59.refs_4_, ...), custom_call_target="tpu_custom_call" | custom-call | flops 3623878656 | bytes 6291456 | tf_op jit(solution)/shard_map/decode_part/pallas_call | solution.py:521
  (131 shorter events, 30.1 us)
Async XLA Ops:
  7.2 24.2 %copy-start.14 = (bf16[4,512,512]{2,1,0:T(8,128)(2,1)S(1)}, bf16[4,512,512]{2,1,0:T(8,128)(2,1)}, u32[]{:S(2)}) copy-start(bf16[4,512,512]{2,1,0:T(8,128)(2,1)} %refs_10_.5) | copy-start | bytes 6291460
  7.2 24.2 %sort.9.cloned.1.call-start = ((), (), s32[]{:S(2)}) async-start(), calls=%async_computation.1 | async-start | bytes 36896 | tf_op jit(solution)/shard_map/sort | solution.py:176
  10.7 20.7 %copy-start.20 = (bf16[1024,512]{1,0:T(8,128)(2,1)S(1)}, bf16[1024,512]{1,0:T(8,128)(2,1)}, u32[]{:S(2)}) copy-start(bf16[1024,512]{1,0:T(8,128)(2,1)} %refs_1_.1) | copy-start | bytes 3145732
  10.7 20.7 %copy-start.35 = (f32[4,512]{1,0:T(4,128)S(1)}, f32[4,512]{1,0:T(4,128)}, u32[]{:S(2)}) copy-start(f32[4,512]{1,0:T(4,128)} %bias_ref.7) | copy-start | bytes 24580
  10.7 20.7 %copy-start.36 = (f32[4,512]{1,0:T(4,128)S(1)}, f32[4,512]{1,0:T(4,128)}, u32[]{:S(2)}) copy-start(f32[4,512]{1,0:T(4,128)} %refs_8_.1) | copy-start | bytes 24580
  10.7 20.7 %copy-start.39 = (bf16[192,512]{1,0:T(8,128)(2,1)S(1)}, bf16[192,512]{1,0:T(8,128)(2,1)}, u32[]{:S(2)}) copy-start(bf16[192,512]{1,0:T(8,128)(2,1)} %refs_6_.2) | copy-start | bytes 589828
  14.0 11.5 %collective-permute-start = (bf16[128,512]{1,0:T(8,128)(2,1)}, bf16[128,512]{1,0:T(8,128)(2,1)}, u32[]{:S(2)}, u32[]{:S(2)}) collective-permute-start(bf16[128,512]{1,0:T(8,128)(2,1)} %get-tuple-element.41), channel_id=1, source_target_pairs={{0,31},{1,24},{2,25},{3,26},{4,27},{5,28},{6,29},{7,30},{8,7},{9,0... | collective-permute-start | bytes 393224 | tf_op jit(solution)/shard_map/ppermute | solution.py:550
  20.3 9.7 %collective-permute-start.1 = (bf16[128,512]{1,0:T(8,128)(2,1)}, bf16[128,512]{1,0:T(8,128)(2,1)}, u32[]{:S(2)}, u32[]{:S(2)}) collective-permute-start(bf16[128,512]{1,0:T(8,128)(2,1)} %get-tuple-element.42), channel_id=1, source_target_pairs={{0,24},{1,25},{2,26},{3,27},{4,28},{5,29},{6,30},{7,31},{8,0},{9,1... | collective-permute-start | bytes 393224 | tf_op jit(solution)/shard_map/ppermute | solution.py:550
  21.2 9.9 %collective-permute-start.2 = (bf16[128,512]{1,0:T(8,128)(2,1)}, bf16[128,512]{1,0:T(8,128)(2,1)}, u32[]{:S(2)}, u32[]{:S(2)}) collective-permute-start(bf16[128,512]{1,0:T(8,128)(2,1)} %get-tuple-element.43), channel_id=1, source_target_pairs={{0,25},{1,26},{2,27},{3,28},{4,29},{5,30},{6,31},{7,24},{8,1},{9,2... | collective-permute-start | bytes 393224 | tf_op jit(solution)/shard_map/ppermute | solution.py:550
  21.2 20.6 %collective-permute-start.3 = (bf16[128,512]{1,0:T(8,128)(2,1)}, bf16[128,512]{1,0:T(8,128)(2,1)}, u32[]{:S(2)}, u32[]{:S(2)}) collective-permute-start(bf16[128,512]{1,0:T(8,128)(2,1)} %get-tuple-element.44), channel_id=1, source_target_pairs={{0,7},{1,0},{2,1},{3,2},{4,3},{5,4},{6,5},{7,6},{8,15},{9,8},{10,9... | collective-permute-start | bytes 393224 | tf_op jit(solution)/shard_map/ppermute | solution.py:550
  25.3 16.5 %collective-permute-start.4 = (bf16[128,512]{1,0:T(8,128)(2,1)}, bf16[128,512]{1,0:T(8,128)(2,1)}, u32[]{:S(2)}, u32[]{:S(2)}) collective-permute-start(bf16[128,512]{1,0:T(8,128)(2,1)} %get-tuple-element.45), channel_id=1, source_target_pairs={{0,1},{1,2},{2,3},{3,4},{4,5},{5,6},{6,7},{7,0},{8,9},{9,10},{10,1... | collective-permute-start | bytes 393224 | tf_op jit(solution)/shard_map/ppermute | solution.py:550
  25.5 16.3 %collective-permute-start.5 = (bf16[128,512]{1,0:T(8,128)(2,1)}, bf16[128,512]{1,0:T(8,128)(2,1)}, u32[]{:S(2)}, u32[]{:S(2)}) collective-permute-start(bf16[128,512]{1,0:T(8,128)(2,1)} %copy-done.42), channel_id=1, source_target_pairs={{0,15},{1,8},{2,9},{3,10},{4,11},{5,12},{6,13},{7,14},{8,23},{9,16... | collective-permute-start | bytes 393224 | tf_op jit(solution)/shard_map/ppermute | solution.py:550
  30.0 11.8 %collective-permute-start.6 = (bf16[128,512]{1,0:T(8,128)(2,1)}, bf16[128,512]{1,0:T(8,128)(2,1)}, u32[]{:S(2)}, u32[]{:S(2)}) collective-permute-start(bf16[128,512]{1,0:T(8,128)(2,1)} %copy-done.41), channel_id=1, source_target_pairs={{0,8},{1,9},{2,10},{3,11},{4,12},{5,13},{6,14},{7,15},{8,16},{9,17... | collective-permute-start | bytes 393224 | tf_op jit(solution)/shard_map/ppermute | solution.py:550
  31.1 10.7 %collective-permute-start.7 = (bf16[128,512]{1,0:T(8,128)(2,1)S(1)}, bf16[128,512]{1,0:T(8,128)(2,1)}, u32[]{:S(2)}, u32[]{:S(2)}) collective-permute-start(bf16[128,512]{1,0:T(8,128)(2,1)S(1)} %get-tuple-element.48), channel_id=1, source_target_pairs={{0,9},{1,10},{2,11},{3,12},{4,13},{5,14},{6,15},{7,8},{8,17},{9,18... | collective-permute-start | bytes 393224 | tf_op jit(solution)/shard_map/ppermute | solution.py:550
  41.9 20.5 %copy-start.46 = (s32[1,32,8]{1,2,0:T(8,128)S(1)}, s32[1,32,8]{1,2,0:T(8,128)}, u32[]{:S(2)}) copy-start(s32[1,32,8]{1,2,0:T(8,128)} %param.23) | copy-start | bytes 3076
  52.8 3.6 %collective-permute-start.8 = (bf16[3,16,512]{2,1,0:T(8,128)(2,1)S(1)}, bf16[3,16,512]{2,1,0:T(8,128)(2,1)S(1)}, u32[]{:S(2)}, u32[]{:S(2)}) collective-permute-start(bf16[3,16,512]{2,1,0:T(8,128)(2,1)S(1)} %get-tuple-element.53), channel_id=1, source_target_pairs={{0,8},{1,9},{2,10},{3,11},{4,12},{5,13},{6,14},{7,15},{8,16},{9,17... | collective-permute-start | bytes 147464 | tf_op jit(solution)/shard_map/ppermute | solution.py:550
  52.8 3.6 %collective-permute-start.9 = (bf16[3,16,512]{2,1,0:T(8,128)(2,1)S(1)}, bf16[3,16,512]{2,1,0:T(8,128)(2,1)S(1)}, u32[]{:S(2)}, u32[]{:S(2)}) collective-permute-start(bf16[3,16,512]{2,1,0:T(8,128)(2,1)S(1)} %get-tuple-element.54), channel_id=1, source_target_pairs={{0,24},{1,25},{2,26},{3,27},{4,28},{5,29},{6,30},{7,31},{8,0},{9,1... | collective-permute-start | bytes 147464 | tf_op jit(solution)/shard_map/ppermute | solution.py:550
  57.0 10.6 %collective-permute-start.10 = (bf16[3,16,512]{2,1,0:T(8,128)(2,1)}, bf16[3,16,512]{2,1,0:T(8,128)(2,1)S(1)}, u32[]{:S(2)}, u32[]{:S(2)}) collective-permute-start(bf16[3,16,512]{2,1,0:T(8,128)(2,1)} %get-tuple-element.57), channel_id=1, source_target_pairs={{0,1},{1,2},{2,3},{3,4},{4,5},{5,6},{6,7},{7,0},{8,9},{9,10},{10,1... | collective-permute-start | bytes 147464 | tf_op jit(solution)/shard_map/ppermute | solution.py:550
  57.0 10.6 %collective-permute-start.11 = (bf16[3,16,512]{2,1,0:T(8,128)(2,1)}, bf16[3,16,512]{2,1,0:T(8,128)(2,1)}, u32[]{:S(2)}, u32[]{:S(2)}) collective-permute-start(bf16[3,16,512]{2,1,0:T(8,128)(2,1)} %get-tuple-element.58), channel_id=1, source_target_pairs={{0,7},{1,0},{2,1},{3,2},{4,3},{5,4},{6,5},{7,6},{8,15},{9,8},{10,9... | collective-permute-start | bytes 147464 | tf_op jit(solution)/shard_map/ppermute | solution.py:550
  79.7 13.2 %all-to-all-start = ((bf16[32,8,512]{2,1,0:T(8,128)(2,1)}), bf16[32,8,512]{2,1,0:T(8,128)(2,1)S(1)}, u32[]{:S(2)}, u32[]{:S(2)}) async-start(bf16[32,8,512]{2,1,0:T(8,128)(2,1)} %bitcast.23), calls=%async_computation | async-start | bytes 524288 | tf_op jit(solution)/shard_map/all_to_all | solution.py:608
  108.0 3.6 %collective-permute-start.12 = (bf16[3,16,512]{2,1,0:T(8,128)(2,1)S(1)}, bf16[3,16,512]{2,1,0:T(8,128)(2,1)S(1)}, u32[]{:S(2)}, u32[]{:S(2)}) collective-permute-start(bf16[3,16,512]{2,1,0:T(8,128)(2,1)S(1)} %get-tuple-element.65), channel_id=1, source_target_pairs={{0,8},{1,9},{2,10},{3,11},{4,12},{5,13},{6,14},{7,15},{8,16},{9,17... | collective-permute-start | bytes 147464 | tf_op jit(solution)/shard_map/ppermute | solution.py:550
  108.1 3.5 %collective-permute-start.13 = (bf16[3,16,512]{2,1,0:T(8,128)(2,1)S(1)}, bf16[3,16,512]{2,1,0:T(8,128)(2,1)S(1)}, u32[]{:S(2)}, u32[]{:S(2)}) collective-permute-start(bf16[3,16,512]{2,1,0:T(8,128)(2,1)S(1)} %get-tuple-element.66), channel_id=1, source_target_pairs={{0,24},{1,25},{2,26},{3,27},{4,28},{5,29},{6,30},{7,31},{8,0},{9,1... | collective-permute-start | bytes 147464 | tf_op jit(solution)/shard_map/ppermute | solution.py:550
  111.6 7.2 %collective-permute-start.14 = (bf16[3,16,512]{2,1,0:T(8,128)(2,1)S(1)}, bf16[3,16,512]{2,1,0:T(8,128)(2,1)S(1)}, u32[]{:S(2)}, u32[]{:S(2)}) collective-permute-start(bf16[3,16,512]{2,1,0:T(8,128)(2,1)S(1)} %get-tuple-element.69), channel_id=1, source_target_pairs={{0,1},{1,2},{2,3},{3,4},{4,5},{5,6},{6,7},{7,0},{8,9},{9,10},{10,1... | collective-permute-start | bytes 147464 | tf_op jit(solution)/shard_map/ppermute | solution.py:550
  112.7 6.1 %collective-permute-start.15 = (bf16[3,16,512]{2,1,0:T(8,128)(2,1)S(1)}, bf16[3,16,512]{2,1,0:T(8,128)(2,1)S(1)}, u32[]{:S(2)}, u32[]{:S(2)}) collective-permute-start(bf16[3,16,512]{2,1,0:T(8,128)(2,1)S(1)} %get-tuple-element.70), channel_id=1, source_target_pairs={{0,7},{1,0},{2,1},{3,2},{4,3},{5,4},{6,5},{7,6},{8,15},{9,8},{10,9... | collective-permute-start | bytes 147464 | tf_op jit(solution)/shard_map/ppermute | solution.py:550
  (42 other events, 124.3 us)
Sparse Core Ops, SparseCore 0:
  10.4 7.8 sort.11.cloned.1.call-done
  (1 shorter events, 0.0 us)

commit v3 on v2

v3 whole, which is shorter than its diff:
```python
import functools

import jax
import jax.numpy as jnp
from jax import lax
from jax.experimental import pallas as pl
from jax.experimental.pallas import tpu as pltpu
from jax.sharding import PartitionSpec as P

EPSILON = 1e-05
AXES = ("aa", "ba")
LANES = 128
BF16 = jnp.bfloat16
F32 = jnp.float32
LIMIT = pltpu.CompilerParams(vmem_limit_bytes=28 * 1024 * 1024)

UP_LISTS = (7, 5, 6)
DOWN_LISTS = (2, 0, 1)
RIGHT_LIST = 4
LEFT_LIST = 3
SEND_ORDER = UP_LISTS + DOWN_LISTS + (RIGHT_LIST, LEFT_LIST)


def dot(left, right):
    return jnp.dot(left, right, preferred_element_type=F32)


def math_block(total, most):
    block = most
    while total % block:
        block -= LANES
    return block


def round_up(value, unit):
    return -(-value // unit) * unit


def column(row):
    tall = jnp.broadcast_to(row, (LANES, row.shape[1]))
    return jnp.transpose(tall).astype(jnp.int16)


def one_hot(ids, width, base=0):
    lane = lax.broadcasted_iota(jnp.int16, ids.shape, 1)
    parts = [
        jnp.where(ids == lane + jnp.int16(base + start), BF16(1), BF16(0))
        for start in range(0, width, LANES)
    ]
    return parts[0] if len(parts) == 1 else jnp.concatenate(parts, 1)


def silu(value):
    half = 0.5 * value
    return half + half * jnp.tanh(half)


def normed(value):
    average = jnp.mean(value, axis=-1, keepdims=True)
    centred = value - average
    spread = jnp.mean(centred * centred, axis=-1, keepdims=True)
    return centred * lax.rsqrt(spread + EPSILON)


def whole(shape):
    return pl.BlockSpec(shape, lambda *_: (0,) * len(shape))


def cost(macs, moved):
    return pl.CostEstimate(flops=2 * macs, bytes_accessed=moved, transcendentals=0)


HBM = pl.BlockSpec(memory_space=pltpu.HBM)
SMEM = pl.BlockSpec(memory_space=pltpu.SMEM)


def stay(stack):
    return pltpu.with_memory_space_constraint(stack, pltpu.HBM)


def near(value):
    return pltpu.with_memory_space_constraint(value, pltpu.VMEM)


def fetch(sources, buffers, arrived):
    copies = [
        pltpu.make_async_copy(source, buffers.at[i], arrived.at[i]) for i, source in enumerate(sources)
    ]
    for copy in copies:
        copy.start()
    return copies


def fetch_scratch(count, width):
    return [pltpu.VMEM((count, width, width), BF16), pltpu.SemaphoreType.DMA((count,))]


def matrices(count, width):
    return pltpu.VMEM((count, width, width), BF16)


def fill(ref, value):
    rows = value.shape[0]
    ref[:rows] = value
    if ref.shape[0] > rows:
        ref[rows:] = jnp.zeros((ref.shape[0] - rows, ref.shape[1]), ref.dtype)


def clear_tail(ref, rows):
    ref[rows:] = jnp.zeros((ref.shape[0] - rows, ref.shape[1]), ref.dtype)


def row_of(ref, index):
    return ref[index : index + 1]


def added(pre, targets, second, slots):
    hidden = silu(pre).astype(BF16)
    message = normed(dot(hidden, second)).astype(BF16)
    member = lax.broadcasted_iota(jnp.int32, (slots, targets.shape[1]), 0) == targets
    return dot(member.astype(BF16), message)


def updated(rows, total, inner, first, second, gain):
    inner = inner + dot(total.astype(BF16), first)
    update = normed(dot(silu(inner).astype(BF16), second)) * gain
    return (rows.astype(F32) + update).astype(BF16)


def side_base():
    return jnp.where(lax.axis_index("aa") % 2 == 0, 5, 0)


def pick_kernel(rows_ref, rim_ref, pair_out, right_out, left_out, *outer_outs):
    depth = right_out.shape[0]
    pair = side_base()
    outer = 5 - pair

    def pick(chosen):
        ids = column(rim_ref[0, pl.ds(chosen, 1), :])
        return dot(one_hot(ids, rows_ref.shape[0]), rows_ref[...]).astype(BF16)

    for index, offset in enumerate((2, 0, 1)):
        pair_out[index * depth : (index + 1) * depth] = pick(pair + offset)
    right_out[...] = pick(RIGHT_LIST)
    left_out[...] = pick(LEFT_LIST)
    for out, offset in zip(outer_outs, (2, 0, 1)):
        out[...] = pick(outer + offset)


def pick_grid(rows, rim):
    count, width = rows.shape
    depth = rim.shape[2]
    block = jax.ShapeDtypeStruct((depth, width), BF16)
    return pl.pallas_call(
        pick_kernel,
        out_shape=[jax.ShapeDtypeStruct((3 * depth, width), BF16)] + [block] * 5,
        compiler_params=LIMIT,
        cost_estimate=cost(8 * depth * count * width, 2 * (count + 8 * depth) * width),
        name="pick_grid",
    )(rows, rim)


def pair_join_kernel(shift, slots, pair_ref, right_ref, left_ref, edges_ref, right_out, left_out, keys_out):
    depth = right_ref.shape[0]
    for index, (own, out) in enumerate(((right_ref, right_out), (left_ref, left_out))):
        out[:depth] = own[...]
        out[depth:] = pair_ref[index * depth : (index + 1) * depth]
    senders, targets = edges_ref[0, 0:1], edges_ref[0, 1:2]
    senders = jnp.where(targets < slots, senders, 1 << 14)
    keys_out[...] = (senders << shift) + targets


def pair_join(pair, right, left, edges, slots):
    depth, width = right.shape
    shift = slots.bit_length()
    joined = jax.ShapeDtypeStruct((2 * depth, width), BF16)
    right, left, keys = pl.pallas_call(
        functools.partial(pair_join_kernel, shift, slots),
        out_shape=[joined, joined, jax.ShapeDtypeStruct((1, edges.shape[2]), jnp.int32)],
        compiler_params=LIMIT,
        name="pair_join",
    )(pair, right, left, edges)
    return right, left, lax.sort(keys.reshape(-1)).reshape(1, -1), shift


def grid_halo(rows, rim, edges, slots):
    pair, right, left, *outer = pick_grid(rows, rim)
    pair = move(pair, lambda i, j: (i ^ 1, j))
    right, left, keys, shift = pair_join(pair, right, left, edges, slots)
    other = lambda i: i + 1 if i % 2 else i - 1
    arrived = [
        move(right, lambda i, j: (i, j + 1)),
        move(left, lambda i, j: (i, j - 1)),
        move(outer[0], lambda i, j: (other(i), j + 1)),
        move(outer[1], lambda i, j: (other(i), j - 1)),
        move(outer[2], lambda i, j: (other(i), j)),
    ]
    return [pair] + arrived, keys, shift


def send_shapes(depth, width):
    return [jax.ShapeDtypeStruct((n, depth, width), BF16) for n in (3, 3, 1, 1)]


def list_rows(proj_out, lists_ref, sends):
    listed = lists_ref.shape[1]
    size = math_block(listed, 256)
    made = []
    for start in range(0, listed, size):
        picked = one_hot(column(lists_ref[0:1, start : start + size]), proj_out.shape[0])
        made.append(dot(picked, proj_out[...]).astype(BF16))
    made = made[0] if len(made) == 1 else jnp.concatenate(made, 0)
    place = 0
    for ref in sends:
        if len(ref.shape) == 2:
            ref[...] = made
            continue
        depth = ref.shape[1]
        for index in range(ref.shape[0]):
            ref[index] = made[place : place + depth]
            place += depth


WINDOW = 512
BLOCK = 512


def below(keys, limit):
    total = keys.shape[1]
    step = 1 << (total.bit_length() - 1)
    found = jnp.int32(0)
    while step:
        place = found + step
        inside = keys[0, jnp.minimum(place, total) - 1] < limit
        found = jnp.where((place <= total) & inside, place, found)
        step //= 2
    return found


def edge_block(start, used, shift, scalars, keys_ref, table, target, pre, second, slots):
    block = pre.shape[0]
    start = pl.multiple_of(start, LANES)
    keys = keys_ref[0:1, pl.ds(start, block)]
    senders = keys >> shift
    targets = keys & ((1 << shift) - 1)
    lowest = pl.multiple_of((scalars[0, start] >> shift) // 16 * 16, 16)
    highest = scalars[0, jnp.minimum(start + block, used) - 1] >> shift

    def window(base):
        ids = column(jnp.clip(senders - base, -1, 1 << 14))
        return dot(one_hot(ids, WINDOW), table[pl.ds(base, WINDOW)])

    pre[...] = window(lowest) + dot(one_hot(column(targets), target.shape[0]), target[...])

    def more(index, carry):
        pre[...] += window(pl.multiple_of(lowest + (index + 1) * WINDOW, 16))
        return carry

    lax.fori_loop(0, (highest - lowest) // WINDOW, more, 0)
    return added(pre[...], targets, second, slots)


def encode_local_kernel(
    section, shift, scalars, keys_ref, grid_ref, mesh_ref, bias_ref, node_bias_ref,
    edge_first, edge_second, node_first, node_second, table_out, target_out, total_out, inner_out, later,
    table, pre, own, arrived, later_arrived,
):
    copies = fetch(
        [edge_first.at[section, 0], edge_first.at[section, 1], node_first.at[section, 0]], own, arrived
    )
    copies += fetch(
        [
            edge_second.at[section], edge_first.at[section, 0], node_first.at[section, 1],
            node_second.at[section], edge_first.at[section + 1, 0],
        ],
        later, later_arrived,
    )
    count, slots = grid_ref.shape[0], mesh_ref.shape[0]
    copies[0].wait()
    proj = dot(grid_ref[...], own[0]).astype(BF16)
    table_out[...] = proj
    fill(table, proj)
    rows = mesh_ref[...]
    copies[1].wait()
    fill(target_out, (dot(rows, own[1]) + row_of(bias_ref, section)).astype(BF16))
    copies[2].wait()
    inner_out[...] = dot(rows, own[2]) + row_of(node_bias_ref, section)
    for copy in copies[3:]:
        copy.wait()
    total_out[...] = jnp.zeros_like(total_out)
    block = pre.shape[0]
    done = below(scalars, count << shift) // block

    def step(index, carry):
        total_out[...] += edge_block(
            index * block, done * block, shift, scalars, keys_ref, table, target_out, pre, later[0], slots
        )
        return carry

    lax.fori_loop(0, done, step, 0)


def encode_local(keys, shift, grid_rows, mesh_rows, weights, section):
    total = keys.shape[1]
    count, width = grid_rows.shape
    slots = mesh_rows.shape[0]
    vmem = pl.BlockSpec(memory_space=pltpu.VMEM)
    return pl.pallas_call(
        functools.partial(encode_local_kernel, section, shift),
        in_specs=[SMEM] + [vmem] * 5 + [HBM] * 4,
        out_shape=[
            pltpu.VMEM((count, width), BF16),
            pltpu.VMEM((round_up(slots, LANES), width), BF16),
            pltpu.VMEM((slots, width), F32),
            pltpu.VMEM((slots, width), F32),
            matrices(5, width),
        ],
        scratch_shapes=[
            pltpu.VMEM((count + WINDOW, width), BF16),
            pltpu.VMEM((math_block(total, BLOCK), width), F32),
            *fetch_scratch(3, width),
            pltpu.SemaphoreType.DMA((5,)),
        ],
        compiler_params=LIMIT,
        name="encode_local",
    )(
        keys, keys, grid_rows, mesh_rows, weights["edge_bias"], weights["node_bias"],
        weights["edge_first"], weights["edge_second"], weights["node_first"], weights["node_second"],
    )


def encode_kernel(section, shift, *refs):
    scalars, keys_ref, local_ref, target, total_ref, inner_ref, stack, mesh_ref = refs[:8]
    pair_ref, right_ref, left_ref, outer_right, outer_left, outer_ref = refs[8:14]
    gain_ref, node_gain_ref, lists_ref = refs[14:17]
    mesh_out, proj_out, up, down, right, left, table, pre, total = refs[17:]
    count, slots = local_ref.shape[0], mesh_ref.shape[0]
    depth = outer_ref.shape[0]
    table[:count] = local_ref[...]
    clear_tail(table, count + 8 * depth)
    pair = side_base()
    outer = 5 - pair
    for ref, start, direction in (
        (pair_ref, 2 * depth, pair + 1),
        (right_ref, 0, 3),
        (right_ref, depth, pair),
        (left_ref, 0, 4),
        (left_ref, depth, pair + 2),
        (outer_right, 0, outer),
        (outer_left, 0, outer + 2),
        (outer_ref, 0, outer + 1),
    ):
        place = pl.multiple_of(count + direction * depth, LANES)
        table[pl.ds(place, depth)] = dot(ref[start : start + depth], stack[1]).astype(BF16)
    total[...] = total_ref[...]
    block = pre.shape[0]
    start = below(scalars, count << shift) // block * block
    used = below(scalars, (count + 8 * depth) << shift)

    def step(index, carry):
        total[...] += edge_block(
            start + index * block, used, shift, scalars, keys_ref, table, target, pre, stack[0], slots
        )
        return carry

    lax.fori_loop(0, (used - start + block - 1) // block, step, 0)
    summed = total[...] * row_of(gain_ref, section)
    fresh = updated(mesh_ref[...], summed, inner_ref[...], stack[2], stack[3], row_of(node_gain_ref, section))
    mesh_out[...] = fresh
    fill(proj_out, dot(fresh, stack[4]).astype(BF16))
    list_rows(proj_out, lists_ref, (up, down, right, left))


def encode(keys, shift, prepared, mesh_rows, remote, lists, depth, weights, section):
    edges = keys.shape[1]
    prepared = [near(value) for value in prepared]
    count, width = prepared[0].shape
    slots = mesh_rows.shape[0]
    vmem = pl.BlockSpec(memory_space=pltpu.VMEM)
    rows = count + 8 * remote[-1].shape[0]
    return pl.pallas_call(
        functools.partial(encode_kernel, section, shift),
        in_specs=[SMEM] + [vmem] * 16,
        out_shape=[
            pltpu.VMEM((slots, width), BF16),
            pltpu.VMEM((round_up(slots, LANES), width), BF16),
        ]
        + send_shapes(depth, width),
        scratch_shapes=[
            pltpu.VMEM((rows + WINDOW, width), BF16),
            pltpu.VMEM((math_block(edges, BLOCK), width), F32),
            pltpu.VMEM((slots, width), F32),
        ],
        compiler_params=LIMIT,
        name="encode",
    )(keys, keys, *prepared, mesh_rows, *remote, weights["edge_gain"], weights["node_gain"], lists)


def prepare_kernel(
    section, mesh_ref, bias_ref, node_bias_ref, edge_first, edge_second, node_first, node_second,
    target_out, inner_out, later, own, arrived, later_arrived,
):
    copies = fetch([edge_first.at[section, 1], node_first.at[section, 0]], own, arrived)
    copies += fetch(
        [
            edge_second.at[section], node_first.at[section, 1], node_second.at[section],
            edge_first.at[section + 1, 0],
        ],
        later, later_arrived,
    )
    rows = mesh_ref[...]
    copies[0].wait()
    fill(target_out, (dot(rows, own[0]) + row_of(bias_ref, section)).astype(BF16))
    copies[1].wait()
    inner_out[...] = dot(rows, own[1]) + row_of(node_bias_ref, section)
    for copy in copies[2:]:
        copy.wait()


def prepare(mesh_rows, weights, section):
    slots, width = mesh_rows.shape
    vmem = pl.BlockSpec(memory_space=pltpu.VMEM)
    return pl.pallas_call(
        functools.partial(prepare_kernel, section),
        in_specs=[vmem] * 3 + [HBM] * 4,
        out_shape=[
            pltpu.VMEM((round_up(slots, LANES), width), BF16),
            pltpu.VMEM((slots, width), F32),
            matrices(4, width),
        ],
        scratch_shapes=fetch_scratch(2, width) + [pltpu.SemaphoreType.DMA((4,))],
        compiler_params=LIMIT,
        name="prepare",
    )(
        near(mesh_rows), weights["edge_bias"], weights["node_bias"],
        weights["edge_first"], weights["edge_second"], weights["node_first"], weights["node_second"],
    )


def place_remote(table, remote, places, base):
    for ref, slots in zip(remote, places):
        depth = ref.shape[1]
        for index, slot in enumerate(slots):
            place = base + slot * depth
            table[place : place + depth] = ref[index]


def round_kernel(section, places, last, *refs):
    edges_ref, local_ref, target, inner_ref, stack, mesh_ref = refs[:6]
    remote = refs[6 : 6 + len(places)]
    gain_ref, node_gain_ref, lists_ref, owned_ref = refs[6 + len(places) : 10 + len(places)]
    rest = refs[10 + len(places) :]
    mesh_out, proj_out = rest[:2]
    sends = rest[2:-1]
    table = rest[-1]
    if last:
        masked_out, sends = sends[0], sends[1:]
    slots, padded = mesh_ref.shape[0], local_ref.shape[0]
    table[:padded] = local_ref[...]
    place_remote(table, remote, places, padded)
    edges = edges_ref.shape[2]
    block = math_block(edges, 1536)
    summed = None
    for start in range(0, edges, block):
        senders = edges_ref[0, 0:1, start : start + block]
        senders = jnp.where(senders < slots, senders, senders + (padded - slots))
        targets = edges_ref[0, 1:2, start : start + block]
        pre = dot(one_hot(column(senders), table.shape[0]), table[...]) + dot(
            one_hot(column(targets), padded), target[...]
        )
        part = added(pre, targets, stack[0], slots)
        summed = part if summed is None else summed + part
    summed = summed * row_of(gain_ref, section)
    fresh = updated(mesh_ref[...], summed, inner_ref[...], stack[1], stack[2], row_of(node_gain_ref, section))
    mesh_out[...] = fresh
    if last:
        alive = lax.broadcasted_iota(jnp.int32, fresh.shape, 0) < owned_ref[0]
        masked_out[...] = jnp.where(alive, fresh, jnp.zeros_like(fresh))
    fill(proj_out, dot(fresh, stack[3]).astype(BF16))
    list_rows(proj_out, lists_ref, sends)


def round_part(edges, local, prepared, mesh_rows, remote, places, lists, owned, sends, weights, section):
    slots, width = mesh_rows.shape
    last = section == 2
    padded = local.shape[0]
    table_rows = padded + sum(r.shape[0] * r.shape[1] for r in remote)
    out_shape = [pltpu.VMEM((slots, width), BF16), pltpu.VMEM((padded, width), BF16)]
    if last:
        out_shape.append(jax.ShapeDtypeStruct((slots, width), BF16))
    vmem = pl.BlockSpec(memory_space=pltpu.VMEM)
    return pl.pallas_call(
        functools.partial(round_kernel, section, places, last),
        in_specs=[vmem] * (9 + len(remote)) + [SMEM],
        out_shape=out_shape + sends,
        scratch_shapes=[pltpu.VMEM((table_rows, width), BF16)],
        compiler_params=LIMIT,
        name="round_part",
    )(
        edges, near(local), *[near(value) for value in prepared], near(mesh_rows), *remote,
        weights["edge_gain"], weights["node_gain"], lists, owned,
    )


def decode_local_kernel(
    section, grid_ref, table_ref, edges_ref, bias_ref, edge_first, edge_second, node_first, node_second,
    pre_ref, later, own, arrived, later_arrived,
):
    copies = fetch([edge_first.at[section, 1]], own, arrived)
    copies += fetch(
        [
            edge_second.at[section], node_first.at[section, 0], node_first.at[section, 1],
            node_second.at[section],
        ],
        later, later_arrived,
    )
    copies[0].wait()
    count = grid_ref.shape[0]
    block = math_block(count, 512)
    for start in range(0, count, block):
        target = dot(grid_ref[start : start + block], own[0]) + row_of(bias_ref, section)
        for sender in range(edges_ref.shape[1]):
            ids = column(edges_ref[0, sender : sender + 1, start : start + block])
            pre = dot(one_hot(ids, table_ref.shape[0]), table_ref[...]) + target
            pre_ref[sender, start : start + block] = pre.astype(BF16)
    for copy in copies[1:]:
        copy.wait()


def decode_local(grid_rows, table, edges, weights, section):
    count, width = grid_rows.shape
    senders = edges.shape[1]
    vmem = pl.BlockSpec(memory_space=pltpu.VMEM)
    return pl.pallas_call(
        functools.partial(decode_local_kernel, section),
        in_specs=[vmem] * 4 + [HBM] * 4,
        out_shape=[pltpu.VMEM((senders, count, width), BF16), matrices(4, width)],
        scratch_shapes=fetch_scratch(1, width) + [pltpu.SemaphoreType.DMA((4,))],
        compiler_params=LIMIT,
        name="decode_local",
    )(
        grid_rows, near(table), edges, weights["edge_bias"],
        weights["edge_first"], weights["edge_second"], weights["node_first"], weights["node_second"],
    )


def decode_kernel(section, places, split, *refs):
    pre_ref, stack, grid_ref, edges_ref = refs[:4]
    remote = refs[4 : 4 + len(places)]
    gain_ref, node_bias_ref, node_gain_ref, out_ref, table, ready, sent = refs[4 + len(places) :]
    place_remote(table, remote, places, 0)
    count = grid_ref.shape[0]
    block = math_block(count, 512)
    copies = []
    for index, start in enumerate(range(0, count, block)):
        part = slice(start, start + block)
        summed = None
        for sender in range(edges_ref.shape[1]):
            ids = column(edges_ref[0, sender : sender + 1, part])
            pre = pre_ref[sender, part].astype(F32) + dot(one_hot(ids, table.shape[0], split), table[...])
            message = normed(dot(silu(pre).astype(BF16), stack[0])).astype(BF16).astype(F32)
            summed = message if summed is None else summed + message
        rows = grid_ref[part]
        summed = (summed * row_of(gain_ref, section)).astype(BF16)
        inner = dot(rows, stack[1]) + dot(summed, stack[2]) + row_of(node_bias_ref, section)
        update = normed(dot(silu(inner).astype(BF16), stack[3])) * row_of(node_gain_ref, section)
        ready[part] = (rows.astype(F32) + update).astype(BF16)
        copies.append(pltpu.make_async_copy(ready.at[part], out_ref.at[part], sent.at[index]))
        copies[-1].start()
    for copy in copies:
        copy.wait()


def decode_part(prepared, grid_rows, edges, remote, places, weights, section, split):
    count, width = grid_rows.shape
    table_rows = sum(r.shape[0] * r.shape[1] for r in remote)
    vmem = pl.BlockSpec(memory_space=pltpu.VMEM)
    return pl.pallas_call(
        functools.partial(decode_kernel, section, places, split),
        in_specs=[vmem] * (7 + len(remote)),
        out_specs=pl.BlockSpec(memory_space=pl.ANY),
        out_shape=jax.ShapeDtypeStruct((count, width), BF16),
        scratch_shapes=[
            pltpu.VMEM((table_rows, width), BF16),
            pltpu.VMEM((count, width), BF16),
            pltpu.SemaphoreType.DMA((count // math_block(count, 512),)),
        ],
        compiler_params=LIMIT,
        name="decode_part",
    )(
        *[near(value) for value in prepared], grid_rows, edges, *remote,
        weights["edge_gain"], weights["node_bias"], weights["node_gain"],
    )


def move(value, target):
    bands, sectors = lax.axis_size("aa"), lax.axis_size("ba")
    pairs = []
    for i in range(bands):
        for j in range(sectors):
            band, sector = target(i, j)
            pairs.append((i * sectors + j, band % bands * sectors + sector % sectors))
    return lax.ppermute(value, AXES, pairs)


def join_kernel(up_ref, down_ref, right_ref, left_ref, right_out, left_out):
    for index, (own, out) in enumerate(((right_ref, right_out), (left_ref, left_out))):
        out[0] = own[0]
        out[1] = up_ref[index]
        out[2] = down_ref[index]


def halo(up, down, right, left):
    from_up = move(up, lambda i, j: (i + 1, j))
    from_down = move(down, lambda i, j: (i - 1, j))
    joined = jax.ShapeDtypeStruct((3,) + right.shape[1:], BF16)
    right, left = pl.pallas_call(
        join_kernel, out_shape=[joined, joined], compiler_params=LIMIT, name="join"
    )(from_up, from_down, right, left)
    from_left = move(right, lambda i, j: (i, j + 1))
    from_right = move(left, lambda i, j: (i, j - 1))
    return [from_up[2:3], from_down[2:3], from_left, from_right], ((1,), (6,), (3, 0, 5), (4, 2, 7))


def per_device(
    grid_nodes, mesh_nodes, owned_nodes, grid_rim, mesh_rim, long_send, g2m_edges, short_edges,
    long_edges, m2g_edges, edge_first, edge_second, edge_bias, edge_gain, node_first, node_second,
    node_bias, node_gain,
):
    weights = dict(
        edge_bias=edge_bias, edge_gain=edge_gain, node_bias=node_bias, node_gain=node_gain,
        edge_first=stay(edge_first), edge_second=stay(edge_second),
        node_first=stay(node_first), node_second=stay(node_second),
    )
    width = grid_nodes.shape[1]
    slots = mesh_nodes.shape[0]
    depth = mesh_rim.shape[2]
    peers, listed = long_send.shape[1:]

    remote, keys, shift = grid_halo(grid_nodes, grid_rim, g2m_edges, slots)
    rim_lists = jnp.concatenate([mesh_rim[0, m : m + 1] for m in SEND_ORDER], 0).reshape(1, 8 * depth)
    long_lists = long_send.reshape(1, peers * listed)
    rim_sends = send_shapes(depth, width)
    prepared = encode_local(keys, shift, grid_nodes, mesh_nodes, weights, 0)
    mesh_one, proj, *sends = encode(keys, shift, prepared, mesh_nodes, remote, rim_lists, depth, weights, 0)

    remote, places = halo(*sends)
    prepared = prepare(mesh_one, weights, 1)
    mesh_two, proj, sent = round_part(
        short_edges, proj, prepared, mesh_one, remote, places, long_lists, owned_nodes,
        [jax.ShapeDtypeStruct((peers * listed, width), BF16)], weights, 1,
    )

    sent = sent.reshape(peers, listed, width)
    arrived = lax.all_to_all(sent, AXES, split_axis=0, concat_axis=0, tiled=True)
    prepared = prepare(mesh_two, weights, 2)
    mesh_three, proj, mesh_out, *sends = round_part(
        long_edges, proj, prepared, mesh_two, [arrived.reshape(1, peers * listed, width)], ((0,),),
        rim_lists, owned_nodes, rim_sends, weights, 2,
    )

    remote, places = halo(*sends)
    prepared = decode_local(grid_nodes, proj, m2g_edges, weights, 3)
    grid_out = decode_part(prepared, grid_nodes, m2g_edges, remote, places, weights, 3, slots)
    return grid_out, mesh_out


def solution(mesh):
    rows = P(AXES, None)
    lists = P(AXES, None, None)
    in_specs = (rows, rows, P(AXES)) + (lists,) * 7 + (P(),) * 8
    return jax.shard_map(
        per_device, mesh=mesh, in_specs=in_specs, out_specs=(rows, rows), check_vma=False
    )
```

time: 137 us -> 101 us (0.74)
  local copies, waits for them, and re-layouts: 37.2 us -> 9.82 us
  between operations: 15.1 us -> 1.79 us
  other arithmetic: 1.52 us -> 5.75 us
  waiting for transfers between devices: 6.89 us -> 11.1 us
  starting transfers between devices: 32.9 us -> 30.1 us
    unnamed x99 -> x48, local copies, waits for them, and re-layouts: 37 us -> 9.61 us
    sort x0 -> x1, other arithmetic: none -> 5.75 us  [pair_join(): return (right, left, lax.sort(keys.reshape(-1)).reshape(1, -1), shift)]
    ppermute x16 -> x14, starting transfers between devices: 30.3 us -> 25.9 us  [move(): return lax.ppermute(value, AXES, pairs)]
    all_to_all x1, waiting for transfers between devices: 3.24 us -> 6.23 us  [per_device(): lax.all_to_all(sent, AXES, split_axis=0, concat_axis=0, tiled=True)]
    pallas_call x1, Pallas kernels: 10.4 us -> 7.54 us  [decode_part(): pl.pallas_call(functools.partial(decode_kernel, section, places, split),...]
    pallas_call x2, Pallas kernels: 1.28 us -> 4.03 us  [prepare(): pl.pallas_call(functools.partial(prepare_kernel, section), in_specs=[vmem...]
    pallas_call x1, Pallas kernels: 5.24 us -> 7.06 us  [encode_local(): pl.pallas_call(functools.partial(encode_local_kernel, section, shift), in...]
    all_to_all x1, starting transfers between devices: 2.58 us -> 4.24 us  [per_device(): lax.all_to_all(sent, AXES, split_axis=0, concat_axis=0, tiled=True)]
  transfers between devices with their start and end apart: 17 -> 15, of which waited for: 3 -> 4; matrix products, arithmetic and copies ran while one was open for 0% -> 6% of each run, Pallas kernels for 6% -> 14%
where the time goes in v3:
time: 101 us
  Pallas kernels  42.2 us (42%)
  starting transfers between devices  30.1 us (30%)
  waiting for transfers between devices  11.1 us (11%)
  local copies, waits for them, and re-layouts  9.82 us (10%)
  other arithmetic  5.75 us (6%)
  between operations  1.79 us (2%)
    ppermute x14, starting transfers between devices, move(): return lax.ppermute(value, AXES, pairs)  25.9 us
    unnamed x48, local copies, waits for them, and re-layouts  9.61 us
    pallas_call x2, Pallas kernels, round_part(): pl.pallas_call(functools.partial(round_kernel, section, places, last), in...  9.46 us
    pallas_call x1, Pallas kernels, encode(): pl.pallas_call(functools.partial(encode_kernel, section, shift), in_specs...  9.09 us
    pallas_call x1, Pallas kernels, decode_part(): pl.pallas_call(functools.partial(decode_kernel, section, places, split),...  7.54 us
    pallas_call x1, Pallas kernels, encode_local(): pl.pallas_call(functools.partial(encode_local_kernel, section, shift), in...  7.06 us
    all_to_all x1, waiting for transfers between devices, per_device(): lax.all_to_all(sent, AXES, split_axis=0, concat_axis=0, tiled=True)  6.23 us
    sort x1, other arithmetic, pair_join(): return (right, left, lax.sort(keys.reshape(-1)).reshape(1, -1), shift)  5.75 us
  transfers between devices with their start and end apart: 15, of which 4 were waited for; matrix products, arithmetic and copies ran while one was open for 6% of the time, Pallas kernels for 14%

profile of v3, /device:TPU:0, one launch (start us, length us, event | category | flops | bytes accessed | tf_op | source)
XLA Modules:
  0.0 100.8 jit_solution(6861451698432904490)
XLA Ops:
  0.6 1.2 %copy-done = bf16[1024,512]{1,0:T(8,128)(2,1)S(1)} copy-done((bf16[1024,512]{1,0:T(8,128)(2,1)S(1)}, bf16[1024,512]{1,0:T(8,128)(2,1)}, u32[]{:S(2)}) %copy-start) | copy-done | bytes 1048600
  2.6 1.9 %pick_grid.1 = (bf16[384,512]{1,0:T(8,128)(2,1)S(1)}, bf16[128,512]{1,0:T(8,128)(2,1)S(1)}, bf16[128,512]{1,0:T(8,128)(2,1)S(1)}, bf16[128,512]{1,0:T(8,128)(2,1...) custom-call(bf16[1024,512]{1,0:T(8,128)(2,1)S(1)} %copy-done, s32[1,8,128]{2,1,0:T(8,128)S(1)} %copy-done.19), custom_call_target="tpu_custom_call" | custom-call | flops 1073741824 | bytes 2097152 | tf_op jit(solution)/shard_map/pick_grid/pallas_call | solution.py:155
  4.9 1.3 %collective-permute-done.pair_ref.refs_8_ = bf16[384,512]{1,0:T(8,128)(2,1)S(1)} collective-permute-done((bf16[384,512]{1,0:T(8,128)(2,1)S(1)}, bf16[384,512]{1,0:T(8,128)(2,1)S(1)}, u32[]{:S(2)}, u32[]{:S(2)}) %collective-permute-start) | collective-permute-done | bytes 393248 | tf_op jit(solution)/shard_map/ppermute | solution.py:604
  6.3 2.9 %collective-permute-start.1 = (bf16[256,512]{1,0:T(8,128)(2,1)S(1)}, bf16[256,512]{1,0:T(8,128)(2,1)S(1)}, u32[]{:S(2)}, u32[]{:S(2)}) collective-permute-start(bf16[256,512]{1,0:T(8,128)(2,1)S(1)} %get-tuple-element.55), channel_id=1, source_target_pairs={{0,1},{1,2},{2,3},{3,4},{4,5},{5,6},{6,7},{7,0},{8,9},{9,10},{10,1... | collective-permute-start | bytes 786440 | tf_op jit(solution)/shard_map/ppermute | solution.py:604
  9.2 3.1 %collective-permute-start.2 = (bf16[256,512]{1,0:T(8,128)(2,1)S(1)}, bf16[256,512]{1,0:T(8,128)(2,1)S(1)}, u32[]{:S(2)}, u32[]{:S(2)}) collective-permute-start(bf16[256,512]{1,0:T(8,128)(2,1)S(1)} %get-tuple-element.56), channel_id=1, source_target_pairs={{0,7},{1,0},{2,1},{3,2},{4,3},{5,4},{6,5},{7,6},{8,15},{9,8},{10,9... | collective-permute-start | bytes 786440 | tf_op jit(solution)/shard_map/ppermute | solution.py:604
  12.3 5.3 %collective-permute-start.4 = (bf16[128,512]{1,0:T(8,128)(2,1)}, bf16[128,512]{1,0:T(8,128)(2,1)S(1)}, u32[]{:S(2)}, u32[]{:S(2)}) collective-permute-start(bf16[128,512]{1,0:T(8,128)(2,1)} %get-tuple-element.58), channel_id=1, source_target_pairs={{0,31},{1,24},{2,25},{3,26},{4,27},{5,28},{6,29},{7,30},{8,23},{9,... | collective-permute-start | bytes 393224 | tf_op jit(solution)/shard_map/ppermute | solution.py:604
  18.8 5.8 %sort.14 = (s32[3072]{0:T(1024)S(1)}, s32[3072]{0:T(1024)}) sort(s32[3072]{0:T(1024)S(1)} %bitcast.25, s32[3072]{0:T(1024)S(1)} %iota.3), dimensions={0}, to_apply=%region_0.0 | sort | flops 36864 | bytes 49152 | tf_op jit(solution)/shard_map/sort | solution.py:184
  24.5 7.1 %encode_local.1 = (bf16[1024,512]{1,0:T(8,128)(2,1)S(1)}, bf16[256,512]{1,0:T(8,128)(2,1)S(1)}, f32[192,512]{1,0:T(8,128)S(1)}, f32[192,512]{1,0:T(8,128)S(1)}, bf16[5,512,512]{2,1,0:T(8,128)(2,1)S(1)}) custom-call(s32[1,3072]{1,0:T(1,128)S(1)} %bitcast.21, s32[1,3072]{1,0:T(1,128)S(1)} %bitcast.22, bf16[1024,512]{1,0:T(8,128)(2,1)S(1)} %copy-done.1, ...), custom_call_target="tpu_custom_call" | custom-call | tf_op jit(solution)/shard_map/encode_local/pallas_call | solution.py:309
  31.7 9.1 %encode.1 = (bf16[192,512]{1,0:T(8,128)(2,1)S(1)}, bf16[256,512]{1,0:T(8,128)(2,1)S(1)}, bf16[3,16,512]{2,1,0:T(8,128)(2,1)S(1)}, bf16[3,16,512]{2,1,0:T(8,128)(...) custom-call(s32[1,3072]{1,0:T(1,128)S(1)} %bitcast.23, s32[1,3072]{1,0:T(1,128)S(1)} %bitcast.24, ...), custom_call_target="tpu_custom_call" | custom-call | tf_op jit(solution)/shard_map/encode/pallas_call | solution.py:382
  40.9 1.7 %collective-permute-start.7 = (bf16[3,16,512]{2,1,0:T(8,128)(2,1)S(1)}, bf16[3,16,512]{2,1,0:T(8,128)(2,1)S(1)}, u32[]{:S(2)}, u32[]{:S(2)}) collective-permute-start(bf16[3,16,512]{2,1,0:T(8,128)(2,1)S(1)} %get-tuple-element.66), channel_id=1, source_target_pairs={{0,24},{1,25},{2,26},{3,27},{4,28},{5,29},{6,30},{7,31},{8,0},{9,1... | collective-permute-start | bytes 147464 | tf_op jit(solution)/shard_map/ppermute | solution.py:604
  42.6 1.8 %collective-permute-done.6.up_ref = bf16[3,16,512]{2,1,0:T(8,128)(2,1)S(1)} collective-permute-done((bf16[3,16,512]{2,1,0:T(8,128)(2,1)S(1)}, bf16[3,16,512]{2,1,0:T(8,128)(2,1)S(1)}, u32[]{:S(2)}, u32[]{:S(2)}) %collective-permute-start.6) | collective-permute-done | bytes 49184 | tf_op jit(solution)/shard_map/ppermute | solution.py:604
  44.4 4.7 %collective-permute-start.9 = (bf16[3,16,512]{2,1,0:T(8,128)(2,1)S(1)}, bf16[3,16,512]{2,1,0:T(8,128)(2,1)S(1)}, u32[]{:S(2)}, u32[]{:S(2)}) collective-permute-start(bf16[3,16,512]{2,1,0:T(8,128)(2,1)S(1)} %get-tuple-element.70), channel_id=1, source_target_pairs={{0,7},{1,0},{2,1},{3,2},{4,3},{5,4},{6,5},{7,6},{8,15},{9,8},{10,9... | collective-permute-start | bytes 147464 | tf_op jit(solution)/shard_map/ppermute | solution.py:604
  50.0 2.0 %prepare.2 = (bf16[256,512]{1,0:T(8,128)(2,1)S(1)}, f32[192,512]{1,0:T(8,128)S(1)}, bf16[4,512,512]{2,1,0:T(8,128)(2,1)S(1)}) custom-call(bf16[192,512]{1,0:T(8,128)(2,1)S(1)} %get-tuple-element.61.mesh_ref.refs_5_, f32[4,512]{1,0:T(4,128)S(1)} %copy-done.12, f32[4,512]{1,0:T(4,128)S(1)} %copy-done.13, bf16[4,2,512,512]{3,2,1,0:T(8,128)(2,1)} %edge_first.7, ...), custom_call_target="tpu_custom_call" | custom-call | tf_op jit(solution)/shard_map/prepare/pallas_call | solution.py:424
  52.1 4.8 %round_part.2 = (bf16[192,512]{1,0:T(8,128)(2,1)S(1)}, bf16[256,512]{1,0:T(8,128)(2,1)S(1)}, bf16[256,512]{1,0:T(8,128)(2,1)}) custom-call(s32[1,2,1536]{2,1,0:T(2,128)S(1)} %copy-done.17, bf16[256,512]{1,0:T(8,128)(2,1)S(1)} %get-tuple-element.60.refs_1_, bf16[256,512]{1,0:T(8,128)(2,1)S(1)} %get-tuple-element.62.refs_2_, ...), custom_call_target="tpu_custom_call" | custom-call | tf_op jit(solution)/shard_map/round_part/pallas_call | solution.py:493
  58.3 4.2 %all-to-all-start = ((bf16[32,8,512]{2,1,0:T(8,128)(2,1)}), bf16[32,8,512]{2,1,0:T(8,128)(2,1)S(1)}, u32[]{:S(2)}, u32[]{:S(2)}) async-start(bf16[32,8,512]{2,1,0:T(8,128)(2,1)} %bitcast.10), calls=%async_computation | async-start | bytes 524288 | tf_op jit(solution)/shard_map/all_to_all | solution.py:656
  63.5 2.0 %prepare.3 = (bf16[256,512]{1,0:T(8,128)(2,1)S(1)}, f32[192,512]{1,0:T(8,128)S(1)}, bf16[4,512,512]{2,1,0:T(8,128)(2,1)S(1)}) custom-call(bf16[192,512]{1,0:T(8,128)(2,1)S(1)} %copy-done.4, f32[4,512]{1,0:T(4,128)S(1)} %copy-done.12, f32[4,512]{1,0:T(4,128)S(1)} %copy-done.13, bf16[4,2,512,512]{3,2,1,0:T(8,128)(2,1)} %edge_first.7, ...), custom_call_target="tpu_custom_call" | custom-call | tf_op jit(solution)/shard_map/prepare/pallas_call | solution.py:424
  66.9 6.2 %all-to-all-done = bf16[32,8,512]{2,1,0:T(8,128)(2,1)S(1)} async-done(((bf16[32,8,512]{2,1,0:T(8,128)(2,1)}), bf16[32,8,512]{2,1,0:T(8,128)(2,1)S(1)}, u32[]{:S(2)}, u32[]{:S(2)}) %all-to-all-start) | async-done | bytes 262176 | tf_op jit(solution)/shard_map/all_to_all | solution.py:656
  77.0 4.6 %round_part.3 = (bf16[192,512]{1,0:T(8,128)(2,1)}, bf16[256,512]{1,0:T(8,128)(2,1)S(1)}, bf16[192,512]{1,0:T(8,128)(2,1)}, bf16[3,16,512]{2,1,0:T(8,128)(2,1)S(1...) custom-call(s32[1,2,1536]{2,1,0:T(2,128)S(1)} %copy-done.18, ...), custom_call_target="tpu_custom_call" | custom-call | tf_op jit(solution)/shard_map/round_part/pallas_call | solution.py:493
  81.6 1.7 %collective-permute-start.11 = (bf16[3,16,512]{2,1,0:T(8,128)(2,1)S(1)}, bf16[3,16,512]{2,1,0:T(8,128)(2,1)S(1)}, u32[]{:S(2)}, u32[]{:S(2)}) collective-permute-start(bf16[3,16,512]{2,1,0:T(8,128)(2,1)S(1)} %get-tuple-element.81), channel_id=1, source_target_pairs={{0,24},{1,25},{2,26},{3,27},{4,28},{5,29},{6,30},{7,31},{8,0},{9,1... | collective-permute-start | bytes 147464 | tf_op jit(solution)/shard_map/ppermute | solution.py:604
  83.4 1.8 %collective-permute-done.10.up_ref = bf16[3,16,512]{2,1,0:T(8,128)(2,1)S(1)} collective-permute-done((bf16[3,16,512]{2,1,0:T(8,128)(2,1)S(1)}, bf16[3,16,512]{2,1,0:T(8,128)(2,1)S(1)}, u32[]{:S(2)}, u32[]{:S(2)}) %collective-permute-start.10) | collective-permute-done | bytes 49184 | tf_op jit(solution)/shard_map/ppermute | solution.py:604
  85.2 1.1 %collective-permute-start.12 = (bf16[3,16,512]{2,1,0:T(8,128)(2,1)S(1)}, bf16[3,16,512]{2,1,0:T(8,128)(2,1)S(1)}, u32[]{:S(2)}, u32[]{:S(2)}) collective-permute-start(bf16[3,16,512]{2,1,0:T(8,128)(2,1)S(1)} %get-tuple-element.84), channel_id=1, source_target_pairs={{0,1},{1,2},{2,3},{3,4},{4,5},{5,6},{6,7},{7,0},{8,9},{9,10},{10,1... | collective-permute-start | bytes 147464 | tf_op jit(solution)/shard_map/ppermute | solution.py:604
  86.2 3.7 %collective-permute-start.13 = (bf16[3,16,512]{2,1,0:T(8,128)(2,1)S(1)}, bf16[3,16,512]{2,1,0:T(8,128)(2,1)S(1)}, u32[]{:S(2)}, u32[]{:S(2)}) collective-permute-start(bf16[3,16,512]{2,1,0:T(8,128)(2,1)S(1)} %get-tuple-element.85), channel_id=1, source_target_pairs={{0,7},{1,0},{2,1},{3,2},{4,3},{5,4},{6,5},{7,6},{8,15},{9,8},{10,9... | collective-permute-start | bytes 147464 | tf_op jit(solution)/shard_map/ppermute | solution.py:604
  90.0 3.1 %decode_local.1 = (bf16[3,1024,512]{2,1,0:T(8,128)(2,1)S(1)}, bf16[4,512,512]{2,1,0:T(8,128)(2,1)S(1)}) custom-call(bf16[1024,512]{1,0:T(8,128)(2,1)S(1)} %copy-done.1, bf16[256,512]{1,0:T(8,128)(2,1)S(1)} %get-tuple-element.77.table_ref, s32[1,3,1024]{2,1,0:T(4,128)S(1)} %copy.24.edges_ref.refs_3_, f32[4,512]{1,0:T(4,128)S(1)} %copy-done.12, ...), custom_call_target="tpu_custom_call" | custom-call | tf_op jit(solution)/shard_map/decode_local/pallas_call | solution.py:535
  93.1 7.5 %decode_part.1 = bf16[1024,512]{1,0:T(8,128)(2,1)} custom-call(bf16[3,1024,512]{2,1,0:T(8,128)(2,1)S(1)} %get-tuple-element.78.refs_0_, bf16[4,512,512]{2,1,0:T(8,128)(2,1)S(1)} %get-tuple-element.79.refs_1_, bf16[1024,512]{1,0:T(8,128)(2,1)S(1)} %copy-done.1, s32[1,3,1024]{2,1,0:T(4,128)S(1)} %copy.24.edges_ref.refs_3_, ...), custom_call_target="tpu_custom_call" | custom-call | tf_op jit(solution)/shard_map/decode_part/pallas_call | solution.py:579
  (76 shorter events, 10.3 us)
Async XLA Ops:
  2.5 16.1 %copy-start.22 = (s32[1,8,16]{2,1,0:T(8,128)S(1)}, s32[1,8,16]{2,1,0:T(8,128)}, u32[]{:S(2)}) copy-start(s32[1,8,16]{2,1,0:T(8,128)} %param.22) | copy-start | bytes 1540
  2.5 22.0 %copy-start.1 = (bf16[1024,512]{1,0:T(8,128)(2,1)S(1)}, bf16[1024,512]{1,0:T(8,128)(2,1)}, u32[]{:S(2)}) copy-start(bf16[1024,512]{1,0:T(8,128)(2,1)} %refs_2_.1) | copy-start | bytes 3145732
  2.6 22.0 %copy-start.2 = (bf16[192,512]{1,0:T(8,128)(2,1)S(1)}, bf16[192,512]{1,0:T(8,128)(2,1)}, u32[]{:S(2)}) copy-start(bf16[192,512]{1,0:T(8,128)(2,1)} %refs_7_.2) | copy-start | bytes 589828
  2.6 22.0 %copy-start.12 = (f32[4,512]{1,0:T(4,128)S(1)}, f32[4,512]{1,0:T(4,128)}, u32[]{:S(2)}) copy-start(f32[4,512]{1,0:T(4,128)} %bias_ref.7) | copy-start | bytes 24580
  2.6 21.9 %copy-start.13 = (f32[4,512]{1,0:T(4,128)S(1)}, f32[4,512]{1,0:T(4,128)}, u32[]{:S(2)}) copy-start(f32[4,512]{1,0:T(4,128)} %refs_9_.1) | copy-start | bytes 24580
  4.4 1.8 %collective-permute-start = (bf16[384,512]{1,0:T(8,128)(2,1)S(1)}, bf16[384,512]{1,0:T(8,128)(2,1)S(1)}, u32[]{:S(2)}, u32[]{:S(2)}) collective-permute-start(bf16[384,512]{1,0:T(8,128)(2,1)S(1)} %get-tuple-element.45), channel_id=1, source_target_pairs={{0,8},{1,9},{2,10},{3,11},{4,12},{5,13},{6,14},{7,15},{8,0},{9,1},... | collective-permute-start | bytes 1179656 | tf_op jit(solution)/shard_map/ppermute | solution.py:604
  6.3 25.4 %collective-permute-start.1 = (bf16[256,512]{1,0:T(8,128)(2,1)S(1)}, bf16[256,512]{1,0:T(8,128)(2,1)S(1)}, u32[]{:S(2)}, u32[]{:S(2)}) collective-permute-start(bf16[256,512]{1,0:T(8,128)(2,1)S(1)} %get-tuple-element.55), channel_id=1, source_target_pairs={{0,1},{1,2},{2,3},{3,4},{4,5},{5,6},{6,7},{7,0},{8,9},{9,10},{10,1... | collective-permute-start | bytes 786440 | tf_op jit(solution)/shard_map/ppermute | solution.py:604
  9.2 22.5 %collective-permute-start.2 = (bf16[256,512]{1,0:T(8,128)(2,1)S(1)}, bf16[256,512]{1,0:T(8,128)(2,1)S(1)}, u32[]{:S(2)}, u32[]{:S(2)}) collective-permute-start(bf16[256,512]{1,0:T(8,128)(2,1)S(1)} %get-tuple-element.56), channel_id=1, source_target_pairs={{0,7},{1,0},{2,1},{3,2},{4,3},{5,4},{6,5},{7,6},{8,15},{9,8},{10,9... | collective-permute-start | bytes 786440 | tf_op jit(solution)/shard_map/ppermute | solution.py:604
  12.3 19.3 %collective-permute-start.3 = (bf16[128,512]{1,0:T(8,128)(2,1)}, bf16[128,512]{1,0:T(8,128)(2,1)S(1)}, u32[]{:S(2)}, u32[]{:S(2)}) collective-permute-start(bf16[128,512]{1,0:T(8,128)(2,1)} %get-tuple-element.57), channel_id=1, source_target_pairs={{0,25},{1,26},{2,27},{3,28},{4,29},{5,30},{6,31},{7,24},{8,17},{9,... | collective-permute-start | bytes 393224 | tf_op jit(solution)/shard_map/ppermute | solution.py:604
  12.3 19.3 %collective-permute-start.4 = (bf16[128,512]{1,0:T(8,128)(2,1)}, bf16[128,512]{1,0:T(8,128)(2,1)S(1)}, u32[]{:S(2)}, u32[]{:S(2)}) collective-permute-start(bf16[128,512]{1,0:T(8,128)(2,1)} %get-tuple-element.58), channel_id=1, source_target_pairs={{0,31},{1,24},{2,25},{3,26},{4,27},{5,28},{6,29},{7,30},{8,23},{9,... | collective-permute-start | bytes 393224 | tf_op jit(solution)/shard_map/ppermute | solution.py:604
  17.6 14.0 %collective-permute-start.5 = (bf16[128,512]{1,0:T(8,128)(2,1)S(1)}, bf16[128,512]{1,0:T(8,128)(2,1)S(1)}, u32[]{:S(2)}, u32[]{:S(2)}) collective-permute-start(bf16[128,512]{1,0:T(8,128)(2,1)S(1)} %get-tuple-element.59), channel_id=1, source_target_pairs={{0,24},{1,25},{2,26},{3,27},{4,28},{5,29},{6,30},{7,31},{8,16},{9,... | collective-permute-start | bytes 393224 | tf_op jit(solution)/shard_map/ppermute | solution.py:604
  24.5 7.1 %copy-start.14 = (f32[4,512]{1,0:T(4,128)S(1)}, f32[4,512]{1,0:T(4,128)}, u32[]{:S(2)}) copy-start(f32[4,512]{1,0:T(4,128)} %refs_8_.3) | copy-start | bytes 24580
  31.7 18.1 %copy-start.21 = (s32[1,32,8]{1,2,0:T(8,128)S(1)}, s32[1,32,8]{1,2,0:T(8,128)}, u32[]{:S(2)}) copy-start(s32[1,32,8]{1,2,0:T(8,128)} %param.23) | copy-start | bytes 3076
  40.8 3.6 %collective-permute-start.6 = (bf16[3,16,512]{2,1,0:T(8,128)(2,1)S(1)}, bf16[3,16,512]{2,1,0:T(8,128)(2,1)S(1)}, u32[]{:S(2)}, u32[]{:S(2)}) collective-permute-start(bf16[3,16,512]{2,1,0:T(8,128)(2,1)S(1)} %get-tuple-element.65), channel_id=1, source_target_pairs={{0,8},{1,9},{2,10},{3,11},{4,12},{5,13},{6,14},{7,15},{8,16},{9,17... | collective-permute-start | bytes 147464 | tf_op jit(solution)/shard_map/ppermute | solution.py:604
  40.9 3.5 %collective-permute-start.7 = (bf16[3,16,512]{2,1,0:T(8,128)(2,1)S(1)}, bf16[3,16,512]{2,1,0:T(8,128)(2,1)S(1)}, u32[]{:S(2)}, u32[]{:S(2)}) collective-permute-start(bf16[3,16,512]{2,1,0:T(8,128)(2,1)S(1)} %get-tuple-element.66), channel_id=1, source_target_pairs={{0,24},{1,25},{2,26},{3,27},{4,28},{5,29},{6,30},{7,31},{8,0},{9,1... | collective-permute-start | bytes 147464 | tf_op jit(solution)/shard_map/ppermute | solution.py:604
  44.4 7.7 %collective-permute-start.8 = (bf16[3,16,512]{2,1,0:T(8,128)(2,1)S(1)}, bf16[3,16,512]{2,1,0:T(8,128)(2,1)S(1)}, u32[]{:S(2)}, u32[]{:S(2)}) collective-permute-start(bf16[3,16,512]{2,1,0:T(8,128)(2,1)S(1)} %get-tuple-element.69), channel_id=1, source_target_pairs={{0,1},{1,2},{2,3},{3,4},{4,5},{5,6},{6,7},{7,0},{8,9},{9,10},{10,1... | collective-permute-start | bytes 147464 | tf_op jit(solution)/shard_map/ppermute | solution.py:604
  44.4 7.6 %collective-permute-start.9 = (bf16[3,16,512]{2,1,0:T(8,128)(2,1)S(1)}, bf16[3,16,512]{2,1,0:T(8,128)(2,1)S(1)}, u32[]{:S(2)}, u32[]{:S(2)}) collective-permute-start(bf16[3,16,512]{2,1,0:T(8,128)(2,1)S(1)} %get-tuple-element.70), channel_id=1, source_target_pairs={{0,7},{1,0},{2,1},{3,2},{4,3},{5,4},{6,5},{7,6},{8,15},{9,8},{10,9... | collective-permute-start | bytes 147464 | tf_op jit(solution)/shard_map/ppermute | solution.py:604
  58.3 14.9 %all-to-all-start = ((bf16[32,8,512]{2,1,0:T(8,128)(2,1)}), bf16[32,8,512]{2,1,0:T(8,128)(2,1)S(1)}, u32[]{:S(2)}, u32[]{:S(2)}) async-start(bf16[32,8,512]{2,1,0:T(8,128)(2,1)} %bitcast.10), calls=%async_computation | async-start | bytes 524288 | tf_op jit(solution)/shard_map/all_to_all | solution.py:656
  63.5 9.7 %copy-start.18 = (s32[1,2,1536]{2,1,0:T(2,128)S(1)}, s32[1,2,1536]{2,1,0:T(2,128)}, u32[]{:S(2)}) copy-start(s32[1,2,1536]{2,1,0:T(2,128)} %refs_0_.3) | copy-start | bytes 36868
  63.5 26.5 %copy-start.20 = (s32[1,3,1024]{2,0,1:T(1,128)S(1)}, s32[1,3,1024]{2,0,1:T(1,128)}, u32[]{:S(2)}) copy-start(s32[1,3,1024]{2,0,1:T(1,128)} %param.27) | copy-start | bytes 36868
  81.6 3.5 %collective-permute-start.10 = (bf16[3,16,512]{2,1,0:T(8,128)(2,1)S(1)}, bf16[3,16,512]{2,1,0:T(8,128)(2,1)S(1)}, u32[]{:S(2)}, u32[]{:S(2)}) collective-permute-start(bf16[3,16,512]{2,1,0:T(8,128)(2,1)S(1)} %get-tuple-element.80), channel_id=1, source_target_pairs={{0,8},{1,9},{2,10},{3,11},{4,12},{5,13},{6,14},{7,15},{8,16},{9,17... | collective-permute-start | bytes 147464 | tf_op jit(solution)/shard_map/ppermute | solution.py:604
  81.6 3.5 %collective-permute-start.11 = (bf16[3,16,512]{2,1,0:T(8,128)(2,1)S(1)}, bf16[3,16,512]{2,1,0:T(8,128)(2,1)S(1)}, u32[]{:S(2)}, u32[]{:S(2)}) collective-permute-start(bf16[3,16,512]{2,1,0:T(8,128)(2,1)S(1)} %get-tuple-element.81), channel_id=1, source_target_pairs={{0,24},{1,25},{2,26},{3,27},{4,28},{5,29},{6,30},{7,31},{8,0},{9,1... | collective-permute-start | bytes 147464 | tf_op jit(solution)/shard_map/ppermute | solution.py:604
  85.2 7.9 %collective-permute-start.12 = (bf16[3,16,512]{2,1,0:T(8,128)(2,1)S(1)}, bf16[3,16,512]{2,1,0:T(8,128)(2,1)S(1)}, u32[]{:S(2)}, u32[]{:S(2)}) collective-permute-start(bf16[3,16,512]{2,1,0:T(8,128)(2,1)S(1)} %get-tuple-element.84), channel_id=1, source_target_pairs={{0,1},{1,2},{2,3},{3,4},{4,5},{5,6},{6,7},{7,0},{8,9},{9,10},{10,1... | collective-permute-start | bytes 147464 | tf_op jit(solution)/shard_map/ppermute | solution.py:604
  86.2 6.9 %collective-permute-start.13 = (bf16[3,16,512]{2,1,0:T(8,128)(2,1)S(1)}, bf16[3,16,512]{2,1,0:T(8,128)(2,1)S(1)}, u32[]{:S(2)}, u32[]{:S(2)}) collective-permute-start(bf16[3,16,512]{2,1,0:T(8,128)(2,1)S(1)} %get-tuple-element.85), channel_id=1, source_target_pairs={{0,7},{1,0},{2,1},{3,2},{4,3},{5,4},{6,5},{7,6},{8,15},{9,8},{10,9... | collective-permute-start | bytes 147464 | tf_op jit(solution)/shard_map/ppermute | solution.py:604
  (14 other events, 22.4 us)

commit v4 on v3

--- a/solution.py
+++ b/solution.py
@@ -82,6 +82,14 @@
     return pltpu.with_memory_space_constraint(value, pltpu.VMEM)
 
 
+def held(value, section):
+    return pltpu.with_memory_space_constraint(value, place_of(section))
+
+
+def place_of(section):
+    return pltpu.HBM if section == 2 else pltpu.VMEM
+
+
 def fetch(sources, buffers, arrived):
     copies = [
         pltpu.make_async_copy(source, buffers.at[i], arrived.at[i]) for i, source in enumerate(sources)
@@ -131,84 +139,20 @@
     return jnp.where(lax.axis_index("aa") % 2 == 0, 5, 0)
 
 
-def pick_kernel(rows_ref, rim_ref, pair_out, right_out, left_out, *outer_outs):
-    depth = right_out.shape[0]
-    pair = side_base()
-    outer = 5 - pair
-
-    def pick(chosen):
-        ids = column(rim_ref[0, pl.ds(chosen, 1), :])
-        return dot(one_hot(ids, rows_ref.shape[0]), rows_ref[...]).astype(BF16)
-
-    for index, offset in enumerate((2, 0, 1)):
-        pair_out[index * depth : (index + 1) * depth] = pick(pair + offset)
-    right_out[...] = pick(RIGHT_LIST)
-    left_out[...] = pick(LEFT_LIST)
-    for out, offset in zip(outer_outs, (2, 0, 1)):
-        out[...] = pick(outer + offset)
-
-
-def pick_grid(rows, rim):
-    count, width = rows.shape
-    depth = rim.shape[2]
-    block = jax.ShapeDtypeStruct((depth, width), BF16)
-    return pl.pallas_call(
-        pick_kernel,
-        out_shape=[jax.ShapeDtypeStruct((3 * depth, width), BF16)] + [block] * 5,
-        compiler_params=LIMIT,
-        cost_estimate=cost(8 * depth * count * width, 2 * (count + 8 * depth) * width),
-        name="pick_grid",
-    )(rows, rim)
-
-
-def pair_join_kernel(shift, slots, pair_ref, right_ref, left_ref, edges_ref, right_out, left_out, keys_out):
-    depth = right_ref.shape[0]
-    for index, (own, out) in enumerate(((right_ref, right_out), (left_ref, left_out))):
-        out[:depth] = own[...]
-        out[depth:] = pair_ref[index * depth : (index + 1) * depth]
-    senders, targets = edges_ref[0, 0:1], edges_ref[0, 1:2]
-    senders = jnp.where(targets < slots, senders, 1 << 14)
-    keys_out[...] = (senders << shift) + targets
-
-
-def pair_join(pair, right, left, edges, slots):
-    depth, width = right.shape
-    shift = slots.bit_length()
-    joined = jax.ShapeDtypeStruct((2 * depth, width), BF16)
-    right, left, keys = pl.pallas_call(
-        functools.partial(pair_join_kernel, shift, slots),
-        out_shape=[joined, joined, jax.ShapeDtypeStruct((1, edges.shape[2]), jnp.int32)],
-        compiler_params=LIMIT,
-        name="pair_join",
-    )(pair, right, left, edges)
-    return right, left, lax.sort(keys.reshape(-1)).reshape(1, -1), shift
-
-
-def grid_halo(rows, rim, edges, slots):
-    pair, right, left, *outer = pick_grid(rows, rim)
-    pair = move(pair, lambda i, j: (i ^ 1, j))
-    right, left, keys, shift = pair_join(pair, right, left, edges, slots)
-    other = lambda i: i + 1 if i % 2 else i - 1
-    arrived = [
-        move(right, lambda i, j: (i, j + 1)),
-        move(left, lambda i, j: (i, j - 1)),
-        move(outer[0], lambda i, j: (other(i), j + 1)),
-        move(outer[1], lambda i, j: (other(i), j - 1)),
-        move(outer[2], lambda i, j: (other(i), j)),
-    ]
-    return [pair] + arrived, keys, shift
-
-
 def send_shapes(depth, width):
     return [jax.ShapeDtypeStruct((n, depth, width), BF16) for n in (3, 3, 1, 1)]
 
 
 def list_rows(proj_out, lists_ref, sends):
-    listed = lists_ref.shape[1]
+    if len(lists_ref.shape) == 3:
+        ids = jnp.concatenate([column(lists_ref[0, m : m + 1]) for m in SEND_ORDER], 0)
+    else:
+        ids = column(lists_ref[...])
+    listed = ids.shape[0]
     size = math_block(listed, 256)
     made = []
     for start in range(0, listed, size):
-        picked = one_hot(column(lists_ref[0:1, start : start + size]), proj_out.shape[0])
+        picked = one_hot(ids[start : start + size], proj_out.shape[0])
         made.append(dot(picked, proj_out[...]).astype(BF16))
     made = made[0] if len(made) == 1 else jnp.concatenate(made, 0)
     place = 0
@@ -222,179 +166,241 @@
             place += depth
 
 
-WINDOW = 512
-BLOCK = 512
-
-
-def below(keys, limit):
-    total = keys.shape[1]
-    step = 1 << (total.bit_length() - 1)
-    found = jnp.int32(0)
-    while step:
-        place = found + step
-        inside = keys[0, jnp.minimum(place, total) - 1] < limit
-        found = jnp.where((place <= total) & inside, place, found)
-        step //= 2
-    return found
-
-
-def edge_block(start, used, shift, scalars, keys_ref, table, target, pre, second, slots):
-    block = pre.shape[0]
-    start = pl.multiple_of(start, LANES)
-    keys = keys_ref[0:1, pl.ds(start, block)]
-    senders = keys >> shift
-    targets = keys & ((1 << shift) - 1)
-    lowest = pl.multiple_of((scalars[0, start] >> shift) // 16 * 16, 16)
-    highest = scalars[0, jnp.minimum(start + block, used) - 1] >> shift
-
-    def window(base):
-        ids = column(jnp.clip(senders - base, -1, 1 << 14))
-        return dot(one_hot(ids, WINDOW), table[pl.ds(base, WINDOW)])
-
-    pre[...] = window(lowest) + dot(one_hot(column(targets), target.shape[0]), target[...])
-
-    def more(index, carry):
-        pre[...] += window(pl.multiple_of(lowest + (index + 1) * WINDOW, 16))
-        return carry
-
-    lax.fori_loop(0, (highest - lowest) // WINDOW, more, 0)
-    return added(pre[...], targets, second, slots)
+def pick_kernel(rows_hbm, rim_hbm, pair_out, *refs):
+    singles, (rows, rim, rows_here, rim_here) = refs[:5], refs[5:]
+    depth = singles[0].shape[0]
+    parts = rows_here.shape[0]
+    size = rows.shape[0] // parts
+    copies = [pltpu.make_async_copy(rim_hbm, rim, rim_here.at[0])]
+    for part in range(parts):
+        span = pl.ds(part * size, size)
+        copies.append(pltpu.make_async_copy(rows_hbm.at[span], rows.at[span], rows_here.at[part]))
+    for copy in copies:
+        copy.start()
+    pair = side_base()
+    outer = 5 - pair
+    chosen = [pair + 2, pair, pair + 1, RIGHT_LIST, LEFT_LIST, outer + 2, outer, outer + 1]
+    copies[0].wait()
+    ids = [column(rim[0, pl.ds(index, 1), :]) for index in chosen]
+    picked = [None] * len(ids)
+    for part in range(parts):
+        copies[part + 1].wait()
+        values = rows[part * size : (part + 1) * size]
+        for index, listed in enumerate(ids):
+            found = dot(one_hot(listed, size, part * size), values)
+            picked[index] = found if part == 0 else picked[index] + found
+    for index in range(3):
+        pair_out[index * depth : (index + 1) * depth] = picked[index].astype(BF16)
+    for out, found in zip(singles, picked[3:]):
+        out[...] = found.astype(BF16)
+
+
+def pick_grid(rows, rim):
+    count, width = rows.shape
+    depth = rim.shape[2]
+    parts = count // 256 if count % 256 == 0 else 1
+    block = pltpu.VMEM((depth, width), BF16)
+    return pl.pallas_call(
+        pick_kernel,
+        in_specs=[HBM, HBM],
+        out_shape=[pltpu.VMEM((3 * depth, width), BF16)] + [block] * 5,
+        scratch_shapes=[
+            pltpu.VMEM((count, width), BF16),
+            pltpu.VMEM(rim.shape, jnp.int32),
+            pltpu.SemaphoreType.DMA((parts,)),
+            pltpu.SemaphoreType.DMA((1,)),
+        ],
+        compiler_params=LIMIT,
+        name="pick_grid",
+    )(stay(rows), stay(rim))
+
+
+def pair_join_kernel(pair_ref, right_ref, left_ref, right_out, left_out):
+    depth = right_ref.shape[0]
+    for index, (own, out) in enumerate(((right_ref, right_out), (left_ref, left_out))):
+        out[:depth] = own[...]
+        out[depth:] = pair_ref[index * depth : (index + 1) * depth]
+
+
+def pair_join(pair, right, left):
+    depth, width = right.shape
+    return pl.pallas_call(
+        pair_join_kernel,
+        out_shape=[pltpu.VMEM((2 * depth, width), BF16)] * 2,
+        compiler_params=LIMIT,
+        name="pair_join",
+    )(pair, right, left)
+
+
+def grid_halo(rows, rim):
+    pair, right, left, *outer = pick_grid(rows, rim)
+    pair = move(pair, lambda i, j: (i ^ 1, j))
+    right, left = pair_join(pair, right, left)
+    other = lambda i: i + 1 if i % 2 else i - 1
+    remote = [
+        pair,
+        move(right, lambda i, j: (i, j + 1)),
+        move(left, lambda i, j: (i, j - 1)),
+        move(outer[0], lambda i, j: (other(i), j + 1)),
+        move(outer[1], lambda i, j: (other(i), j - 1)),
+        move(outer[2], lambda i, j: (other(i), j)),
+    ]
+    return remote, right
 
 
 def encode_local_kernel(
-    section, shift, scalars, keys_ref, grid_ref, mesh_ref, bias_ref, node_bias_ref,
-    edge_first, edge_second, node_first, node_second, table_out, target_out, total_out, inner_out, later,
-    table, pre, own, arrived, later_arrived,
+    section, grid_hbm, mesh_ref, edges_ref, bias_ref, node_bias_ref, gain_ref, node_gain_ref, after_ref,
+    edge_first, edge_second, node_first, node_second,
+    pre_out, inner_out, later, edges_out, mesh_out, gains_out,
+    grid_rows, table, target, own, grid_arrived, arrived, later_arrived,
 ):
+    grid_copy = pltpu.make_async_copy(grid_hbm, grid_rows, grid_arrived.at[0])
+    grid_copy.start()
     copies = fetch(
-        [edge_first.at[section, 0], edge_first.at[section, 1], node_first.at[section, 0]], own, arrived
+        [edge_first.at[section, 1], edge_first.at[section, 0], node_first.at[section, 0]], own, arrived
     )
     copies += fetch(
         [
-            edge_second.at[section], edge_first.at[section, 0], node_first.at[section, 1],
+            edge_first.at[section, 0], edge_second.at[section], node_first.at[section, 1],
             node_second.at[section], edge_first.at[section + 1, 0],
         ],
         later, later_arrived,
     )
-    count, slots = grid_ref.shape[0], mesh_ref.shape[0]
+    edges_out[...] = edges_ref[...]
+    gains_out[0:1] = row_of(gain_ref, section)
+    gains_out[1:2] = row_of(node_gain_ref, section)
+    rows = mesh_ref[...]
+    mesh_out[...] = rows
     copies[0].wait()
-    proj = dot(grid_ref[...], own[0]).astype(BF16)
-    table_out[...] = proj
-    fill(table, proj)
-    rows = mesh_ref[...]
+    fill(target, (dot(rows, own[0]) + row_of(bias_ref, section)).astype(BF16))
+    grid_copy.wait()
     copies[1].wait()
-    fill(target_out, (dot(rows, own[1]) + row_of(bias_ref, section)).astype(BF16))
+    fill(table, dot(grid_rows[...], own[1]).astype(BF16))
+    edges = edges_ref.shape[2]
+    block = math_block(edges, 1024)
+    for start in range(0, edges, block):
+        part = slice(start, start + block)
+        senders = column(edges_ref[0, 0:1, part])
+        targets = column(edges_ref[0, 1:2, part])
+        pre_out[part] = dot(one_hot(senders, table.shape[0]), table[...]) + dot(
+            one_hot(targets, target.shape[0]), target[...]
+        )
     copies[2].wait()
     inner_out[...] = dot(rows, own[2]) + row_of(node_bias_ref, section)
     for copy in copies[3:]:
         copy.wait()
-    total_out[...] = jnp.zeros_like(total_out)
-    block = pre.shape[0]
-    done = below(scalars, count << shift) // block
-
-    def step(index, carry):
-        total_out[...] += edge_block(
-            index * block, done * block, shift, scalars, keys_ref, table, target_out, pre, later[0], slots
-        )
-        return carry
-
-    lax.fori_loop(0, done, step, 0)
-
-
-def encode_local(keys, shift, grid_rows, mesh_rows, weights, section):
-    total = keys.shape[1]
+
+
+def encode_local(grid_rows, mesh_rows, edges, after, weights, section):
+    total = edges.shape[2]
     count, width = grid_rows.shape
     slots = mesh_rows.shape[0]
     vmem = pl.BlockSpec(memory_space=pltpu.VMEM)
     return pl.pallas_call(
-        functools.partial(encode_local_kernel, section, shift),
-        in_specs=[SMEM] + [vmem] * 5 + [HBM] * 4,
+        functools.partial(encode_local_kernel, section),
+        in_specs=[HBM] + [vmem] * 6 + [pl.BlockSpec(memory_space=pl.ANY)] + [HBM] * 4,
         out_shape=[
-            pltpu.VMEM((count, width), BF16),
-            pltpu.VMEM((round_up(slots, LANES), width), BF16),
-            pltpu.VMEM((slots, width), F32),
+            pltpu.VMEM((total, width), F32),
             pltpu.VMEM((slots, width), F32),
             matrices(5, width),
+            pltpu.VMEM(edges.shape, edges.dtype),
+            pltpu.VMEM(mesh_rows.shape, BF16),
+            pltpu.VMEM((2, width), F32),
         ],
         scratch_shapes=[
-            pltpu.VMEM((count + WINDOW, width), BF16),
-            pltpu.VMEM((math_block(total, BLOCK), width), F32),
-            *fetch_scratch(3, width),
+            pltpu.VMEM((count, width), BF16),
+            pltpu.VMEM((round_up(count, LANES), width), BF16),
+            pltpu.VMEM((round_up(slots, LANES), width), BF16),
+            pltpu.VMEM((3, width, width), BF16),
+            pltpu.SemaphoreType.DMA((1,)),
+            pltpu.SemaphoreType.DMA((3,)),
             pltpu.SemaphoreType.DMA((5,)),
         ],
         compiler_params=LIMIT,
         name="encode_local",
     )(
-        keys, keys, grid_rows, mesh_rows, weights["edge_bias"], weights["node_bias"],
+        stay(grid_rows), stay(mesh_rows), stay(edges), stay(weights["edge_bias"]), stay(weights["node_bias"]),
+        stay(weights["edge_gain"]), stay(weights["node_gain"]), after,
         weights["edge_first"], weights["edge_second"], weights["node_first"], weights["node_second"],
     )
 
 
-def encode_kernel(section, shift, *refs):
-    scalars, keys_ref, local_ref, target, total_ref, inner_ref, stack, mesh_ref = refs[:8]
-    pair_ref, right_ref, left_ref, outer_right, outer_left, outer_ref = refs[8:14]
-    gain_ref, node_gain_ref, lists_ref = refs[14:17]
-    mesh_out, proj_out, up, down, right, left, table, pre, total = refs[17:]
-    count, slots = local_ref.shape[0], mesh_ref.shape[0]
-    depth = outer_ref.shape[0]
-    table[:count] = local_ref[...]
-    clear_tail(table, count + 8 * depth)
+def halo_part(pre, edges_ref, part, table, base):
+    senders = edges_ref[0, 0:1, part] - base
+    return pre + dot(one_hot(column(senders), table.shape[0]), table[...])
+
+
+def encode_sides_kernel(count, pre_ref, edges_ref, stack, pair_ref, right_ref, left_ref, pre_out, table):
+    depth = right_ref.shape[0] // 2
     pair = side_base()
-    outer = 5 - pair
+    first = jnp.where(pair == 0, 0, 3)
     for ref, start, direction in (
         (pair_ref, 2 * depth, pair + 1),
         (right_ref, 0, 3),
         (right_ref, depth, pair),
         (left_ref, 0, 4),
         (left_ref, depth, pair + 2),
-        (outer_right, 0, outer),
-        (outer_left, 0, outer + 2),
-        (outer_ref, 0, outer + 1),
     ):
-        place = pl.multiple_of(count + direction * depth, LANES)
-        table[pl.ds(place, depth)] = dot(ref[start : start + depth], stack[1]).astype(BF16)
-    total[...] = total_ref[...]
-    block = pre.shape[0]
-    start = below(scalars, count << shift) // block * block
-    used = below(scalars, (count + 8 * depth) << shift)
-
-    def step(index, carry):
-        total[...] += edge_block(
-            start + index * block, used, shift, scalars, keys_ref, table, target, pre, stack[0], slots
-        )
-        return carry
-
-    lax.fori_loop(0, (used - start + block - 1) // block, step, 0)
-    summed = total[...] * row_of(gain_ref, section)
-    fresh = updated(mesh_ref[...], summed, inner_ref[...], stack[2], stack[3], row_of(node_gain_ref, section))
+        place = pl.multiple_of((direction - first) * depth, LANES)
+        table[pl.ds(place, depth)] = dot(ref[start : start + depth], stack[0]).astype(BF16)
+    edges = pre_ref.shape[0]
+    block = math_block(edges, 1024)
+    for start in range(0, edges, block):
+        part = slice(start, start + block)
+        pre_out[part] = halo_part(pre_ref[part], edges_ref, part, table, count + first * depth)
+
+
+def encode_sides(pre, edges, stack, remote, count):
+    depth, width = remote[1].shape[0] // 2, pre.shape[1]
+    return pl.pallas_call(
+        functools.partial(encode_sides_kernel, count),
+        out_shape=pltpu.VMEM(pre.shape, F32),
+        scratch_shapes=[pltpu.VMEM((5 * depth, width), BF16)],
+        input_output_aliases={0: 0},
+        compiler_params=LIMIT,
+        name="encode_sides",
+    )(near(pre), near(edges), near(stack), *remote)
+
+
+def encode_kernel(count, *refs):
+    pre_ref, edges_ref, stack, inner_ref, mesh_ref, outer_right, outer_left, outer_ref = refs[:8]
+    gains_ref, lists_ref = refs[8:10]
+    mesh_out, proj_out, up, down, right, left, table = refs[10:]
+    slots = mesh_ref.shape[0]
+    depth = outer_ref.shape[0]
+    for index, ref in enumerate((outer_right, outer_ref, outer_left)):
+        table[index * depth : (index + 1) * depth] = dot(ref[...], stack[0]).astype(BF16)
+    base = count + (5 - side_base()) * depth
+    edges = pre_ref.shape[0]
+    block = math_block(edges, 1024)
+    summed = None
+    for start in range(0, edges, block):
+        part = slice(start, start + block)
+        pre = halo_part(pre_ref[part], edges_ref, part, table, base)
+        made = added(pre, edges_ref[0, 1:2, part], stack[1], slots)
+        summed = made if summed is None else summed + made
+    summed = summed * row_of(gains_ref, 0)
+    fresh = updated(mesh_ref[...], summed, inner_ref[...], stack[2], stack[3], row_of(gains_ref, 1))
     mesh_out[...] = fresh
     fill(proj_out, dot(fresh, stack[4]).astype(BF16))
     list_rows(proj_out, lists_ref, (up, down, right, left))
 
 
-def encode(keys, shift, prepared, mesh_rows, remote, lists, depth, weights, section):
-    edges = keys.shape[1]
-    prepared = [near(value) for value in prepared]
-    count, width = prepared[0].shape
-    slots = mesh_rows.shape[0]
-    vmem = pl.BlockSpec(memory_space=pltpu.VMEM)
-    rows = count + 8 * remote[-1].shape[0]
-    return pl.pallas_call(
-        functools.partial(encode_kernel, section, shift),
-        in_specs=[SMEM] + [vmem] * 16,
+def encode(prepared, remote, lists, depth, count):
+    pre, inner, stack, edges, mesh_rows, gains = [near(value) for value in prepared]
+    slots, width = mesh_rows.shape
+    pre = near(encode_sides(pre, edges, stack, remote[:3], count))
+    return pl.pallas_call(
+        functools.partial(encode_kernel, count),
         out_shape=[
             pltpu.VMEM((slots, width), BF16),
             pltpu.VMEM((round_up(slots, LANES), width), BF16),
         ]
         + send_shapes(depth, width),
-        scratch_shapes=[
-            pltpu.VMEM((rows + WINDOW, width), BF16),
-            pltpu.VMEM((math_block(edges, BLOCK), width), F32),
-            pltpu.VMEM((slots, width), F32),
-        ],
+        scratch_shapes=[pltpu.VMEM((3 * remote[-1].shape[0], width), BF16)],
         compiler_params=LIMIT,
         name="encode",
-    )(keys, keys, *prepared, mesh_rows, *remote, weights["edge_gain"], weights["node_gain"], lists)
+    )(pre, edges, stack, inner, mesh_rows, *remote[3:], gains, lists)
 
 
 def prepare_kernel(
@@ -425,15 +431,15 @@
         functools.partial(prepare_kernel, section),
         in_specs=[vmem] * 3 + [HBM] * 4,
         out_shape=[
-            pltpu.VMEM((round_up(slots, LANES), width), BF16),
-            pltpu.VMEM((slots, width), F32),
+            place_of(section)((round_up(slots, LANES), width), BF16),
+            place_of(section)((slots, width), F32),
             matrices(4, width),
         ],
         scratch_shapes=fetch_scratch(2, width) + [pltpu.SemaphoreType.DMA((4,))],
         compiler_params=LIMIT,
         name="prepare",
     )(
-        near(mesh_rows), weights["edge_bias"], weights["node_bias"],
+        held(mesh_rows, section), weights["edge_bias"], weights["node_bias"],
         weights["edge_first"], weights["edge_second"], weights["node_first"], weights["node_second"],
     )
 
@@ -486,7 +492,8 @@
     last = section == 2
     padded = local.shape[0]
     table_rows = padded + sum(r.shape[0] * r.shape[1] for r in remote)
-    out_shape = [pltpu.VMEM((slots, width), BF16), pltpu.VMEM((padded, width), BF16)]
+    space = place_of(section + 1)
+    out_shape = [space((slots, width), BF16), space((padded, width), BF16)]
     if last:
         out_shape.append(jax.ShapeDtypeStruct((slots, width), BF16))
     vmem = pl.BlockSpec(memory_space=pltpu.VMEM)
@@ -498,7 +505,8 @@
         compiler_params=LIMIT,
         name="round_part",
     )(
-        edges, near(local), *[near(value) for value in prepared], near(mesh_rows), *remote,
+        edges, held(local, section), *[held(value, section) for value in prepared[:2]], near(prepared[2]),
+        held(mesh_rows, section), *remote,
         weights["edge_gain"], weights["node_gain"], lists, owned,
     )
 
@@ -638,12 +646,11 @@
     depth = mesh_rim.shape[2]
     peers, listed = long_send.shape[1:]
 
-    remote, keys, shift = grid_halo(grid_nodes, grid_rim, g2m_edges, slots)
-    rim_lists = jnp.concatenate([mesh_rim[0, m : m + 1] for m in SEND_ORDER], 0).reshape(1, 8 * depth)
+    remote, joined = grid_halo(grid_nodes, grid_rim)
     long_lists = long_send.reshape(1, peers * listed)
     rim_sends = send_shapes(depth, width)
-    prepared = encode_local(keys, shift, grid_nodes, mesh_nodes, weights, 0)
-    mesh_one, proj, *sends = encode(keys, shift, prepared, mesh_nodes, remote, rim_lists, depth, weights, 0)
+    prepared = encode_local(grid_nodes, mesh_nodes, g2m_edges, joined, weights, 0)
+    mesh_one, proj, *sends = encode(prepared, remote, mesh_rim, depth, grid_nodes.shape[0])
 
     remote, places = halo(*sends)
     prepared = prepare(mesh_one, weights, 1)
@@ -657,7 +664,7 @@
     prepared = prepare(mesh_two, weights, 2)
     mesh_three, proj, mesh_out, *sends = round_part(
         long_edges, proj, prepared, mesh_two, [arrived.reshape(1, peers * listed, width)], ((0,),),
-        rim_lists, owned_nodes, rim_sends, weights, 2,
+        mesh_rim, owned_nodes, rim_sends, weights, 2,
     )
 
     remote, places = halo(*sends)

time: 101 us -> 93.7 us (0.928)
  local copies, waits for them, and re-layouts: 9.82 us -> 0.25 us
  Pallas kernels: 42.2 us -> 48.5 us
  other arithmetic: 5.75 us -> 0 us
    unnamed x48 -> x22, local copies, waits for them, and re-layouts: 9.61 us -> 0.14 us
    sort x1 -> x0, other arithmetic: 5.75 us -> none  [pair_join(): return (right, left, lax.sort(keys.reshape(-1)).reshape(1, -1), shift)]
    pallas_call x4 -> x5, Pallas kernels: 18.1 us -> 21.6 us  [the longest x1 8.45 us: encode_local(): pl.pallas_call(functools.partial(encode_local_kernel, section), in_specs=...]
    pallas_call x2, Pallas kernels: 4.03 us -> 5.77 us  [prepare(): pl.pallas_call(functools.partial(prepare_kernel, section), in_specs=[vmem...]
    pallas_call x2, Pallas kernels: 9.46 us -> 10.5 us  [round_part(): pl.pallas_call(functools.partial(round_kernel, section, places, last), in...]
  transfers between devices with their start and end apart: 15 -> 15, of which waited for: 4 -> 4; matrix products, arithmetic and copies ran while one was open for 6% -> 0% of each run, Pallas kernels for 14% -> 23%
where the time goes in v4:
time: 93.7 us; the launch traced here: 93.3 us
  Pallas kernels  48.5 us (52%)
  starting transfers between devices  31 us (33%)
  waiting for transfers between devices  11.8 us (13%)
  between operations  1.79 us (2%)
    ppermute x14, starting transfers between devices, move(): return lax.ppermute(value, AXES, pairs)  26 us
    pallas_call x2, Pallas kernels, round_part(): pl.pallas_call(functools.partial(round_kernel, section, places, last), in...  10.5 us
    pallas_call x1, Pallas kernels, encode_local(): pl.pallas_call(functools.partial(encode_local_kernel, section), in_specs=...  8.45 us
    pallas_call x1, Pallas kernels, decode_part(): pl.pallas_call(functools.partial(decode_kernel, section, places, split),...  7.54 us
    all_to_all x1, waiting for transfers between devices, per_device(): lax.all_to_all(sent, AXES, split_axis=0, concat_axis=0, tiled=True)  6.84 us
    pallas_call x1, Pallas kernels, encode(): pl.pallas_call(functools.partial(encode_kernel, count), out_shape=[pltpu....  6.73 us
    pallas_call x2, Pallas kernels, prepare(): pl.pallas_call(functools.partial(prepare_kernel, section), in_specs=[vmem...  5.77 us
    all_to_all x1, starting transfers between devices, per_device(): lax.all_to_all(sent, AXES, split_axis=0, concat_axis=0, tiled=True)  5.04 us
  transfers between devices with their start and end apart: 15, of which 4 were waited for; matrix products, arithmetic and copies ran while one was open for 0% of the time, Pallas kernels for 23%

profile of v4, /device:TPU:0, one launch (start us, length us, event | category | flops | bytes accessed | tf_op | source)
XLA Modules:
  0.0 93.3 jit_solution(13832505365631725282)
XLA Ops:
  0.6 2.6 %pick_grid.1 = (bf16[384,512]{1,0:T(8,128)(2,1)S(1)}, bf16[128,512]{1,0:T(8,128)(2,1)S(1)}, bf16[128,512]{1,0:T(8,128)(2,1)S(1)}, bf16[128,512]{1,0:T(8,128)(2,1...) custom-call(bf16[1024,512]{1,0:T(8,128)(2,1)} %refs_2_.1, s32[1,8,128]{2,1,0:T(8,128)} %rim_hbm.1), custom_call_target="tpu_custom_call" | custom-call | tf_op jit(solution)/shard_map/pick_grid/pallas_call | solution.py:203
  3.7 1.3 %collective-permute-done.pair_ref = bf16[384,512]{1,0:T(8,128)(2,1)S(1)} collective-permute-done((bf16[384,512]{1,0:T(8,128)(2,1)S(1)}, bf16[384,512]{1,0:T(8,128)(2,1)S(1)}, u32[]{:S(2)}, u32[]{:S(2)}) %collective-permute-start) | collective-permute-done | bytes 393248 | tf_op jit(solution)/shard_map/ppermute | solution.py:612
  5.1 2.9 %collective-permute-start.1 = (bf16[256,512]{1,0:T(8,128)(2,1)S(1)}, bf16[256,512]{1,0:T(8,128)(2,1)S(1)}, u32[]{:S(2)}, u32[]{:S(2)}) collective-permute-start(bf16[256,512]{1,0:T(8,128)(2,1)S(1)} %get-tuple-element.46.after_ref), channel_id=1, source_target_pairs={{0,1},{1,2},{2,3},{3,4},{4,5},{5,6},{6,7},{7,0},{8,9},{9,10},{10,1... | collective-permute-start | bytes 786440 | tf_op jit(solution)/shard_map/ppermute | solution.py:612
  8.0 3.1 %collective-permute-start.2 = (bf16[256,512]{1,0:T(8,128)(2,1)S(1)}, bf16[256,512]{1,0:T(8,128)(2,1)S(1)}, u32[]{:S(2)}, u32[]{:S(2)}) collective-permute-start(bf16[256,512]{1,0:T(8,128)(2,1)S(1)} %get-tuple-element.50), channel_id=1, source_target_pairs={{0,7},{1,0},{2,1},{3,2},{4,3},{5,4},{6,5},{7,6},{8,15},{9,8},{10,9... | collective-permute-start | bytes 786440 | tf_op jit(solution)/shard_map/ppermute | solution.py:612
  11.1 5.3 %collective-permute-start.4 = (bf16[128,512]{1,0:T(8,128)(2,1)S(1)}, bf16[128,512]{1,0:T(8,128)(2,1)S(1)}, u32[]{:S(2)}, u32[]{:S(2)}) collective-permute-start(bf16[128,512]{1,0:T(8,128)(2,1)S(1)} %get-tuple-element.54), channel_id=1, source_target_pairs={{0,31},{1,24},{2,25},{3,26},{4,27},{5,28},{6,29},{7,30},{8,23},{9,... | collective-permute-start | bytes 393224 | tf_op jit(solution)/shard_map/ppermute | solution.py:612
  16.5 1.0 %collective-permute-start.5 = (bf16[128,512]{1,0:T(8,128)(2,1)S(1)}, bf16[128,512]{1,0:T(8,128)(2,1)S(1)}, u32[]{:S(2)}, u32[]{:S(2)}) collective-permute-start(bf16[128,512]{1,0:T(8,128)(2,1)S(1)} %get-tuple-element.55), channel_id=1, source_target_pairs={{0,24},{1,25},{2,26},{3,27},{4,28},{5,29},{6,30},{7,31},{8,16},{9,... | collective-permute-start | bytes 393224 | tf_op jit(solution)/shard_map/ppermute | solution.py:612
  17.5 8.4 %encode_local.1 = (f32[3072,512]{1,0:T(8,128)S(1)}, f32[192,512]{1,0:T(8,128)S(1)}, bf16[5,512,512]{2,1,0:T(8,128)(2,1)S(1)}, s32[1,2,3072]{2,1,0:T(2,128)S(1)},...) custom-call(bf16[1024,512]{1,0:T(8,128)(2,1)} %refs_2_.1, bf16[192,512]{1,0:T(8,128)(2,1)} %mesh_ref.1, ...), custom_call_target="tpu_custom_call" | custom-call | tf_op jit(solution)/shard_map/encode_local/pallas_call | solution.py:299
  26.0 3.8 %encode_sides.1.refs_0_ = f32[3072,512]{1,0:T(8,128)S(1)} custom-call(f32[3072,512]{1,0:T(8,128)S(1)} %get-tuple-element.47.pre_ref, s32[1,2,3072]{2,1,0:T(2,128)S(1)} %get-tuple-element.48.edges_ref.refs_1_, bf16[5,512,512]{2,1,0:T(8,128)(2,1)S(1)} %get-tuple-element.49.stack.refs_2_, ...), custom_call_target="tpu_custom_call", output_to_operand_aliasing={{}: (0, {})} | custom-call | tf_op jit(solution)/shard_map/encode_sides/pallas_call | solution.py:355
  29.8 6.7 %encode.1 = (bf16[192,512]{1,0:T(8,128)(2,1)S(1)}, bf16[256,512]{1,0:T(8,128)(2,1)S(1)}, bf16[3,16,512]{2,1,0:T(8,128)(2,1)S(1)}, bf16[3,16,512]{2,1,0:T(8,128)(...) custom-call(f32[3072,512]{1,0:T(8,128)S(1)} %encode_sides.1.refs_0_, ...), custom_call_target="tpu_custom_call" | custom-call | tf_op jit(solution)/shard_map/encode/pallas_call | solution.py:393
  37.4 1.0 %collective-permute-start.7 = (bf16[3,16,512]{2,1,0:T(8,128)(2,1)S(1)}, bf16[3,16,512]{2,1,0:T(8,128)(2,1)S(1)}, u32[]{:S(2)}, u32[]{:S(2)}) collective-permute-start(bf16[3,16,512]{2,1,0:T(8,128)(2,1)S(1)} %get-tuple-element.63), channel_id=1, source_target_pairs={{0,24},{1,25},{2,26},{3,27},{4,28},{5,29},{6,30},{7,31},{8,0},{9,1... | collective-permute-start | bytes 147464 | tf_op jit(solution)/shard_map/ppermute | solution.py:612
  38.3 1.8 %collective-permute-done.6.up_ref = bf16[3,16,512]{2,1,0:T(8,128)(2,1)S(1)} collective-permute-done((bf16[3,16,512]{2,1,0:T(8,128)(2,1)S(1)}, bf16[3,16,512]{2,1,0:T(8,128)(2,1)S(1)}, u32[]{:S(2)}, u32[]{:S(2)}) %collective-permute-start.6) | collective-permute-done | bytes 49184 | tf_op jit(solution)/shard_map/ppermute | solution.py:612
  40.2 4.7 %collective-permute-start.9 = (bf16[3,16,512]{2,1,0:T(8,128)(2,1)S(1)}, bf16[3,16,512]{2,1,0:T(8,128)(2,1)S(1)}, u32[]{:S(2)}, u32[]{:S(2)}) collective-permute-start(bf16[3,16,512]{2,1,0:T(8,128)(2,1)S(1)} %get-tuple-element.67), channel_id=1, source_target_pairs={{0,7},{1,0},{2,1},{3,2},{4,3},{5,4},{6,5},{7,6},{8,15},{9,8},{10,9... | collective-permute-start | bytes 147464 | tf_op jit(solution)/shard_map/ppermute | solution.py:612
  45.8 2.0 %prepare.2 = (bf16[256,512]{1,0:T(8,128)(2,1)S(1)}, f32[192,512]{1,0:T(8,128)S(1)}, bf16[4,512,512]{2,1,0:T(8,128)(2,1)S(1)}) custom-call(bf16[192,512]{1,0:T(8,128)(2,1)S(1)} %get-tuple-element.58.mesh_ref.refs_5_, f32[4,512]{1,0:T(4,128)S(1)} %copy-done.1, f32[4,512]{1,0:T(4,128)S(1)} %copy-done.2, bf16[4,2,512,512]{3,2,1,0:T(8,128)(2,1)} %edge_first.7, ...), custom_call_target="tpu_custom_call" | custom-call | tf_op jit(solution)/shard_map/prepare/pallas_call | solution.py:430
  47.9 4.8 %round_part.2 = (bf16[192,512]{1,0:T(8,128)(2,1)}, bf16[256,512]{1,0:T(8,128)(2,1)}, bf16[256,512]{1,0:T(8,128)(2,1)}) custom-call(s32[1,2,1536]{2,1,0:T(2,128)S(1)} %copy-done.6, bf16[256,512]{1,0:T(8,128)(2,1)S(1)} %get-tuple-element.57.refs_1_, bf16[256,512]{1,0:T(8,128)(2,1)S(1)} %get-tuple-element.59.refs_2_, f32[192,512]{1,0:T(8,128)S(1)} %get-tuple-element.60.refs_3_, ...), custom_call_target="tpu_custom_call" | custom-call | tf_op jit(solution)/shard_map/round_part/pallas_call | solution.py:500
  52.7 5.0 %all-to-all-start = ((bf16[32,8,512]{2,1,0:T(8,128)(2,1)}), bf16[32,8,512]{2,1,0:T(8,128)(2,1)S(1)}, u32[]{:S(2)}, u32[]{:S(2)}) async-start(bf16[32,8,512]{2,1,0:T(8,128)(2,1)} %bitcast), calls=%async_computation | async-start | bytes 524288 | tf_op jit(solution)/shard_map/all_to_all | solution.py:663
  57.8 3.8 %prepare.3 = (bf16[256,512]{1,0:T(8,128)(2,1)}, f32[192,512]{1,0:T(8,128)}, bf16[4,512,512]{2,1,0:T(8,128)(2,1)S(1)}) custom-call(bf16[192,512]{1,0:T(8,128)(2,1)} %get-tuple-element.69.mesh_ref.refs_5_, f32[4,512]{1,0:T(4,128)S(1)} %copy-done.1, f32[4,512]{1,0:T(4,128)S(1)} %copy-done.2, bf16[4,2,512,512]{3,2,1,0:T(8,128)(2,1)} %edge_first.7, ...), custom_call_target="tpu_custom_call" | custom-call | tf_op jit(solution)/shard_map/prepare/pallas_call | solution.py:430
  61.6 6.8 %all-to-all-done = bf16[32,8,512]{2,1,0:T(8,128)(2,1)S(1)} async-done(((bf16[32,8,512]{2,1,0:T(8,128)(2,1)}), bf16[32,8,512]{2,1,0:T(8,128)(2,1)S(1)}, u32[]{:S(2)}, u32[]{:S(2)}) %all-to-all-start) | async-done | bytes 262176 | tf_op jit(solution)/shard_map/all_to_all | solution.py:663
  68.4 5.7 %round_part.3 = (bf16[192,512]{1,0:T(8,128)(2,1)}, bf16[256,512]{1,0:T(8,128)(2,1)S(1)}, bf16[192,512]{1,0:T(8,128)(2,1)}, bf16[3,16,512]{2,1,0:T(8,128)(2,1)S(1...) custom-call(s32[1,2,1536]{2,1,0:T(2,128)S(1)} %copy-done.7, ...), custom_call_target="tpu_custom_call" | custom-call | tf_op jit(solution)/shard_map/round_part/pallas_call | solution.py:500
  74.1 1.7 %collective-permute-start.11 = (bf16[3,16,512]{2,1,0:T(8,128)(2,1)S(1)}, bf16[3,16,512]{2,1,0:T(8,128)(2,1)S(1)}, u32[]{:S(2)}, u32[]{:S(2)}) collective-permute-start(bf16[3,16,512]{2,1,0:T(8,128)(2,1)S(1)} %get-tuple-element.78), channel_id=1, source_target_pairs={{0,24},{1,25},{2,26},{3,27},{4,28},{5,29},{6,30},{7,31},{8,0},{9,1... | collective-permute-start | bytes 147464 | tf_op jit(solution)/shard_map/ppermute | solution.py:612
  75.9 1.8 %collective-permute-done.10.up_ref = bf16[3,16,512]{2,1,0:T(8,128)(2,1)S(1)} collective-permute-done((bf16[3,16,512]{2,1,0:T(8,128)(2,1)S(1)}, bf16[3,16,512]{2,1,0:T(8,128)(2,1)S(1)}, u32[]{:S(2)}, u32[]{:S(2)}) %collective-permute-start.10) | collective-permute-done | bytes 49184 | tf_op jit(solution)/shard_map/ppermute | solution.py:612
  77.6 1.1 %collective-permute-start.12 = (bf16[3,16,512]{2,1,0:T(8,128)(2,1)S(1)}, bf16[3,16,512]{2,1,0:T(8,128)(2,1)S(1)}, u32[]{:S(2)}, u32[]{:S(2)}) collective-permute-start(bf16[3,16,512]{2,1,0:T(8,128)(2,1)S(1)} %get-tuple-element.81), channel_id=1, source_target_pairs={{0,1},{1,2},{2,3},{3,4},{4,5},{5,6},{6,7},{7,0},{8,9},{9,10},{10,1... | collective-permute-start | bytes 147464 | tf_op jit(solution)/shard_map/ppermute | solution.py:612
  78.7 3.7 %collective-permute-start.13 = (bf16[3,16,512]{2,1,0:T(8,128)(2,1)S(1)}, bf16[3,16,512]{2,1,0:T(8,128)(2,1)S(1)}, u32[]{:S(2)}, u32[]{:S(2)}) collective-permute-start(bf16[3,16,512]{2,1,0:T(8,128)(2,1)S(1)} %get-tuple-element.82), channel_id=1, source_target_pairs={{0,7},{1,0},{2,1},{3,2},{4,3},{5,4},{6,5},{7,6},{8,15},{9,8},{10,9... | collective-permute-start | bytes 147464 | tf_op jit(solution)/shard_map/ppermute | solution.py:612
  82.4 3.1 %decode_local.1 = (bf16[3,1024,512]{2,1,0:T(8,128)(2,1)S(1)}, bf16[4,512,512]{2,1,0:T(8,128)(2,1)S(1)}) custom-call(bf16[1024,512]{1,0:T(8,128)(2,1)S(1)} %copy-done, bf16[256,512]{1,0:T(8,128)(2,1)S(1)} %get-tuple-element.74.table_ref, s32[1,3,1024]{2,1,0:T(4,128)S(1)} %copy.25.edges_ref.refs_3_, f32[4,512]{1,0:T(4,128)S(1)} %copy-done.1, ...), custom_call_target="tpu_custom_call" | custom-call | tf_op jit(solution)/shard_map/decode_local/pallas_call | solution.py:543
  85.6 7.5 %decode_part.1 = bf16[1024,512]{1,0:T(8,128)(2,1)} custom-call(bf16[3,1024,512]{2,1,0:T(8,128)(2,1)S(1)} %get-tuple-element.75.refs_0_, bf16[4,512,512]{2,1,0:T(8,128)(2,1)S(1)} %get-tuple-element.76.refs_1_, bf16[1024,512]{1,0:T(8,128)(2,1)S(1)} %copy-done, s32[1,3,1024]{2,1,0:T(4,128)S(1)} %copy.25.edges_ref.refs_3_, ...), custom_call_target="tpu_custom_call" | custom-call | tf_op jit(solution)/shard_map/decode_part/pallas_call | solution.py:587
  (46 shorter events, 1.7 us)
Async XLA Ops:
  3.2 1.9 %collective-permute-start = (bf16[384,512]{1,0:T(8,128)(2,1)S(1)}, bf16[384,512]{1,0:T(8,128)(2,1)S(1)}, u32[]{:S(2)}, u32[]{:S(2)}) collective-permute-start(bf16[384,512]{1,0:T(8,128)(2,1)S(1)} %get-tuple-element.43), channel_id=1, source_target_pairs={{0,8},{1,9},{2,10},{3,11},{4,12},{5,13},{6,14},{7,15},{8,0},{9,1},... | collective-permute-start | bytes 1179656 | tf_op jit(solution)/shard_map/ppermute | solution.py:612
  5.1 20.8 %collective-permute-start.1 = (bf16[256,512]{1,0:T(8,128)(2,1)S(1)}, bf16[256,512]{1,0:T(8,128)(2,1)S(1)}, u32[]{:S(2)}, u32[]{:S(2)}) collective-permute-start(bf16[256,512]{1,0:T(8,128)(2,1)S(1)} %get-tuple-element.46.after_ref), channel_id=1, source_target_pairs={{0,1},{1,2},{2,3},{3,4},{4,5},{5,6},{6,7},{7,0},{8,9},{9,10},{10,1... | collective-permute-start | bytes 786440 | tf_op jit(solution)/shard_map/ppermute | solution.py:612
  8.0 17.9 %collective-permute-start.2 = (bf16[256,512]{1,0:T(8,128)(2,1)S(1)}, bf16[256,512]{1,0:T(8,128)(2,1)S(1)}, u32[]{:S(2)}, u32[]{:S(2)}) collective-permute-start(bf16[256,512]{1,0:T(8,128)(2,1)S(1)} %get-tuple-element.50), channel_id=1, source_target_pairs={{0,7},{1,0},{2,1},{3,2},{4,3},{5,4},{6,5},{7,6},{8,15},{9,8},{10,9... | collective-permute-start | bytes 786440 | tf_op jit(solution)/shard_map/ppermute | solution.py:612
  11.1 18.6 %collective-permute-start.3 = (bf16[128,512]{1,0:T(8,128)(2,1)S(1)}, bf16[128,512]{1,0:T(8,128)(2,1)S(1)}, u32[]{:S(2)}, u32[]{:S(2)}) collective-permute-start(bf16[128,512]{1,0:T(8,128)(2,1)S(1)} %get-tuple-element.53), channel_id=1, source_target_pairs={{0,25},{1,26},{2,27},{3,28},{4,29},{5,30},{6,31},{7,24},{8,17},{9,... | collective-permute-start | bytes 393224 | tf_op jit(solution)/shard_map/ppermute | solution.py:612
  11.1 18.6 %collective-permute-start.4 = (bf16[128,512]{1,0:T(8,128)(2,1)S(1)}, bf16[128,512]{1,0:T(8,128)(2,1)S(1)}, u32[]{:S(2)}, u32[]{:S(2)}) collective-permute-start(bf16[128,512]{1,0:T(8,128)(2,1)S(1)} %get-tuple-element.54), channel_id=1, source_target_pairs={{0,31},{1,24},{2,25},{3,26},{4,27},{5,28},{6,29},{7,30},{8,23},{9,... | collective-permute-start | bytes 393224 | tf_op jit(solution)/shard_map/ppermute | solution.py:612
  16.5 13.3 %collective-permute-start.5 = (bf16[128,512]{1,0:T(8,128)(2,1)S(1)}, bf16[128,512]{1,0:T(8,128)(2,1)S(1)}, u32[]{:S(2)}, u32[]{:S(2)}) collective-permute-start(bf16[128,512]{1,0:T(8,128)(2,1)S(1)} %get-tuple-element.55), channel_id=1, source_target_pairs={{0,24},{1,25},{2,26},{3,27},{4,28},{5,29},{6,30},{7,31},{8,16},{9,... | collective-permute-start | bytes 393224 | tf_op jit(solution)/shard_map/ppermute | solution.py:612
  25.9 3.8 %copy-start.5 = (s32[1,8,16]{2,1,0:T(8,128)S(1)}, s32[1,8,16]{2,1,0:T(8,128)}, u32[]{:S(2)}) copy-start(s32[1,8,16]{2,1,0:T(8,128)} %refs_9_.4) | copy-start | bytes 1540
  29.8 15.8 %copy-start.9 = (s32[1,32,8]{1,2,0:T(8,128)S(1)}, s32[1,32,8]{1,2,0:T(8,128)}, u32[]{:S(2)}) copy-start(s32[1,32,8]{1,2,0:T(8,128)} %param.23) | copy-start | bytes 3076
  29.8 15.9 %copy-start.1 = (f32[4,512]{1,0:T(4,128)S(1)}, f32[4,512]{1,0:T(4,128)}, u32[]{:S(2)}) copy-start(f32[4,512]{1,0:T(4,128)} %bias_ref.7) | copy-start | bytes 24580
  29.8 15.9 %copy-start.2 = (f32[4,512]{1,0:T(4,128)S(1)}, f32[4,512]{1,0:T(4,128)}, u32[]{:S(2)}) copy-start(f32[4,512]{1,0:T(4,128)} %refs_9_.5) | copy-start | bytes 24580
  36.6 3.6 %collective-permute-start.6 = (bf16[3,16,512]{2,1,0:T(8,128)(2,1)S(1)}, bf16[3,16,512]{2,1,0:T(8,128)(2,1)S(1)}, u32[]{:S(2)}, u32[]{:S(2)}) collective-permute-start(bf16[3,16,512]{2,1,0:T(8,128)(2,1)S(1)} %get-tuple-element.62), channel_id=1, source_target_pairs={{0,8},{1,9},{2,10},{3,11},{4,12},{5,13},{6,14},{7,15},{8,16},{9,17... | collective-permute-start | bytes 147464 | tf_op jit(solution)/shard_map/ppermute | solution.py:612
  37.4 2.7 %collective-permute-start.7 = (bf16[3,16,512]{2,1,0:T(8,128)(2,1)S(1)}, bf16[3,16,512]{2,1,0:T(8,128)(2,1)S(1)}, u32[]{:S(2)}, u32[]{:S(2)}) collective-permute-start(bf16[3,16,512]{2,1,0:T(8,128)(2,1)S(1)} %get-tuple-element.63), channel_id=1, source_target_pairs={{0,24},{1,25},{2,26},{3,27},{4,28},{5,29},{6,30},{7,31},{8,0},{9,1... | collective-permute-start | bytes 147464 | tf_op jit(solution)/shard_map/ppermute | solution.py:612
  40.1 7.7 %collective-permute-start.8 = (bf16[3,16,512]{2,1,0:T(8,128)(2,1)S(1)}, bf16[3,16,512]{2,1,0:T(8,128)(2,1)S(1)}, u32[]{:S(2)}, u32[]{:S(2)}) collective-permute-start(bf16[3,16,512]{2,1,0:T(8,128)(2,1)S(1)} %get-tuple-element.66), channel_id=1, source_target_pairs={{0,1},{1,2},{2,3},{3,4},{4,5},{5,6},{6,7},{7,0},{8,9},{9,10},{10,1... | collective-permute-start | bytes 147464 | tf_op jit(solution)/shard_map/ppermute | solution.py:612
  40.2 7.6 %collective-permute-start.9 = (bf16[3,16,512]{2,1,0:T(8,128)(2,1)S(1)}, bf16[3,16,512]{2,1,0:T(8,128)(2,1)S(1)}, u32[]{:S(2)}, u32[]{:S(2)}) collective-permute-start(bf16[3,16,512]{2,1,0:T(8,128)(2,1)S(1)} %get-tuple-element.67), channel_id=1, source_target_pairs={{0,7},{1,0},{2,1},{3,2},{4,3},{5,4},{6,5},{7,6},{8,15},{9,8},{10,9... | collective-permute-start | bytes 147464 | tf_op jit(solution)/shard_map/ppermute | solution.py:612
  45.8 2.1 %copy-start.3 = (f32[4,512]{1,0:T(4,128)S(1)}, f32[4,512]{1,0:T(4,128)}, u32[]{:S(2)}) copy-start(f32[4,512]{1,0:T(4,128)} %refs_8_.3) | copy-start | bytes 24580
  45.8 2.1 %copy-start.4 = (f32[4,512]{1,0:T(4,128)S(1)}, f32[4,512]{1,0:T(4,128)}, u32[]{:S(2)}) copy-start(f32[4,512]{1,0:T(4,128)} %refs_10_.4) | copy-start | bytes 24580
  52.7 15.7 %all-to-all-start = ((bf16[32,8,512]{2,1,0:T(8,128)(2,1)}), bf16[32,8,512]{2,1,0:T(8,128)(2,1)S(1)}, u32[]{:S(2)}, u32[]{:S(2)}) async-start(bf16[32,8,512]{2,1,0:T(8,128)(2,1)} %bitcast), calls=%async_computation | async-start | bytes 524288 | tf_op jit(solution)/shard_map/all_to_all | solution.py:663
  57.8 10.6 %copy-start.7 = (s32[1,2,1536]{2,1,0:T(2,128)S(1)}, s32[1,2,1536]{2,1,0:T(2,128)}, u32[]{:S(2)}) copy-start(s32[1,2,1536]{2,1,0:T(2,128)} %refs_0_.3) | copy-start | bytes 36868
  61.5 20.9 %copy-start.8 = (s32[1,3,1024]{2,0,1:T(1,128)S(1)}, s32[1,3,1024]{2,0,1:T(1,128)}, u32[]{:S(2)}) copy-start(s32[1,3,1024]{2,0,1:T(1,128)} %param.27) | copy-start | bytes 36868
  61.5 20.9 %copy-start = (bf16[1024,512]{1,0:T(8,128)(2,1)S(1)}, bf16[1024,512]{1,0:T(8,128)(2,1)}, u32[]{:S(2)}) copy-start(bf16[1024,512]{1,0:T(8,128)(2,1)} %refs_2_.1) | copy-start | bytes 3145732
  74.1 3.5 %collective-permute-start.10 = (bf16[3,16,512]{2,1,0:T(8,128)(2,1)S(1)}, bf16[3,16,512]{2,1,0:T(8,128)(2,1)S(1)}, u32[]{:S(2)}, u32[]{:S(2)}) collective-permute-start(bf16[3,16,512]{2,1,0:T(8,128)(2,1)S(1)} %get-tuple-element.77), channel_id=1, source_target_pairs={{0,8},{1,9},{2,10},{3,11},{4,12},{5,13},{6,14},{7,15},{8,16},{9,17... | collective-permute-start | bytes 147464 | tf_op jit(solution)/shard_map/ppermute | solution.py:612
  74.1 3.5 %collective-permute-start.11 = (bf16[3,16,512]{2,1,0:T(8,128)(2,1)S(1)}, bf16[3,16,512]{2,1,0:T(8,128)(2,1)S(1)}, u32[]{:S(2)}, u32[]{:S(2)}) collective-permute-start(bf16[3,16,512]{2,1,0:T(8,128)(2,1)S(1)} %get-tuple-element.78), channel_id=1, source_target_pairs={{0,24},{1,25},{2,26},{3,27},{4,28},{5,29},{6,30},{7,31},{8,0},{9,1... | collective-permute-start | bytes 147464 | tf_op jit(solution)/shard_map/ppermute | solution.py:612
  77.6 8.0 %collective-permute-start.12 = (bf16[3,16,512]{2,1,0:T(8,128)(2,1)S(1)}, bf16[3,16,512]{2,1,0:T(8,128)(2,1)S(1)}, u32[]{:S(2)}, u32[]{:S(2)}) collective-permute-start(bf16[3,16,512]{2,1,0:T(8,128)(2,1)S(1)} %get-tuple-element.81), channel_id=1, source_target_pairs={{0,1},{1,2},{2,3},{3,4},{4,5},{5,6},{6,7},{7,0},{8,9},{9,10},{10,1... | collective-permute-start | bytes 147464 | tf_op jit(solution)/shard_map/ppermute | solution.py:612
  78.7 6.9 %collective-permute-start.13 = (bf16[3,16,512]{2,1,0:T(8,128)(2,1)S(1)}, bf16[3,16,512]{2,1,0:T(8,128)(2,1)S(1)}, u32[]{:S(2)}, u32[]{:S(2)}) collective-permute-start(bf16[3,16,512]{2,1,0:T(8,128)(2,1)S(1)} %get-tuple-element.82), channel_id=1, source_target_pairs={{0,7},{1,0},{2,1},{3,2},{4,3},{5,4},{6,5},{7,6},{8,15},{9,8},{10,9... | collective-permute-start | bytes 147464 | tf_op jit(solution)/shard_map/ppermute | solution.py:612
  (1 other events, 2.1 us)

commit v5 on v4

--- a/solution.py
+++ b/solution.py
@@ -51,15 +51,18 @@
 
 
 def silu(value):
-    half = 0.5 * value
+    half = (0.5 * value).astype(BF16)
     return half + half * jnp.tanh(half)
 
 
+def centre(ref, index):
+    weight = ref[index].astype(F32)
+    ref[index] = (weight - jnp.mean(weight, axis=-1, keepdims=True)).astype(BF16)
+
+
 def normed(value):
-    average = jnp.mean(value, axis=-1, keepdims=True)
-    centred = value - average
-    spread = jnp.mean(centred * centred, axis=-1, keepdims=True)
-    return centred * lax.rsqrt(spread + EPSILON)
+    spread = jnp.mean(value * value, axis=-1, keepdims=True)
+    return value * lax.rsqrt(spread + EPSILON)
 
 
 def whole(shape):
@@ -123,7 +126,7 @@
 
 
 def added(pre, targets, second, slots):
-    hidden = silu(pre).astype(BF16)
+    hidden = silu(pre)
     message = normed(dot(hidden, second)).astype(BF16)
     member = lax.broadcasted_iota(jnp.int32, (slots, targets.shape[1]), 0) == targets
     return dot(member.astype(BF16), message)
@@ -131,7 +134,7 @@
 
 def updated(rows, total, inner, first, second, gain):
     inner = inner + dot(total.astype(BF16), first)
-    update = normed(dot(silu(inner).astype(BF16), second)) * gain
+    update = normed(dot(silu(inner), second)) * gain
     return (rows.astype(F32) + update).astype(BF16)
 
 
@@ -166,9 +169,8 @@
             place += depth
 
 
-def pick_kernel(rows_hbm, rim_hbm, pair_out, *refs):
-    singles, (rows, rim, rows_here, rim_here) = refs[:5], refs[5:]
-    depth = singles[0].shape[0]
+def pick_pair_kernel(rows_hbm, rim_hbm, pair_out, rows, rim, rows_here, rim_here):
+    depth = rim.shape[2]
     parts = rows_here.shape[0]
     size = rows.shape[0] // parts
     copies = [pltpu.make_async_copy(rim_hbm, rim, rim_here.at[0])]
@@ -178,10 +180,8 @@
     for copy in copies:
         copy.start()
     pair = side_base()
-    outer = 5 - pair
-    chosen = [pair + 2, pair, pair + 1, RIGHT_LIST, LEFT_LIST, outer + 2, outer, outer + 1]
     copies[0].wait()
-    ids = [column(rim[0, pl.ds(index, 1), :]) for index in chosen]
+    ids = [column(rim[0, pl.ds(pair + offset, 1), :]) for offset in (2, 0, 1)]
     picked = [None] * len(ids)
     for part in range(parts):
         copies[part + 1].wait()
@@ -189,30 +189,72 @@
         for index, listed in enumerate(ids):
             found = dot(one_hot(listed, size, part * size), values)
             picked[index] = found if part == 0 else picked[index] + found
-    for index in range(3):
-        pair_out[index * depth : (index + 1) * depth] = picked[index].astype(BF16)
-    for out, found in zip(singles, picked[3:]):
-        out[...] = found.astype(BF16)
-
-
-def pick_grid(rows, rim):
+    for index, found in enumerate(picked):
+        pair_out[index * depth : (index + 1) * depth] = found.astype(BF16)
+
+
+def pick_pair(rows, rim):
     count, width = rows.shape
-    depth = rim.shape[2]
     parts = count // 256 if count % 256 == 0 else 1
-    block = pltpu.VMEM((depth, width), BF16)
-    return pl.pallas_call(
-        pick_kernel,
+    return pl.pallas_call(
+        pick_pair_kernel,
         in_specs=[HBM, HBM],
-        out_shape=[pltpu.VMEM((3 * depth, width), BF16)] + [block] * 5,
-        scratch_shapes=[
+        out_shape=[
+            pltpu.VMEM((3 * rim.shape[2], width), BF16),
             pltpu.VMEM((count, width), BF16),
             pltpu.VMEM(rim.shape, jnp.int32),
-            pltpu.SemaphoreType.DMA((parts,)),
-            pltpu.SemaphoreType.DMA((1,)),
-        ],
-        compiler_params=LIMIT,
-        name="pick_grid",
+        ],
+        scratch_shapes=[pltpu.SemaphoreType.DMA((parts,)), pltpu.SemaphoreType.DMA((1,))],
+        compiler_params=LIMIT,
+        name="pick_pair",
     )(stay(rows), stay(rim))
+
+
+def pick_rest_kernel(section, rows_ref, rim_ref, edge_first, node_first, mesh_hbm, edges_hbm, *refs):
+    vectors, refs = refs[:4], refs[4:]
+    outs, (stack, mesh, edges, rows_of, arrived, mesh_here, edges_here, vectors_here) = refs[:5], refs[5:]
+    copies = fetch(
+        [edge_first.at[section, 1], edge_first.at[section, 0], node_first.at[section, 0]], stack, arrived
+    )
+    copies.append(pltpu.make_async_copy(mesh_hbm, mesh, mesh_here.at[0]))
+    copies.append(pltpu.make_async_copy(edges_hbm, edges, edges_here.at[0]))
+    for index, vector in enumerate(vectors):
+        copies.append(
+            pltpu.make_async_copy(
+                vector.at[pl.ds(section, 1)], rows_of.at[pl.ds(index, 1)], vectors_here.at[index]
+            )
+        )
+    for copy in copies[3:]:
+        copy.start()
+    outer = 5 - side_base()
+    for out, chosen in zip(outs, (RIGHT_LIST, LEFT_LIST, outer + 2, outer, outer + 1)):
+        ids = column(rim_ref[0, pl.ds(chosen, 1), :])
+        out[...] = dot(one_hot(ids, rows_ref.shape[0]), rows_ref[...]).astype(BF16)
+    for copy in copies:
+        copy.wait()
+
+
+def pick_rest(rows, rim, mesh_rows, edges, weights, section):
+    width = rows.shape[1]
+    vmem = pl.BlockSpec(memory_space=pltpu.VMEM)
+    return pl.pallas_call(
+        functools.partial(pick_rest_kernel, section),
+        in_specs=[vmem] * 2 + [HBM] * 8,
+        out_shape=[pltpu.VMEM((rim.shape[2], width), BF16)] * 5
+        + [
+            matrices(3, width),
+            pltpu.VMEM(mesh_rows.shape, BF16),
+            pltpu.VMEM(edges.shape, edges.dtype),
+            pltpu.VMEM((4, width), F32),
+        ],
+        scratch_shapes=[pltpu.SemaphoreType.DMA((n,)) for n in (3, 1, 1, 4)],
+        compiler_params=LIMIT,
+        name="pick_rest",
+    )(
+        near(rows), near(rim), weights["edge_first"], weights["node_first"], stay(mesh_rows), stay(edges),
+        stay(weights["edge_bias"]), stay(weights["node_bias"]), stay(weights["edge_gain"]),
+        stay(weights["node_gain"]),
+    )
 
 
 def pair_join_kernel(pair_ref, right_ref, left_ref, right_out, left_out):
@@ -232,9 +274,11 @@
     )(pair, right, left)
 
 
-def grid_halo(rows, rim):
-    pair, right, left, *outer = pick_grid(rows, rim)
+def grid_halo(rows, rim, mesh_rows, edges, weights, section):
+    pair, rows, rim = pick_pair(rows, rim)
     pair = move(pair, lambda i, j: (i ^ 1, j))
+    right, left, *rest = pick_rest(rows, rim, mesh_rows, edges, weights, section)
+    outer, kept = rest[:3], rest[3:]
     right, left = pair_join(pair, right, left)
     other = lambda i: i + 1 if i % 2 else i - 1
     remote = [
@@ -245,37 +289,24 @@
         move(outer[1], lambda i, j: (other(i), j - 1)),
         move(outer[2], lambda i, j: (other(i), j)),
     ]
-    return remote, right
+    return remote, right, rows, kept
 
 
 def encode_local_kernel(
-    section, grid_hbm, mesh_ref, edges_ref, bias_ref, node_bias_ref, gain_ref, node_gain_ref, after_ref,
-    edge_first, edge_second, node_first, node_second,
-    pre_out, inner_out, later, edges_out, mesh_out, gains_out,
-    grid_rows, table, target, own, grid_arrived, arrived, later_arrived,
+    section, grid_ref, stack, mesh_ref, edges_ref, vectors, after_ref,
+    edge_first, edge_second, node_first, node_second, pre_out, inner_out, later, table, target, arrived,
 ):
-    grid_copy = pltpu.make_async_copy(grid_hbm, grid_rows, grid_arrived.at[0])
-    grid_copy.start()
     copies = fetch(
-        [edge_first.at[section, 1], edge_first.at[section, 0], node_first.at[section, 0]], own, arrived
-    )
-    copies += fetch(
         [
             edge_first.at[section, 0], edge_second.at[section], node_first.at[section, 1],
             node_second.at[section], edge_first.at[section + 1, 0],
         ],
-        later, later_arrived,
-    )
-    edges_out[...] = edges_ref[...]
-    gains_out[0:1] = row_of(gain_ref, section)
-    gains_out[1:2] = row_of(node_gain_ref, section)
+        later, arrived,
+    )
     rows = mesh_ref[...]
-    mesh_out[...] = rows
-    copies[0].wait()
-    fill(target, (dot(rows, own[0]) + row_of(bias_ref, section)).astype(BF16))
-    grid_copy.wait()
-    copies[1].wait()
-    fill(table, dot(grid_rows[...], own[1]).astype(BF16))
+    fill(target, (dot(rows, stack[0]) + row_of(vectors, 0)).astype(BF16))
+    fill(table, dot(grid_ref[...], stack[1]).astype(BF16))
+    inner_out[...] = dot(rows, stack[2]) + row_of(vectors, 1)
     edges = edges_ref.shape[2]
     block = math_block(edges, 1024)
     for start in range(0, edges, block):
@@ -285,42 +316,35 @@
         pre_out[part] = dot(one_hot(senders, table.shape[0]), table[...]) + dot(
             one_hot(targets, target.shape[0]), target[...]
         )
-    copies[2].wait()
-    inner_out[...] = dot(rows, own[2]) + row_of(node_bias_ref, section)
-    for copy in copies[3:]:
+    for copy in copies:
         copy.wait()
-
-
-def encode_local(grid_rows, mesh_rows, edges, after, weights, section):
+    centre(later, 1)
+    centre(later, 3)
+
+
+def encode_local(grid_rows, kept, after, weights, section):
+    stack, mesh_rows, edges, vectors = [near(value) for value in kept]
     total = edges.shape[2]
     count, width = grid_rows.shape
     slots = mesh_rows.shape[0]
     vmem = pl.BlockSpec(memory_space=pltpu.VMEM)
     return pl.pallas_call(
         functools.partial(encode_local_kernel, section),
-        in_specs=[HBM] + [vmem] * 6 + [pl.BlockSpec(memory_space=pl.ANY)] + [HBM] * 4,
+        in_specs=[vmem] * 5 + [pl.BlockSpec(memory_space=pl.ANY)] + [HBM] * 4,
         out_shape=[
             pltpu.VMEM((total, width), F32),
             pltpu.VMEM((slots, width), F32),
             matrices(5, width),
-            pltpu.VMEM(edges.shape, edges.dtype),
-            pltpu.VMEM(mesh_rows.shape, BF16),
-            pltpu.VMEM((2, width), F32),
         ],
         scratch_shapes=[
-            pltpu.VMEM((count, width), BF16),
             pltpu.VMEM((round_up(count, LANES), width), BF16),
             pltpu.VMEM((round_up(slots, LANES), width), BF16),
-            pltpu.VMEM((3, width, width), BF16),
-            pltpu.SemaphoreType.DMA((1,)),
-            pltpu.SemaphoreType.DMA((3,)),
             pltpu.SemaphoreType.DMA((5,)),
         ],
         compiler_params=LIMIT,
         name="encode_local",
     )(
-        stay(grid_rows), stay(mesh_rows), stay(edges), stay(weights["edge_bias"]), stay(weights["node_bias"]),
-        stay(weights["edge_gain"]), stay(weights["node_gain"]), after,
+        near(grid_rows), stack, mesh_rows, edges, vectors, after,
         weights["edge_first"], weights["edge_second"], weights["node_first"], weights["node_second"],
     )
 
@@ -364,7 +388,7 @@
 
 def encode_kernel(count, *refs):
     pre_ref, edges_ref, stack, inner_ref, mesh_ref, outer_right, outer_left, outer_ref = refs[:8]
-    gains_ref, lists_ref = refs[8:10]
+    vectors, lists_ref = refs[8:10]
     mesh_out, proj_out, up, down, right, left, table = refs[10:]
     slots = mesh_ref.shape[0]
     depth = outer_ref.shape[0]
@@ -379,15 +403,16 @@
         pre = halo_part(pre_ref[part], edges_ref, part, table, base)
         made = added(pre, edges_ref[0, 1:2, part], stack[1], slots)
         summed = made if summed is None else summed + made
-    summed = summed * row_of(gains_ref, 0)
-    fresh = updated(mesh_ref[...], summed, inner_ref[...], stack[2], stack[3], row_of(gains_ref, 1))
+    summed = summed * row_of(vectors, 2)
+    fresh = updated(mesh_ref[...], summed, inner_ref[...], stack[2], stack[3], row_of(vectors, 3))
     mesh_out[...] = fresh
     fill(proj_out, dot(fresh, stack[4]).astype(BF16))
     list_rows(proj_out, lists_ref, (up, down, right, left))
 
 
-def encode(prepared, remote, lists, depth, count):
-    pre, inner, stack, edges, mesh_rows, gains = [near(value) for value in prepared]
+def encode(prepared, kept, remote, lists, depth, count):
+    pre, inner, stack = [near(value) for value in prepared]
+    mesh_rows, edges, vectors = [near(value) for value in kept[1:]]
     slots, width = mesh_rows.shape
     pre = near(encode_sides(pre, edges, stack, remote[:3], count))
     return pl.pallas_call(
@@ -400,7 +425,7 @@
         scratch_shapes=[pltpu.VMEM((3 * remote[-1].shape[0], width), BF16)],
         compiler_params=LIMIT,
         name="encode",
-    )(pre, edges, stack, inner, mesh_rows, *remote[3:], gains, lists)
+    )(pre, edges, stack, inner, mesh_rows, *remote[3:], vectors, lists)
 
 
 def prepare_kernel(
@@ -422,6 +447,8 @@
     inner_out[...] = dot(rows, own[1]) + row_of(node_bias_ref, section)
     for copy in copies[2:]:
         copy.wait()
+    centre(later, 0)
+    centre(later, 2)
 
 
 def prepare(mesh_rows, weights, section):
@@ -457,14 +484,31 @@
     remote = refs[6 : 6 + len(places)]
     gain_ref, node_gain_ref, lists_ref, owned_ref = refs[6 + len(places) : 10 + len(places)]
     rest = refs[10 + len(places) :]
+    slots, padded = mesh_ref.shape[0], local_ref.shape[0]
+    if last:
+        table, target_here, inner_here, mesh_here, here = rest[-5:]
+        rest = rest[:-5]
+        copies = [
+            pltpu.make_async_copy(local_ref, table.at[pl.ds(0, padded)], here.at[0]),
+            pltpu.make_async_copy(target, target_here, here.at[1]),
+            pltpu.make_async_copy(inner_ref, inner_here, here.at[2]),
+            pltpu.make_async_copy(mesh_ref, mesh_here, here.at[3]),
+        ]
+        for copy in copies:
+            copy.start()
+        target, inner_ref, mesh_ref = target_here, inner_here, mesh_here
+    else:
+        table = rest[-1]
+        rest = rest[:-1]
+        table[:padded] = local_ref[...]
     mesh_out, proj_out = rest[:2]
-    sends = rest[2:-1]
-    table = rest[-1]
+    sends = rest[2:]
     if last:
         masked_out, sends = sends[0], sends[1:]
-    slots, padded = mesh_ref.shape[0], local_ref.shape[0]
-    table[:padded] = local_ref[...]
     place_remote(table, remote, places, padded)
+    if last:
+        for copy in copies:
+            copy.wait()
     edges = edges_ref.shape[2]
     block = math_block(edges, 1536)
     summed = None
@@ -496,12 +540,18 @@
     out_shape = [space((slots, width), BF16), space((padded, width), BF16)]
     if last:
         out_shape.append(jax.ShapeDtypeStruct((slots, width), BF16))
+    scratch = [pltpu.VMEM((table_rows, width), BF16)]
+    if last:
+        scratch += [pltpu.VMEM(value.shape, value.dtype) for value in (*prepared[:2], mesh_rows)]
+        scratch.append(pltpu.SemaphoreType.DMA((4,)))
     vmem = pl.BlockSpec(memory_space=pltpu.VMEM)
     return pl.pallas_call(
         functools.partial(round_kernel, section, places, last),
-        in_specs=[vmem] * (9 + len(remote)) + [SMEM],
+        in_specs=[vmem] + [HBM if last else vmem] * 3 + [vmem] + [HBM if last else vmem]
+        + [vmem] * (3 + len(remote))
+        + [SMEM],
         out_shape=out_shape + sends,
-        scratch_shapes=[pltpu.VMEM((table_rows, width), BF16)],
+        scratch_shapes=scratch,
         compiler_params=LIMIT,
         name="round_part",
     )(
@@ -534,6 +584,8 @@
             pre_ref[sender, start : start + block] = pre.astype(BF16)
     for copy in copies[1:]:
         copy.wait()
+    centre(later, 0)
+    centre(later, 3)
 
 
 def decode_local(grid_rows, table, edges, weights, section):
@@ -567,12 +619,12 @@
         for sender in range(edges_ref.shape[1]):
             ids = column(edges_ref[0, sender : sender + 1, part])
             pre = pre_ref[sender, part].astype(F32) + dot(one_hot(ids, table.shape[0], split), table[...])
-            message = normed(dot(silu(pre).astype(BF16), stack[0])).astype(BF16).astype(F32)
+            message = normed(dot(silu(pre), stack[0])).astype(BF16).astype(F32)
             summed = message if summed is None else summed + message
         rows = grid_ref[part]
         summed = (summed * row_of(gain_ref, section)).astype(BF16)
         inner = dot(rows, stack[1]) + dot(summed, stack[2]) + row_of(node_bias_ref, section)
-        update = normed(dot(silu(inner).astype(BF16), stack[3])) * row_of(node_gain_ref, section)
+        update = normed(dot(silu(inner), stack[3])) * row_of(node_gain_ref, section)
         ready[part] = (rows.astype(F32) + update).astype(BF16)
         copies.append(pltpu.make_async_copy(ready.at[part], out_ref.at[part], sent.at[index]))
         copies[-1].start()
@@ -646,11 +698,11 @@
     depth = mesh_rim.shape[2]
     peers, listed = long_send.shape[1:]
 
-    remote, joined = grid_halo(grid_nodes, grid_rim)
     long_lists = long_send.reshape(1, peers * listed)
     rim_sends = send_shapes(depth, width)
-    prepared = encode_local(grid_nodes, mesh_nodes, g2m_edges, joined, weights, 0)
-    mesh_one, proj, *sends = encode(prepared, remote, mesh_rim, depth, grid_nodes.shape[0])
+    remote, joined, tile, kept = grid_halo(grid_nodes, grid_rim, mesh_nodes, g2m_edges, weights, 0)
+    prepared = encode_local(tile, kept, joined, weights, 0)
+    mesh_one, proj, *sends = encode(prepared, kept, remote, mesh_rim, depth, grid_nodes.shape[0])
 
     remote, places = halo(*sends)
     prepared = prepare(mesh_one, weights, 1)

time: 93.7 us -> 89.9 us (0.959)
  Pallas kernels: 48.5 us -> 43.7 us
  waiting for transfers between devices: 11.8 us -> 12.8 us
    pallas_call x1, Pallas kernels: 8.45 us -> 5.36 us  [encode_local(): pl.pallas_call(functools.partial(encode_local_kernel, section), in_specs=...]
    pallas_call x1, Pallas kernels: 7.54 us -> 5.96 us  [decode_part(): pl.pallas_call(functools.partial(decode_kernel, section, places, split),...]
    pallas_call x1 -> x2, Pallas kernels: 2.58 us -> 3.87 us  [the longest x1 2.06 us: pick_rest(): pl.pallas_call(functools.partial(pick_rest_kernel, section), in_specs=[vm...]
    pallas_call x1, Pallas kernels: 6.73 us -> 5.52 us  [encode(): pl.pallas_call(functools.partial(encode_kernel, count), out_shape=[pltpu....]
    ppermute x14, waiting for transfers between devices: 4.92 us -> 5.98 us  [move(): return lax.ppermute(value, AXES, pairs)]
where the time goes in v5:
time: 89.9 us; the launch traced here: 89.6 us
  Pallas kernels  43.7 us (49%)
  starting transfers between devices  31 us (34%)
  waiting for transfers between devices  12.8 us (14%)
  between operations  1.83 us (2%)
    ppermute x14, starting transfers between devices, move(): return lax.ppermute(value, AXES, pairs)  26.2 us
    pallas_call x2, Pallas kernels, round_part(): pl.pallas_call(functools.partial(round_kernel, section, places, last), in...  9.66 us
    all_to_all x1, waiting for transfers between devices, per_device(): lax.all_to_all(sent, AXES, split_axis=0, concat_axis=0, tiled=True)  6.84 us
    pallas_call x2, Pallas kernels, prepare(): pl.pallas_call(functools.partial(prepare_kernel, section), in_specs=[vmem...  6.11 us
    ppermute x14, waiting for transfers between devices, move(): return lax.ppermute(value, AXES, pairs)  5.98 us
    pallas_call x1, Pallas kernels, decode_part(): pl.pallas_call(functools.partial(decode_kernel, section, places, split),...  5.96 us
    pallas_call x1, Pallas kernels, encode(): pl.pallas_call(functools.partial(encode_kernel, count), out_shape=[pltpu....  5.52 us
    pallas_call x1, Pallas kernels, encode_local(): pl.pallas_call(functools.partial(encode_local_kernel, section), in_specs=...  5.36 us
  transfers between devices with their start and end apart: 15, of which 4 were waited for; matrix products, arithmetic and copies ran while one was open for 0% of the time, Pallas kernels for 23%

profile of v5, /device:TPU:0, one launch (start us, length us, event | category | flops | bytes accessed | tf_op | source)
XLA Modules:
  0.0 89.6 jit_solution(9339291222335993889)
XLA Ops:
  0.6 1.8 %pick_pair.1 = (bf16[384,512]{1,0:T(8,128)(2,1)S(1)}, bf16[1024,512]{1,0:T(8,128)(2,1)S(1)}, s32[1,8,128]{2,1,0:T(8,128)S(1)}) custom-call(bf16[1024,512]{1,0:T(8,128)(2,1)} %refs_2_.3, s32[1,8,128]{2,1,0:T(8,128)} %rim_hbm.1), custom_call_target="tpu_custom_call" | custom-call | tf_op jit(solution)/shard_map/pick_pair/pallas_call | solution.py:199
  3.0 2.1 %pick_rest.1 = (bf16[128,512]{1,0:T(8,128)(2,1)S(1)}, bf16[128,512]{1,0:T(8,128)(2,1)S(1)}, bf16[128,512]{1,0:T(8,128)(2,1)S(1)}, bf16[128,512]{1,0:T(8,128)(2,1...) custom-call(bf16[1024,512]{1,0:T(8,128)(2,1)S(1)} %get-tuple-element, ...), custom_call_target="tpu_custom_call" | custom-call | tf_op jit(solution)/shard_map/pick_rest/pallas_call | solution.py:240
  5.1 2.6 %collective-permute-start.1 = (bf16[256,512]{1,0:T(8,128)(2,1)S(1)}, bf16[256,512]{1,0:T(8,128)(2,1)S(1)}, u32[]{:S(2)}, u32[]{:S(2)}) collective-permute-start(bf16[256,512]{1,0:T(8,128)(2,1)S(1)} %get-tuple-element.55.after_ref), channel_id=1, source_target_pairs={{0,1},{1,2},{2,3},{3,4},{4,5},{5,6},{6,7},{7,0},{8,9},{9,10},{10,1... | collective-permute-start | bytes 786440 | tf_op jit(solution)/shard_map/ppermute | solution.py:664
  7.7 3.1 %collective-permute-start.2 = (bf16[256,512]{1,0:T(8,128)(2,1)S(1)}, bf16[256,512]{1,0:T(8,128)(2,1)S(1)}, u32[]{:S(2)}, u32[]{:S(2)}) collective-permute-start(bf16[256,512]{1,0:T(8,128)(2,1)S(1)} %get-tuple-element.58), channel_id=1, source_target_pairs={{0,7},{1,0},{2,1},{3,2},{4,3},{5,4},{6,5},{7,6},{8,15},{9,8},{10,9... | collective-permute-start | bytes 786440 | tf_op jit(solution)/shard_map/ppermute | solution.py:664
  10.8 5.3 %collective-permute-start.4 = (bf16[128,512]{1,0:T(8,128)(2,1)S(1)}, bf16[128,512]{1,0:T(8,128)(2,1)S(1)}, u32[]{:S(2)}, u32[]{:S(2)}) collective-permute-start(bf16[128,512]{1,0:T(8,128)(2,1)S(1)} %get-tuple-element.61), channel_id=1, source_target_pairs={{0,31},{1,24},{2,25},{3,26},{4,27},{5,28},{6,29},{7,30},{8,23},{9,... | collective-permute-start | bytes 393224 | tf_op jit(solution)/shard_map/ppermute | solution.py:664
  16.1 1.3 %collective-permute-start.5 = (bf16[128,512]{1,0:T(8,128)(2,1)S(1)}, bf16[128,512]{1,0:T(8,128)(2,1)S(1)}, u32[]{:S(2)}, u32[]{:S(2)}) collective-permute-start(bf16[128,512]{1,0:T(8,128)(2,1)S(1)} %get-tuple-element.62), channel_id=1, source_target_pairs={{0,24},{1,25},{2,26},{3,27},{4,28},{5,29},{6,30},{7,31},{8,16},{9,... | collective-permute-start | bytes 393224 | tf_op jit(solution)/shard_map/ppermute | solution.py:664
  17.4 5.4 %encode_local.1 = (f32[3072,512]{1,0:T(8,128)S(1)}, f32[192,512]{1,0:T(8,128)S(1)}, bf16[5,512,512]{2,1,0:T(8,128)(2,1)S(1)}) custom-call(bf16[1024,512]{1,0:T(8,128)(2,1)S(1)} %get-tuple-element.46.rows_ref.grid_ref, bf16[3,512,512]{2,1,0:T(8,128)(2,1)S(1)} %get-tuple-element.48.stack, bf16[192,512]{1,0:T(8,128)(2,1)S(1)} %get-tuple-element.49.mesh_ref.refs_4_, ...), custom_call_target="tpu_custom_call" | custom-call | tf_op jit(solution)/shard_map/encode_local/pallas_call | solution.py:331
  22.8 2.4 %collective-permute-done.2.left_ref = bf16[256,512]{1,0:T(8,128)(2,1)S(1)} collective-permute-done((bf16[256,512]{1,0:T(8,128)(2,1)S(1)}, bf16[256,512]{1,0:T(8,128)(2,1)S(1)}, u32[]{:S(2)}, u32[]{:S(2)}) %collective-permute-start.2) | collective-permute-done | bytes 262176 | tf_op jit(solution)/shard_map/ppermute | solution.py:664
  25.2 3.8 %encode_sides.1.refs_0_ = f32[3072,512]{1,0:T(8,128)S(1)} custom-call(f32[3072,512]{1,0:T(8,128)S(1)} %get-tuple-element.56.pre_ref, s32[1,2,3072]{2,1,0:T(2,128)S(1)} %get-tuple-element.50.edges_ref.refs_1_, bf16[5,512,512]{2,1,0:T(8,128)(2,1)S(1)} %get-tuple-element.57.stack.refs_2_, ...), custom_call_target="tpu_custom_call", output_to_operand_aliasing={{}: (0, {})} | custom-call | tf_op jit(solution)/shard_map/encode_sides/pallas_call | solution.py:379
  29.1 5.5 %encode.1 = (bf16[192,512]{1,0:T(8,128)(2,1)S(1)}, bf16[256,512]{1,0:T(8,128)(2,1)S(1)}, bf16[3,16,512]{2,1,0:T(8,128)(2,1)S(1)}, bf16[3,16,512]{2,1,0:T(8,128)(...) custom-call(f32[3072,512]{1,0:T(8,128)S(1)} %encode_sides.1.refs_0_, ...), custom_call_target="tpu_custom_call" | custom-call | tf_op jit(solution)/shard_map/encode/pallas_call | solution.py:418
  34.9 1.7 %collective-permute-start.7 = (bf16[3,16,512]{2,1,0:T(8,128)(2,1)S(1)}, bf16[3,16,512]{2,1,0:T(8,128)(2,1)S(1)}, u32[]{:S(2)}, u32[]{:S(2)}) collective-permute-start(bf16[3,16,512]{2,1,0:T(8,128)(2,1)S(1)} %get-tuple-element.69), channel_id=1, source_target_pairs={{0,24},{1,25},{2,26},{3,27},{4,28},{5,29},{6,30},{7,31},{8,0},{9,1... | collective-permute-start | bytes 147464 | tf_op jit(solution)/shard_map/ppermute | solution.py:664
  36.6 1.8 %collective-permute-done.6.up_ref = bf16[3,16,512]{2,1,0:T(8,128)(2,1)S(1)} collective-permute-done((bf16[3,16,512]{2,1,0:T(8,128)(2,1)S(1)}, bf16[3,16,512]{2,1,0:T(8,128)(2,1)S(1)}, u32[]{:S(2)}, u32[]{:S(2)}) %collective-permute-start.6) | collective-permute-done | bytes 49184 | tf_op jit(solution)/shard_map/ppermute | solution.py:664
  38.4 4.7 %collective-permute-start.9 = (bf16[3,16,512]{2,1,0:T(8,128)(2,1)S(1)}, bf16[3,16,512]{2,1,0:T(8,128)(2,1)S(1)}, u32[]{:S(2)}, u32[]{:S(2)}) collective-permute-start(bf16[3,16,512]{2,1,0:T(8,128)(2,1)S(1)} %get-tuple-element.73), channel_id=1, source_target_pairs={{0,7},{1,0},{2,1},{3,2},{4,3},{5,4},{6,5},{7,6},{8,15},{9,8},{10,9... | collective-permute-start | bytes 147464 | tf_op jit(solution)/shard_map/ppermute | solution.py:664
  44.0 2.3 %prepare.2 = (bf16[256,512]{1,0:T(8,128)(2,1)S(1)}, f32[192,512]{1,0:T(8,128)S(1)}, bf16[4,512,512]{2,1,0:T(8,128)(2,1)S(1)}) custom-call(bf16[192,512]{1,0:T(8,128)(2,1)S(1)} %get-tuple-element.64.mesh_ref.refs_5_, f32[4,512]{1,0:T(4,128)S(1)} %copy-done.1, f32[4,512]{1,0:T(4,128)S(1)} %copy-done.2, bf16[4,2,512,512]{3,2,1,0:T(8,128)(2,1)} %edge_first.9, ...), custom_call_target="tpu_custom_call" | custom-call | tf_op jit(solution)/shard_map/prepare/pallas_call | solution.py:457
  46.5 4.3 %round_part.2 = (bf16[192,512]{1,0:T(8,128)(2,1)}, bf16[256,512]{1,0:T(8,128)(2,1)}, bf16[256,512]{1,0:T(8,128)(2,1)}) custom-call(s32[1,2,1536]{2,1,0:T(2,128)S(1)} %copy-done.6, bf16[256,512]{1,0:T(8,128)(2,1)S(1)} %get-tuple-element.63.refs_1_, bf16[256,512]{1,0:T(8,128)(2,1)S(1)} %get-tuple-element.65.refs_2_, f32[192,512]{1,0:T(8,128)S(1)} %get-tuple-element.66.refs_3_, ...), custom_call_target="tpu_custom_call" | custom-call | tf_op jit(solution)/shard_map/round_part/pallas_call | solution.py:548
  50.8 4.8 %all-to-all-start = ((bf16[32,8,512]{2,1,0:T(8,128)(2,1)}), bf16[32,8,512]{2,1,0:T(8,128)(2,1)S(1)}, u32[]{:S(2)}, u32[]{:S(2)}) async-start(bf16[32,8,512]{2,1,0:T(8,128)(2,1)} %bitcast), calls=%async_computation | async-start | bytes 524288 | tf_op jit(solution)/shard_map/all_to_all | solution.py:715
  55.6 3.8 %prepare.3 = (bf16[256,512]{1,0:T(8,128)(2,1)}, f32[192,512]{1,0:T(8,128)}, bf16[4,512,512]{2,1,0:T(8,128)(2,1)S(1)}) custom-call(bf16[192,512]{1,0:T(8,128)(2,1)} %get-tuple-element.75.mesh_ref.refs_5_, f32[4,512]{1,0:T(4,128)S(1)} %copy-done.1, f32[4,512]{1,0:T(4,128)S(1)} %copy-done.2, bf16[4,2,512,512]{3,2,1,0:T(8,128)(2,1)} %edge_first.9, ...), custom_call_target="tpu_custom_call" | custom-call | tf_op jit(solution)/shard_map/prepare/pallas_call | solution.py:457
  59.4 6.8 %all-to-all-done = bf16[32,8,512]{2,1,0:T(8,128)(2,1)S(1)} async-done(((bf16[32,8,512]{2,1,0:T(8,128)(2,1)}), bf16[32,8,512]{2,1,0:T(8,128)(2,1)S(1)}, u32[]{:S(2)}, u32[]{:S(2)}) %all-to-all-start) | async-done | bytes 262176 | tf_op jit(solution)/shard_map/all_to_all | solution.py:715
  66.3 5.3 %round_part.3 = (bf16[192,512]{1,0:T(8,128)(2,1)}, bf16[256,512]{1,0:T(8,128)(2,1)S(1)}, bf16[192,512]{1,0:T(8,128)(2,1)}, bf16[3,16,512]{2,1,0:T(8,128)(2,1)S(1...) custom-call(s32[1,2,1536]{2,1,0:T(2,128)S(1)} %copy-done.7, ...), custom_call_target="tpu_custom_call" | custom-call | tf_op jit(solution)/shard_map/round_part/pallas_call | solution.py:548
  71.7 1.7 %collective-permute-start.11 = (bf16[3,16,512]{2,1,0:T(8,128)(2,1)S(1)}, bf16[3,16,512]{2,1,0:T(8,128)(2,1)S(1)}, u32[]{:S(2)}, u32[]{:S(2)}) collective-permute-start(bf16[3,16,512]{2,1,0:T(8,128)(2,1)S(1)} %get-tuple-element.84), channel_id=1, source_target_pairs={{0,24},{1,25},{2,26},{3,27},{4,28},{5,29},{6,30},{7,31},{8,0},{9,1... | collective-permute-start | bytes 147464 | tf_op jit(solution)/shard_map/ppermute | solution.py:664
  73.4 1.8 %collective-permute-done.10.up_ref = bf16[3,16,512]{2,1,0:T(8,128)(2,1)S(1)} collective-permute-done((bf16[3,16,512]{2,1,0:T(8,128)(2,1)S(1)}, bf16[3,16,512]{2,1,0:T(8,128)(2,1)S(1)}, u32[]{:S(2)}, u32[]{:S(2)}) %collective-permute-start.10) | collective-permute-done | bytes 49184 | tf_op jit(solution)/shard_map/ppermute | solution.py:664
  76.2 3.7 %collective-permute-start.13 = (bf16[3,16,512]{2,1,0:T(8,128)(2,1)S(1)}, bf16[3,16,512]{2,1,0:T(8,128)(2,1)S(1)}, u32[]{:S(2)}, u32[]{:S(2)}) collective-permute-start(bf16[3,16,512]{2,1,0:T(8,128)(2,1)S(1)} %get-tuple-element.88), channel_id=1, source_target_pairs={{0,7},{1,0},{2,1},{3,2},{4,3},{5,4},{6,5},{7,6},{8,15},{9,8},{10,9... | collective-permute-start | bytes 147464 | tf_op jit(solution)/shard_map/ppermute | solution.py:664
  80.0 3.4 %decode_local.1 = (bf16[3,1024,512]{2,1,0:T(8,128)(2,1)S(1)}, bf16[4,512,512]{2,1,0:T(8,128)(2,1)S(1)}) custom-call(bf16[1024,512]{1,0:T(8,128)(2,1)S(1)} %copy-done, bf16[256,512]{1,0:T(8,128)(2,1)S(1)} %get-tuple-element.80.table_ref, s32[1,3,1024]{2,1,0:T(4,128)S(1)} %copy.25.edges_ref.refs_3_, f32[4,512]{1,0:T(4,128)S(1)} %copy-done.1, ...), custom_call_target="tpu_custom_call" | custom-call | tf_op jit(solution)/shard_map/decode_local/pallas_call | solution.py:595
  83.5 6.0 %decode_part.1 = bf16[1024,512]{1,0:T(8,128)(2,1)} custom-call(bf16[3,1024,512]{2,1,0:T(8,128)(2,1)S(1)} %get-tuple-element.81.refs_0_, bf16[4,512,512]{2,1,0:T(8,128)(2,1)S(1)} %get-tuple-element.82.refs_1_, bf16[1024,512]{1,0:T(8,128)(2,1)S(1)} %copy-done, s32[1,3,1024]{2,1,0:T(4,128)S(1)} %copy.25.edges_ref.refs_3_, ...), custom_call_target="tpu_custom_call" | custom-call | tf_op jit(solution)/shard_map/decode_part/pallas_call | solution.py:639
  (47 shorter events, 2.3 us)
Async XLA Ops:
  2.4 2.6 %collective-permute-start = (bf16[384,512]{1,0:T(8,128)(2,1)S(1)}, bf16[384,512]{1,0:T(8,128)(2,1)S(1)}, u32[]{:S(2)}, u32[]{:S(2)}) collective-permute-start(bf16[384,512]{1,0:T(8,128)(2,1)S(1)} %get-tuple-element.52), channel_id=1, source_target_pairs={{0,8},{1,9},{2,10},{3,11},{4,12},{5,13},{6,14},{7,15},{8,0},{9,1},... | collective-permute-start | bytes 1179656 | tf_op jit(solution)/shard_map/ppermute | solution.py:664
  5.1 17.7 %collective-permute-start.1 = (bf16[256,512]{1,0:T(8,128)(2,1)S(1)}, bf16[256,512]{1,0:T(8,128)(2,1)S(1)}, u32[]{:S(2)}, u32[]{:S(2)}) collective-permute-start(bf16[256,512]{1,0:T(8,128)(2,1)S(1)} %get-tuple-element.55.after_ref), channel_id=1, source_target_pairs={{0,1},{1,2},{2,3},{3,4},{4,5},{5,6},{6,7},{7,0},{8,9},{9,10},{10,1... | collective-permute-start | bytes 786440 | tf_op jit(solution)/shard_map/ppermute | solution.py:664
  7.7 17.6 %collective-permute-start.2 = (bf16[256,512]{1,0:T(8,128)(2,1)S(1)}, bf16[256,512]{1,0:T(8,128)(2,1)S(1)}, u32[]{:S(2)}, u32[]{:S(2)}) collective-permute-start(bf16[256,512]{1,0:T(8,128)(2,1)S(1)} %get-tuple-element.58), channel_id=1, source_target_pairs={{0,7},{1,0},{2,1},{3,2},{4,3},{5,4},{6,5},{7,6},{8,15},{9,8},{10,9... | collective-permute-start | bytes 786440 | tf_op jit(solution)/shard_map/ppermute | solution.py:664
  10.8 18.3 %collective-permute-start.3 = (bf16[128,512]{1,0:T(8,128)(2,1)S(1)}, bf16[128,512]{1,0:T(8,128)(2,1)S(1)}, u32[]{:S(2)}, u32[]{:S(2)}) collective-permute-start(bf16[128,512]{1,0:T(8,128)(2,1)S(1)} %get-tuple-element.60), channel_id=1, source_target_pairs={{0,25},{1,26},{2,27},{3,28},{4,29},{5,30},{6,31},{7,24},{8,17},{9,... | collective-permute-start | bytes 393224 | tf_op jit(solution)/shard_map/ppermute | solution.py:664
  10.8 18.3 %collective-permute-start.4 = (bf16[128,512]{1,0:T(8,128)(2,1)S(1)}, bf16[128,512]{1,0:T(8,128)(2,1)S(1)}, u32[]{:S(2)}, u32[]{:S(2)}) collective-permute-start(bf16[128,512]{1,0:T(8,128)(2,1)S(1)} %get-tuple-element.61), channel_id=1, source_target_pairs={{0,31},{1,24},{2,25},{3,26},{4,27},{5,28},{6,29},{7,30},{8,23},{9,... | collective-permute-start | bytes 393224 | tf_op jit(solution)/shard_map/ppermute | solution.py:664
  16.1 12.9 %collective-permute-start.5 = (bf16[128,512]{1,0:T(8,128)(2,1)S(1)}, bf16[128,512]{1,0:T(8,128)(2,1)S(1)}, u32[]{:S(2)}, u32[]{:S(2)}) collective-permute-start(bf16[128,512]{1,0:T(8,128)(2,1)S(1)} %get-tuple-element.62), channel_id=1, source_target_pairs={{0,24},{1,25},{2,26},{3,27},{4,28},{5,29},{6,30},{7,31},{8,16},{9,... | collective-permute-start | bytes 393224 | tf_op jit(solution)/shard_map/ppermute | solution.py:664
  25.2 3.8 %copy-start.5 = (s32[1,8,16]{2,1,0:T(8,128)S(1)}, s32[1,8,16]{2,1,0:T(8,128)}, u32[]{:S(2)}) copy-start(s32[1,8,16]{2,1,0:T(8,128)} %refs_9_.4) | copy-start | bytes 1540
  29.1 14.8 %copy-start.9 = (s32[1,32,8]{1,2,0:T(8,128)S(1)}, s32[1,32,8]{1,2,0:T(8,128)}, u32[]{:S(2)}) copy-start(s32[1,32,8]{1,2,0:T(8,128)} %param.23) | copy-start | bytes 3076
  29.1 14.9 %copy-start.1 = (f32[4,512]{1,0:T(4,128)S(1)}, f32[4,512]{1,0:T(4,128)}, u32[]{:S(2)}) copy-start(f32[4,512]{1,0:T(4,128)} %bias_ref.5) | copy-start | bytes 24580
  29.1 14.9 %copy-start.2 = (f32[4,512]{1,0:T(4,128)S(1)}, f32[4,512]{1,0:T(4,128)}, u32[]{:S(2)}) copy-start(f32[4,512]{1,0:T(4,128)} %refs_9_.5) | copy-start | bytes 24580
  34.6 3.7 %collective-permute-start.6 = (bf16[3,16,512]{2,1,0:T(8,128)(2,1)S(1)}, bf16[3,16,512]{2,1,0:T(8,128)(2,1)S(1)}, u32[]{:S(2)}, u32[]{:S(2)}) collective-permute-start(bf16[3,16,512]{2,1,0:T(8,128)(2,1)S(1)} %get-tuple-element.68), channel_id=1, source_target_pairs={{0,8},{1,9},{2,10},{3,11},{4,12},{5,13},{6,14},{7,15},{8,16},{9,17... | collective-permute-start | bytes 147464 | tf_op jit(solution)/shard_map/ppermute | solution.py:664
  34.9 3.5 %collective-permute-start.7 = (bf16[3,16,512]{2,1,0:T(8,128)(2,1)S(1)}, bf16[3,16,512]{2,1,0:T(8,128)(2,1)S(1)}, u32[]{:S(2)}, u32[]{:S(2)}) collective-permute-start(bf16[3,16,512]{2,1,0:T(8,128)(2,1)S(1)} %get-tuple-element.69), channel_id=1, source_target_pairs={{0,24},{1,25},{2,26},{3,27},{4,28},{5,29},{6,30},{7,31},{8,0},{9,1... | collective-permute-start | bytes 147464 | tf_op jit(solution)/shard_map/ppermute | solution.py:664
  38.4 8.0 %collective-permute-start.8 = (bf16[3,16,512]{2,1,0:T(8,128)(2,1)S(1)}, bf16[3,16,512]{2,1,0:T(8,128)(2,1)S(1)}, u32[]{:S(2)}, u32[]{:S(2)}) collective-permute-start(bf16[3,16,512]{2,1,0:T(8,128)(2,1)S(1)} %get-tuple-element.72), channel_id=1, source_target_pairs={{0,1},{1,2},{2,3},{3,4},{4,5},{5,6},{6,7},{7,0},{8,9},{9,10},{10,1... | collective-permute-start | bytes 147464 | tf_op jit(solution)/shard_map/ppermute | solution.py:664
  38.4 8.0 %collective-permute-start.9 = (bf16[3,16,512]{2,1,0:T(8,128)(2,1)S(1)}, bf16[3,16,512]{2,1,0:T(8,128)(2,1)S(1)}, u32[]{:S(2)}, u32[]{:S(2)}) collective-permute-start(bf16[3,16,512]{2,1,0:T(8,128)(2,1)S(1)} %get-tuple-element.73), channel_id=1, source_target_pairs={{0,7},{1,0},{2,1},{3,2},{4,3},{5,4},{6,5},{7,6},{8,15},{9,8},{10,9... | collective-permute-start | bytes 147464 | tf_op jit(solution)/shard_map/ppermute | solution.py:664
  44.0 2.4 %copy-start.3 = (f32[4,512]{1,0:T(4,128)S(1)}, f32[4,512]{1,0:T(4,128)}, u32[]{:S(2)}) copy-start(f32[4,512]{1,0:T(4,128)} %refs_8_.3) | copy-start | bytes 24580
  44.0 2.4 %copy-start.4 = (f32[4,512]{1,0:T(4,128)S(1)}, f32[4,512]{1,0:T(4,128)}, u32[]{:S(2)}) copy-start(f32[4,512]{1,0:T(4,128)} %refs_10_.4) | copy-start | bytes 24580
  50.8 15.5 %all-to-all-start = ((bf16[32,8,512]{2,1,0:T(8,128)(2,1)}), bf16[32,8,512]{2,1,0:T(8,128)(2,1)S(1)}, u32[]{:S(2)}, u32[]{:S(2)}) async-start(bf16[32,8,512]{2,1,0:T(8,128)(2,1)} %bitcast), calls=%async_computation | async-start | bytes 524288 | tf_op jit(solution)/shard_map/all_to_all | solution.py:715
  55.6 10.6 %copy-start.7 = (s32[1,2,1536]{2,1,0:T(2,128)S(1)}, s32[1,2,1536]{2,1,0:T(2,128)}, u32[]{:S(2)}) copy-start(s32[1,2,1536]{2,1,0:T(2,128)} %refs_0_.5) | copy-start | bytes 36868
  59.4 20.6 %copy-start.8 = (s32[1,3,1024]{2,0,1:T(1,128)S(1)}, s32[1,3,1024]{2,0,1:T(1,128)}, u32[]{:S(2)}) copy-start(s32[1,3,1024]{2,0,1:T(1,128)} %param.27) | copy-start | bytes 36868
  59.4 20.6 %copy-start = (bf16[1024,512]{1,0:T(8,128)(2,1)S(1)}, bf16[1024,512]{1,0:T(8,128)(2,1)}, u32[]{:S(2)}) copy-start(bf16[1024,512]{1,0:T(8,128)(2,1)} %refs_2_.3) | copy-start | bytes 3145732
  71.6 3.6 %collective-permute-start.10 = (bf16[3,16,512]{2,1,0:T(8,128)(2,1)S(1)}, bf16[3,16,512]{2,1,0:T(8,128)(2,1)S(1)}, u32[]{:S(2)}, u32[]{:S(2)}) collective-permute-start(bf16[3,16,512]{2,1,0:T(8,128)(2,1)S(1)} %get-tuple-element.83), channel_id=1, source_target_pairs={{0,8},{1,9},{2,10},{3,11},{4,12},{5,13},{6,14},{7,15},{8,16},{9,17... | collective-permute-start | bytes 147464 | tf_op jit(solution)/shard_map/ppermute | solution.py:664
  71.7 3.5 %collective-permute-start.11 = (bf16[3,16,512]{2,1,0:T(8,128)(2,1)S(1)}, bf16[3,16,512]{2,1,0:T(8,128)(2,1)S(1)}, u32[]{:S(2)}, u32[]{:S(2)}) collective-permute-start(bf16[3,16,512]{2,1,0:T(8,128)(2,1)S(1)} %get-tuple-element.84), channel_id=1, source_target_pairs={{0,24},{1,25},{2,26},{3,27},{4,28},{5,29},{6,30},{7,31},{8,0},{9,1... | collective-permute-start | bytes 147464 | tf_op jit(solution)/shard_map/ppermute | solution.py:664
  75.2 8.3 %collective-permute-start.12 = (bf16[3,16,512]{2,1,0:T(8,128)(2,1)S(1)}, bf16[3,16,512]{2,1,0:T(8,128)(2,1)S(1)}, u32[]{:S(2)}, u32[]{:S(2)}) collective-permute-start(bf16[3,16,512]{2,1,0:T(8,128)(2,1)S(1)} %get-tuple-element.87), channel_id=1, source_target_pairs={{0,1},{1,2},{2,3},{3,4},{4,5},{5,6},{6,7},{7,0},{8,9},{9,10},{10,1... | collective-permute-start | bytes 147464 | tf_op jit(solution)/shard_map/ppermute | solution.py:664
  76.2 7.2 %collective-permute-start.13 = (bf16[3,16,512]{2,1,0:T(8,128)(2,1)S(1)}, bf16[3,16,512]{2,1,0:T(8,128)(2,1)S(1)}, u32[]{:S(2)}, u32[]{:S(2)}) collective-permute-start(bf16[3,16,512]{2,1,0:T(8,128)(2,1)S(1)} %get-tuple-element.88), channel_id=1, source_target_pairs={{0,7},{1,0},{2,1},{3,2},{4,3},{5,4},{6,5},{7,6},{8,15},{9,8},{10,9... | collective-permute-start | bytes 147464 | tf_op jit(solution)/shard_map/ppermute | solution.py:664
  (1 other events, 2.4 us)

commit v6 on v5

--- a/solution.py
+++ b/solution.py
@@ -12,7 +12,7 @@
 LANES = 128
 BF16 = jnp.bfloat16
 F32 = jnp.float32
-LIMIT = pltpu.CompilerParams(vmem_limit_bytes=28 * 1024 * 1024)
+LIMIT = pltpu.CompilerParams(vmem_limit_bytes=20 * 1024 * 1024)
 
 UP_LISTS = (7, 5, 6)
 DOWN_LISTS = (2, 0, 1)
@@ -55,9 +55,9 @@
     return half + half * jnp.tanh(half)
 
 
-def centre(ref, index):
-    weight = ref[index].astype(F32)
-    ref[index] = (weight - jnp.mean(weight, axis=-1, keepdims=True)).astype(BF16)
+def centred(weight):
+    weight = weight.astype(F32)
+    return (weight - jnp.mean(weight, axis=-1, keepdims=True)).astype(BF16)
 
 
 def normed(value):
@@ -210,9 +210,27 @@
     )(stay(rows), stay(rim))
 
 
+def pick_outer_kernel(rows_ref, rim_ref, after_ref, *outs):
+    outer = 5 - side_base()
+    for out, offset in zip(outs, (2, 0, 1)):
+        ids = column(rim_ref[0, pl.ds(outer + offset, 1), :])
+        out[...] = dot(one_hot(ids, rows_ref.shape[0]), rows_ref[...]).astype(BF16)
+
+
+def pick_outer(rows, rim, after):
+    vmem = pl.BlockSpec(memory_space=pltpu.VMEM)
+    return pl.pallas_call(
+        pick_outer_kernel,
+        in_specs=[vmem, vmem, pl.BlockSpec(memory_space=pl.ANY)],
+        out_shape=[pltpu.VMEM((rim.shape[2], rows.shape[1]), BF16)] * 3,
+        compiler_params=LIMIT,
+        name="pick_outer",
+    )(near(rows), near(rim), after)
+
+
 def pick_rest_kernel(section, rows_ref, rim_ref, edge_first, node_first, mesh_hbm, edges_hbm, *refs):
     vectors, refs = refs[:4], refs[4:]
-    outs, (stack, mesh, edges, rows_of, arrived, mesh_here, edges_here, vectors_here) = refs[:5], refs[5:]
+    outs, (stack, mesh, edges, rows_of, arrived, mesh_here, edges_here, vectors_here) = refs[:2], refs[2:]
     copies = fetch(
         [edge_first.at[section, 1], edge_first.at[section, 0], node_first.at[section, 0]], stack, arrived
     )
@@ -226,8 +244,7 @@
         )
     for copy in copies[3:]:
         copy.start()
-    outer = 5 - side_base()
-    for out, chosen in zip(outs, (RIGHT_LIST, LEFT_LIST, outer + 2, outer, outer + 1)):
+    for out, chosen in zip(outs, (RIGHT_LIST, LEFT_LIST)):
         ids = column(rim_ref[0, pl.ds(chosen, 1), :])
         out[...] = dot(one_hot(ids, rows_ref.shape[0]), rows_ref[...]).astype(BF16)
     for copy in copies:
@@ -240,7 +257,7 @@
     return pl.pallas_call(
         functools.partial(pick_rest_kernel, section),
         in_specs=[vmem] * 2 + [HBM] * 8,
-        out_shape=[pltpu.VMEM((rim.shape[2], width), BF16)] * 5
+        out_shape=[pltpu.VMEM((rim.shape[2], width), BF16)] * 2
         + [
             matrices(3, width),
             pltpu.VMEM(mesh_rows.shape, BF16),
@@ -277,16 +294,18 @@
 def grid_halo(rows, rim, mesh_rows, edges, weights, section):
     pair, rows, rim = pick_pair(rows, rim)
     pair = move(pair, lambda i, j: (i ^ 1, j))
-    right, left, *rest = pick_rest(rows, rim, mesh_rows, edges, weights, section)
-    outer, kept = rest[:3], rest[3:]
+    right, left, *kept = pick_rest(rows, rim, mesh_rows, edges, weights, section)
     right, left = pair_join(pair, right, left)
+    outer = pick_outer(rows, rim, right)
+    bands = lax.axis_size("aa")
     other = lambda i: i + 1 if i % 2 else i - 1
+    inside = lambda i: 0 <= other(i) < bands
     remote = [
         pair,
         move(right, lambda i, j: (i, j + 1)),
         move(left, lambda i, j: (i, j - 1)),
-        move(outer[0], lambda i, j: (other(i), j + 1)),
-        move(outer[1], lambda i, j: (other(i), j - 1)),
+        move(outer[0], lambda i, j: (other(i), j + 1) if inside(i) else None),
+        move(outer[1], lambda i, j: (other(i), j - 1) if inside(i) else None),
         move(outer[2], lambda i, j: (other(i), j)),
     ]
     return remote, right, rows, kept
@@ -318,8 +337,8 @@
         )
     for copy in copies:
         copy.wait()
-    centre(later, 1)
-    centre(later, 3)
+    later[1] = centred(later[1])
+    later[3] = centred(later[3])
 
 
 def encode_local(grid_rows, kept, after, weights, section):
@@ -349,58 +368,34 @@
     )
 
 
-def halo_part(pre, edges_ref, part, table, base):
-    senders = edges_ref[0, 0:1, part] - base
-    return pre + dot(one_hot(column(senders), table.shape[0]), table[...])
-
-
-def encode_sides_kernel(count, pre_ref, edges_ref, stack, pair_ref, right_ref, left_ref, pre_out, table):
-    depth = right_ref.shape[0] // 2
+def encode_kernel(count, *refs):
+    pre_ref, edges_ref, stack, inner_ref, mesh_ref = refs[:5]
+    pair_ref, right_ref, left_ref, outer_right, outer_left, outer_ref = refs[5:11]
+    vectors, lists_ref = refs[11:13]
+    mesh_out, proj_out, up, down, right, left, table = refs[13:]
+    slots = mesh_ref.shape[0]
+    depth = outer_ref.shape[0]
     pair = side_base()
-    first = jnp.where(pair == 0, 0, 3)
+    outer = 5 - pair
     for ref, start, direction in (
         (pair_ref, 2 * depth, pair + 1),
         (right_ref, 0, 3),
         (right_ref, depth, pair),
         (left_ref, 0, 4),
         (left_ref, depth, pair + 2),
+        (outer_right, 0, outer),
+        (outer_left, 0, outer + 2),
+        (outer_ref, 0, outer + 1),
     ):
-        place = pl.multiple_of((direction - first) * depth, LANES)
+        place = pl.multiple_of(direction * depth, LANES)
         table[pl.ds(place, depth)] = dot(ref[start : start + depth], stack[0]).astype(BF16)
-    edges = pre_ref.shape[0]
-    block = math_block(edges, 1024)
-    for start in range(0, edges, block):
-        part = slice(start, start + block)
-        pre_out[part] = halo_part(pre_ref[part], edges_ref, part, table, count + first * depth)
-
-
-def encode_sides(pre, edges, stack, remote, count):
-    depth, width = remote[1].shape[0] // 2, pre.shape[1]
-    return pl.pallas_call(
-        functools.partial(encode_sides_kernel, count),
-        out_shape=pltpu.VMEM(pre.shape, F32),
-        scratch_shapes=[pltpu.VMEM((5 * depth, width), BF16)],
-        input_output_aliases={0: 0},
-        compiler_params=LIMIT,
-        name="encode_sides",
-    )(near(pre), near(edges), near(stack), *remote)
-
-
-def encode_kernel(count, *refs):
-    pre_ref, edges_ref, stack, inner_ref, mesh_ref, outer_right, outer_left, outer_ref = refs[:8]
-    vectors, lists_ref = refs[8:10]
-    mesh_out, proj_out, up, down, right, left, table = refs[10:]
-    slots = mesh_ref.shape[0]
-    depth = outer_ref.shape[0]
-    for index, ref in enumerate((outer_right, outer_ref, outer_left)):
-        table[index * depth : (index + 1) * depth] = dot(ref[...], stack[0]).astype(BF16)
-    base = count + (5 - side_base()) * depth
     edges = pre_ref.shape[0]
     block = math_block(edges, 1024)
     summed = None
     for start in range(0, edges, block):
         part = slice(start, start + block)
-        pre = halo_part(pre_ref[part], edges_ref, part, table, base)
+        senders = column(edges_ref[0, 0:1, part] - count)
+        pre = pre_ref[part] + dot(one_hot(senders, table.shape[0]), table[...])
         made = added(pre, edges_ref[0, 1:2, part], stack[1], slots)
         summed = made if summed is None else summed + made
     summed = summed * row_of(vectors, 2)
@@ -414,7 +409,6 @@
     pre, inner, stack = [near(value) for value in prepared]
     mesh_rows, edges, vectors = [near(value) for value in kept[1:]]
     slots, width = mesh_rows.shape
-    pre = near(encode_sides(pre, edges, stack, remote[:3], count))
     return pl.pallas_call(
         functools.partial(encode_kernel, count),
         out_shape=[
@@ -422,10 +416,10 @@
             pltpu.VMEM((round_up(slots, LANES), width), BF16),
         ]
         + send_shapes(depth, width),
-        scratch_shapes=[pltpu.VMEM((3 * remote[-1].shape[0], width), BF16)],
+        scratch_shapes=[pltpu.VMEM((8 * remote[-1].shape[0], width), BF16)],
         compiler_params=LIMIT,
         name="encode",
-    )(pre, edges, stack, inner, mesh_rows, *remote[3:], vectors, lists)
+    )(pre, edges, stack, inner, mesh_rows, *remote, vectors, lists)
 
 
 def prepare_kernel(
@@ -435,7 +429,7 @@
     copies = fetch([edge_first.at[section, 1], node_first.at[section, 0]], own, arrived)
     copies += fetch(
         [
-            edge_second.at[section], node_first.at[section, 1], node_second.at[section],
+            edge_second.at[section], node_second.at[section], node_first.at[section, 1],
             edge_first.at[section + 1, 0],
         ],
         later, later_arrived,
@@ -447,8 +441,8 @@
     inner_out[...] = dot(rows, own[1]) + row_of(node_bias_ref, section)
     for copy in copies[2:]:
         copy.wait()
-    centre(later, 0)
-    centre(later, 2)
+    later[0] = centred(later[0])
+    later[1] = centred(later[1])
 
 
 def prepare(mesh_rows, weights, section):
@@ -469,6 +463,55 @@
         held(mesh_rows, section), weights["edge_bias"], weights["node_bias"],
         weights["edge_first"], weights["edge_second"], weights["node_first"], weights["node_second"],
     )
+
+
+def receivers_kernel(section, mesh_ref, bias_ref, node_bias_ref, edge_first, node_first, target_out, inner_out, own, arrived):
+    copies = fetch([edge_first.at[section, 1], node_first.at[section, 0]], own, arrived)
+    rows = mesh_ref[...]
+    copies[0].wait()
+    fill(target_out, (dot(rows, own[0]) + row_of(bias_ref, section)).astype(BF16))
+    copies[1].wait()
+    inner_out[...] = dot(rows, own[1]) + row_of(node_bias_ref, section)
+
+
+def receivers(mesh_rows, weights, section):
+    slots, width = mesh_rows.shape
+    vmem = pl.BlockSpec(memory_space=pltpu.VMEM)
+    return pl.pallas_call(
+        functools.partial(receivers_kernel, section),
+        in_specs=[vmem] * 3 + [HBM] * 2,
+        out_shape=[pltpu.VMEM((round_up(slots, LANES), width), BF16), pltpu.VMEM((slots, width), F32)],
+        scratch_shapes=fetch_scratch(2, width),
+        compiler_params=LIMIT,
+        name="receivers",
+    )(near(mesh_rows), weights["edge_bias"], weights["node_bias"], weights["edge_first"], weights["node_first"])
+
+
+def layers_kernel(section, after_ref, edge_first, edge_second, node_first, node_second, later, arrived):
+    copies = fetch(
+        [
+            edge_second.at[section], node_second.at[section], node_first.at[section, 1],
+            edge_first.at[section + 1, 0],
+        ],
+        later, arrived,
+    )
+    for index in (0, 1):
+        copies[index].wait()
+        later[index] = centred(later[index])
+    for copy in copies[2:]:
+        copy.wait()
+
+
+def layers(after, weights, section):
+    width = after.shape[-1]
+    return pl.pallas_call(
+        functools.partial(layers_kernel, section),
+        in_specs=[pl.BlockSpec(memory_space=pl.ANY)] + [HBM] * 4,
+        out_shape=matrices(4, width),
+        scratch_shapes=[pltpu.SemaphoreType.DMA((4,))],
+        compiler_params=LIMIT,
+        name="layers",
+    )(after, weights["edge_first"], weights["edge_second"], weights["node_first"], weights["node_second"])
 
 
 def place_remote(table, remote, places, base):
@@ -503,8 +546,6 @@
         table[:padded] = local_ref[...]
     mesh_out, proj_out = rest[:2]
     sends = rest[2:]
-    if last:
-        masked_out, sends = sends[0], sends[1:]
     place_remote(table, remote, places, padded)
     if last:
         for copy in copies:
@@ -522,11 +563,12 @@
         part = added(pre, targets, stack[0], slots)
         summed = part if summed is None else summed + part
     summed = summed * row_of(gain_ref, section)
-    fresh = updated(mesh_ref[...], summed, inner_ref[...], stack[1], stack[2], row_of(node_gain_ref, section))
-    mesh_out[...] = fresh
+    fresh = updated(mesh_ref[...], summed, inner_ref[...], stack[2], stack[1], row_of(node_gain_ref, section))
     if last:
         alive = lax.broadcasted_iota(jnp.int32, fresh.shape, 0) < owned_ref[0]
-        masked_out[...] = jnp.where(alive, fresh, jnp.zeros_like(fresh))
+        mesh_out[...] = jnp.where(alive, fresh, jnp.zeros_like(fresh))
+    else:
+        mesh_out[...] = fresh
     fill(proj_out, dot(fresh, stack[3]).astype(BF16))
     list_rows(proj_out, lists_ref, sends)
 
@@ -537,9 +579,10 @@
     padded = local.shape[0]
     table_rows = padded + sum(r.shape[0] * r.shape[1] for r in remote)
     space = place_of(section + 1)
-    out_shape = [space((slots, width), BF16), space((padded, width), BF16)]
-    if last:
-        out_shape.append(jax.ShapeDtypeStruct((slots, width), BF16))
+    out_shape = [
+        jax.ShapeDtypeStruct((slots, width), BF16) if last else space((slots, width), BF16),
+        space((padded, width), BF16),
+    ]
     scratch = [pltpu.VMEM((table_rows, width), BF16)]
     if last:
         scratch += [pltpu.VMEM(value.shape, value.dtype) for value in (*prepared[:2], mesh_rows)]
@@ -561,54 +604,66 @@
     )
 
 
+def grid_receivers_kernel(section, grid_ref, bias_ref, edge_first, edge_second, target_out, later, own, arrived, later_arrived):
+    copies = fetch([edge_first.at[section, 1]], own, arrived)
+    copies += fetch([edge_second.at[section]], later, later_arrived)
+    copies[0].wait()
+    target_out[...] = (dot(grid_ref[...], own[0]) + row_of(bias_ref, section)).astype(BF16)
+    copies[1].wait()
+    later[0] = centred(later[0])
+
+
+def grid_receivers(grid_rows, weights, section):
+    vmem = pl.BlockSpec(memory_space=pltpu.VMEM)
+    width = grid_rows.shape[1]
+    return pl.pallas_call(
+        functools.partial(grid_receivers_kernel, section),
+        in_specs=[vmem] * 2 + [HBM] * 2,
+        out_shape=[pltpu.VMEM(grid_rows.shape, BF16), matrices(1, width)],
+        scratch_shapes=fetch_scratch(1, width) + [pltpu.SemaphoreType.DMA((1,))],
+        compiler_params=LIMIT,
+        name="grid_receivers",
+    )(grid_rows, weights["edge_bias"], weights["edge_first"], weights["edge_second"])
+
+
 def decode_local_kernel(
-    section, grid_ref, table_ref, edges_ref, bias_ref, edge_first, edge_second, node_first, node_second,
-    pre_ref, later, own, arrived, later_arrived,
+    section, target_ref, table_ref, edges_ref, after_ref, node_first, node_second, pre_ref, later, arrived
 ):
-    copies = fetch([edge_first.at[section, 1]], own, arrived)
-    copies += fetch(
-        [
-            edge_second.at[section], node_first.at[section, 0], node_first.at[section, 1],
-            node_second.at[section],
-        ],
-        later, later_arrived,
-    )
-    copies[0].wait()
-    count = grid_ref.shape[0]
+    copies = fetch(
+        [node_second.at[section], node_first.at[section, 0], node_first.at[section, 1]], later, arrived
+    )
+    count = target_ref.shape[0]
     block = math_block(count, 512)
     for start in range(0, count, block):
-        target = dot(grid_ref[start : start + block], own[0]) + row_of(bias_ref, section)
+        target = target_ref[start : start + block].astype(F32)
         for sender in range(edges_ref.shape[1]):
             ids = column(edges_ref[0, sender : sender + 1, start : start + block])
             pre = dot(one_hot(ids, table_ref.shape[0]), table_ref[...]) + target
             pre_ref[sender, start : start + block] = pre.astype(BF16)
+    copies[0].wait()
+    later[0] = centred(later[0])
     for copy in copies[1:]:
         copy.wait()
-    centre(later, 0)
-    centre(later, 3)
-
-
-def decode_local(grid_rows, table, edges, weights, section):
-    count, width = grid_rows.shape
+
+
+def decode_local(target, table, edges, after, weights, section):
+    count, width = target.shape
     senders = edges.shape[1]
     vmem = pl.BlockSpec(memory_space=pltpu.VMEM)
     return pl.pallas_call(
         functools.partial(decode_local_kernel, section),
-        in_specs=[vmem] * 4 + [HBM] * 4,
-        out_shape=[pltpu.VMEM((senders, count, width), BF16), matrices(4, width)],
-        scratch_shapes=fetch_scratch(1, width) + [pltpu.SemaphoreType.DMA((4,))],
+        in_specs=[vmem] * 3 + [pl.BlockSpec(memory_space=pl.ANY), HBM, HBM],
+        out_shape=[pltpu.VMEM((senders, count, width), BF16), matrices(3, width)],
+        scratch_shapes=[pltpu.SemaphoreType.DMA((3,))],
         compiler_params=LIMIT,
         name="decode_local",
-    )(
-        grid_rows, near(table), edges, weights["edge_bias"],
-        weights["edge_first"], weights["edge_second"], weights["node_first"], weights["node_second"],
-    )
+    )(near(target), near(table), edges, after, weights["node_first"], weights["node_second"])
 
 
 def decode_kernel(section, places, split, *refs):
-    pre_ref, stack, grid_ref, edges_ref = refs[:4]
-    remote = refs[4 : 4 + len(places)]
-    gain_ref, node_bias_ref, node_gain_ref, out_ref, table, ready, sent = refs[4 + len(places) :]
+    pre_ref, second, layers, grid_ref, edges_ref = refs[:5]
+    remote = refs[5 : 5 + len(places)]
+    gain_ref, node_bias_ref, node_gain_ref, out_ref, table, ready, sent = refs[5 + len(places) :]
     place_remote(table, remote, places, 0)
     count = grid_ref.shape[0]
     block = math_block(count, 512)
@@ -619,12 +674,12 @@
         for sender in range(edges_ref.shape[1]):
             ids = column(edges_ref[0, sender : sender + 1, part])
             pre = pre_ref[sender, part].astype(F32) + dot(one_hot(ids, table.shape[0], split), table[...])
-            message = normed(dot(silu(pre), stack[0])).astype(BF16).astype(F32)
+            message = normed(dot(silu(pre), second[0])).astype(BF16).astype(F32)
             summed = message if summed is None else summed + message
         rows = grid_ref[part]
         summed = (summed * row_of(gain_ref, section)).astype(BF16)
-        inner = dot(rows, stack[1]) + dot(summed, stack[2]) + row_of(node_bias_ref, section)
-        update = normed(dot(silu(inner), stack[3])) * row_of(node_gain_ref, section)
+        inner = dot(rows, layers[1]) + dot(summed, layers[2]) + row_of(node_bias_ref, section)
+        update = normed(dot(silu(inner), layers[0])) * row_of(node_gain_ref, section)
         ready[part] = (rows.astype(F32) + update).astype(BF16)
         copies.append(pltpu.make_async_copy(ready.at[part], out_ref.at[part], sent.at[index]))
         copies[-1].start()
@@ -638,7 +693,7 @@
     vmem = pl.BlockSpec(memory_space=pltpu.VMEM)
     return pl.pallas_call(
         functools.partial(decode_kernel, section, places, split),
-        in_specs=[vmem] * (7 + len(remote)),
+        in_specs=[vmem] * (8 + len(remote)),
         out_specs=pl.BlockSpec(memory_space=pl.ANY),
         out_shape=jax.ShapeDtypeStruct((count, width), BF16),
         scratch_shapes=[
@@ -659,28 +714,36 @@
     pairs = []
     for i in range(bands):
         for j in range(sectors):
-            band, sector = target(i, j)
+            place = target(i, j)
+            if place is None:
+                continue
+            band, sector = place
             pairs.append((i * sectors + j, band % bands * sectors + sector % sectors))
     return lax.ppermute(value, AXES, pairs)
 
 
-def join_kernel(up_ref, down_ref, right_ref, left_ref, right_out, left_out):
+def join_kernel(up_ref, down_ref, right_ref, left_ref, after_ref, right_out, left_out):
     for index, (own, out) in enumerate(((right_ref, right_out), (left_ref, left_out))):
         out[0] = own[0]
         out[1] = up_ref[index]
         out[2] = down_ref[index]
 
 
-def halo(up, down, right, left):
+def halo(up, down, right, left, after):
     from_up = move(up, lambda i, j: (i + 1, j))
     from_down = move(down, lambda i, j: (i - 1, j))
     joined = jax.ShapeDtypeStruct((3,) + right.shape[1:], BF16)
     right, left = pl.pallas_call(
-        join_kernel, out_shape=[joined, joined], compiler_params=LIMIT, name="join"
-    )(from_up, from_down, right, left)
+        join_kernel,
+        in_specs=[pl.BlockSpec(memory_space=pltpu.VMEM)] * 4 + [pl.BlockSpec(memory_space=pl.ANY)],
+        out_shape=[joined, joined],
+        compiler_params=LIMIT,
+        name="join",
+    )(from_up, from_down, right, left, after)
     from_left = move(right, lambda i, j: (i, j + 1))
     from_right = move(left, lambda i, j: (i, j - 1))
-    return [from_up[2:3], from_down[2:3], from_left, from_right], ((1,), (6,), (3, 0, 5), (4, 2, 7))
+    blocks = [from_up[2:3], from_down[2:3], from_left, from_right]
+    return blocks, ((1,), (6,), (3, 0, 5), (4, 2, 7)), right
 
 
 def per_device(
@@ -704,8 +767,9 @@
     prepared = encode_local(tile, kept, joined, weights, 0)
     mesh_one, proj, *sends = encode(prepared, kept, remote, mesh_rim, depth, grid_nodes.shape[0])
 
-    remote, places = halo(*sends)
-    prepared = prepare(mesh_one, weights, 1)
+    target, inner = receivers(mesh_one, weights, 1)
+    remote, places, joined = halo(*sends, target)
+    prepared = target, inner, layers(joined, weights, 1)
     mesh_two, proj, sent = round_part(
         short_edges, proj, prepared, mesh_one, remote, places, long_lists, owned_nodes,
         [jax.ShapeDtypeStruct((peers * listed, width), BF16)], weights, 1,
@@ -714,14 +778,17 @@
     sent = sent.reshape(peers, listed, width)
     arrived = lax.all_to_all(sent, AXES, split_axis=0, concat_axis=0, tiled=True)
     prepared = prepare(mesh_two, weights, 2)
-    mesh_three, proj, mesh_out, *sends = round_part(
+    mesh_out, proj, *sends = round_part(
         long_edges, proj, prepared, mesh_two, [arrived.reshape(1, peers * listed, width)], ((0,),),
         mesh_rim, owned_nodes, rim_sends, weights, 2,
     )
 
-    remote, places = halo(*sends)
-    prepared = decode_local(grid_nodes, proj, m2g_edges, weights, 3)
-    grid_out = decode_part(prepared, grid_nodes, m2g_edges, remote, places, weights, 3, slots)
+    target, second = grid_receivers(grid_nodes, weights, 3)
+    remote, places, joined = halo(*sends, target)
+    pre, stack = decode_local(target, proj, m2g_edges, joined, weights, 3)
+    grid_out = decode_part(
+        (pre, second, stack), grid_nodes, m2g_edges, remote, places, weights, 3, slots
+    )
     return grid_out, mesh_out
 
 

time: 89.9 us -> 87.5 us (0.973)
  waiting for transfers between devices: 12.8 us -> 11.4 us
    pallas_call x2 -> x1, Pallas kernels: 6.11 us -> 3.77 us  [prepare(): pl.pallas_call(functools.partial(prepare_kernel, section), in_specs=[vmem...]
    pallas_call x1, Pallas kernels: 5.52 us -> 7.58 us  [encode(): pl.pallas_call(functools.partial(encode_kernel, count), out_shape=[pltpu....]
    pallas_call x3 -> x6, Pallas kernels: 3.79 us -> 5.76 us  [the longest x1 1.94 us: grid_receivers(): pl.pallas_call(functools.partial(grid_receivers_kernel, section), in_spec...]
    ppermute x14, starting transfers between devices: 26.2 us -> 24.3 us  [move(): return lax.ppermute(value, AXES, pairs)]
    pallas_call x1, Pallas kernels: 3.44 us -> 1.89 us  [decode_local(): pl.pallas_call(functools.partial(decode_local_kernel, section), in_specs=...]
    ppermute x14, waiting for transfers between devices: 5.98 us -> 4.58 us  [move(): return lax.ppermute(value, AXES, pairs)]
    all_to_all x1, starting transfers between devices: 4.81 us -> 5.93 us  [per_device(): lax.all_to_all(sent, AXES, split_axis=0, concat_axis=0, tiled=True)]
  transfers between devices with their start and end apart: 15 -> 15, of which waited for: 4 -> 5; matrix products, arithmetic and copies ran while one was open for 0% -> 0% of each run, Pallas kernels for 23% -> 21%
where the time goes in v6:
time: 87.5 us; the launch traced here: 87.1 us
  Pallas kernels  43.4 us (50%)
  starting transfers between devices  30.2 us (35%)
  waiting for transfers between devices  11.4 us (13%)
  between operations  1.81 us (2%)
    ppermute x14, starting transfers between devices, move(): return lax.ppermute(value, AXES, pairs)  24.3 us
    pallas_call x2, Pallas kernels, round_part(): pl.pallas_call(functools.partial(round_kernel, section, places, last), in...  9.65 us
    pallas_call x1, Pallas kernels, encode(): pl.pallas_call(functools.partial(encode_kernel, count), out_shape=[pltpu....  7.58 us
    all_to_all x1, waiting for transfers between devices, per_device(): lax.all_to_all(sent, AXES, split_axis=0, concat_axis=0, tiled=True)  6.85 us
    all_to_all x1, starting transfers between devices, per_device(): lax.all_to_all(sent, AXES, split_axis=0, concat_axis=0, tiled=True)  5.93 us
    pallas_call x1, Pallas kernels, decode_part(): pl.pallas_call(functools.partial(decode_kernel, section, places, split),...  5.93 us
    pallas_call x1, Pallas kernels, encode_local(): pl.pallas_call(functools.partial(encode_local_kernel, section), in_specs=...  5.36 us
    ppermute x14, waiting for transfers between devices, move(): return lax.ppermute(value, AXES, pairs)  4.58 us
  transfers between devices with their start and end apart: 15, of which 5 were waited for; matrix products, arithmetic and copies ran while one was open for 0% of the time, Pallas kernels for 21%

profile of v6, /device:TPU:0, one launch (start us, length us, event | category | flops | bytes accessed | tf_op | source)
XLA Modules:
  0.0 87.1 jit_solution(13951756298468539434)
XLA Ops:
  0.6 1.8 %pick_pair.1 = (bf16[384,512]{1,0:T(8,128)(2,1)S(1)}, bf16[1024,512]{1,0:T(8,128)(2,1)S(1)}, s32[1,8,128]{2,1,0:T(8,128)S(1)}) custom-call(bf16[1024,512]{1,0:T(8,128)(2,1)} %refs_3_.3, s32[1,8,128]{2,1,0:T(8,128)} %rim_hbm.1), custom_call_target="tpu_custom_call" | custom-call | tf_op jit(solution)/shard_map/pick_pair/pallas_call | solution.py:199
  3.0 1.6 %pick_rest.1 = (bf16[128,512]{1,0:T(8,128)(2,1)S(1)}, bf16[128,512]{1,0:T(8,128)(2,1)S(1)}, bf16[3,512,512]{2,1,0:T(8,128)(2,1)S(1)}, bf16[192,512]{1,0:T(8,128)...) custom-call(bf16[1024,512]{1,0:T(8,128)(2,1)S(1)} %get-tuple-element.48.rows_ref.grid_ref, ...), custom_call_target="tpu_custom_call" | custom-call | tf_op jit(solution)/shard_map/pick_rest/pallas_call | solution.py:257
  4.7 2.6 %collective-permute-start.1 = (bf16[256,512]{1,0:T(8,128)(2,1)S(1)}, bf16[256,512]{1,0:T(8,128)(2,1)S(1)}, u32[]{:S(2)}, u32[]{:S(2)}) collective-permute-start(bf16[256,512]{1,0:T(8,128)(2,1)S(1)} %get-tuple-element.57.after_ref), channel_id=1, source_target_pairs={{0,1},{1,2},{2,3},{3,4},{4,5},{5,6},{6,7},{7,0},{8,9},{9,10},{10,1... | collective-permute-start | bytes 786440 | tf_op jit(solution)/shard_map/ppermute | solution.py:722
  7.3 3.1 %collective-permute-start.2 = (bf16[256,512]{1,0:T(8,128)(2,1)S(1)}, bf16[256,512]{1,0:T(8,128)(2,1)S(1)}, u32[]{:S(2)}, u32[]{:S(2)}) collective-permute-start(bf16[256,512]{1,0:T(8,128)(2,1)S(1)} %get-tuple-element.61), channel_id=1, source_target_pairs={{0,7},{1,0},{2,1},{3,2},{4,3},{5,4},{6,5},{7,6},{8,15},{9,8},{10,9... | collective-permute-start | bytes 786440 | tf_op jit(solution)/shard_map/ppermute | solution.py:722
  12.4 1.4 %collective-permute-start.5 = (bf16[128,512]{1,0:T(8,128)(2,1)S(1)}, bf16[128,512]{1,0:T(8,128)(2,1)S(1)}, u32[]{:S(2)}, u32[]{:S(2)}) collective-permute-start(bf16[128,512]{1,0:T(8,128)(2,1)S(1)} %get-tuple-element.64), channel_id=1, source_target_pairs={{0,24},{1,25},{2,26},{3,27},{4,28},{5,29},{6,30},{7,31},{8,16},{9,... | collective-permute-start | bytes 393224 | tf_op jit(solution)/shard_map/ppermute | solution.py:722
  13.7 5.4 %encode_local.1 = (f32[3072,512]{1,0:T(8,128)S(1)}, f32[192,512]{1,0:T(8,128)S(1)}, bf16[5,512,512]{2,1,0:T(8,128)(2,1)S(1)}) custom-call(bf16[1024,512]{1,0:T(8,128)(2,1)S(1)} %get-tuple-element.48.rows_ref.grid_ref, bf16[3,512,512]{2,1,0:T(8,128)(2,1)S(1)} %get-tuple-element.50.stack, bf16[192,512]{1,0:T(8,128)(2,1)S(1)} %get-tuple-element.51.mesh_ref.refs_4_, ...), custom_call_target="tpu_custom_call" | custom-call | tf_op jit(solution)/shard_map/encode_local/pallas_call | solution.py:350
  19.1 1.8 %collective-permute-done.1.refs_6_ = bf16[256,512]{1,0:T(8,128)(2,1)S(1)} collective-permute-done((bf16[256,512]{1,0:T(8,128)(2,1)S(1)}, bf16[256,512]{1,0:T(8,128)(2,1)S(1)}, u32[]{:S(2)}, u32[]{:S(2)}) %collective-permute-start.1) | collective-permute-done | bytes 262176 | tf_op jit(solution)/shard_map/ppermute | solution.py:722
  20.9 2.5 %collective-permute-done.2.refs_7_ = bf16[256,512]{1,0:T(8,128)(2,1)S(1)} collective-permute-done((bf16[256,512]{1,0:T(8,128)(2,1)S(1)}, bf16[256,512]{1,0:T(8,128)(2,1)S(1)}, u32[]{:S(2)}, u32[]{:S(2)}) %collective-permute-start.2) | collective-permute-done | bytes 262176 | tf_op jit(solution)/shard_map/ppermute | solution.py:722
  23.4 7.6 %encode.1 = (bf16[192,512]{1,0:T(8,128)(2,1)S(1)}, bf16[256,512]{1,0:T(8,128)(2,1)S(1)}, bf16[3,16,512]{2,1,0:T(8,128)(2,1)S(1)}, bf16[3,16,512]{2,1,0:T(8,128)(...) custom-call(f32[3072,512]{1,0:T(8,128)S(1)} %get-tuple-element.58.refs_0_, ...), custom_call_target="tpu_custom_call" | custom-call | tf_op jit(solution)/shard_map/encode/pallas_call | solution.py:412
  31.0 4.1 %collective-permute-start.6 = (bf16[3,16,512]{2,1,0:T(8,128)(2,1)S(1)}, bf16[3,16,512]{2,1,0:T(8,128)(2,1)S(1)}, u32[]{:S(2)}, u32[]{:S(2)}) collective-permute-start(bf16[3,16,512]{2,1,0:T(8,128)(2,1)S(1)} %get-tuple-element.69), channel_id=1, source_target_pairs={{0,8},{1,9},{2,10},{3,11},{4,12},{5,13},{6,14},{7,15},{8,16},{9,17... | collective-permute-start | bytes 147464 | tf_op jit(solution)/shard_map/ppermute | solution.py:722
  35.1 1.6 %receivers.1 = (bf16[256,512]{1,0:T(8,128)(2,1)S(1)}, f32[192,512]{1,0:T(8,128)S(1)}) custom-call(bf16[192,512]{1,0:T(8,128)(2,1)S(1)} %get-tuple-element.66.mesh_ref.refs_5_, f32[4,512]{1,0:T(4,128)S(1)} %copy-done.3, f32[4,512]{1,0:T(4,128)S(1)} %copy-done.4, bf16[4,2,512,512]{3,2,1,0:T(8,128)(2,1)} %edge_first.11, bf16[4,2,512,512]{3,2,1,0:T(8,128)(2,1)} %node_first.11), custom_call_target="tpu_custom_call" | custom-call | tf_op jit(solution)/shard_map/receivers/pallas_call | solution.py:480
  36.9 4.7 %collective-permute-start.9 = (bf16[3,16,512]{2,1,0:T(8,128)(2,1)S(1)}, bf16[3,16,512]{2,1,0:T(8,128)(2,1)S(1)}, u32[]{:S(2)}, u32[]{:S(2)}) collective-permute-start(bf16[3,16,512]{2,1,0:T(8,128)(2,1)S(1)} %get-tuple-element.74), channel_id=1, source_target_pairs={{0,7},{1,0},{2,1},{3,2},{4,3},{5,4},{6,5},{7,6},{8,15},{9,8},{10,9... | collective-permute-start | bytes 147464 | tf_op jit(solution)/shard_map/ppermute | solution.py:722
  42.5 1.6 %layers.1.refs_4_ = bf16[4,512,512]{2,1,0:T(8,128)(2,1)S(1)} custom-call(bf16[3,16,512]{2,1,0:T(8,128)(2,1)S(1)} %get-tuple-element.73.after_ref, bf16[4,2,512,512]{3,2,1,0:T(8,128)(2,1)} %edge_first.11, bf16[4,512,512]{2,1,0:T(8,128)(2,1)} %edge_second.7, bf16[4,2,512,512]{3,2,1,0:T(8,128)(2,1)} %node_first.11, bf16[4,512,512]{2,1,0:T(8,128)(2,1)} %node_second.7), custom_call_target="tpu_custom_call" | custom-call | tf_op jit(solution)/shard_map/layers/pallas_call | solution.py:507
  44.1 4.3 %round_part.2 = (bf16[192,512]{1,0:T(8,128)(2,1)}, bf16[256,512]{1,0:T(8,128)(2,1)}, bf16[256,512]{1,0:T(8,128)(2,1)}) custom-call(s32[1,2,1536]{2,1,0:T(2,128)S(1)} %copy-done.6, bf16[256,512]{1,0:T(8,128)(2,1)S(1)} %get-tuple-element.65.refs_1_, bf16[256,512]{1,0:T(8,128)(2,1)S(1)} %get-tuple-element.67.after_ref.refs_2_, ...), custom_call_target="tpu_custom_call" | custom-call | tf_op jit(solution)/shard_map/round_part/pallas_call | solution.py:591
  48.5 5.9 %all-to-all-start = ((bf16[32,8,512]{2,1,0:T(8,128)(2,1)}), bf16[32,8,512]{2,1,0:T(8,128)(2,1)S(1)}, u32[]{:S(2)}, u32[]{:S(2)}) async-start(bf16[32,8,512]{2,1,0:T(8,128)(2,1)} %bitcast), calls=%async_computation | async-start | bytes 524288 | tf_op jit(solution)/shard_map/all_to_all | solution.py:779
  54.4 3.8 %prepare.1 = (bf16[256,512]{1,0:T(8,128)(2,1)}, f32[192,512]{1,0:T(8,128)}, bf16[4,512,512]{2,1,0:T(8,128)(2,1)S(1)}) custom-call(bf16[192,512]{1,0:T(8,128)(2,1)} %get-tuple-element.76.mesh_ref.refs_5_, f32[4,512]{1,0:T(4,128)S(1)} %copy-done.3, f32[4,512]{1,0:T(4,128)S(1)} %copy-done.4, bf16[4,2,512,512]{3,2,1,0:T(8,128)(2,1)} %edge_first.11, ...), custom_call_target="tpu_custom_call" | custom-call | tf_op jit(solution)/shard_map/prepare/pallas_call | solution.py:451
  58.2 6.8 %all-to-all-done = bf16[32,8,512]{2,1,0:T(8,128)(2,1)S(1)} async-done(((bf16[32,8,512]{2,1,0:T(8,128)(2,1)}), bf16[32,8,512]{2,1,0:T(8,128)(2,1)S(1)}, u32[]{:S(2)}, u32[]{:S(2)}) %all-to-all-start) | async-done | bytes 262176 | tf_op jit(solution)/shard_map/all_to_all | solution.py:779
  65.1 5.3 %round_part.3 = (bf16[192,512]{1,0:T(8,128)(2,1)}, bf16[256,512]{1,0:T(8,128)(2,1)S(1)}, bf16[3,16,512]{2,1,0:T(8,128)(2,1)S(1)}, bf16[3,16,512]{2,1,0:T(8,128)(...) custom-call(s32[1,2,1536]{2,1,0:T(2,128)S(1)} %copy-done.7, ...), custom_call_target="tpu_custom_call" | custom-call | tf_op jit(solution)/shard_map/round_part/pallas_call | solution.py:591
  70.5 1.7 %collective-permute-start.11 = (bf16[3,16,512]{2,1,0:T(8,128)(2,1)S(1)}, bf16[3,16,512]{2,1,0:T(8,128)(2,1)S(1)}, u32[]{:S(2)}, u32[]{:S(2)}) collective-permute-start(bf16[3,16,512]{2,1,0:T(8,128)(2,1)S(1)} %get-tuple-element.83), channel_id=1, source_target_pairs={{0,24},{1,25},{2,26},{3,27},{4,28},{5,29},{6,30},{7,31},{8,0},{9,1... | collective-permute-start | bytes 147464 | tf_op jit(solution)/shard_map/ppermute | solution.py:722
  72.2 1.9 %grid_receivers.1 = (bf16[1024,512]{1,0:T(8,128)(2,1)S(1)}, bf16[1,512,512]{2,1,0:T(8,128)(2,1)S(1)}) custom-call(bf16[1024,512]{1,0:T(8,128)(2,1)S(1)} %copy-done, f32[4,512]{1,0:T(4,128)S(1)} %copy-done.3, bf16[4,2,512,512]{3,2,1,0:T(8,128)(2,1)} %edge_first.11, bf16[4,512,512]{2,1,0:T(8,128)(2,1)} %edge_second.7), custom_call_target="tpu_custom_call" | custom-call | tf_op jit(solution)/shard_map/grid_receivers/pallas_call | solution.py:619
  74.2 1.1 %collective-permute-start.12 = (bf16[3,16,512]{2,1,0:T(8,128)(2,1)S(1)}, bf16[3,16,512]{2,1,0:T(8,128)(2,1)S(1)}, u32[]{:S(2)}, u32[]{:S(2)}) collective-permute-start(bf16[3,16,512]{2,1,0:T(8,128)(2,1)S(1)} %get-tuple-element.86.after_ref), channel_id=1, source_target_pairs={{0,1},{1,2},{2,3},{3,4},{4,5},{5,6},{6,7},{7,0},{8,9},{9,10},{10,1... | collective-permute-start | bytes 147464 | tf_op jit(solution)/shard_map/ppermute | solution.py:722
  75.2 3.7 %collective-permute-start.13 = (bf16[3,16,512]{2,1,0:T(8,128)(2,1)S(1)}, bf16[3,16,512]{2,1,0:T(8,128)(2,1)S(1)}, u32[]{:S(2)}, u32[]{:S(2)}) collective-permute-start(bf16[3,16,512]{2,1,0:T(8,128)(2,1)S(1)} %get-tuple-element.90), channel_id=1, source_target_pairs={{0,7},{1,0},{2,1},{3,2},{4,3},{5,4},{6,5},{7,6},{8,15},{9,8},{10,9... | collective-permute-start | bytes 147464 | tf_op jit(solution)/shard_map/ppermute | solution.py:722
  79.0 1.9 %decode_local.1 = (bf16[3,1024,512]{2,1,0:T(8,128)(2,1)S(1)}, bf16[3,512,512]{2,1,0:T(8,128)(2,1)S(1)}) custom-call(bf16[1024,512]{1,0:T(8,128)(2,1)S(1)} %get-tuple-element.47.after_ref.target_ref, bf16[256,512]{1,0:T(8,128)(2,1)S(1)} %get-tuple-element.81.table_ref, s32[1,3,1024]{2,1,0:T(4,128)S(1)} %copy.24.edges_ref.refs_4_, ...), custom_call_target="tpu_custom_call" | custom-call | tf_op jit(solution)/shard_map/decode_local/pallas_call | solution.py:653
  81.0 5.9 %decode_part.1 = bf16[1024,512]{1,0:T(8,128)(2,1)} custom-call(bf16[3,1024,512]{2,1,0:T(8,128)(2,1)S(1)} %get-tuple-element.87.refs_0_, bf16[1,512,512]{2,1,0:T(8,128)(2,1)S(1)} %get-tuple-element.88.refs_1_, bf16[3,512,512]{2,1,0:T(8,128)(2,1)S(1)} %get-tuple-element.89.refs_2_, bf16[1024,512]{1,0:T(8,128)(2,1)S(1)} %copy-done, ...), custom_call_target="tpu_custom_call" | custom-call | tf_op jit(solution)/shard_map/decode_part/pallas_call | solution.py:694
  (49 shorter events, 3.1 us)
Async XLA Ops:
  2.4 2.2 %collective-permute-start = (bf16[384,512]{1,0:T(8,128)(2,1)S(1)}, bf16[384,512]{1,0:T(8,128)(2,1)S(1)}, u32[]{:S(2)}, u32[]{:S(2)}) collective-permute-start(bf16[384,512]{1,0:T(8,128)(2,1)S(1)} %get-tuple-element.54), channel_id=1, source_target_pairs={{0,8},{1,9},{2,10},{3,11},{4,12},{5,13},{6,14},{7,15},{8,0},{9,1},... | collective-permute-start | bytes 1179656 | tf_op jit(solution)/shard_map/ppermute | solution.py:722
  4.7 16.2 %collective-permute-start.1 = (bf16[256,512]{1,0:T(8,128)(2,1)S(1)}, bf16[256,512]{1,0:T(8,128)(2,1)S(1)}, u32[]{:S(2)}, u32[]{:S(2)}) collective-permute-start(bf16[256,512]{1,0:T(8,128)(2,1)S(1)} %get-tuple-element.57.after_ref), channel_id=1, source_target_pairs={{0,1},{1,2},{2,3},{3,4},{4,5},{5,6},{6,7},{7,0},{8,9},{9,10},{10,1... | collective-permute-start | bytes 786440 | tf_op jit(solution)/shard_map/ppermute | solution.py:722
  7.3 16.2 %collective-permute-start.2 = (bf16[256,512]{1,0:T(8,128)(2,1)S(1)}, bf16[256,512]{1,0:T(8,128)(2,1)S(1)}, u32[]{:S(2)}, u32[]{:S(2)}) collective-permute-start(bf16[256,512]{1,0:T(8,128)(2,1)S(1)} %get-tuple-element.61), channel_id=1, source_target_pairs={{0,7},{1,0},{2,1},{3,2},{4,3},{5,4},{6,5},{7,6},{8,15},{9,8},{10,9... | collective-permute-start | bytes 786440 | tf_op jit(solution)/shard_map/ppermute | solution.py:722
  11.0 8.1 %collective-permute-start.3 = (bf16[128,512]{1,0:T(8,128)(2,1)S(1)}, bf16[128,512]{1,0:T(8,128)(2,1)S(1)}, u32[]{:S(2)}, u32[]{:S(2)}) collective-permute-start(bf16[128,512]{1,0:T(8,128)(2,1)S(1)} %get-tuple-element.62), channel_id=1, source_target_pairs={{8,17},{9,18},{10,19},{11,20},{12,21},{13,22},{14,23},{15,16},{16,... | collective-permute-start | bytes 393224 | tf_op jit(solution)/shard_map/ppermute | solution.py:722
  11.7 7.4 %collective-permute-start.4 = (bf16[128,512]{1,0:T(8,128)(2,1)S(1)}, bf16[128,512]{1,0:T(8,128)(2,1)S(1)}, u32[]{:S(2)}, u32[]{:S(2)}) collective-permute-start(bf16[128,512]{1,0:T(8,128)(2,1)S(1)} %get-tuple-element.63), channel_id=1, source_target_pairs={{8,23},{9,16},{10,17},{11,18},{12,19},{13,20},{14,21},{15,22},{16,... | collective-permute-start | bytes 393224 | tf_op jit(solution)/shard_map/ppermute | solution.py:722
  12.4 6.8 %collective-permute-start.5 = (bf16[128,512]{1,0:T(8,128)(2,1)S(1)}, bf16[128,512]{1,0:T(8,128)(2,1)S(1)}, u32[]{:S(2)}, u32[]{:S(2)}) collective-permute-start(bf16[128,512]{1,0:T(8,128)(2,1)S(1)} %get-tuple-element.64), channel_id=1, source_target_pairs={{0,24},{1,25},{2,26},{3,27},{4,28},{5,29},{6,30},{7,31},{8,16},{9,... | collective-permute-start | bytes 393224 | tf_op jit(solution)/shard_map/ppermute | solution.py:722
  13.7 9.7 %copy-start.5 = (s32[1,8,16]{2,1,0:T(8,128)S(1)}, s32[1,8,16]{2,1,0:T(8,128)}, u32[]{:S(2)}) copy-start(s32[1,8,16]{2,1,0:T(8,128)} %refs_9_.2) | copy-start | bytes 1540
  23.4 11.7 %copy-start.3 = (f32[4,512]{1,0:T(4,128)S(1)}, f32[4,512]{1,0:T(4,128)}, u32[]{:S(2)}) copy-start(f32[4,512]{1,0:T(4,128)} %bias_ref.5) | copy-start | bytes 24580
  23.4 11.7 %copy-start.4 = (f32[4,512]{1,0:T(4,128)S(1)}, f32[4,512]{1,0:T(4,128)}, u32[]{:S(2)}) copy-start(f32[4,512]{1,0:T(4,128)} %refs_10_.4) | copy-start | bytes 24580
  31.0 5.7 %collective-permute-start.6 = (bf16[3,16,512]{2,1,0:T(8,128)(2,1)S(1)}, bf16[3,16,512]{2,1,0:T(8,128)(2,1)S(1)}, u32[]{:S(2)}, u32[]{:S(2)}) collective-permute-start(bf16[3,16,512]{2,1,0:T(8,128)(2,1)S(1)} %get-tuple-element.69), channel_id=1, source_target_pairs={{0,8},{1,9},{2,10},{3,11},{4,12},{5,13},{6,14},{7,15},{8,16},{9,17... | collective-permute-start | bytes 147464 | tf_op jit(solution)/shard_map/ppermute | solution.py:722
  35.1 1.8 %collective-permute-start.7 = (bf16[3,16,512]{2,1,0:T(8,128)(2,1)S(1)}, bf16[3,16,512]{2,1,0:T(8,128)(2,1)S(1)}, u32[]{:S(2)}, u32[]{:S(2)}) collective-permute-start(bf16[3,16,512]{2,1,0:T(8,128)(2,1)S(1)} %get-tuple-element.70), channel_id=1, source_target_pairs={{0,24},{1,25},{2,26},{3,27},{4,28},{5,29},{6,30},{7,31},{8,0},{9,1... | collective-permute-start | bytes 147464 | tf_op jit(solution)/shard_map/ppermute | solution.py:722
  35.1 7.2 %copy-start.9 = (s32[1,32,8]{1,2,0:T(8,128)S(1)}, s32[1,32,8]{1,2,0:T(8,128)}, u32[]{:S(2)}) copy-start(s32[1,32,8]{1,2,0:T(8,128)} %param.23) | copy-start | bytes 3076
  36.9 7.2 %collective-permute-start.8 = (bf16[3,16,512]{2,1,0:T(8,128)(2,1)S(1)}, bf16[3,16,512]{2,1,0:T(8,128)(2,1)S(1)}, u32[]{:S(2)}, u32[]{:S(2)}) collective-permute-start(bf16[3,16,512]{2,1,0:T(8,128)(2,1)S(1)} %get-tuple-element.73.after_ref), channel_id=1, source_target_pairs={{0,1},{1,2},{2,3},{3,4},{4,5},{5,6},{6,7},{7,0},{8,9},{9,10},{10,1... | collective-permute-start | bytes 147464 | tf_op jit(solution)/shard_map/ppermute | solution.py:722
  36.9 7.2 %collective-permute-start.9 = (bf16[3,16,512]{2,1,0:T(8,128)(2,1)S(1)}, bf16[3,16,512]{2,1,0:T(8,128)(2,1)S(1)}, u32[]{:S(2)}, u32[]{:S(2)}) collective-permute-start(bf16[3,16,512]{2,1,0:T(8,128)(2,1)S(1)} %get-tuple-element.74), channel_id=1, source_target_pairs={{0,7},{1,0},{2,1},{3,2},{4,3},{5,4},{6,5},{7,6},{8,15},{9,8},{10,9... | collective-permute-start | bytes 147464 | tf_op jit(solution)/shard_map/ppermute | solution.py:722
  42.5 1.7 %copy-start.1 = (f32[4,512]{1,0:T(4,128)S(1)}, f32[4,512]{1,0:T(4,128)}, u32[]{:S(2)}) copy-start(f32[4,512]{1,0:T(4,128)} %refs_9_.3) | copy-start | bytes 24580
  42.5 1.7 %copy-start.2 = (f32[4,512]{1,0:T(4,128)S(1)}, f32[4,512]{1,0:T(4,128)}, u32[]{:S(2)}) copy-start(f32[4,512]{1,0:T(4,128)} %refs_11_.3) | copy-start | bytes 24580
  48.5 16.6 %all-to-all-start = ((bf16[32,8,512]{2,1,0:T(8,128)(2,1)}), bf16[32,8,512]{2,1,0:T(8,128)(2,1)S(1)}, u32[]{:S(2)}, u32[]{:S(2)}) async-start(bf16[32,8,512]{2,1,0:T(8,128)(2,1)} %bitcast), calls=%async_computation | async-start | bytes 524288 | tf_op jit(solution)/shard_map/all_to_all | solution.py:779
  54.4 10.6 %copy-start.7 = (s32[1,2,1536]{2,1,0:T(2,128)S(1)}, s32[1,2,1536]{2,1,0:T(2,128)}, u32[]{:S(2)}) copy-start(s32[1,2,1536]{2,1,0:T(2,128)} %refs_0_.5) | copy-start | bytes 36868
  58.2 14.0 %copy-start = (bf16[1024,512]{1,0:T(8,128)(2,1)S(1)}, bf16[1024,512]{1,0:T(8,128)(2,1)}, u32[]{:S(2)}) copy-start(bf16[1024,512]{1,0:T(8,128)(2,1)} %refs_3_.3) | copy-start | bytes 3145732
  70.4 3.8 %collective-permute-start.10 = (bf16[3,16,512]{2,1,0:T(8,128)(2,1)S(1)}, bf16[3,16,512]{2,1,0:T(8,128)(2,1)S(1)}, u32[]{:S(2)}, u32[]{:S(2)}) collective-permute-start(bf16[3,16,512]{2,1,0:T(8,128)(2,1)S(1)} %get-tuple-element.82), channel_id=1, source_target_pairs={{0,8},{1,9},{2,10},{3,11},{4,12},{5,13},{6,14},{7,15},{8,16},{9,17... | collective-permute-start | bytes 147464 | tf_op jit(solution)/shard_map/ppermute | solution.py:722
  70.4 8.5 %copy-start.8 = (s32[1,3,1024]{2,0,1:T(1,128)S(1)}, s32[1,3,1024]{2,0,1:T(1,128)}, u32[]{:S(2)}) copy-start(s32[1,3,1024]{2,0,1:T(1,128)} %param.27) | copy-start | bytes 36868
  70.5 3.7 %collective-permute-start.11 = (bf16[3,16,512]{2,1,0:T(8,128)(2,1)S(1)}, bf16[3,16,512]{2,1,0:T(8,128)(2,1)S(1)}, u32[]{:S(2)}, u32[]{:S(2)}) collective-permute-start(bf16[3,16,512]{2,1,0:T(8,128)(2,1)S(1)} %get-tuple-element.83), channel_id=1, source_target_pairs={{0,24},{1,25},{2,26},{3,27},{4,28},{5,29},{6,30},{7,31},{8,0},{9,1... | collective-permute-start | bytes 147464 | tf_op jit(solution)/shard_map/ppermute | solution.py:722
  74.2 6.8 %collective-permute-start.12 = (bf16[3,16,512]{2,1,0:T(8,128)(2,1)S(1)}, bf16[3,16,512]{2,1,0:T(8,128)(2,1)S(1)}, u32[]{:S(2)}, u32[]{:S(2)}) collective-permute-start(bf16[3,16,512]{2,1,0:T(8,128)(2,1)S(1)} %get-tuple-element.86.after_ref), channel_id=1, source_target_pairs={{0,1},{1,2},{2,3},{3,4},{4,5},{5,6},{6,7},{7,0},{8,9},{9,10},{10,1... | collective-permute-start | bytes 147464 | tf_op jit(solution)/shard_map/ppermute | solution.py:722
  75.2 5.8 %collective-permute-start.13 = (bf16[3,16,512]{2,1,0:T(8,128)(2,1)S(1)}, bf16[3,16,512]{2,1,0:T(8,128)(2,1)S(1)}, u32[]{:S(2)}, u32[]{:S(2)}) collective-permute-start(bf16[3,16,512]{2,1,0:T(8,128)(2,1)S(1)} %get-tuple-element.90), channel_id=1, source_target_pairs={{0,7},{1,0},{2,1},{3,2},{4,3},{5,4},{6,5},{7,6},{8,15},{9,8},{10,9... | collective-permute-start | bytes 147464 | tf_op jit(solution)/shard_map/ppermute | solution.py:722
  (1 other events, 1.6 us)

commit v7 on v6

--- a/solution.py
+++ b/solution.py
@@ -547,22 +547,26 @@
     mesh_out, proj_out = rest[:2]
     sends = rest[2:]
     place_remote(table, remote, places, padded)
-    if last:
-        for copy in copies:
-            copy.wait()
+    waiting = copies if last else []
     edges = edges_ref.shape[2]
     block = math_block(edges, 1536)
     summed = None
     for start in range(0, edges, block):
         senders = edges_ref[0, 0:1, start : start + block]
-        senders = jnp.where(senders < slots, senders, senders + (padded - slots))
         targets = edges_ref[0, 1:2, start : start + block]
-        pre = dot(one_hot(column(senders), table.shape[0]), table[...]) + dot(
-            one_hot(column(targets), padded), target[...]
-        )
+        senders = column(senders)
+        pre = dot(one_hot(senders, table.shape[0] - padded, slots), table[padded:])
+        for copy in waiting[:2]:
+            copy.wait()
+        waiting = []
+        own = jnp.where(senders < slots, senders, jnp.int16(-1))
+        pre = pre + dot(one_hot(own, padded), table[:padded])
+        pre = pre + dot(one_hot(column(targets), padded), target[...])
         part = added(pre, targets, stack[0], slots)
         summed = part if summed is None else summed + part
     summed = summed * row_of(gain_ref, section)
+    for copy in copies[2:] if last else []:
+        copy.wait()
     fresh = updated(mesh_ref[...], summed, inner_ref[...], stack[2], stack[1], row_of(node_gain_ref, section))
     if last:
         alive = lax.broadcasted_iota(jnp.int32, fresh.shape, 0) < owned_ref[0]

time: 87.5 us -> 87.3 us (level)
  no operation moved by 1% of the time
where the time goes in v7:
time: 87.3 us; the launch traced here: 86.9 us
  Pallas kernels  43.2 us (49%)
  starting transfers between devices  30.2 us (35%)
  waiting for transfers between devices  11.4 us (13%)
  between operations  1.81 us (2%)
    ppermute x14, starting transfers between devices, move(): return lax.ppermute(value, AXES, pairs)  24.3 us
    pallas_call x2, Pallas kernels, round_part(): pl.pallas_call(functools.partial(round_kernel, section, places, last), in...  9.44 us
    pallas_call x1, Pallas kernels, encode(): pl.pallas_call(functools.partial(encode_kernel, count), out_shape=[pltpu....  7.58 us
    all_to_all x1, waiting for transfers between devices, per_device(): lax.all_to_all(sent, AXES, split_axis=0, concat_axis=0, tiled=True)  6.85 us
    all_to_all x1, starting transfers between devices, per_device(): lax.all_to_all(sent, AXES, split_axis=0, concat_axis=0, tiled=True)  5.94 us
    pallas_call x1, Pallas kernels, decode_part(): pl.pallas_call(functools.partial(decode_kernel, section, places, split),...  5.93 us
    pallas_call x1, Pallas kernels, encode_local(): pl.pallas_call(functools.partial(encode_local_kernel, section), in_specs=...  5.36 us
    ppermute x14, waiting for transfers between devices, move(): return lax.ppermute(value, AXES, pairs)  4.59 us
  transfers between devices with their start and end apart: 15, of which 5 were waited for; matrix products, arithmetic and copies ran while one was open for 0% of the time, Pallas kernels for 21%

profile of v7, /device:TPU:0, one launch (start us, length us, event | category | flops | bytes accessed | tf_op | source)
XLA Modules:
  0.0 86.9 jit_solution(3757163233152774636)
XLA Ops:
  0.6 1.8 %pick_pair.1 = (bf16[384,512]{1,0:T(8,128)(2,1)S(1)}, bf16[1024,512]{1,0:T(8,128)(2,1)S(1)}, s32[1,8,128]{2,1,0:T(8,128)S(1)}) custom-call(bf16[1024,512]{1,0:T(8,128)(2,1)} %refs_3_.3, s32[1,8,128]{2,1,0:T(8,128)} %rim_hbm.1), custom_call_target="tpu_custom_call" | custom-call | tf_op jit(solution)/shard_map/pick_pair/pallas_call | solution.py:199
  3.0 1.6 %pick_rest.1 = (bf16[128,512]{1,0:T(8,128)(2,1)S(1)}, bf16[128,512]{1,0:T(8,128)(2,1)S(1)}, bf16[3,512,512]{2,1,0:T(8,128)(2,1)S(1)}, bf16[192,512]{1,0:T(8,128)...) custom-call(bf16[1024,512]{1,0:T(8,128)(2,1)S(1)} %get-tuple-element.48.rows_ref.grid_ref, ...), custom_call_target="tpu_custom_call" | custom-call | tf_op jit(solution)/shard_map/pick_rest/pallas_call | solution.py:257
  4.7 2.6 %collective-permute-start.1 = (bf16[256,512]{1,0:T(8,128)(2,1)S(1)}, bf16[256,512]{1,0:T(8,128)(2,1)S(1)}, u32[]{:S(2)}, u32[]{:S(2)}) collective-permute-start(bf16[256,512]{1,0:T(8,128)(2,1)S(1)} %get-tuple-element.57.after_ref), channel_id=1, source_target_pairs={{0,1},{1,2},{2,3},{3,4},{4,5},{5,6},{6,7},{7,0},{8,9},{9,10},{10,1... | collective-permute-start | bytes 786440 | tf_op jit(solution)/shard_map/ppermute | solution.py:726
  7.3 3.1 %collective-permute-start.2 = (bf16[256,512]{1,0:T(8,128)(2,1)S(1)}, bf16[256,512]{1,0:T(8,128)(2,1)S(1)}, u32[]{:S(2)}, u32[]{:S(2)}) collective-permute-start(bf16[256,512]{1,0:T(8,128)(2,1)S(1)} %get-tuple-element.61), channel_id=1, source_target_pairs={{0,7},{1,0},{2,1},{3,2},{4,3},{5,4},{6,5},{7,6},{8,15},{9,8},{10,9... | collective-permute-start | bytes 786440 | tf_op jit(solution)/shard_map/ppermute | solution.py:726
  12.4 1.4 %collective-permute-start.5 = (bf16[128,512]{1,0:T(8,128)(2,1)S(1)}, bf16[128,512]{1,0:T(8,128)(2,1)S(1)}, u32[]{:S(2)}, u32[]{:S(2)}) collective-permute-start(bf16[128,512]{1,0:T(8,128)(2,1)S(1)} %get-tuple-element.64), channel_id=1, source_target_pairs={{0,24},{1,25},{2,26},{3,27},{4,28},{5,29},{6,30},{7,31},{8,16},{9,... | collective-permute-start | bytes 393224 | tf_op jit(solution)/shard_map/ppermute | solution.py:726
  13.7 5.4 %encode_local.1 = (f32[3072,512]{1,0:T(8,128)S(1)}, f32[192,512]{1,0:T(8,128)S(1)}, bf16[5,512,512]{2,1,0:T(8,128)(2,1)S(1)}) custom-call(bf16[1024,512]{1,0:T(8,128)(2,1)S(1)} %get-tuple-element.48.rows_ref.grid_ref, bf16[3,512,512]{2,1,0:T(8,128)(2,1)S(1)} %get-tuple-element.50.stack, bf16[192,512]{1,0:T(8,128)(2,1)S(1)} %get-tuple-element.51.mesh_ref.refs_4_, ...), custom_call_target="tpu_custom_call" | custom-call | tf_op jit(solution)/shard_map/encode_local/pallas_call | solution.py:350
  19.1 1.8 %collective-permute-done.1.refs_6_ = bf16[256,512]{1,0:T(8,128)(2,1)S(1)} collective-permute-done((bf16[256,512]{1,0:T(8,128)(2,1)S(1)}, bf16[256,512]{1,0:T(8,128)(2,1)S(1)}, u32[]{:S(2)}, u32[]{:S(2)}) %collective-permute-start.1) | collective-permute-done | bytes 262176 | tf_op jit(solution)/shard_map/ppermute | solution.py:726
  20.9 2.5 %collective-permute-done.2.refs_7_ = bf16[256,512]{1,0:T(8,128)(2,1)S(1)} collective-permute-done((bf16[256,512]{1,0:T(8,128)(2,1)S(1)}, bf16[256,512]{1,0:T(8,128)(2,1)S(1)}, u32[]{:S(2)}, u32[]{:S(2)}) %collective-permute-start.2) | collective-permute-done | bytes 262176 | tf_op jit(solution)/shard_map/ppermute | solution.py:726
  23.4 7.6 %encode.1 = (bf16[192,512]{1,0:T(8,128)(2,1)S(1)}, bf16[256,512]{1,0:T(8,128)(2,1)S(1)}, bf16[3,16,512]{2,1,0:T(8,128)(2,1)S(1)}, bf16[3,16,512]{2,1,0:T(8,128)(...) custom-call(f32[3072,512]{1,0:T(8,128)S(1)} %get-tuple-element.58.refs_0_, ...), custom_call_target="tpu_custom_call" | custom-call | tf_op jit(solution)/shard_map/encode/pallas_call | solution.py:412
  31.0 4.1 %collective-permute-start.6 = (bf16[3,16,512]{2,1,0:T(8,128)(2,1)S(1)}, bf16[3,16,512]{2,1,0:T(8,128)(2,1)S(1)}, u32[]{:S(2)}, u32[]{:S(2)}) collective-permute-start(bf16[3,16,512]{2,1,0:T(8,128)(2,1)S(1)} %get-tuple-element.69), channel_id=1, source_target_pairs={{0,8},{1,9},{2,10},{3,11},{4,12},{5,13},{6,14},{7,15},{8,16},{9,17... | collective-permute-start | bytes 147464 | tf_op jit(solution)/shard_map/ppermute | solution.py:726
  35.1 1.6 %receivers.1 = (bf16[256,512]{1,0:T(8,128)(2,1)S(1)}, f32[192,512]{1,0:T(8,128)S(1)}) custom-call(bf16[192,512]{1,0:T(8,128)(2,1)S(1)} %get-tuple-element.66.mesh_ref.refs_5_, f32[4,512]{1,0:T(4,128)S(1)} %copy-done.3, f32[4,512]{1,0:T(4,128)S(1)} %copy-done.4, bf16[4,2,512,512]{3,2,1,0:T(8,128)(2,1)} %edge_first.11, bf16[4,2,512,512]{3,2,1,0:T(8,128)(2,1)} %node_first.11), custom_call_target="tpu_custom_call" | custom-call | tf_op jit(solution)/shard_map/receivers/pallas_call | solution.py:480
  36.9 4.7 %collective-permute-start.9 = (bf16[3,16,512]{2,1,0:T(8,128)(2,1)S(1)}, bf16[3,16,512]{2,1,0:T(8,128)(2,1)S(1)}, u32[]{:S(2)}, u32[]{:S(2)}) collective-permute-start(bf16[3,16,512]{2,1,0:T(8,128)(2,1)S(1)} %get-tuple-element.74), channel_id=1, source_target_pairs={{0,7},{1,0},{2,1},{3,2},{4,3},{5,4},{6,5},{7,6},{8,15},{9,8},{10,9... | collective-permute-start | bytes 147464 | tf_op jit(solution)/shard_map/ppermute | solution.py:726
  42.5 1.6 %layers.1.refs_4_ = bf16[4,512,512]{2,1,0:T(8,128)(2,1)S(1)} custom-call(bf16[3,16,512]{2,1,0:T(8,128)(2,1)S(1)} %get-tuple-element.73.after_ref, bf16[4,2,512,512]{3,2,1,0:T(8,128)(2,1)} %edge_first.11, bf16[4,512,512]{2,1,0:T(8,128)(2,1)} %edge_second.7, bf16[4,2,512,512]{3,2,1,0:T(8,128)(2,1)} %node_first.11, bf16[4,512,512]{2,1,0:T(8,128)(2,1)} %node_second.7), custom_call_target="tpu_custom_call" | custom-call | tf_op jit(solution)/shard_map/layers/pallas_call | solution.py:507
  44.1 4.3 %round_part.2 = (bf16[192,512]{1,0:T(8,128)(2,1)}, bf16[256,512]{1,0:T(8,128)(2,1)}, bf16[256,512]{1,0:T(8,128)(2,1)}) custom-call(s32[1,2,1536]{2,1,0:T(2,128)S(1)} %copy-done.6, bf16[256,512]{1,0:T(8,128)(2,1)S(1)} %get-tuple-element.65.refs_1_, bf16[256,512]{1,0:T(8,128)(2,1)S(1)} %get-tuple-element.67.after_ref.refs_2_, ...), custom_call_target="tpu_custom_call" | custom-call | tf_op jit(solution)/shard_map/round_part/pallas_call | solution.py:595
  48.4 5.9 %all-to-all-start = ((bf16[32,8,512]{2,1,0:T(8,128)(2,1)}), bf16[32,8,512]{2,1,0:T(8,128)(2,1)S(1)}, u32[]{:S(2)}, u32[]{:S(2)}) async-start(bf16[32,8,512]{2,1,0:T(8,128)(2,1)} %bitcast), calls=%async_computation | async-start | bytes 524288 | tf_op jit(solution)/shard_map/all_to_all | solution.py:783
  54.4 3.8 %prepare.1 = (bf16[256,512]{1,0:T(8,128)(2,1)}, f32[192,512]{1,0:T(8,128)}, bf16[4,512,512]{2,1,0:T(8,128)(2,1)S(1)}) custom-call(bf16[192,512]{1,0:T(8,128)(2,1)} %get-tuple-element.76.mesh_ref.refs_5_, f32[4,512]{1,0:T(4,128)S(1)} %copy-done.3, f32[4,512]{1,0:T(4,128)S(1)} %copy-done.4, bf16[4,2,512,512]{3,2,1,0:T(8,128)(2,1)} %edge_first.11, ...), custom_call_target="tpu_custom_call" | custom-call | tf_op jit(solution)/shard_map/prepare/pallas_call | solution.py:451
  58.2 6.8 %all-to-all-done = bf16[32,8,512]{2,1,0:T(8,128)(2,1)S(1)} async-done(((bf16[32,8,512]{2,1,0:T(8,128)(2,1)}), bf16[32,8,512]{2,1,0:T(8,128)(2,1)S(1)}, u32[]{:S(2)}, u32[]{:S(2)}) %all-to-all-start) | async-done | bytes 262176 | tf_op jit(solution)/shard_map/all_to_all | solution.py:783
  65.0 5.1 %round_part.3 = (bf16[192,512]{1,0:T(8,128)(2,1)}, bf16[256,512]{1,0:T(8,128)(2,1)S(1)}, bf16[3,16,512]{2,1,0:T(8,128)(2,1)S(1)}, bf16[3,16,512]{2,1,0:T(8,128)(...) custom-call(s32[1,2,1536]{2,1,0:T(2,128)S(1)} %copy-done.7, ...), custom_call_target="tpu_custom_call" | custom-call | tf_op jit(solution)/shard_map/round_part/pallas_call | solution.py:595
  70.3 1.7 %collective-permute-start.11 = (bf16[3,16,512]{2,1,0:T(8,128)(2,1)S(1)}, bf16[3,16,512]{2,1,0:T(8,128)(2,1)S(1)}, u32[]{:S(2)}, u32[]{:S(2)}) collective-permute-start(bf16[3,16,512]{2,1,0:T(8,128)(2,1)S(1)} %get-tuple-element.83), channel_id=1, source_target_pairs={{0,24},{1,25},{2,26},{3,27},{4,28},{5,29},{6,30},{7,31},{8,0},{9,1... | collective-permute-start | bytes 147464 | tf_op jit(solution)/shard_map/ppermute | solution.py:726
  72.0 1.9 %grid_receivers.1 = (bf16[1024,512]{1,0:T(8,128)(2,1)S(1)}, bf16[1,512,512]{2,1,0:T(8,128)(2,1)S(1)}) custom-call(bf16[1024,512]{1,0:T(8,128)(2,1)S(1)} %copy-done, f32[4,512]{1,0:T(4,128)S(1)} %copy-done.3, bf16[4,2,512,512]{3,2,1,0:T(8,128)(2,1)} %edge_first.11, bf16[4,512,512]{2,1,0:T(8,128)(2,1)} %edge_second.7), custom_call_target="tpu_custom_call" | custom-call | tf_op jit(solution)/shard_map/grid_receivers/pallas_call | solution.py:623
  74.0 1.1 %collective-permute-start.12 = (bf16[3,16,512]{2,1,0:T(8,128)(2,1)S(1)}, bf16[3,16,512]{2,1,0:T(8,128)(2,1)S(1)}, u32[]{:S(2)}, u32[]{:S(2)}) collective-permute-start(bf16[3,16,512]{2,1,0:T(8,128)(2,1)S(1)} %get-tuple-element.86.after_ref), channel_id=1, source_target_pairs={{0,1},{1,2},{2,3},{3,4},{4,5},{5,6},{6,7},{7,0},{8,9},{9,10},{10,1... | collective-permute-start | bytes 147464 | tf_op jit(solution)/shard_map/ppermute | solution.py:726
  75.1 3.7 %collective-permute-start.13 = (bf16[3,16,512]{2,1,0:T(8,128)(2,1)S(1)}, bf16[3,16,512]{2,1,0:T(8,128)(2,1)S(1)}, u32[]{:S(2)}, u32[]{:S(2)}) collective-permute-start(bf16[3,16,512]{2,1,0:T(8,128)(2,1)S(1)} %get-tuple-element.90), channel_id=1, source_target_pairs={{0,7},{1,0},{2,1},{3,2},{4,3},{5,4},{6,5},{7,6},{8,15},{9,8},{10,9... | collective-permute-start | bytes 147464 | tf_op jit(solution)/shard_map/ppermute | solution.py:726
  78.8 1.9 %decode_local.1 = (bf16[3,1024,512]{2,1,0:T(8,128)(2,1)S(1)}, bf16[3,512,512]{2,1,0:T(8,128)(2,1)S(1)}) custom-call(bf16[1024,512]{1,0:T(8,128)(2,1)S(1)} %get-tuple-element.47.after_ref.target_ref, bf16[256,512]{1,0:T(8,128)(2,1)S(1)} %get-tuple-element.81.table_ref, s32[1,3,1024]{2,1,0:T(4,128)S(1)} %copy.24.edges_ref.refs_4_, ...), custom_call_target="tpu_custom_call" | custom-call | tf_op jit(solution)/shard_map/decode_local/pallas_call | solution.py:657
  80.8 5.9 %decode_part.1 = bf16[1024,512]{1,0:T(8,128)(2,1)} custom-call(bf16[3,1024,512]{2,1,0:T(8,128)(2,1)S(1)} %get-tuple-element.87.refs_0_, bf16[1,512,512]{2,1,0:T(8,128)(2,1)S(1)} %get-tuple-element.88.refs_1_, bf16[3,512,512]{2,1,0:T(8,128)(2,1)S(1)} %get-tuple-element.89.refs_2_, bf16[1024,512]{1,0:T(8,128)(2,1)S(1)} %copy-done, ...), custom_call_target="tpu_custom_call" | custom-call | tf_op jit(solution)/shard_map/decode_part/pallas_call | solution.py:698
  (49 shorter events, 3.1 us)
Async XLA Ops:
  2.4 2.2 %collective-permute-start = (bf16[384,512]{1,0:T(8,128)(2,1)S(1)}, bf16[384,512]{1,0:T(8,128)(2,1)S(1)}, u32[]{:S(2)}, u32[]{:S(2)}) collective-permute-start(bf16[384,512]{1,0:T(8,128)(2,1)S(1)} %get-tuple-element.54), channel_id=1, source_target_pairs={{0,8},{1,9},{2,10},{3,11},{4,12},{5,13},{6,14},{7,15},{8,0},{9,1},... | collective-permute-start | bytes 1179656 | tf_op jit(solution)/shard_map/ppermute | solution.py:726
  4.7 16.2 %collective-permute-start.1 = (bf16[256,512]{1,0:T(8,128)(2,1)S(1)}, bf16[256,512]{1,0:T(8,128)(2,1)S(1)}, u32[]{:S(2)}, u32[]{:S(2)}) collective-permute-start(bf16[256,512]{1,0:T(8,128)(2,1)S(1)} %get-tuple-element.57.after_ref), channel_id=1, source_target_pairs={{0,1},{1,2},{2,3},{3,4},{4,5},{5,6},{6,7},{7,0},{8,9},{9,10},{10,1... | collective-permute-start | bytes 786440 | tf_op jit(solution)/shard_map/ppermute | solution.py:726
  7.3 16.2 %collective-permute-start.2 = (bf16[256,512]{1,0:T(8,128)(2,1)S(1)}, bf16[256,512]{1,0:T(8,128)(2,1)S(1)}, u32[]{:S(2)}, u32[]{:S(2)}) collective-permute-start(bf16[256,512]{1,0:T(8,128)(2,1)S(1)} %get-tuple-element.61), channel_id=1, source_target_pairs={{0,7},{1,0},{2,1},{3,2},{4,3},{5,4},{6,5},{7,6},{8,15},{9,8},{10,9... | collective-permute-start | bytes 786440 | tf_op jit(solution)/shard_map/ppermute | solution.py:726
  11.0 8.1 %collective-permute-start.3 = (bf16[128,512]{1,0:T(8,128)(2,1)S(1)}, bf16[128,512]{1,0:T(8,128)(2,1)S(1)}, u32[]{:S(2)}, u32[]{:S(2)}) collective-permute-start(bf16[128,512]{1,0:T(8,128)(2,1)S(1)} %get-tuple-element.62), channel_id=1, source_target_pairs={{8,17},{9,18},{10,19},{11,20},{12,21},{13,22},{14,23},{15,16},{16,... | collective-permute-start | bytes 393224 | tf_op jit(solution)/shard_map/ppermute | solution.py:726
  11.7 7.4 %collective-permute-start.4 = (bf16[128,512]{1,0:T(8,128)(2,1)S(1)}, bf16[128,512]{1,0:T(8,128)(2,1)S(1)}, u32[]{:S(2)}, u32[]{:S(2)}) collective-permute-start(bf16[128,512]{1,0:T(8,128)(2,1)S(1)} %get-tuple-element.63), channel_id=1, source_target_pairs={{8,23},{9,16},{10,17},{11,18},{12,19},{13,20},{14,21},{15,22},{16,... | collective-permute-start | bytes 393224 | tf_op jit(solution)/shard_map/ppermute | solution.py:726
  12.4 6.8 %collective-permute-start.5 = (bf16[128,512]{1,0:T(8,128)(2,1)S(1)}, bf16[128,512]{1,0:T(8,128)(2,1)S(1)}, u32[]{:S(2)}, u32[]{:S(2)}) collective-permute-start(bf16[128,512]{1,0:T(8,128)(2,1)S(1)} %get-tuple-element.64), channel_id=1, source_target_pairs={{0,24},{1,25},{2,26},{3,27},{4,28},{5,29},{6,30},{7,31},{8,16},{9,... | collective-permute-start | bytes 393224 | tf_op jit(solution)/shard_map/ppermute | solution.py:726
  13.7 9.7 %copy-start.5 = (s32[1,8,16]{2,1,0:T(8,128)S(1)}, s32[1,8,16]{2,1,0:T(8,128)}, u32[]{:S(2)}) copy-start(s32[1,8,16]{2,1,0:T(8,128)} %refs_9_.2) | copy-start | bytes 1540
  23.4 11.7 %copy-start.3 = (f32[4,512]{1,0:T(4,128)S(1)}, f32[4,512]{1,0:T(4,128)}, u32[]{:S(2)}) copy-start(f32[4,512]{1,0:T(4,128)} %bias_ref.5) | copy-start | bytes 24580
  23.4 11.7 %copy-start.4 = (f32[4,512]{1,0:T(4,128)S(1)}, f32[4,512]{1,0:T(4,128)}, u32[]{:S(2)}) copy-start(f32[4,512]{1,0:T(4,128)} %refs_10_.4) | copy-start | bytes 24580
  31.0 5.7 %collective-permute-start.6 = (bf16[3,16,512]{2,1,0:T(8,128)(2,1)S(1)}, bf16[3,16,512]{2,1,0:T(8,128)(2,1)S(1)}, u32[]{:S(2)}, u32[]{:S(2)}) collective-permute-start(bf16[3,16,512]{2,1,0:T(8,128)(2,1)S(1)} %get-tuple-element.69), channel_id=1, source_target_pairs={{0,8},{1,9},{2,10},{3,11},{4,12},{5,13},{6,14},{7,15},{8,16},{9,17... | collective-permute-start | bytes 147464 | tf_op jit(solution)/shard_map/ppermute | solution.py:726
  35.1 1.8 %collective-permute-start.7 = (bf16[3,16,512]{2,1,0:T(8,128)(2,1)S(1)}, bf16[3,16,512]{2,1,0:T(8,128)(2,1)S(1)}, u32[]{:S(2)}, u32[]{:S(2)}) collective-permute-start(bf16[3,16,512]{2,1,0:T(8,128)(2,1)S(1)} %get-tuple-element.70), channel_id=1, source_target_pairs={{0,24},{1,25},{2,26},{3,27},{4,28},{5,29},{6,30},{7,31},{8,0},{9,1... | collective-permute-start | bytes 147464 | tf_op jit(solution)/shard_map/ppermute | solution.py:726
  35.1 7.2 %copy-start.9 = (s32[1,32,8]{1,2,0:T(8,128)S(1)}, s32[1,32,8]{1,2,0:T(8,128)}, u32[]{:S(2)}) copy-start(s32[1,32,8]{1,2,0:T(8,128)} %param.23) | copy-start | bytes 3076
  36.9 7.2 %collective-permute-start.8 = (bf16[3,16,512]{2,1,0:T(8,128)(2,1)S(1)}, bf16[3,16,512]{2,1,0:T(8,128)(2,1)S(1)}, u32[]{:S(2)}, u32[]{:S(2)}) collective-permute-start(bf16[3,16,512]{2,1,0:T(8,128)(2,1)S(1)} %get-tuple-element.73.after_ref), channel_id=1, source_target_pairs={{0,1},{1,2},{2,3},{3,4},{4,5},{5,6},{6,7},{7,0},{8,9},{9,10},{10,1... | collective-permute-start | bytes 147464 | tf_op jit(solution)/shard_map/ppermute | solution.py:726
  36.9 7.2 %collective-permute-start.9 = (bf16[3,16,512]{2,1,0:T(8,128)(2,1)S(1)}, bf16[3,16,512]{2,1,0:T(8,128)(2,1)S(1)}, u32[]{:S(2)}, u32[]{:S(2)}) collective-permute-start(bf16[3,16,512]{2,1,0:T(8,128)(2,1)S(1)} %get-tuple-element.74), channel_id=1, source_target_pairs={{0,7},{1,0},{2,1},{3,2},{4,3},{5,4},{6,5},{7,6},{8,15},{9,8},{10,9... | collective-permute-start | bytes 147464 | tf_op jit(solution)/shard_map/ppermute | solution.py:726
  42.5 1.7 %copy-start.1 = (f32[4,512]{1,0:T(4,128)S(1)}, f32[4,512]{1,0:T(4,128)}, u32[]{:S(2)}) copy-start(f32[4,512]{1,0:T(4,128)} %refs_9_.3) | copy-start | bytes 24580
  42.5 1.7 %copy-start.2 = (f32[4,512]{1,0:T(4,128)S(1)}, f32[4,512]{1,0:T(4,128)}, u32[]{:S(2)}) copy-start(f32[4,512]{1,0:T(4,128)} %refs_11_.3) | copy-start | bytes 24580
  48.4 16.6 %all-to-all-start = ((bf16[32,8,512]{2,1,0:T(8,128)(2,1)}), bf16[32,8,512]{2,1,0:T(8,128)(2,1)S(1)}, u32[]{:S(2)}, u32[]{:S(2)}) async-start(bf16[32,8,512]{2,1,0:T(8,128)(2,1)} %bitcast), calls=%async_computation | async-start | bytes 524288 | tf_op jit(solution)/shard_map/all_to_all | solution.py:783
  54.4 10.6 %copy-start.7 = (s32[1,2,1536]{2,1,0:T(2,128)S(1)}, s32[1,2,1536]{2,1,0:T(2,128)}, u32[]{:S(2)}) copy-start(s32[1,2,1536]{2,1,0:T(2,128)} %refs_0_.5) | copy-start | bytes 36868
  58.2 13.8 %copy-start = (bf16[1024,512]{1,0:T(8,128)(2,1)S(1)}, bf16[1024,512]{1,0:T(8,128)(2,1)}, u32[]{:S(2)}) copy-start(bf16[1024,512]{1,0:T(8,128)(2,1)} %refs_3_.3) | copy-start | bytes 3145732
  70.2 3.8 %collective-permute-start.10 = (bf16[3,16,512]{2,1,0:T(8,128)(2,1)S(1)}, bf16[3,16,512]{2,1,0:T(8,128)(2,1)S(1)}, u32[]{:S(2)}, u32[]{:S(2)}) collective-permute-start(bf16[3,16,512]{2,1,0:T(8,128)(2,1)S(1)} %get-tuple-element.82), channel_id=1, source_target_pairs={{0,8},{1,9},{2,10},{3,11},{4,12},{5,13},{6,14},{7,15},{8,16},{9,17... | collective-permute-start | bytes 147464 | tf_op jit(solution)/shard_map/ppermute | solution.py:726
  70.2 8.5 %copy-start.8 = (s32[1,3,1024]{2,0,1:T(1,128)S(1)}, s32[1,3,1024]{2,0,1:T(1,128)}, u32[]{:S(2)}) copy-start(s32[1,3,1024]{2,0,1:T(1,128)} %param.27) | copy-start | bytes 36868
  70.3 3.7 %collective-permute-start.11 = (bf16[3,16,512]{2,1,0:T(8,128)(2,1)S(1)}, bf16[3,16,512]{2,1,0:T(8,128)(2,1)S(1)}, u32[]{:S(2)}, u32[]{:S(2)}) collective-permute-start(bf16[3,16,512]{2,1,0:T(8,128)(2,1)S(1)} %get-tuple-element.83), channel_id=1, source_target_pairs={{0,24},{1,25},{2,26},{3,27},{4,28},{5,29},{6,30},{7,31},{8,0},{9,1... | collective-permute-start | bytes 147464 | tf_op jit(solution)/shard_map/ppermute | solution.py:726
  74.0 6.8 %collective-permute-start.12 = (bf16[3,16,512]{2,1,0:T(8,128)(2,1)S(1)}, bf16[3,16,512]{2,1,0:T(8,128)(2,1)S(1)}, u32[]{:S(2)}, u32[]{:S(2)}) collective-permute-start(bf16[3,16,512]{2,1,0:T(8,128)(2,1)S(1)} %get-tuple-element.86.after_ref), channel_id=1, source_target_pairs={{0,1},{1,2},{2,3},{3,4},{4,5},{5,6},{6,7},{7,0},{8,9},{9,10},{10,1... | collective-permute-start | bytes 147464 | tf_op jit(solution)/shard_map/ppermute | solution.py:726
  75.1 5.8 %collective-permute-start.13 = (bf16[3,16,512]{2,1,0:T(8,128)(2,1)S(1)}, bf16[3,16,512]{2,1,0:T(8,128)(2,1)S(1)}, u32[]{:S(2)}, u32[]{:S(2)}) collective-permute-start(bf16[3,16,512]{2,1,0:T(8,128)(2,1)S(1)} %get-tuple-element.90), channel_id=1, source_target_pairs={{0,7},{1,0},{2,1},{3,2},{4,3},{5,4},{6,5},{7,6},{8,15},{9,8},{10,9... | collective-permute-start | bytes 147464 | tf_op jit(solution)/shard_map/ppermute | solution.py:726
  (1 other events, 1.6 us)

commit v8 on v7

--- a/solution.py
+++ b/solution.py
@@ -537,7 +537,7 @@
             pltpu.make_async_copy(inner_ref, inner_here, here.at[2]),
             pltpu.make_async_copy(mesh_ref, mesh_here, here.at[3]),
         ]
-        for copy in copies:
+        for copy in copies[:2]:
             copy.start()
         target, inner_ref, mesh_ref = target_here, inner_here, mesh_here
     else:
@@ -558,6 +558,8 @@
         pre = dot(one_hot(senders, table.shape[0] - padded, slots), table[padded:])
         for copy in waiting[:2]:
             copy.wait()
+        for copy in waiting[2:]:
+            copy.start()
         waiting = []
         own = jnp.where(senders < slots, senders, jnp.int16(-1))
         pre = pre + dot(one_hot(own, padded), table[:padded])

time: 87.3 us -> 87.3 us (level)
  no operation moved by 1% of the time
where the time goes in v8:
time: 87.3 us; the launch traced here: 86.9 us
  Pallas kernels  43.2 us (49%)
  starting transfers between devices  30.2 us (35%)
  waiting for transfers between devices  11.4 us (13%)
  between operations  1.81 us (2%)
    ppermute x14, starting transfers between devices, move(): return lax.ppermute(value, AXES, pairs)  24.3 us
    pallas_call x2, Pallas kernels, round_part(): pl.pallas_call(functools.partial(round_kernel, section, places, last), in...  9.44 us
    pallas_call x1, Pallas kernels, encode(): pl.pallas_call(functools.partial(encode_kernel, count), out_shape=[pltpu....  7.58 us
    all_to_all x1, waiting for transfers between devices, per_device(): lax.all_to_all(sent, AXES, split_axis=0, concat_axis=0, tiled=True)  6.85 us
    all_to_all x1, starting transfers between devices, per_device(): lax.all_to_all(sent, AXES, split_axis=0, concat_axis=0, tiled=True)  5.94 us
    pallas_call x1, Pallas kernels, decode_part(): pl.pallas_call(functools.partial(decode_kernel, section, places, split),...  5.93 us
    pallas_call x1, Pallas kernels, encode_local(): pl.pallas_call(functools.partial(encode_local_kernel, section), in_specs=...  5.36 us
    ppermute x14, waiting for transfers between devices, move(): return lax.ppermute(value, AXES, pairs)  4.59 us
  transfers between devices with their start and end apart: 15, of which 5 were waited for; matrix products, arithmetic and copies ran while one was open for 0% of the time, Pallas kernels for 21%

profile of v8, /device:TPU:0, one launch (start us, length us, event | category | flops | bytes accessed | tf_op | source)
XLA Modules:
  0.0 86.9 jit_solution(2423096703536424889)
XLA Ops:
  0.6 1.8 %pick_pair.1 = (bf16[384,512]{1,0:T(8,128)(2,1)S(1)}, bf16[1024,512]{1,0:T(8,128)(2,1)S(1)}, s32[1,8,128]{2,1,0:T(8,128)S(1)}) custom-call(bf16[1024,512]{1,0:T(8,128)(2,1)} %refs_3_.3, s32[1,8,128]{2,1,0:T(8,128)} %rim_hbm.1), custom_call_target="tpu_custom_call" | custom-call | tf_op jit(solution)/shard_map/pick_pair/pallas_call | solution.py:199
  3.0 1.6 %pick_rest.1 = (bf16[128,512]{1,0:T(8,128)(2,1)S(1)}, bf16[128,512]{1,0:T(8,128)(2,1)S(1)}, bf16[3,512,512]{2,1,0:T(8,128)(2,1)S(1)}, bf16[192,512]{1,0:T(8,128)...) custom-call(bf16[1024,512]{1,0:T(8,128)(2,1)S(1)} %get-tuple-element.48.rows_ref.grid_ref, ...), custom_call_target="tpu_custom_call" | custom-call | tf_op jit(solution)/shard_map/pick_rest/pallas_call | solution.py:257
  4.7 2.6 %collective-permute-start.1 = (bf16[256,512]{1,0:T(8,128)(2,1)S(1)}, bf16[256,512]{1,0:T(8,128)(2,1)S(1)}, u32[]{:S(2)}, u32[]{:S(2)}) collective-permute-start(bf16[256,512]{1,0:T(8,128)(2,1)S(1)} %get-tuple-element.57.after_ref), channel_id=1, source_target_pairs={{0,1},{1,2},{2,3},{3,4},{4,5},{5,6},{6,7},{7,0},{8,9},{9,10},{10,1... | collective-permute-start | bytes 786440 | tf_op jit(solution)/shard_map/ppermute | solution.py:728
  7.3 3.1 %collective-permute-start.2 = (bf16[256,512]{1,0:T(8,128)(2,1)S(1)}, bf16[256,512]{1,0:T(8,128)(2,1)S(1)}, u32[]{:S(2)}, u32[]{:S(2)}) collective-permute-start(bf16[256,512]{1,0:T(8,128)(2,1)S(1)} %get-tuple-element.61), channel_id=1, source_target_pairs={{0,7},{1,0},{2,1},{3,2},{4,3},{5,4},{6,5},{7,6},{8,15},{9,8},{10,9... | collective-permute-start | bytes 786440 | tf_op jit(solution)/shard_map/ppermute | solution.py:728
  12.4 1.4 %collective-permute-start.5 = (bf16[128,512]{1,0:T(8,128)(2,1)S(1)}, bf16[128,512]{1,0:T(8,128)(2,1)S(1)}, u32[]{:S(2)}, u32[]{:S(2)}) collective-permute-start(bf16[128,512]{1,0:T(8,128)(2,1)S(1)} %get-tuple-element.64), channel_id=1, source_target_pairs={{0,24},{1,25},{2,26},{3,27},{4,28},{5,29},{6,30},{7,31},{8,16},{9,... | collective-permute-start | bytes 393224 | tf_op jit(solution)/shard_map/ppermute | solution.py:728
  13.7 5.4 %encode_local.1 = (f32[3072,512]{1,0:T(8,128)S(1)}, f32[192,512]{1,0:T(8,128)S(1)}, bf16[5,512,512]{2,1,0:T(8,128)(2,1)S(1)}) custom-call(bf16[1024,512]{1,0:T(8,128)(2,1)S(1)} %get-tuple-element.48.rows_ref.grid_ref, bf16[3,512,512]{2,1,0:T(8,128)(2,1)S(1)} %get-tuple-element.50.stack, bf16[192,512]{1,0:T(8,128)(2,1)S(1)} %get-tuple-element.51.mesh_ref.refs_4_, ...), custom_call_target="tpu_custom_call" | custom-call | tf_op jit(solution)/shard_map/encode_local/pallas_call | solution.py:350
  19.1 1.8 %collective-permute-done.1.refs_6_ = bf16[256,512]{1,0:T(8,128)(2,1)S(1)} collective-permute-done((bf16[256,512]{1,0:T(8,128)(2,1)S(1)}, bf16[256,512]{1,0:T(8,128)(2,1)S(1)}, u32[]{:S(2)}, u32[]{:S(2)}) %collective-permute-start.1) | collective-permute-done | bytes 262176 | tf_op jit(solution)/shard_map/ppermute | solution.py:728
  20.9 2.5 %collective-permute-done.2.refs_7_ = bf16[256,512]{1,0:T(8,128)(2,1)S(1)} collective-permute-done((bf16[256,512]{1,0:T(8,128)(2,1)S(1)}, bf16[256,512]{1,0:T(8,128)(2,1)S(1)}, u32[]{:S(2)}, u32[]{:S(2)}) %collective-permute-start.2) | collective-permute-done | bytes 262176 | tf_op jit(solution)/shard_map/ppermute | solution.py:728
  23.4 7.6 %encode.1 = (bf16[192,512]{1,0:T(8,128)(2,1)S(1)}, bf16[256,512]{1,0:T(8,128)(2,1)S(1)}, bf16[3,16,512]{2,1,0:T(8,128)(2,1)S(1)}, bf16[3,16,512]{2,1,0:T(8,128)(...) custom-call(f32[3072,512]{1,0:T(8,128)S(1)} %get-tuple-element.58.refs_0_, ...), custom_call_target="tpu_custom_call" | custom-call | tf_op jit(solution)/shard_map/encode/pallas_call | solution.py:412
  31.0 4.1 %collective-permute-start.6 = (bf16[3,16,512]{2,1,0:T(8,128)(2,1)S(1)}, bf16[3,16,512]{2,1,0:T(8,128)(2,1)S(1)}, u32[]{:S(2)}, u32[]{:S(2)}) collective-permute-start(bf16[3,16,512]{2,1,0:T(8,128)(2,1)S(1)} %get-tuple-element.69), channel_id=1, source_target_pairs={{0,8},{1,9},{2,10},{3,11},{4,12},{5,13},{6,14},{7,15},{8,16},{9,17... | collective-permute-start | bytes 147464 | tf_op jit(solution)/shard_map/ppermute | solution.py:728
  35.1 1.6 %receivers.1 = (bf16[256,512]{1,0:T(8,128)(2,1)S(1)}, f32[192,512]{1,0:T(8,128)S(1)}) custom-call(bf16[192,512]{1,0:T(8,128)(2,1)S(1)} %get-tuple-element.66.mesh_ref.refs_5_, f32[4,512]{1,0:T(4,128)S(1)} %copy-done.3, f32[4,512]{1,0:T(4,128)S(1)} %copy-done.4, bf16[4,2,512,512]{3,2,1,0:T(8,128)(2,1)} %edge_first.11, bf16[4,2,512,512]{3,2,1,0:T(8,128)(2,1)} %node_first.11), custom_call_target="tpu_custom_call" | custom-call | tf_op jit(solution)/shard_map/receivers/pallas_call | solution.py:480
  36.9 4.7 %collective-permute-start.9 = (bf16[3,16,512]{2,1,0:T(8,128)(2,1)S(1)}, bf16[3,16,512]{2,1,0:T(8,128)(2,1)S(1)}, u32[]{:S(2)}, u32[]{:S(2)}) collective-permute-start(bf16[3,16,512]{2,1,0:T(8,128)(2,1)S(1)} %get-tuple-element.74), channel_id=1, source_target_pairs={{0,7},{1,0},{2,1},{3,2},{4,3},{5,4},{6,5},{7,6},{8,15},{9,8},{10,9... | collective-permute-start | bytes 147464 | tf_op jit(solution)/shard_map/ppermute | solution.py:728
  42.5 1.6 %layers.1.refs_4_ = bf16[4,512,512]{2,1,0:T(8,128)(2,1)S(1)} custom-call(bf16[3,16,512]{2,1,0:T(8,128)(2,1)S(1)} %get-tuple-element.73.after_ref, bf16[4,2,512,512]{3,2,1,0:T(8,128)(2,1)} %edge_first.11, bf16[4,512,512]{2,1,0:T(8,128)(2,1)} %edge_second.7, bf16[4,2,512,512]{3,2,1,0:T(8,128)(2,1)} %node_first.11, bf16[4,512,512]{2,1,0:T(8,128)(2,1)} %node_second.7), custom_call_target="tpu_custom_call" | custom-call | tf_op jit(solution)/shard_map/layers/pallas_call | solution.py:507
  44.1 4.3 %round_part.2 = (bf16[192,512]{1,0:T(8,128)(2,1)}, bf16[256,512]{1,0:T(8,128)(2,1)}, bf16[256,512]{1,0:T(8,128)(2,1)}) custom-call(s32[1,2,1536]{2,1,0:T(2,128)S(1)} %copy-done.6, bf16[256,512]{1,0:T(8,128)(2,1)S(1)} %get-tuple-element.65.refs_1_, bf16[256,512]{1,0:T(8,128)(2,1)S(1)} %get-tuple-element.67.after_ref.refs_2_, ...), custom_call_target="tpu_custom_call" | custom-call | tf_op jit(solution)/shard_map/round_part/pallas_call | solution.py:597
  48.4 5.9 %all-to-all-start = ((bf16[32,8,512]{2,1,0:T(8,128)(2,1)}), bf16[32,8,512]{2,1,0:T(8,128)(2,1)S(1)}, u32[]{:S(2)}, u32[]{:S(2)}) async-start(bf16[32,8,512]{2,1,0:T(8,128)(2,1)} %bitcast), calls=%async_computation | async-start | bytes 524288 | tf_op jit(solution)/shard_map/all_to_all | solution.py:785
  54.4 3.8 %prepare.1 = (bf16[256,512]{1,0:T(8,128)(2,1)}, f32[192,512]{1,0:T(8,128)}, bf16[4,512,512]{2,1,0:T(8,128)(2,1)S(1)}) custom-call(bf16[192,512]{1,0:T(8,128)(2,1)} %get-tuple-element.76.mesh_ref.refs_5_, f32[4,512]{1,0:T(4,128)S(1)} %copy-done.3, f32[4,512]{1,0:T(4,128)S(1)} %copy-done.4, bf16[4,2,512,512]{3,2,1,0:T(8,128)(2,1)} %edge_first.11, ...), custom_call_target="tpu_custom_call" | custom-call | tf_op jit(solution)/shard_map/prepare/pallas_call | solution.py:451
  58.2 6.8 %all-to-all-done = bf16[32,8,512]{2,1,0:T(8,128)(2,1)S(1)} async-done(((bf16[32,8,512]{2,1,0:T(8,128)(2,1)}), bf16[32,8,512]{2,1,0:T(8,128)(2,1)S(1)}, u32[]{:S(2)}, u32[]{:S(2)}) %all-to-all-start) | async-done | bytes 262176 | tf_op jit(solution)/shard_map/all_to_all | solution.py:785
  65.0 5.1 %round_part.3 = (bf16[192,512]{1,0:T(8,128)(2,1)}, bf16[256,512]{1,0:T(8,128)(2,1)S(1)}, bf16[3,16,512]{2,1,0:T(8,128)(2,1)S(1)}, bf16[3,16,512]{2,1,0:T(8,128)(...) custom-call(s32[1,2,1536]{2,1,0:T(2,128)S(1)} %copy-done.7, ...), custom_call_target="tpu_custom_call" | custom-call | tf_op jit(solution)/shard_map/round_part/pallas_call | solution.py:597
  70.3 1.7 %collective-permute-start.11 = (bf16[3,16,512]{2,1,0:T(8,128)(2,1)S(1)}, bf16[3,16,512]{2,1,0:T(8,128)(2,1)S(1)}, u32[]{:S(2)}, u32[]{:S(2)}) collective-permute-start(bf16[3,16,512]{2,1,0:T(8,128)(2,1)S(1)} %get-tuple-element.83), channel_id=1, source_target_pairs={{0,24},{1,25},{2,26},{3,27},{4,28},{5,29},{6,30},{7,31},{8,0},{9,1... | collective-permute-start | bytes 147464 | tf_op jit(solution)/shard_map/ppermute | solution.py:728
  72.0 1.9 %grid_receivers.1 = (bf16[1024,512]{1,0:T(8,128)(2,1)S(1)}, bf16[1,512,512]{2,1,0:T(8,128)(2,1)S(1)}) custom-call(bf16[1024,512]{1,0:T(8,128)(2,1)S(1)} %copy-done, f32[4,512]{1,0:T(4,128)S(1)} %copy-done.3, bf16[4,2,512,512]{3,2,1,0:T(8,128)(2,1)} %edge_first.11, bf16[4,512,512]{2,1,0:T(8,128)(2,1)} %edge_second.7), custom_call_target="tpu_custom_call" | custom-call | tf_op jit(solution)/shard_map/grid_receivers/pallas_call | solution.py:625
  74.0 1.1 %collective-permute-start.12 = (bf16[3,16,512]{2,1,0:T(8,128)(2,1)S(1)}, bf16[3,16,512]{2,1,0:T(8,128)(2,1)S(1)}, u32[]{:S(2)}, u32[]{:S(2)}) collective-permute-start(bf16[3,16,512]{2,1,0:T(8,128)(2,1)S(1)} %get-tuple-element.86.after_ref), channel_id=1, source_target_pairs={{0,1},{1,2},{2,3},{3,4},{4,5},{5,6},{6,7},{7,0},{8,9},{9,10},{10,1... | collective-permute-start | bytes 147464 | tf_op jit(solution)/shard_map/ppermute | solution.py:728
  75.1 3.7 %collective-permute-start.13 = (bf16[3,16,512]{2,1,0:T(8,128)(2,1)S(1)}, bf16[3,16,512]{2,1,0:T(8,128)(2,1)S(1)}, u32[]{:S(2)}, u32[]{:S(2)}) collective-permute-start(bf16[3,16,512]{2,1,0:T(8,128)(2,1)S(1)} %get-tuple-element.90), channel_id=1, source_target_pairs={{0,7},{1,0},{2,1},{3,2},{4,3},{5,4},{6,5},{7,6},{8,15},{9,8},{10,9... | collective-permute-start | bytes 147464 | tf_op jit(solution)/shard_map/ppermute | solution.py:728
  78.8 1.9 %decode_local.1 = (bf16[3,1024,512]{2,1,0:T(8,128)(2,1)S(1)}, bf16[3,512,512]{2,1,0:T(8,128)(2,1)S(1)}) custom-call(bf16[1024,512]{1,0:T(8,128)(2,1)S(1)} %get-tuple-element.47.after_ref.target_ref, bf16[256,512]{1,0:T(8,128)(2,1)S(1)} %get-tuple-element.81.table_ref, s32[1,3,1024]{2,1,0:T(4,128)S(1)} %copy.24.edges_ref.refs_4_, ...), custom_call_target="tpu_custom_call" | custom-call | tf_op jit(solution)/shard_map/decode_local/pallas_call | solution.py:659
  80.8 5.9 %decode_part.1 = bf16[1024,512]{1,0:T(8,128)(2,1)} custom-call(bf16[3,1024,512]{2,1,0:T(8,128)(2,1)S(1)} %get-tuple-element.87.refs_0_, bf16[1,512,512]{2,1,0:T(8,128)(2,1)S(1)} %get-tuple-element.88.refs_1_, bf16[3,512,512]{2,1,0:T(8,128)(2,1)S(1)} %get-tuple-element.89.refs_2_, bf16[1024,512]{1,0:T(8,128)(2,1)S(1)} %copy-done, ...), custom_call_target="tpu_custom_call" | custom-call | tf_op jit(solution)/shard_map/decode_part/pallas_call | solution.py:700
  (49 shorter events, 3.1 us)
Async XLA Ops:
  2.4 2.2 %collective-permute-start = (bf16[384,512]{1,0:T(8,128)(2,1)S(1)}, bf16[384,512]{1,0:T(8,128)(2,1)S(1)}, u32[]{:S(2)}, u32[]{:S(2)}) collective-permute-start(bf16[384,512]{1,0:T(8,128)(2,1)S(1)} %get-tuple-element.54), channel_id=1, source_target_pairs={{0,8},{1,9},{2,10},{3,11},{4,12},{5,13},{6,14},{7,15},{8,0},{9,1},... | collective-permute-start | bytes 1179656 | tf_op jit(solution)/shard_map/ppermute | solution.py:728
  4.7 16.2 %collective-permute-start.1 = (bf16[256,512]{1,0:T(8,128)(2,1)S(1)}, bf16[256,512]{1,0:T(8,128)(2,1)S(1)}, u32[]{:S(2)}, u32[]{:S(2)}) collective-permute-start(bf16[256,512]{1,0:T(8,128)(2,1)S(1)} %get-tuple-element.57.after_ref), channel_id=1, source_target_pairs={{0,1},{1,2},{2,3},{3,4},{4,5},{5,6},{6,7},{7,0},{8,9},{9,10},{10,1... | collective-permute-start | bytes 786440 | tf_op jit(solution)/shard_map/ppermute | solution.py:728
  7.3 16.2 %collective-permute-start.2 = (bf16[256,512]{1,0:T(8,128)(2,1)S(1)}, bf16[256,512]{1,0:T(8,128)(2,1)S(1)}, u32[]{:S(2)}, u32[]{:S(2)}) collective-permute-start(bf16[256,512]{1,0:T(8,128)(2,1)S(1)} %get-tuple-element.61), channel_id=1, source_target_pairs={{0,7},{1,0},{2,1},{3,2},{4,3},{5,4},{6,5},{7,6},{8,15},{9,8},{10,9... | collective-permute-start | bytes 786440 | tf_op jit(solution)/shard_map/ppermute | solution.py:728
  11.0 8.1 %collective-permute-start.3 = (bf16[128,512]{1,0:T(8,128)(2,1)S(1)}, bf16[128,512]{1,0:T(8,128)(2,1)S(1)}, u32[]{:S(2)}, u32[]{:S(2)}) collective-permute-start(bf16[128,512]{1,0:T(8,128)(2,1)S(1)} %get-tuple-element.62), channel_id=1, source_target_pairs={{8,17},{9,18},{10,19},{11,20},{12,21},{13,22},{14,23},{15,16},{16,... | collective-permute-start | bytes 393224 | tf_op jit(solution)/shard_map/ppermute | solution.py:728
  11.7 7.4 %collective-permute-start.4 = (bf16[128,512]{1,0:T(8,128)(2,1)S(1)}, bf16[128,512]{1,0:T(8,128)(2,1)S(1)}, u32[]{:S(2)}, u32[]{:S(2)}) collective-permute-start(bf16[128,512]{1,0:T(8,128)(2,1)S(1)} %get-tuple-element.63), channel_id=1, source_target_pairs={{8,23},{9,16},{10,17},{11,18},{12,19},{13,20},{14,21},{15,22},{16,... | collective-permute-start | bytes 393224 | tf_op jit(solution)/shard_map/ppermute | solution.py:728
  12.4 6.8 %collective-permute-start.5 = (bf16[128,512]{1,0:T(8,128)(2,1)S(1)}, bf16[128,512]{1,0:T(8,128)(2,1)S(1)}, u32[]{:S(2)}, u32[]{:S(2)}) collective-permute-start(bf16[128,512]{1,0:T(8,128)(2,1)S(1)} %get-tuple-element.64), channel_id=1, source_target_pairs={{0,24},{1,25},{2,26},{3,27},{4,28},{5,29},{6,30},{7,31},{8,16},{9,... | collective-permute-start | bytes 393224 | tf_op jit(solution)/shard_map/ppermute | solution.py:728
  13.7 9.7 %copy-start.5 = (s32[1,8,16]{2,1,0:T(8,128)S(1)}, s32[1,8,16]{2,1,0:T(8,128)}, u32[]{:S(2)}) copy-start(s32[1,8,16]{2,1,0:T(8,128)} %refs_9_.2) | copy-start | bytes 1540
  23.4 11.7 %copy-start.3 = (f32[4,512]{1,0:T(4,128)S(1)}, f32[4,512]{1,0:T(4,128)}, u32[]{:S(2)}) copy-start(f32[4,512]{1,0:T(4,128)} %bias_ref.5) | copy-start | bytes 24580
  23.4 11.7 %copy-start.4 = (f32[4,512]{1,0:T(4,128)S(1)}, f32[4,512]{1,0:T(4,128)}, u32[]{:S(2)}) copy-start(f32[4,512]{1,0:T(4,128)} %refs_10_.4) | copy-start | bytes 24580
  31.0 5.7 %collective-permute-start.6 = (bf16[3,16,512]{2,1,0:T(8,128)(2,1)S(1)}, bf16[3,16,512]{2,1,0:T(8,128)(2,1)S(1)}, u32[]{:S(2)}, u32[]{:S(2)}) collective-permute-start(bf16[3,16,512]{2,1,0:T(8,128)(2,1)S(1)} %get-tuple-element.69), channel_id=1, source_target_pairs={{0,8},{1,9},{2,10},{3,11},{4,12},{5,13},{6,14},{7,15},{8,16},{9,17... | collective-permute-start | bytes 147464 | tf_op jit(solution)/shard_map/ppermute | solution.py:728
  35.1 1.8 %collective-permute-start.7 = (bf16[3,16,512]{2,1,0:T(8,128)(2,1)S(1)}, bf16[3,16,512]{2,1,0:T(8,128)(2,1)S(1)}, u32[]{:S(2)}, u32[]{:S(2)}) collective-permute-start(bf16[3,16,512]{2,1,0:T(8,128)(2,1)S(1)} %get-tuple-element.70), channel_id=1, source_target_pairs={{0,24},{1,25},{2,26},{3,27},{4,28},{5,29},{6,30},{7,31},{8,0},{9,1... | collective-permute-start | bytes 147464 | tf_op jit(solution)/shard_map/ppermute | solution.py:728
  35.1 7.2 %copy-start.9 = (s32[1,32,8]{1,2,0:T(8,128)S(1)}, s32[1,32,8]{1,2,0:T(8,128)}, u32[]{:S(2)}) copy-start(s32[1,32,8]{1,2,0:T(8,128)} %param.23) | copy-start | bytes 3076
  36.9 7.2 %collective-permute-start.8 = (bf16[3,16,512]{2,1,0:T(8,128)(2,1)S(1)}, bf16[3,16,512]{2,1,0:T(8,128)(2,1)S(1)}, u32[]{:S(2)}, u32[]{:S(2)}) collective-permute-start(bf16[3,16,512]{2,1,0:T(8,128)(2,1)S(1)} %get-tuple-element.73.after_ref), channel_id=1, source_target_pairs={{0,1},{1,2},{2,3},{3,4},{4,5},{5,6},{6,7},{7,0},{8,9},{9,10},{10,1... | collective-permute-start | bytes 147464 | tf_op jit(solution)/shard_map/ppermute | solution.py:728
  36.9 7.2 %collective-permute-start.9 = (bf16[3,16,512]{2,1,0:T(8,128)(2,1)S(1)}, bf16[3,16,512]{2,1,0:T(8,128)(2,1)S(1)}, u32[]{:S(2)}, u32[]{:S(2)}) collective-permute-start(bf16[3,16,512]{2,1,0:T(8,128)(2,1)S(1)} %get-tuple-element.74), channel_id=1, source_target_pairs={{0,7},{1,0},{2,1},{3,2},{4,3},{5,4},{6,5},{7,6},{8,15},{9,8},{10,9... | collective-permute-start | bytes 147464 | tf_op jit(solution)/shard_map/ppermute | solution.py:728
  42.5 1.7 %copy-start.1 = (f32[4,512]{1,0:T(4,128)S(1)}, f32[4,512]{1,0:T(4,128)}, u32[]{:S(2)}) copy-start(f32[4,512]{1,0:T(4,128)} %refs_9_.3) | copy-start | bytes 24580
  42.5 1.7 %copy-start.2 = (f32[4,512]{1,0:T(4,128)S(1)}, f32[4,512]{1,0:T(4,128)}, u32[]{:S(2)}) copy-start(f32[4,512]{1,0:T(4,128)} %refs_11_.3) | copy-start | bytes 24580
  48.4 16.6 %all-to-all-start = ((bf16[32,8,512]{2,1,0:T(8,128)(2,1)}), bf16[32,8,512]{2,1,0:T(8,128)(2,1)S(1)}, u32[]{:S(2)}, u32[]{:S(2)}) async-start(bf16[32,8,512]{2,1,0:T(8,128)(2,1)} %bitcast), calls=%async_computation | async-start | bytes 524288 | tf_op jit(solution)/shard_map/all_to_all | solution.py:785
  54.4 10.6 %copy-start.7 = (s32[1,2,1536]{2,1,0:T(2,128)S(1)}, s32[1,2,1536]{2,1,0:T(2,128)}, u32[]{:S(2)}) copy-start(s32[1,2,1536]{2,1,0:T(2,128)} %refs_0_.5) | copy-start | bytes 36868
  58.2 13.8 %copy-start = (bf16[1024,512]{1,0:T(8,128)(2,1)S(1)}, bf16[1024,512]{1,0:T(8,128)(2,1)}, u32[]{:S(2)}) copy-start(bf16[1024,512]{1,0:T(8,128)(2,1)} %refs_3_.3) | copy-start | bytes 3145732
  70.2 3.8 %collective-permute-start.10 = (bf16[3,16,512]{2,1,0:T(8,128)(2,1)S(1)}, bf16[3,16,512]{2,1,0:T(8,128)(2,1)S(1)}, u32[]{:S(2)}, u32[]{:S(2)}) collective-permute-start(bf16[3,16,512]{2,1,0:T(8,128)(2,1)S(1)} %get-tuple-element.82), channel_id=1, source_target_pairs={{0,8},{1,9},{2,10},{3,11},{4,12},{5,13},{6,14},{7,15},{8,16},{9,17... | collective-permute-start | bytes 147464 | tf_op jit(solution)/shard_map/ppermute | solution.py:728
  70.2 8.5 %copy-start.8 = (s32[1,3,1024]{2,0,1:T(1,128)S(1)}, s32[1,3,1024]{2,0,1:T(1,128)}, u32[]{:S(2)}) copy-start(s32[1,3,1024]{2,0,1:T(1,128)} %param.27) | copy-start | bytes 36868
  70.3 3.7 %collective-permute-start.11 = (bf16[3,16,512]{2,1,0:T(8,128)(2,1)S(1)}, bf16[3,16,512]{2,1,0:T(8,128)(2,1)S(1)}, u32[]{:S(2)}, u32[]{:S(2)}) collective-permute-start(bf16[3,16,512]{2,1,0:T(8,128)(2,1)S(1)} %get-tuple-element.83), channel_id=1, source_target_pairs={{0,24},{1,25},{2,26},{3,27},{4,28},{5,29},{6,30},{7,31},{8,0},{9,1... | collective-permute-start | bytes 147464 | tf_op jit(solution)/shard_map/ppermute | solution.py:728
  74.0 6.8 %collective-permute-start.12 = (bf16[3,16,512]{2,1,0:T(8,128)(2,1)S(1)}, bf16[3,16,512]{2,1,0:T(8,128)(2,1)S(1)}, u32[]{:S(2)}, u32[]{:S(2)}) collective-permute-start(bf16[3,16,512]{2,1,0:T(8,128)(2,1)S(1)} %get-tuple-element.86.after_ref), channel_id=1, source_target_pairs={{0,1},{1,2},{2,3},{3,4},{4,5},{5,6},{6,7},{7,0},{8,9},{9,10},{10,1... | collective-permute-start | bytes 147464 | tf_op jit(solution)/shard_map/ppermute | solution.py:728
  75.1 5.8 %collective-permute-start.13 = (bf16[3,16,512]{2,1,0:T(8,128)(2,1)S(1)}, bf16[3,16,512]{2,1,0:T(8,128)(2,1)S(1)}, u32[]{:S(2)}, u32[]{:S(2)}) collective-permute-start(bf16[3,16,512]{2,1,0:T(8,128)(2,1)S(1)} %get-tuple-element.90), channel_id=1, source_target_pairs={{0,7},{1,0},{2,1},{3,2},{4,3},{5,4},{6,5},{7,6},{8,15},{9,8},{10,9... | collective-permute-start | bytes 147464 | tf_op jit(solution)/shard_map/ppermute | solution.py:728
  (1 other events, 1.6 us)
